TPU v7x, 32 devices: a whole 2x2x4 slice. The times are simulated.
32 devices in a mesh: groups: 2 (over y), ctx: 8 (over z, x), head: 2 (over core).
Axes of the slice: x: 2, y: 2, z: 4, core: 2. Of those that a mesh axis runs over, the one named last changes fastest.
Arguments:
- queries: bfloat16 [1024, 4096], P(('groups', 'ctx', 'head')), parts along dimension 0, may hold values from -6 to 6
- latents: bfloat16 [16, 64, 1280], P(('groups', 'ctx')), parts along dimension 0, may hold values from -6 to 6
- image_span: int32 [10, 2], P('groups'), parts along dimension 0, may hold values from 0 to 512, as said below
- image_owner: int32 [10], P('groups'), parts along dimension 0, may hold values from 0 to 7, as said below
- kv_weight: bfloat16 [1280, 2, 4096], P('ctx', None, 'head'), may hold values from -0.15625 to 0.15625
- attn_gate: float32 [4096], P('head'), may hold values from -1.5 to 1.5
Outputs:
- context: bfloat16 [1024, 4096], P(('groups', 'ctx', 'head')), parts along dimension 0
There are 2 independent parts, one for each index of `groups`. A program takes and returns all parts, laid end to end along the dimension named above; an argument that names none is the same for every part. Nothing has to cross between parts.
Inputs may be any that keep to these rules, and one draw needn't show every extreme that they name: `image_span`: images are in order of position; spans are disjoint and not empty; each image starts 22 or more tokens after the previous one starts. The tokens of one ctx index, [c * 64, (c + 1) * 64), meet at most 4 spans, and some ctx index meets exactly 4. `image_owner`: owners are distinct; stores of ctx indices that own no image are not read.
All inputs are finite; a program needn't handle non-finite values.
Results may differ from a plain program's by a relative error of at most 0.0069.
Values may be sent and summed in bfloat16 or wider, within the bound.
No kernel may reach another device: no remote copies, remote signals or barrier semaphores. Data moves between devices by JAX's collectives and lax.ppermute only.
A program may use at most 64 MiB of HBM per device.

v0:
```python
import jax
import jax.numpy as jnp
from jax import lax
from jax.sharding import PartitionSpec as P

DH = 128
MAXIMG = 4


def head_norm(x, size):
    shaped = x.reshape(x.shape[:-1] + (x.shape[-1] // size, size))
    mean = jnp.mean(shaped, -1, keepdims=True)
    centered = shaped - mean
    spread = jnp.mean(centered * centered, -1, keepdims=True)
    return (centered * lax.rsqrt(spread + 1e-05)).reshape(x.shape)


def shards(queries, latents, image_span, image_owner, kv_weight, attn_gate):
    ctx_count = lax.axis_size("ctx")
    rows = lax.all_to_all(queries, "head", split_axis=1, concat_axis=0, tiled=True)
    tok = rows.shape[0]
    width = rows.shape[1]
    lat = latents.shape[1]
    images = image_span.shape[0]
    query_norm = head_norm(rows.astype(jnp.float32), DH).astype(jnp.bfloat16)
    starts = image_span[:, 0]
    ends = image_span[:, 1]
    block_low = jnp.arange(ctx_count, dtype=jnp.int32) * tok
    meets = (starts[None, :] < (block_low + tok)[:, None]) & (ends[None, :] > block_low[:, None])
    counts = jnp.sum(meets.astype(jnp.int32), 1)
    firsts = jnp.sum((ends[None, :] <= block_low[:, None]).astype(jnp.int32), 1)
    slot_iota = jnp.arange(MAXIMG, dtype=jnp.int32)
    wanted = jnp.minimum(firsts[:, None] + slot_iota[None, :], images - 1)
    live = slot_iota[None, :] < counts[:, None]
    holders = image_owner[wanted]
    pieces = lax.all_to_all(latents, "ctx", split_axis=2, concat_axis=0, tiled=True)
    outgoing = jnp.where(live[:, :, None, None], pieces[holders], jnp.zeros((), jnp.bfloat16))
    panels = lax.all_to_all(outgoing, "ctx", split_axis=0, concat_axis=3, tiled=True)
    gathered = lax.all_gather(kv_weight, "ctx", axis=0, tiled=True)
    flat_weight = gathered.reshape(gathered.shape[0], 2 * width)
    both = jnp.dot(
        panels.reshape(MAXIMG * lat, panels.shape[3]),
        flat_weight,
        preferred_element_type=jnp.float32,
    )
    keys_out = head_norm(both[:, :width], DH).astype(jnp.bfloat16)
    values_out = both[:, width:].astype(jnp.bfloat16)
    mine = lax.axis_index("ctx")
    positions = mine * tok + jnp.arange(tok, dtype=jnp.int32)
    inside = (positions[:, None] >= starts[None, :]) & (positions[:, None] < ends[None, :])
    has_image = jnp.any(inside, 1)
    which = jnp.sum(jnp.where(inside, jnp.arange(images, dtype=jnp.int32)[None, :], 0), 1)
    my_first = jnp.sum((ends <= mine * tok).astype(jnp.int32))
    slot = which - my_first
    heads_here = width // DH
    query_heads = query_norm.reshape(tok, heads_here, DH)
    key_heads = keys_out.reshape(MAXIMG * lat, heads_here, DH)
    value_heads = values_out.reshape(MAXIMG * lat, heads_here, DH)
    scores = jnp.einsum(
        "thd,khd->thk", query_heads, key_heads, preferred_element_type=jnp.float32
    ) * DH ** (-0.5)
    owner_slot = jnp.arange(MAXIMG * lat, dtype=jnp.int32) // lat
    selected = (has_image[:, None] & (owner_slot[None, :] == slot[:, None])).astype(jnp.float32)
    weighted = jnp.exp(scores) * selected[:, None, :]
    total = (
        jnp.sum(weighted, -1, keepdims=True) + (1.0 - has_image.astype(jnp.float32))[:, None, None]
    )
    probs = (weighted / total).astype(jnp.bfloat16)
    attended = jnp.einsum("thk,khd->thd", probs, value_heads, preferred_element_type=jnp.float32)
    attended = attended.reshape(tok, width)
    gated = (jnp.tanh(attn_gate)[None, :] * attended).astype(jnp.bfloat16)
    return lax.all_to_all(gated, "head", split_axis=0, concat_axis=1, tiled=True)


def solution(mesh):
    placed = (
        P(("groups", "ctx", "head"), None),
        P(("groups", "ctx"), None, None),
        P("groups", None),
        P("groups"),
        P("ctx", None, "head"),
        P("head"),
    )
    return jax.shard_map(
        shards,
        mesh=mesh,
        in_specs=placed,
        out_specs=P(("groups", "ctx", "head"), None),
        check_vma=False,
    )
```

profile of v0, /device:TPU:0, one launch (start us, length us, event | category | flops | bytes accessed | tf_op | source)
XLA Modules:
  0.0 228.6 jit_solution(6265741477507643769)
XLA Ops:
  6.5 0.0 copy-start
  6.5 0.0 copy-start.5
  6.5 0.0 all-gather.2.cloned.1.call-start
  6.5 0.7 all-gather.2.cloned.1.call-update
  7.3 1.7 copy.80
  8.9 3.4 %all-to-all-start.2 = ((bf16[32,2,2048]{2,0,1:T(8,128)(2,1)}), bf16[32,2,2048]{2,0,1:T(8,128)(2,1)S(1)}, u32[]{:S(2)}, u32[]{:S(2)}) async-start(bf16[32,2,2048]{2,0,1:T(8,128)(2,1)} %bitcast.80), calls=%async_computation.2 | async-start | bytes 524288 | tf_op jit(solution)/shard_map/all_to_all | solution.py:20
  12.4 0.0 copy-done.5
  12.4 0.2 convert_reduce_fusion.1
  12.6 0.1 compare_select_fusion.1
  12.7 0.1 reshape.244
  12.8 0.0 copy-done
  12.8 0.0 copy-start.3
  12.8 0.7 gather_fusion
  13.5 0.1 gather.9
  13.6 0.1 reshape.252
  13.7 0.0 copy-done.3
  13.7 0.5 copy.33
  14.2 0.6 broadcast.241
  14.8 7.5 %reduce = bf16[1280,64]{1,0:T(8,128)(2,1)S(1)} reduce(bf16[1280,1,64]{2,1,0:T(2,128)(2,1)S(1)} %bitcast.92, bf16[]{:T(256)} %broadcast.241), dimensions={1}, to_apply=%bitcast.66.reduce_sub_computation | reduce | bytes 327682
  22.3 0.9 reshape.262
  23.2 0.0 all-to-all-done.2
  23.2 7.3 %all-to-all-start = ((bf16[8,2,5120]{2,1,0:T(2,128)(2,1)}), bf16[8,2,5120]{2,1,0:T(2,128)(2,1)S(1)}, u32[]{:S(2)}, u32[]{:S(2)}) async-start(bf16[8,2,5120]{2,1,0:T(2,128)(2,1)} %reshape.262), calls=%async_computation | async-start | bytes 327680 | tf_op jit(solution)/shard_map/all_to_all | solution.py:36
  30.5 0.1 copy.54
  30.6 0.2 reduce_sum.85
  30.8 0.6 fusion.13
  31.4 0.1 fusion.12
  31.5 0.1 select_reduce_fusion
  31.6 0.4 multiply_reduce_fusion.1
  32.0 0.1 iota_compare_fusion
  32.1 10.1 %all-to-all-done = bf16[8,2,5120]{2,1,0:T(2,128)(2,1)S(1)} async-done(((bf16[8,2,5120]{2,1,0:T(2,128)(2,1)}), bf16[8,2,5120]{2,1,0:T(2,128)(2,1)S(1)}, u32[]{:S(2)}, u32[]{:S(2)}) %all-to-all-start) | async-done | bytes 163872 | tf_op jit(solution)/shard_map/all_to_all | solution.py:36
  42.2 0.3 reshape.263
  42.6 0.2 copy.35
  42.8 0.6 gather_fusion.1
  43.4 0.0 copy-start.4
  43.4 1.1 broadcast_select_fusion
  44.5 3.7 %all-to-all-start.1 = ((bf16[8,4,64,160]{3,2,1,0:T(8,128)(2,1)}), bf16[8,4,64,160]{3,2,1,0:T(8,128)(2,1)S(1)}, u32[]{:S(2)}, u32[]{:S(2)}) async-start(bf16[8,4,64,160]{3,2,1,0:T(8,128)(2,1)} %broadcast_select_fusion), calls=%async_computation.1 | async-start | bytes 2097152 | tf_op jit(solution)/shard_map/all_to_all | solution.py:38
  48.3 0.0 copy-done.4
  48.3 0.7 broadcast_subtract_fusion
  49.0 0.1 and_convert_fusion
  49.1 0.3 multiply_convert_fusion.1
  49.4 44.4 %all-to-all-done.1 = bf16[8,4,64,160]{3,2,1,0:T(8,128)(2,1)S(1)} async-done(((bf16[8,4,64,160]{3,2,1,0:T(8,128)(2,1)}), bf16[8,4,64,160]{3,2,1,0:T(8,128)(2,1)S(1)}, u32[]{:S(2)}, u32[]{:S(2)}) %all-to-all-start.1) | async-done | bytes 655392 | tf_op jit(solution)/shard_map/all_to_all | solution.py:38
  93.8 0.6 copy.36
  94.4 1.2 reshape.235
  95.6 92.1 %all-gather.2.cloned.1.call-done = bf16[1280,2,2048]{2,1,0:T(2,128)(2,1)} async-done(((bf16[160,2,2048]{2,1,0:T(2,128)(2,1)}), bf16[1280,2,2048]{2,1,0:T(2,128)(2,1)}) %all-gather.2.cloned.1.call-update) | async-done | bytes 10485776 | tf_op jit(solution)/shard_map/all_gather | solution.py:39
  187.7 14.6 %copy.50 = bf16[160,8,2,2048]{3,1,2,0:T(8,128)(2,1)} copy(bf16[160,8,2,2048]{3,2,1,0:T(2,128)(2,1)} %bitcast.83) | data formatting | bytes 20971520
  202.3 5.7 %fusion.15 = f32[256,4096]{1,0:T(8,128)S(1)} fusion(bf16[256,1280]{1,0:T(8,128)(2,1)S(1)} %reshape.235, bf16[1280,4096]{1,0:T(8,128)(2,1)} %bitcast.84), kind=kOutput, calls=%fused_computation.57 | convolution fusion | flops 2684354560 | bytes 15335424 | tf_op jit(solution)/shard_map/dot_general | solution.py:41
  208.0 0.0 copy-start.1
  208.0 0.1 slice_bitcast_fusion
  208.1 1.8 copy-done.1
  209.9 0.4 copy.51
  210.3 0.6 reduce_sum.83
  210.9 1.5 multiply_reduce_fusion
  212.5 0.0 copy-start.2
  212.5 0.6 mul.72
  213.1 0.6 sub.49
  213.7 1.0 copy-done.2
  214.7 1.5 fusion.14
  216.3 0.4 convolution_bitcast_fusion
  216.6 0.3 copy.41
  217.0 0.1 reshape.240
  217.1 3.9 %all_to_all.62 = bf16[2,32,2048]{2,1,0:T(8,128)(2,1)S(1)} all-to-all(bf16[2,32,2048]{2,1,0:T(8,128)(2,1)S(1)} %multiply_convert_fusion), channel_id=1, replica_groups=mesh['groups'=2,'ctx'=8,'head'=2] {'head'}, dimensions={0} | all-to-all | bytes 524288 | tf_op jit(solution)/shard_map/all_to_all | solution.py:72
  221.0 0.7 copy.49
  (17 shorter events, 0.2 us)
Async XLA Ops:
  6.5 6.3 %copy-start = (s32[5]{0:T(128)S(1)}, s32[5]{0:T(128)}, u32[]{:S(2)}) copy-start(s32[5]{0:T(128)} %param.9) | copy-start | bytes 64
  6.5 5.9 %copy-start.5 = (s32[5,2]{0,1:T(2,128)S(1)}, s32[5,2]{0,1:T(2,128)}, u32[]{:S(2)}) copy-start(s32[5,2]{0,1:T(2,128)} %param.8) | copy-start | bytes 124
  6.5 181.2 %all-gather.2.cloned.1.call-start = ((), (), s32[]{:S(2)}) async-start(), calls=%async_computation.4 | async-start | bytes 11796480 | tf_op jit(solution)/shard_map/all_gather | solution.py:39
  8.9 14.2 %all-to-all-start.2 = ((bf16[32,2,2048]{2,0,1:T(8,128)(2,1)}), bf16[32,2,2048]{2,0,1:T(8,128)(2,1)S(1)}, u32[]{:S(2)}, u32[]{:S(2)}) async-start(bf16[32,2,2048]{2,0,1:T(8,128)(2,1)} %bitcast.80), calls=%async_computation.2 | async-start | bytes 524288 | tf_op jit(solution)/shard_map/all_to_all | solution.py:20
  12.8 0.9 copy-start.3
  23.2 19.0 %all-to-all-start = ((bf16[8,2,5120]{2,1,0:T(2,128)(2,1)}), bf16[8,2,5120]{2,1,0:T(2,128)(2,1)S(1)}, u32[]{:S(2)}, u32[]{:S(2)}) async-start(bf16[8,2,5120]{2,1,0:T(2,128)(2,1)} %reshape.262), calls=%async_computation | async-start | bytes 327680 | tf_op jit(solution)/shard_map/all_to_all | solution.py:36
  43.4 4.9 %copy-start.4 = (f32[2048]{0:T(1024)S(1)}, f32[2048]{0:T(1024)}, u32[]{:S(2)}) copy-start(f32[2048]{0:T(1024)} %param.11) | copy-start | bytes 24580
  44.5 49.3 %all-to-all-start.1 = ((bf16[8,4,64,160]{3,2,1,0:T(8,128)(2,1)}), bf16[8,4,64,160]{3,2,1,0:T(8,128)(2,1)S(1)}, u32[]{:S(2)}, u32[]{:S(2)}) async-start(bf16[8,4,64,160]{3,2,1,0:T(8,128)(2,1)} %broadcast_select_fusion), calls=%async_computation.1 | async-start | bytes 2097152 | tf_op jit(solution)/shard_map/all_to_all | solution.py:38
  208.0 1.9 copy-start.1
  212.5 2.2 copy-start.2
Sparse Core Ops, SparseCore 0:
  9.5 178.1 all-gather.1
where the time goes:
time: 229 us
  waiting for transfers between devices  147 us (64%)
  local copies, waits for them, and re-layouts  27.9 us (12%)
  starting transfers between devices  14.4 us (6%)
  other arithmetic  13.7 us (6%)
  between operations  13.7 us (6%)
  matrix products  7.57 us (3%)
  blocking collectives  3.94 us (2%)
    all_gather x1, waiting for transfers between devices, shards(): gathered = lax.all_gather(kv_weight, 'ctx', axis=0, tiled=True)  92.1 us
    all_to_all x1, waiting for transfers between devices, shards(): lax.all_to_all(outgoing, 'ctx', split_axis=0, concat_axis=3, tiled=True)  44.4 us
    unnamed x21, local copies, waits for them, and re-layouts  20.4 us
    all_to_all x1, waiting for transfers between devices, shards(): lax.all_to_all(latents, 'ctx', split_axis=2, concat_axis=0, tiled=True)  10.1 us
    unnamed x1, other arithmetic  7.47 us
    all_to_all x1, starting transfers between devices, shards(): lax.all_to_all(latents, 'ctx', split_axis=2, concat_axis=0, tiled=True)  7.25 us
    dot_general x1, matrix products, shards(): jnp.dot(panels.reshape(MAXIMG * lat, panels.shape[3]), flat_weight, prefe...  5.65 us
  transfers between devices with their start and end apart: 4, of which 3 were waited for; matrix products, arithmetic and copies ran while one was open for 8% of the time, Pallas kernels for 0%

commit v1 on v0

--- a/solution.py
+++ b/solution.py
@@ -1,6 +1,10 @@
+import functools
+
 import jax
 import jax.numpy as jnp
 from jax import lax
+from jax.experimental import pallas as pl
+from jax.experimental.pallas import tpu as pltpu
 from jax.sharding import PartitionSpec as P
 
 DH = 128
@@ -15,7 +19,115 @@
     return (centered * lax.rsqrt(spread + 1e-05)).reshape(x.shape)
 
 
-def shards(queries, latents, image_span, image_owner, kv_weight, attn_gate):
+def row_norm(x):
+    centered = x - jnp.mean(x, -1, keepdims=True)
+    spread = jnp.mean(centered * centered, -1, keepdims=True)
+    return centered * lax.rsqrt(spread + 1e-05)
+
+
+def attend_kernel(
+    sizes, span_ref, owner_ref, gate_ref, got_ref, other_ref, out_ref, panel, weight
+):
+    ctx_count, rows, lat, tok, heads, images = sizes
+    half = ctx_count // 2 * rows
+    blocks = half // DH
+    w_rows = heads * 2 * rows
+    q_at = w_rows
+    l_at = w_rows + heads * tok
+    mine = lax.axis_index("head")
+    for i in range(images):
+        store = owner_ref[i]
+        for b in range(blocks):
+            at = slice(b * DH, (b + 1) * DH)
+            panel[i * lat : (i + 1) * lat, at] = got_ref[store, l_at + b * lat : l_at + (b + 1) * lat, :]
+            at = slice(half + b * DH, half + (b + 1) * DH)
+            panel[i * lat : (i + 1) * lat, at] = other_ref[store, b * lat : (b + 1) * lat, :]
+    for part in range(2):
+        first = (mine if part == 0 else 1 - mine) * (ctx_count // 2)
+        for s in range(ctx_count // 2):
+            at = (part * (ctx_count // 2) + s) * rows
+            for n in range(heads * 2):
+                weight[at : at + rows, n * DH : (n + 1) * DH] = got_ref[
+                    first + s, n * rows : (n + 1) * rows, :
+                ]
+    both = jnp.dot(panel[...], weight[...], preferred_element_type=jnp.float32)
+    count = ctx_count * tok
+    row = lax.broadcasted_iota(jnp.int32, (count, 1), 0)
+    within = row % tok
+    part = jnp.where(within < tok // 2, mine, 1 - mine)
+    position = row // tok * tok + part * (tok // 2) + within % (tok // 2)
+    slot = lax.broadcasted_iota(jnp.int32, (1, images * lat), 1) // lat
+    low = jnp.zeros_like(slot)
+    high = jnp.zeros_like(slot)
+    for i in range(images):
+        low = jnp.where(slot == i, span_ref[i, 0], low)
+        high = jnp.where(slot == i, span_ref[i, 1], high)
+    inside = (position >= low) & (position < high)
+    for n in range(heads):
+        keys = row_norm(both[:, n * 2 * DH : n * 2 * DH + DH]).astype(jnp.bfloat16)
+        values = both[:, n * 2 * DH + DH : (n + 1) * 2 * DH].astype(jnp.bfloat16)
+        query = got_ref[:, q_at + n * tok : q_at + (n + 1) * tok, :].reshape(count, DH)
+        query = row_norm(query.astype(jnp.float32)).astype(jnp.bfloat16)
+        scores = lax.dot_general(
+            query, keys, (((1,), (1,)), ((), ())), preferred_element_type=jnp.float32
+        ) * DH ** (-0.5)
+        weighted = jnp.where(inside, jnp.exp(scores), 0.0)
+        total = jnp.sum(weighted, -1, keepdims=True)
+        total = jnp.where(total > 0.0, total, 1.0)
+        probs = (weighted / total).astype(jnp.bfloat16)
+        attended = jnp.dot(probs, values, preferred_element_type=jnp.float32)
+        gate = jnp.tanh(gate_ref[n : n + 1, :])
+        gated = (gate * attended).astype(jnp.bfloat16).reshape(ctx_count, 2, tok // 2, DH)
+        for c in range(ctx_count):
+            out_ref[c * 2 + mine, :, n * DH : (n + 1) * DH] = gated[c, 0]
+            out_ref[c * 2 + 1 - mine, :, n * DH : (n + 1) * DH] = gated[c, 1]
+
+
+def by_heads(queries, latents, image_span, image_owner, kv_weight, attn_gate):
+    ctx_count = lax.axis_size("ctx")
+    mine = lax.axis_index("head")
+    place = lax.axis_index("ctx")
+    tok = queries.shape[0] * 2
+    width = kv_weight.shape[2]
+    heads = width // DH // ctx_count
+    rows = kv_weight.shape[0]
+    lat, depth = latents.shape[1:]
+    half = depth // 2
+    images = image_span.shape[0]
+    swap = [(0, 1), (1, 0)]
+    kept = lax.dynamic_slice_in_dim(queries, mine * width, width, 1)
+    sent = lax.dynamic_slice_in_dim(queries, (1 - mine) * width, width, 1)
+    came = lax.ppermute(sent, "head", swap)
+    query = jnp.concatenate([kept, came], 0).reshape(tok, ctx_count, heads, DH)
+    query = query.transpose(1, 2, 0, 3).reshape(ctx_count, heads * tok, DH)
+    weight = kv_weight.reshape(rows, 2, ctx_count, heads, DH).transpose(2, 3, 1, 0, 4)
+    weight = weight.reshape(ctx_count, heads * 2 * rows, DH)
+    share = lax.dynamic_slice_in_dim(latents[0], mine * half, half, 1)
+    share = share.reshape(lat, half // DH, DH).transpose(1, 0, 2).reshape(1, lat * (half // DH), DH)
+    share = jnp.broadcast_to(share, (ctx_count,) + share.shape[1:])
+    outgoing = jnp.concatenate([weight, query, share], 1)
+    got = lax.all_to_all(outgoing, "ctx", split_axis=0, concat_axis=0, tiled=True)
+    other = lax.ppermute(got[:, heads * (2 * rows + tok) :, :], "head", swap)
+    gate = lax.dynamic_slice_in_dim(attn_gate.reshape(-1, DH), place * heads, heads, 0)
+    smem = pl.BlockSpec(memory_space=pltpu.SMEM)
+    vmem = pl.BlockSpec(memory_space=pltpu.VMEM)
+    gated = pl.pallas_call(
+        functools.partial(attend_kernel, (ctx_count, rows, lat, tok, heads, images)),
+        out_shape=jax.ShapeDtypeStruct((ctx_count * 2, tok // 2, heads * DH), jnp.bfloat16),
+        in_specs=[smem, smem, vmem, vmem, vmem],
+        out_specs=vmem,
+        scratch_shapes=[
+            pltpu.VMEM((images * lat, depth), jnp.bfloat16),
+            pltpu.VMEM((depth, heads * 2 * DH), jnp.bfloat16),
+        ],
+        compiler_params=pltpu.CompilerParams(vmem_limit_bytes=40 * 1024 * 1024),
+    )(image_span, image_owner, gate, got, other)
+    back = lax.all_to_all(gated, ("ctx", "head"), split_axis=0, concat_axis=0, tiled=True)
+    back = back.reshape(ctx_count, 2, tok // 2, heads * DH).transpose(2, 1, 0, 3)
+    return back.reshape(tok // 2, 2 * width)
+
+
+def by_tokens(queries, latents, image_span, image_owner, kv_weight, attn_gate):
     ctx_count = lax.axis_size("ctx")
     rows = lax.all_to_all(queries, "head", split_axis=1, concat_axis=0, tiled=True)
     tok = rows.shape[0]
@@ -72,6 +184,16 @@
     return lax.all_to_all(gated, "head", split_axis=0, concat_axis=1, tiled=True)
 
 
+def shards(*args):
+    ctx_count = lax.axis_size("ctx")
+    weight = args[4]
+    whole_heads = weight.shape[2] % (ctx_count * DH) == 0
+    whole_blocks = args[1].shape[2] % (2 * DH) == 0 and weight.shape[0] % 16 == 0
+    if whole_heads and whole_blocks and lax.axis_size("head") == 2 and ctx_count % 2 == 0:
+        return by_heads(*args)
+    return by_tokens(*args)
+
+
 def solution(mesh):
     placed = (
         P(("groups", "ctx", "head"), None),

time: 229 us -> 86.1 us (0.38)
  waiting for transfers between devices: 147 us -> 1.52 us
  blocking collectives: 3.94 us -> 71.9 us
  local copies, waits for them, and re-layouts: 27.9 us -> 8.9 us
  starting transfers between devices: 14.4 us -> 0.52 us
  between operations: 13.7 us -> 0.11 us
  other arithmetic: 13.7 us -> 0.17 us
  matrix products: 7.57 us -> 0 us
  Pallas kernels: 0 us -> 2.74 us
    all_gather x1 -> x0, waiting for transfers between devices: 92.1 us -> none  [shards(): gathered = lax.all_gather(kv_weight, 'ctx', axis=0, tiled=True)]
    all_to_all x1 -> x2, blocking collectives: 3.94 us -> 71.9 us  [the longest x1 58.6 us: by_heads(): lax.all_to_all(outgoing, 'ctx', split_axis=0, concat_axis=0, tiled=True)]
    all_to_all x3 -> x0, waiting for transfers between devices: 54.5 us -> none  [the longest x1 44.4 us: shards(): lax.all_to_all(outgoing, 'ctx', split_axis=0, concat_axis=3, tiled=True)]
    unnamed x21 -> x8, local copies, waits for them, and re-layouts: 20.4 us -> 0.89 us
    all_to_all x3 -> x0, starting transfers between devices: 14.4 us -> none  [the longest x1 7.25 us: shards(): lax.all_to_all(latents, 'ctx', split_axis=2, concat_axis=0, tiled=True)]
    dot_general x3 -> x0, matrix products: 7.57 us -> none  [the longest x1 5.65 us: shards(): jnp.dot(panels.reshape(MAXIMG * lat, panels.shape[3]), flat_weight, prefe...]
    unnamed x1 -> x0, other arithmetic: 7.47 us -> none
    reshape x2 -> x5, local copies, waits for them, and re-layouts: 1.28 us -> 5.15 us  [the longest x2 4.8 us: by_heads(): kv_weight.reshape(rows, 2, ctx_count, heads, DH).transpose(2, 3, 1, 0, 4)]
  transfers between devices with their start and end apart: 4 -> 2, of which waited for: 3 -> 1; matrix products, arithmetic and copies ran while one was open for 8% -> 7% of each run, Pallas kernels for 0% -> 0%
where the time goes in v1:
time: 86.1 us; the launch traced here: 85.8 us
  blocking collectives  71.9 us (84%)
  local copies, waits for them, and re-layouts  8.9 us (10%)
  Pallas kernels  2.74 us (3%)
  waiting for transfers between devices  1.52 us (2%)
    all_to_all x1, blocking collectives, by_heads(): lax.all_to_all(outgoing, 'ctx', split_axis=0, concat_axis=0, tiled=True)  58.6 us
    all_to_all x1, blocking collectives, by_heads(): lax.all_to_all(gated, ('ctx', 'head'), split_axis=0, concat_axis=0, tiled...  13.2 us
    reshape x2, local copies, waits for them, and re-layouts, by_heads(): kv_weight.reshape(rows, 2, ctx_count, heads, DH).transpose(2, 3, 1, 0, 4)  4.8 us
    pallas_call x1, Pallas kernels, by_heads(): pl.pallas_call(functools.partial(attend_kernel, (ctx_count, rows, lat, to...  2.74 us
  transfers between devices with their start and end apart: 2, of which 1 were waited for; matrix products, arithmetic and copies ran while one was open for 7% of the time, Pallas kernels for 0%

profile of v1, /device:TPU:0, one launch (start us, length us, event | category | flops | bytes accessed | tf_op | source)
XLA Modules:
  0.0 85.8 jit_solution(1276398087073277552)
XLA Ops:
  0.0 0.0 copy-start
  0.0 1.0 %constant_dynamic-slice_fusion.2 = (bf16[32,2048]{1,0:T(8,128)(2,1)S(1)}, bf16[32,2048]{1,0:T(8,128)(2,1)S(1)}) fusion(bf16[32,4096]{1,0:T(8,128)(2,1)} %param.6, s32[]{:T(128)S(6)} %select_n.13, s32[]{:T(128)S(6)} %select_n.14), kind=kLoop, calls=%fused_computation.4 | loop fusion | bytes 524296 | tf_op jit(solution)/shard_map/dynamic_slice | solution.py:98
  1.0 0.5 collective-permute-start
  1.5 0.0 copy-done
  1.6 0.1 reshape.33
  1.7 4.3 %reshape.29 = bf16[160,2,8,2,128]{4,3,2,1,0:T(2,128)(2,1)S(1)} reshape(bf16[160,2,2048]{2,1,0:T(2,128)(2,1)} %param.10) | data formatting | bytes 2621440 | tf_op jit(solution)/shard_map/reshape | solution.py:103
  6.0 0.5 copy.15
  6.5 0.0 collective-permute-done
  6.6 0.2 reshape.31
  6.7 0.1 copy.16
  6.8 0.1 broadcast_in_dim.8
  6.9 0.1 pad_maximum_fusion
  7.1 0.0 copy-start.2
  7.1 0.0 copy-start.1
  7.1 58.6 %all_to_all.10.got_ref = bf16[8,1088,128]{2,1,0:T(8,128)(2,1)S(1)} all-to-all(bf16[8,1088,128]{2,1,0:T(8,128)(2,1)S(1)} %pad_maximum_fusion), channel_id=1, replica_groups=mesh['groups'=2,'ctx'=8,'head'=2] {'ctx'}, dimensions={0} | all-to-all | bytes 4456448 | tf_op jit(solution)/shard_map/all_to_all | solution.py:109
  65.7 0.9 %slice.4 = bf16[8,320,128]{2,1,0:T(8,128)(2,1)} slice(bf16[8,1088,128]{2,1,0:T(8,128)(2,1)S(1)} %all_to_all.10.got_ref), slice={[0:8], [768:1088], [0:128]} | slice | bytes 1310720 | tf_op jit(solution)/shard_map/slice | solution.py:110
  66.6 0.0 collective-permute-start.1
  66.6 0.0 copy-done.2
  66.6 0.1 copy.18.span_ref
  66.7 0.7 constant_dynamic-slice_fusion.3.gate_ref
  67.4 1.5 %collective-permute-done.1.other_ref = bf16[8,320,128]{2,1,0:T(8,128)(2,1)S(1)} collective-permute-done((bf16[8,320,128]{2,1,0:T(8,128)(2,1)}, bf16[8,320,128]{2,1,0:T(8,128)(2,1)S(1)}, u32[]{:S(2)}, u32[]{:S(2)}) %collective-permute-start.1) | collective-permute-done | bytes 655392 | tf_op jit(solution)/shard_map/ppermute | solution.py:110
  68.9 0.0 copy-done.1
  68.9 2.7 %shard_map.64 = bf16[16,32,256]{2,1,0:T(8,128)(2,1)S(1)} custom-call(s32[5,2]{1,0:T(8,128)S(1)} %copy.18.span_ref, s32[5]{0:T(128)S(1)} %copy-done.1, f32[2,128]{1,0:T(2,128)S(1)} %constant_dynamic-slice_fusion.3.gate_ref, bf16[8,1088,128]{2,1,0:T(8,128)(2,1)S(1)} %all_to_all.10.got_ref, bf16[8,320,128]{2,1,0:T(8,128)(2,1)S(1)} %collective-permute-done.1.other_ref), custom_call_target="tpu_custom_call" | custom-call | tf_op jit(solution)/shard_map/pallas_call | solution.py:114
  71.7 13.2 %all_to_all.11 = bf16[16,32,256]{2,1,0:T(8,128)(2,1)S(1)} all-to-all(bf16[16,32,256]{2,1,0:T(8,128)(2,1)S(1)} %shard_map.64), channel_id=1, replica_groups=mesh['groups'=2,'ctx'=8,'head'=2] {'ctx','head'}, dimensions={0} | all-to-all | bytes 524288 | tf_op jit(solution)/shard_map/all_to_all | solution.py:125
  84.9 0.1 copy.19
  85.0 0.8 copy.20
  (3 shorter events, 0.0 us)
Async XLA Ops:
  0.0 1.5 %copy-start = (bf16[1,64,1280]{2,1,0:T(8,128)(2,1)S(1)}, bf16[1,64,1280]{2,1,0:T(8,128)(2,1)}, u32[]{:S(2)}) copy-start(bf16[1,64,1280]{2,1,0:T(8,128)(2,1)} %param.7) | copy-start | bytes 491524
  1.0 5.5 %collective-permute-start = (bf16[32,2048]{1,0:T(8,128)(2,1)S(1)}, bf16[32,2048]{1,0:T(8,128)(2,1)S(1)}, u32[]{:S(2)}, u32[]{:S(2)}) collective-permute-start(bf16[32,2048]{1,0:T(8,128)(2,1)S(1)} %get-tuple-element.6), channel_id=1, source_target_pairs={{0,1},{1,0},{2,3},{3,2},{4,5},{5,4},{6,7},{7,6},{8,9},{9,8},{10,11... | collective-permute-start | bytes 393224 | tf_op jit(solution)/shard_map/ppermute | solution.py:100
  7.1 59.6 %copy-start.2 = (s32[5,2]{0,1:T(2,128)S(1)}, s32[5,2]{0,1:T(2,128)}, u32[]{:S(2)}) copy-start(s32[5,2]{0,1:T(2,128)} %param.8) | copy-start | bytes 124
  7.1 61.9 %copy-start.1 = (s32[5]{0:T(128)S(1)}, s32[5]{0:T(128)}, u32[]{:S(2)}) copy-start(s32[5]{0:T(128)} %owner_ref.1) | copy-start | bytes 64
  66.6 2.3 %collective-permute-start.1 = (bf16[8,320,128]{2,1,0:T(8,128)(2,1)}, bf16[8,320,128]{2,1,0:T(8,128)(2,1)S(1)}, u32[]{:S(2)}, u32[]{:S(2)}) collective-permute-start(bf16[8,320,128]{2,1,0:T(8,128)(2,1)} %slice.4), channel_id=1, source_target_pairs={{0,1},{1,0},{2,3},{3,2},{4,5},{5,4},{6,7},{7,6},{8,9},{9,8},{10,11... | collective-permute-start | bytes 1966088 | tf_op jit(solution)/shard_map/ppermute | solution.py:110

commit v2 on v0

--- a/solution.py
+++ b/solution.py
@@ -1,6 +1,10 @@
+import functools
+
 import jax
 import jax.numpy as jnp
 from jax import lax
+from jax.experimental import pallas as pl
+from jax.experimental.pallas import tpu as pltpu
 from jax.sharding import PartitionSpec as P
 
 DH = 128
@@ -15,7 +19,163 @@
     return (centered * lax.rsqrt(spread + 1e-05)).reshape(x.shape)
 
 
-def shards(queries, latents, image_span, image_owner, kv_weight, attn_gate):
+def row_norm(x):
+    centered = x - jnp.mean(x, -1, keepdims=True)
+    spread = jnp.mean(centered * centered, -1, keepdims=True)
+    return centered * lax.rsqrt(spread + 1e-05)
+
+
+def attend_kernel(sizes, mine_ref, theirs_ref, gate_ref, got_ref, *rest):
+    stores, (out_ref, panel, weight) = rest[:-3], rest[-3:]
+    ctx_count, rows, lat, part, heads, images = sizes
+    half = ctx_count // 2 * rows
+    blocks = half // DH
+    q_at = heads * 2 * rows
+    group = lax.axis_index("groups")
+    place = lax.axis_index("ctx")
+    core = lax.axis_index("head")
+    for r, meta in enumerate((mine_ref, theirs_ref)):
+        for i in range(images):
+            turn = meta[i, 2] ^ place
+            slot = turn // 2
+            to = slice((r * images + i) * lat, (r * images + i + 1) * lat)
+            for k in range(2):
+                near, far = stores[4 * k + 2 * r : 4 * k + 2 * r + 2]
+                for b in range(blocks):
+                    come = slice(b * lat, (b + 1) * lat)
+                    panel[to, k * half + b * DH : k * half + (b + 1) * DH] = jnp.where(
+                        turn % 2 == 0, near[slot, come, :], far[slot, come, :]
+                    )
+    for k in range(2):
+        first = (core ^ k) * (ctx_count // 2)
+        for s in range(ctx_count // 2):
+            to = slice(k * half + s * rows, k * half + (s + 1) * rows)
+            for n in range(heads * 2):
+                weight[to, n * DH : (n + 1) * DH] = got_ref[first + s, n * rows : (n + 1) * rows, :]
+    both = jnp.dot(panel[...], weight[...], preferred_element_type=jnp.float32)
+    count = ctx_count * 2 * part
+    row = lax.broadcasted_iota(jnp.int32, (count, 1), 0)
+    block = row // part
+    position = (block // 2 * 2 + (block % 2 ^ core)) * part + row % part
+    slot = lax.broadcasted_iota(jnp.int32, (1, images * lat), 1) // lat
+    for r, meta in enumerate((mine_ref, theirs_ref)):
+        low = jnp.zeros_like(slot)
+        high = jnp.zeros_like(slot)
+        for i in range(images):
+            low = jnp.where(slot == i, meta[i, 0], low)
+            high = jnp.where(slot == i, meta[i, 1], high)
+        inside = (position >= low) & (position < high)
+        these = both[r * images * lat : (r + 1) * images * lat, :]
+        for n in range(heads):
+            keys = row_norm(these[:, n * 2 * DH : n * 2 * DH + DH]).astype(jnp.bfloat16)
+            values = these[:, n * 2 * DH + DH : (n + 1) * 2 * DH].astype(jnp.bfloat16)
+            at = q_at + (n * 2 + r) * 2 * part
+            query = got_ref[:, at : at + 2 * part, :].reshape(count, DH)
+            query = row_norm(query.astype(jnp.float32)).astype(jnp.bfloat16)
+            scores = lax.dot_general(
+                query, keys, (((1,), (1,)), ((), ())), preferred_element_type=jnp.float32
+            ) * DH ** (-0.5)
+            weighted = jnp.where(inside, jnp.exp(scores), 0.0)
+            total = jnp.sum(weighted, -1, keepdims=True)
+            total = jnp.where(total > 0.0, total, 1.0)
+            probs = (weighted / total).astype(jnp.bfloat16)
+            attended = jnp.dot(probs, values, preferred_element_type=jnp.float32)
+            gate = jnp.tanh(gate_ref[n : n + 1, :])
+            gated = (gate * attended).astype(jnp.bfloat16).reshape(ctx_count, 2, part, DH)
+            for c in range(ctx_count):
+                for d in range(2):
+                    to = ((group ^ r) * ctx_count + c) * 2 + (core ^ d)
+                    out_ref[to, :, n * DH : (n + 1) * DH] = gated[c, d]
+
+
+def split_kernel(query_ref, latents_ref, own_ref, core_ref, group_ref, both_ref, share_ref):
+    group = lax.axis_index("groups")
+    core = lax.axis_index("head")
+    count, part = own_ref.shape[:2]
+    for k, to in enumerate((own_ref, core_ref, group_ref, both_ref)):
+        first = (core ^ k % 2) * 2 + (group ^ k // 2)
+        for c in range(count):
+            to[c] = query_ref[:, pl.ds(pl.multiple_of((first * count + c) * DH, DH), DH)]
+    lat = latents_ref.shape[1]
+    blocks = share_ref.shape[0] // lat
+    for b in range(blocks):
+        at = pl.ds(pl.multiple_of((core * blocks + b) * DH, DH), DH)
+        share_ref[b * lat : (b + 1) * lat, :] = latents_ref[0, :, at]
+
+
+def join_kernel(weight_ref, *rest):
+    *pieces, out_ref = rest
+    rows = weight_ref.shape[1]
+    part = pieces[0].shape[1]
+    out_ref[:, :rows, :] = weight_ref[...]
+    for k, piece in enumerate(pieces):
+        out_ref[:, rows + k * part : rows + (k + 1) * part, :] = piece[...]
+
+
+def by_heads(queries, latents, image_span, image_owner, kv_weight, attn_gate):
+    ctx_count = lax.axis_size("ctx")
+    group = lax.axis_index("groups")
+    place = lax.axis_index("ctx")
+    core = lax.axis_index("head")
+    part = queries.shape[0]
+    width = kv_weight.shape[2]
+    span = width // 2
+    rows = kv_weight.shape[0]
+    lat, depth = latents.shape[1:]
+    images = image_span.shape[0]
+    swap = [(0, 1), (1, 0)]
+    smem = pl.BlockSpec(memory_space=pltpu.SMEM)
+    vmem = pl.BlockSpec(memory_space=pltpu.VMEM)
+
+    def across(x, turn):
+        return lax.ppermute(x, "ctx", [(i, i ^ turn) for i in range(ctx_count)])
+
+    piece = jax.ShapeDtypeStruct((ctx_count, part, DH), jnp.bfloat16)
+    share = jax.ShapeDtypeStruct((depth // 2 // DH * lat, DH), jnp.bfloat16)
+    *query, share = pl.pallas_call(
+        split_kernel, out_shape=[piece] * 4 + [share], in_specs=[vmem] * 2, out_specs=[vmem] * 5
+    )(queries, latents)
+    query[1] = lax.ppermute(query[1], "head", swap)
+    query[2] = lax.ppermute(query[2], "groups", swap)
+    query[3] = lax.ppermute(query[3], ("groups", "head"), [(i, 3 - i) for i in range(4)])
+    held = [share] + [across(share, 2 * k) for k in range(1, ctx_count // 2)]
+    weight = lax.dynamic_slice_in_dim(kv_weight, group * span, span, 2)
+    weight = weight.reshape(rows, 2, ctx_count, DH).transpose(2, 1, 0, 3)
+    weight = weight.reshape(ctx_count, 2 * rows, DH)
+    outgoing = pl.pallas_call(
+        join_kernel,
+        out_shape=jax.ShapeDtypeStruct((ctx_count, 2 * rows + 4 * part, DH), jnp.bfloat16),
+        in_specs=[vmem] * 5,
+        out_specs=vmem,
+    )(weight, *query)
+    outgoing, *held = lax.optimization_barrier((outgoing, *held))
+    got = lax.all_to_all(outgoing, "ctx", split_axis=0, concat_axis=0, tiled=True)
+    meta = jnp.concatenate([image_span, image_owner[:, None]], 1)
+    meta_y = lax.ppermute(meta, "groups", swap)
+    near = jnp.stack(held)
+    near_y = lax.ppermute(near, "groups", swap)
+    near_y, meta_y = lax.optimization_barrier((near_y, meta_y))
+    stores = [near, across(near, 1), near_y, across(near_y, 1)]
+    stores += [lax.ppermute(x, "head", swap) for x in stores]
+    gate = lax.dynamic_slice_in_dim(attn_gate.reshape(-1, DH), group * ctx_count + place, 1, 0)
+    gated = pl.pallas_call(
+        functools.partial(attend_kernel, (ctx_count, rows, lat, part, 1, images)),
+        out_shape=jax.ShapeDtypeStruct((ctx_count * 4, part, DH), jnp.bfloat16),
+        in_specs=[smem] * 2 + [vmem] * 10,
+        out_specs=vmem,
+        scratch_shapes=[
+            pltpu.VMEM((2 * images * lat, depth), jnp.bfloat16),
+            pltpu.VMEM((depth, 2 * DH), jnp.bfloat16),
+        ],
+        compiler_params=pltpu.CompilerParams(vmem_limit_bytes=40 * 1024 * 1024),
+    )(meta, meta_y, gate, got, *stores)
+    every = ("groups", "ctx", "head")
+    back = lax.all_to_all(gated, every, split_axis=0, concat_axis=0, tiled=True)
+    back = back.reshape(2, ctx_count, 2, part, DH).transpose(3, 2, 0, 1, 4)
+    return back.reshape(part, 2 * width)
+
+
+def by_tokens(queries, latents, image_span, image_owner, kv_weight, attn_gate):
     ctx_count = lax.axis_size("ctx")
     rows = lax.all_to_all(queries, "head", split_axis=1, concat_axis=0, tiled=True)
     tok = rows.shape[0]
@@ -72,6 +232,17 @@
     return lax.all_to_all(gated, "head", split_axis=0, concat_axis=1, tiled=True)
 
 
+def shards(*args):
+    ctx_count = lax.axis_size("ctx")
+    weight = args[4]
+    pairs = lax.axis_size("groups") == 2 and lax.axis_size("head") == 2
+    whole_heads = weight.shape[2] == 2 * ctx_count * DH
+    whole_blocks = args[1].shape[2] % (2 * DH) == 0 and weight.shape[0] % 16 == 0
+    if pairs and whole_heads and whole_blocks and ctx_count & (ctx_count - 1) == 0:
+        return by_heads(*args)
+    return by_tokens(*args)
+
+
 def solution(mesh):
     placed = (
         P(("groups", "ctx", "head"), None),

time: 229 us -> 70.5 us (0.31)
  waiting for transfers between devices: 147 us -> 23.1 us
  local copies, waits for them, and re-layouts: 27.9 us -> 4.4 us
  between operations: 13.7 us -> 0.11 us
  other arithmetic: 13.7 us -> 0.12 us
  blocking collectives: 3.94 us -> 14.7 us
  Pallas kernels: 0 us -> 8.02 us
  matrix products: 7.57 us -> 0 us
  starting transfers between devices: 14.4 us -> 19.8 us
    all_gather x1 -> x0, waiting for transfers between devices: 92.1 us -> none  [shards(): gathered = lax.all_gather(kv_weight, 'ctx', axis=0, tiled=True)]
    all_to_all x3 -> x1, waiting for transfers between devices: 54.5 us -> 0.01 us  [by_heads(): lax.all_to_all(outgoing, 'ctx', split_axis=0, concat_axis=0, tiled=True)]
    ppermute x0 -> x14, waiting for transfers between devices: none -> 23.1 us  [the longest x5 14.7 us: across(): return lax.ppermute(x, 'ctx', [(i, i ^ turn) for i in range(ctx_count)])]
    unnamed x21 -> x16, local copies, waits for them, and re-layouts: 20.4 us -> 1.53 us
    ppermute x0 -> x14, starting transfers between devices: none -> 13.7 us  [the longest x5 8.98 us: across(): return lax.ppermute(x, 'ctx', [(i, i ^ turn) for i in range(ctx_count)])]
    all_to_all x1, blocking collectives: 3.94 us -> 14.7 us  [by_heads(): back = lax.all_to_all(gated, every, split_axis=0, concat_axis=0, tiled=True)]
    all_to_all x3 -> x1, starting transfers between devices: 14.4 us -> 6.07 us  [by_heads(): lax.all_to_all(outgoing, 'ctx', split_axis=0, concat_axis=0, tiled=True)]
    pallas_call x0 -> x3, Pallas kernels: none -> 8.02 us  [the longest x1 3.96 us: by_heads(): pl.pallas_call(functools.partial(attend_kernel, (ctx_count, rows, lat, pa...]
  transfers between devices with their start and end apart: 4 -> 15, of which waited for: 3 -> 6; matrix products, arithmetic and copies ran while one was open for 8% -> 4% of each run, Pallas kernels for 0% -> 3%
where the time goes in v2:
time: 70.5 us; the launch traced here: 70.2 us
  waiting for transfers between devices  23.1 us (33%)
  starting transfers between devices  19.8 us (28%)
  blocking collectives  14.7 us (21%)
  Pallas kernels  8.02 us (11%)
  local copies, waits for them, and re-layouts  4.4 us (6%)
    ppermute x5, waiting for transfers between devices, across(): return lax.ppermute(x, 'ctx', [(i, i ^ turn) for i in range(ctx_count)])  14.7 us
    all_to_all x1, blocking collectives, by_heads(): back = lax.all_to_all(gated, every, split_axis=0, concat_axis=0, tiled=True)  14.7 us
    ppermute x5, starting transfers between devices, across(): return lax.ppermute(x, 'ctx', [(i, i ^ turn) for i in range(ctx_count)])  8.98 us
    all_to_all x1, starting transfers between devices, by_heads(): lax.all_to_all(outgoing, 'ctx', split_axis=0, concat_axis=0, tiled=True)  6.07 us
    ppermute x1, waiting for transfers between devices, by_heads(): meta_y = lax.ppermute(meta, 'groups', swap)  4.99 us
    pallas_call x1, Pallas kernels, by_heads(): pl.pallas_call(functools.partial(attend_kernel, (ctx_count, rows, lat, pa...  3.96 us
    pallas_call x1, Pallas kernels, by_heads(): pl.pallas_call(join_kernel, out_shape=jax.ShapeDtypeStruct((ctx_count, 2...  2.17 us
    pallas_call x1, Pallas kernels, by_heads(): pl.pallas_call(split_kernel, out_shape=[piece] * 4 + [share], in_specs=[v...  1.9 us
  transfers between devices with their start and end apart: 15, of which 6 were waited for; matrix products, arithmetic and copies ran while one was open for 4% of the time, Pallas kernels for 3%

profile of v2, /device:TPU:0, one launch (start us, length us, event | category | flops | bytes accessed | tf_op | source)
XLA Modules:
  0.0 70.2 jit_solution(11990559569531738186)
XLA Ops:
  0.0 0.0 copy-start
  0.0 1.9 %shard_map.64 = (bf16[8,32,128]{2,1,0:T(8,128)(2,1)}, bf16[8,32,128]{2,1,0:T(8,128)(2,1)}, bf16[8,32,128]{2,1,0:T(8,128)(2,1)}, bf16[8,32,128]{2,1,0:T(8,128)(2,1)}, bf16[320,128]{1,0:T(8,128)(2,1)}) custom-call(bf16[32,4096]{1,0:T(8,128)(2,1)} %query_ref.1, bf16[1,64,1280]{2,1,0:T(8,128)(2,1)} %latents_ref.1), custom_call_target="tpu_custom_call" | custom-call | tf_op jit(solution)/shard_map/pallas_call | solution.py:135
  1.9 0.5 collective-permute-start
  2.4 4.6 %collective-permute-start.5 = (bf16[320,128]{1,0:T(8,128)(2,1)}, bf16[320,128]{1,0:T(8,128)(2,1)S(1)}, u32[]{:S(2)}, u32[]{:S(2)}) collective-permute-start(bf16[320,128]{1,0:T(8,128)(2,1)} %get-tuple-element.22), channel_id=1, source_target_pairs={{0,12},{2,14},{4,8},{6,10},{8,4},{10,6},{12,0},{14,2},{1,13},{3,15... | collective-permute-start | bytes 245768 | tf_op jit(solution)/shard_map/ppermute | solution.py:131
  7.0 0.0 collective-permute-start.4
  7.0 0.6 collective-permute-start.3
  7.6 1.7 %collective-permute-start.1 = (bf16[8,32,128]{2,1,0:T(8,128)(2,1)}, bf16[8,32,128]{2,1,0:T(8,128)(2,1)S(1)}, u32[]{:S(2)}, u32[]{:S(2)}) collective-permute-start(bf16[8,32,128]{2,1,0:T(8,128)(2,1)} %get-tuple-element.19), channel_id=1, source_target_pairs={{0,16},{16,0},{1,17},{17,1},{2,18},{18,2},{3,19},{19,3},{4,20},{20... | collective-permute-start | bytes 196616 | tf_op jit(solution)/shard_map/ppermute | solution.py:139
  9.3 0.0 collective-permute-done.rest_1_
  9.3 0.0 copy-start.2
  9.3 0.0 collective-permute-start.2
  9.3 0.0 copy-done
  9.3 0.5 constant_dynamic-slice_fusion.1
  9.7 0.4 reshape.20
  10.2 0.0 copy-done.2
  10.2 1.0 %copy.13 = bf16[8,2,160,128]{3,2,1,0:T(8,128)(2,1)} copy(bf16[8,2,160,128]{3,0,1,2:T(8,128)(2,1)S(1)} %bitcast.18) | data formatting | bytes 1310720 | tf_op jit(solution)/shard_map/transpose | solution.py:143
  11.2 0.8 %collective-permute-done.1.rest_2_ = bf16[8,32,128]{2,1,0:T(8,128)(2,1)S(1)} collective-permute-done((bf16[8,32,128]{2,1,0:T(8,128)(2,1)}, bf16[8,32,128]{2,1,0:T(8,128)(2,1)S(1)}, u32[]{:S(2)}, u32[]{:S(2)}) %collective-permute-start.1) | collective-permute-done | bytes 65568 | tf_op jit(solution)/shard_map/ppermute | solution.py:139
  12.1 0.0 copy-start.3
  12.1 1.4 %collective-permute-done.2.rest_3_ = bf16[8,32,128]{2,1,0:T(8,128)(2,1)S(1)} collective-permute-done((bf16[8,32,128]{2,1,0:T(8,128)(2,1)}, bf16[8,32,128]{2,1,0:T(8,128)(2,1)S(1)}, u32[]{:S(2)}, u32[]{:S(2)}) %collective-permute-start.2) | collective-permute-done | bytes 65568 | tf_op jit(solution)/shard_map/ppermute | solution.py:140
  13.5 0.0 copy-start.4
  13.5 0.0 copy-done.3
  13.5 0.6 copy-done.4
  14.1 2.2 %shard_map.65 = bf16[8,448,128]{2,1,0:T(8,128)(2,1)} custom-call(bf16[8,320,128]{2,1,0:T(8,128)(2,1)} %bitcast.17, bf16[8,32,128]{2,1,0:T(8,128)(2,1)} %get-tuple-element.17.rest_0_, bf16[8,32,128]{2,1,0:T(8,128)(2,1)} %copy-done.2, bf16[8,32,128]{2,1,0:T(8,128)(2,1)} %copy-done.3, bf16[8,32,128]{2,1,0:T(8,128)(2,1)} %copy-done.4), custom_call_target="tpu_custom_call" | custom-call | tf_op jit(solution)/shard_map/pallas_call | solution.py:145
  16.3 0.0 copy-start.1
  16.3 0.0 copy-start.5
  16.3 0.0 copy-start.6
  16.3 0.0 collective-permute-done.5
  16.3 0.0 collective-permute-done.4
  16.3 0.0 collective-permute-done.3
  16.3 6.1 %all-to-all-start = ((bf16[8,448,128]{2,1,0:T(8,128)(2,1)}), bf16[8,448,128]{2,1,0:T(8,128)(2,1)S(1)}, u32[]{:S(2)}, u32[]{:S(2)}) async-start(bf16[8,448,128]{2,1,0:T(8,128)(2,1)} %shard_map.65), calls=%async_computation | async-start | bytes 1835008 | tf_op jit(solution)/shard_map/all_to_all | solution.py:152
  22.4 0.0 copy-done.1
  22.4 0.9 %collective-permute-start.6 = (bf16[4,320,128]{2,1,0:T(8,128)(2,1)S(1)}, bf16[4,320,128]{2,1,0:T(8,128)(2,1)S(1)}, u32[]{:S(2)}, u32[]{:S(2)}) collective-permute-start(bf16[4,320,128]{2,1,0:T(8,128)(2,1)S(1)} %pad_maximum_fusion.rest_0_), channel_id=1, source_target_pairs={{0,16},{16,0},{1,17},{17,1},{2,18},{18,2},{3,19},{19,3},{4,20},{20... | collective-permute-start | bytes 983048 | tf_op jit(solution)/shard_map/ppermute | solution.py:156
  23.3 0.0 copy-done.5
  23.3 0.1 copy.10
  23.4 0.0 copy-done.6
  23.4 0.1 copy.11
  23.5 0.1 pad_add_fusion.mine_ref
  23.6 1.2 %collective-permute-start.7 = (s32[5,3]{1,0:T(8,128)S(1)}, s32[5,3]{1,0:T(8,128)S(1)}, u32[]{:S(2)}, u32[]{:S(2)}) collective-permute-start(s32[5,3]{1,0:T(8,128)S(1)} %pad_add_fusion.mine_ref), channel_id=1, source_target_pairs={{0,16},{16,0},{1,17},{17,1},{2,18},{18,2},{3,19},{19,3},{4,20},{20... | collective-permute-start | bytes 188 | tf_op jit(solution)/shard_map/ppermute | solution.py:154
  24.8 2.0 %collective-permute-start.8 = (bf16[4,320,128]{2,1,0:T(8,128)(2,1)S(1)}, bf16[4,320,128]{2,1,0:T(8,128)(2,1)S(1)}, u32[]{:S(2)}, u32[]{:S(2)}) collective-permute-start(bf16[4,320,128]{2,1,0:T(8,128)(2,1)S(1)} %pad_maximum_fusion.rest_0_), channel_id=1, source_target_pairs={{0,2},{2,0},{4,6},{6,4},{8,10},{10,8},{12,14},{14,12},{1,3},{3,1},... | collective-permute-start | bytes 983048 | tf_op jit(solution)/shard_map/ppermute | solution.py:131
  26.8 5.0 %collective-permute-done.7.theirs_ref = s32[5,3]{1,0:T(8,128)S(1)} collective-permute-done((s32[5,3]{1,0:T(8,128)S(1)}, s32[5,3]{1,0:T(8,128)S(1)}, u32[]{:S(2)}, u32[]{:S(2)}) %collective-permute-start.7) | collective-permute-done | bytes 92 | tf_op jit(solution)/shard_map/ppermute | solution.py:154
  31.8 0.0 collective-permute-done.6.rest_2_
  31.8 1.7 %collective-permute-start.9 = (bf16[4,320,128]{2,1,0:T(8,128)(2,1)S(1)}, bf16[4,320,128]{2,1,0:T(8,128)(2,1)S(1)}, u32[]{:S(2)}, u32[]{:S(2)}) collective-permute-start(bf16[4,320,128]{2,1,0:T(8,128)(2,1)S(1)} %collective-permute-done.6.rest_2_), channel_id=1, source_target_pairs={{0,2},{2,0},{4,6},{6,4},{8,10},{10,8},{12,14},{14,12},{1,3},{3,1},... | collective-permute-start | bytes 983048 | tf_op jit(solution)/shard_map/ppermute | solution.py:131
  33.5 0.0 collective-permute-start.10
  33.5 0.5 collective-permute-start.12
  34.1 8.6 %collective-permute-done.8.rest_1_ = bf16[4,320,128]{2,1,0:T(8,128)(2,1)S(1)} collective-permute-done((bf16[4,320,128]{2,1,0:T(8,128)(2,1)S(1)}, bf16[4,320,128]{2,1,0:T(8,128)(2,1)S(1)}, u32[]{:S(2)}, u32[]{:S(2)}) %collective-permute-start.8) | collective-permute-done | bytes 327712 | tf_op jit(solution)/shard_map/ppermute | solution.py:131
  42.7 0.0 collective-permute-start.11
  42.7 6.1 %collective-permute-done.9.rest_3_ = bf16[4,320,128]{2,1,0:T(8,128)(2,1)S(1)} collective-permute-done((bf16[4,320,128]{2,1,0:T(8,128)(2,1)S(1)}, bf16[4,320,128]{2,1,0:T(8,128)(2,1)S(1)}, u32[]{:S(2)}, u32[]{:S(2)}) %collective-permute-start.9) | collective-permute-done | bytes 327712 | tf_op jit(solution)/shard_map/ppermute | solution.py:131
  48.8 0.0 collective-permute-start.13
  48.8 0.7 constant_dynamic-slice_fusion.gate_ref
  49.5 0.0 collective-permute-done.10.rest_4_
  49.5 0.0 collective-permute-done.11.rest_5_
  49.5 0.0 collective-permute-done.12.rest_6_
  49.5 1.0 %collective-permute-done.13.rest_7_ = bf16[4,320,128]{2,1,0:T(8,128)(2,1)} collective-permute-done((bf16[4,320,128]{2,1,0:T(8,128)(2,1)S(1)}, bf16[4,320,128]{2,1,0:T(8,128)(2,1)}, u32[]{:S(2)}, u32[]{:S(2)}) %collective-permute-start.13) | collective-permute-done | bytes 327712 | tf_op jit(solution)/shard_map/ppermute | solution.py:159
  50.6 0.0 all-to-all-done.got_ref
  50.6 4.0 %shard_map.66 = bf16[32,32,128]{2,1,0:T(8,128)(2,1)S(1)} custom-call(s32[5,3]{1,0:T(8,128)S(1)} %pad_add_fusion.mine_ref, s32[5,3]{1,0:T(8,128)S(1)} %collective-permute-done.7.theirs_ref, f32[1,128]{1,0:T(1,128)S(1)} %constant_dynamic-slice_fusion.gate_ref, bf16[8,448,128]{2,1,0:T(8,128)(2,1)S(1)} %all-to-all-done.got_ref, ...), custom_call_target="tpu_custom_call" | custom-call | tf_op jit(solution)/shard_map/pallas_call | solution.py:161
  54.5 14.7 %all_to_all.10 = bf16[32,32,128]{2,1,0:T(8,128)(2,1)S(1)} all-to-all(bf16[32,32,128]{2,1,0:T(8,128)(2,1)S(1)} %shard_map.66), channel_id=1, replica_groups=mesh['groups'=2,'ctx'=8,'head'=2] {'groups','ctx','head'}, dimensions={0} | all-to-all | bytes 524288 | tf_op jit(solution)/shard_map/all_to_all | solution.py:173
  69.2 0.2 copy.14
  69.4 0.8 %copy.19 = bf16[4,8,32,128]{3,1,2,0:T(8,128)(2,1)} copy(bf16[4,8,32,128]{3,2,1,0:T(8,128)(2,1)S(1)} %bitcast.20) | data formatting | bytes 524288
  (1 shorter events, 0.0 us)
Async XLA Ops:
  0.0 9.3 %copy-start = (bf16[160,2,2048]{2,1,0:T(2,128)(2,1)S(1)}, bf16[160,2,2048]{2,1,0:T(2,128)(2,1)}, u32[]{:S(2)}) copy-start(bf16[160,2,2048]{2,1,0:T(2,128)(2,1)} %param.10) | copy-start | bytes 3932164
  1.9 7.4 %collective-permute-start = (bf16[8,32,128]{2,1,0:T(8,128)(2,1)}, bf16[8,32,128]{2,1,0:T(8,128)(2,1)S(1)}, u32[]{:S(2)}, u32[]{:S(2)}) collective-permute-start(bf16[8,32,128]{2,1,0:T(8,128)(2,1)} %get-tuple-element.18), channel_id=1, source_target_pairs={{0,1},{1,0},{2,3},{3,2},{4,5},{5,4},{6,7},{7,6},{8,9},{9,8},{10,11... | collective-permute-start | bytes 196616 | tf_op jit(solution)/shard_map/ppermute | solution.py:138
  2.4 13.9 %collective-permute-start.5 = (bf16[320,128]{1,0:T(8,128)(2,1)}, bf16[320,128]{1,0:T(8,128)(2,1)S(1)}, u32[]{:S(2)}, u32[]{:S(2)}) collective-permute-start(bf16[320,128]{1,0:T(8,128)(2,1)} %get-tuple-element.22), channel_id=1, source_target_pairs={{0,12},{2,14},{4,8},{6,10},{8,4},{10,6},{12,0},{14,2},{1,13},{3,15... | collective-permute-start | bytes 245768 | tf_op jit(solution)/shard_map/ppermute | solution.py:131
  7.0 9.3 %collective-permute-start.4 = (bf16[320,128]{1,0:T(8,128)(2,1)}, bf16[320,128]{1,0:T(8,128)(2,1)S(1)}, u32[]{:S(2)}, u32[]{:S(2)}) collective-permute-start(bf16[320,128]{1,0:T(8,128)(2,1)} %get-tuple-element.22), channel_id=1, source_target_pairs={{0,8},{2,10},{4,12},{6,14},{8,0},{10,2},{12,4},{14,6},{1,9},{3,11}... | collective-permute-start | bytes 245768 | tf_op jit(solution)/shard_map/ppermute | solution.py:131
  7.0 9.3 %collective-permute-start.3 = (bf16[320,128]{1,0:T(8,128)(2,1)}, bf16[320,128]{1,0:T(8,128)(2,1)S(1)}, u32[]{:S(2)}, u32[]{:S(2)}) collective-permute-start(bf16[320,128]{1,0:T(8,128)(2,1)} %get-tuple-element.22), channel_id=1, source_target_pairs={{0,4},{2,6},{4,0},{6,2},{8,12},{10,14},{12,8},{14,10},{1,5},{3,7},... | collective-permute-start | bytes 245768 | tf_op jit(solution)/shard_map/ppermute | solution.py:131
  7.6 4.5 %collective-permute-start.1 = (bf16[8,32,128]{2,1,0:T(8,128)(2,1)}, bf16[8,32,128]{2,1,0:T(8,128)(2,1)S(1)}, u32[]{:S(2)}, u32[]{:S(2)}) collective-permute-start(bf16[8,32,128]{2,1,0:T(8,128)(2,1)} %get-tuple-element.19), channel_id=1, source_target_pairs={{0,16},{16,0},{1,17},{17,1},{2,18},{18,2},{3,19},{19,3},{4,20},{20... | collective-permute-start | bytes 196616 | tf_op jit(solution)/shard_map/ppermute | solution.py:139
  9.3 0.9 %copy-start.2 = (bf16[8,32,128]{2,1,0:T(8,128)(2,1)}, bf16[8,32,128]{2,1,0:T(8,128)(2,1)S(1)}, u32[]{:S(2)}) copy-start(bf16[8,32,128]{2,1,0:T(8,128)(2,1)S(1)} %collective-permute-done.rest_1_) | copy-start | bytes 196612
  9.3 4.2 %collective-permute-start.2 = (bf16[8,32,128]{2,1,0:T(8,128)(2,1)}, bf16[8,32,128]{2,1,0:T(8,128)(2,1)S(1)}, u32[]{:S(2)}, u32[]{:S(2)}) collective-permute-start(bf16[8,32,128]{2,1,0:T(8,128)(2,1)} %get-tuple-element.20), channel_id=1, source_target_pairs={{0,17},{1,16},{16,1},{17,0},{2,19},{3,18},{18,3},{19,2},{4,21},{5,... | collective-permute-start | bytes 196616 | tf_op jit(solution)/shard_map/ppermute | solution.py:140
  12.1 1.4 %copy-start.3 = (bf16[8,32,128]{2,1,0:T(8,128)(2,1)}, bf16[8,32,128]{2,1,0:T(8,128)(2,1)S(1)}, u32[]{:S(2)}) copy-start(bf16[8,32,128]{2,1,0:T(8,128)(2,1)S(1)} %collective-permute-done.1.rest_2_) | copy-start | bytes 196612
  13.5 0.6 copy-start.4
  16.3 6.1 %copy-start.1 = (bf16[320,128]{1,0:T(8,128)(2,1)S(1)}, bf16[320,128]{1,0:T(8,128)(2,1)}, u32[]{:S(2)}) copy-start(bf16[320,128]{1,0:T(8,128)(2,1)} %get-tuple-element.22) | copy-start | bytes 245764
  16.3 7.0 %copy-start.5 = (s32[5,2]{0,1:T(2,128)S(1)}, s32[5,2]{0,1:T(2,128)}, u32[]{:S(2)}) copy-start(s32[5,2]{0,1:T(2,128)} %param.8) | copy-start | bytes 124
  16.3 7.1 %copy-start.6 = (s32[5]{0:T(128)S(1)}, s32[5]{0:T(128)}, u32[]{:S(2)}) copy-start(s32[5]{0:T(128)} %param.9) | copy-start | bytes 64
  16.3 34.2 %all-to-all-start = ((bf16[8,448,128]{2,1,0:T(8,128)(2,1)}), bf16[8,448,128]{2,1,0:T(8,128)(2,1)S(1)}, u32[]{:S(2)}, u32[]{:S(2)}) async-start(bf16[8,448,128]{2,1,0:T(8,128)(2,1)} %shard_map.65), calls=%async_computation | async-start | bytes 1835008 | tf_op jit(solution)/shard_map/all_to_all | solution.py:152
  22.4 9.4 %collective-permute-start.6 = (bf16[4,320,128]{2,1,0:T(8,128)(2,1)S(1)}, bf16[4,320,128]{2,1,0:T(8,128)(2,1)S(1)}, u32[]{:S(2)}, u32[]{:S(2)}) collective-permute-start(bf16[4,320,128]{2,1,0:T(8,128)(2,1)S(1)} %pad_maximum_fusion.rest_0_), channel_id=1, source_target_pairs={{0,16},{16,0},{1,17},{17,1},{2,18},{18,2},{3,19},{19,3},{4,20},{20... | collective-permute-start | bytes 983048 | tf_op jit(solution)/shard_map/ppermute | solution.py:156
  23.6 8.2 %collective-permute-start.7 = (s32[5,3]{1,0:T(8,128)S(1)}, s32[5,3]{1,0:T(8,128)S(1)}, u32[]{:S(2)}, u32[]{:S(2)}) collective-permute-start(s32[5,3]{1,0:T(8,128)S(1)} %pad_add_fusion.mine_ref), channel_id=1, source_target_pairs={{0,16},{16,0},{1,17},{17,1},{2,18},{18,2},{3,19},{19,3},{4,20},{20... | collective-permute-start | bytes 188 | tf_op jit(solution)/shard_map/ppermute | solution.py:154
  24.8 17.9 %collective-permute-start.8 = (bf16[4,320,128]{2,1,0:T(8,128)(2,1)S(1)}, bf16[4,320,128]{2,1,0:T(8,128)(2,1)S(1)}, u32[]{:S(2)}, u32[]{:S(2)}) collective-permute-start(bf16[4,320,128]{2,1,0:T(8,128)(2,1)S(1)} %pad_maximum_fusion.rest_0_), channel_id=1, source_target_pairs={{0,2},{2,0},{4,6},{6,4},{8,10},{10,8},{12,14},{14,12},{1,3},{3,1},... | collective-permute-start | bytes 983048 | tf_op jit(solution)/shard_map/ppermute | solution.py:131
  31.8 17.0 %collective-permute-start.9 = (bf16[4,320,128]{2,1,0:T(8,128)(2,1)S(1)}, bf16[4,320,128]{2,1,0:T(8,128)(2,1)S(1)}, u32[]{:S(2)}, u32[]{:S(2)}) collective-permute-start(bf16[4,320,128]{2,1,0:T(8,128)(2,1)S(1)} %collective-permute-done.6.rest_2_), channel_id=1, source_target_pairs={{0,2},{2,0},{4,6},{6,4},{8,10},{10,8},{12,14},{14,12},{1,3},{3,1},... | collective-permute-start | bytes 983048 | tf_op jit(solution)/shard_map/ppermute | solution.py:131
  33.5 16.0 %collective-permute-start.10 = (bf16[4,320,128]{2,1,0:T(8,128)(2,1)S(1)}, bf16[4,320,128]{2,1,0:T(8,128)(2,1)}, u32[]{:S(2)}, u32[]{:S(2)}) collective-permute-start(bf16[4,320,128]{2,1,0:T(8,128)(2,1)S(1)} %pad_maximum_fusion.rest_0_), channel_id=1, source_target_pairs={{0,1},{1,0},{2,3},{3,2},{4,5},{5,4},{6,7},{7,6},{8,9},{9,8},{10,11... | collective-permute-start | bytes 983048 | tf_op jit(solution)/shard_map/ppermute | solution.py:159
  33.5 16.0 %collective-permute-start.12 = (bf16[4,320,128]{2,1,0:T(8,128)(2,1)S(1)}, bf16[4,320,128]{2,1,0:T(8,128)(2,1)}, u32[]{:S(2)}, u32[]{:S(2)}) collective-permute-start(bf16[4,320,128]{2,1,0:T(8,128)(2,1)S(1)} %collective-permute-done.6.rest_2_), channel_id=1, source_target_pairs={{0,1},{1,0},{2,3},{3,2},{4,5},{5,4},{6,7},{7,6},{8,9},{9,8},{10,11... | collective-permute-start | bytes 983048 | tf_op jit(solution)/shard_map/ppermute | solution.py:159
  42.7 6.8 %collective-permute-start.11 = (bf16[4,320,128]{2,1,0:T(8,128)(2,1)S(1)}, bf16[4,320,128]{2,1,0:T(8,128)(2,1)}, u32[]{:S(2)}, u32[]{:S(2)}) collective-permute-start(bf16[4,320,128]{2,1,0:T(8,128)(2,1)S(1)} %collective-permute-done.8.rest_1_), channel_id=1, source_target_pairs={{0,1},{1,0},{2,3},{3,2},{4,5},{5,4},{6,7},{7,6},{8,9},{9,8},{10,11... | collective-permute-start | bytes 983048 | tf_op jit(solution)/shard_map/ppermute | solution.py:159
  48.8 1.8 %collective-permute-start.13 = (bf16[4,320,128]{2,1,0:T(8,128)(2,1)S(1)}, bf16[4,320,128]{2,1,0:T(8,128)(2,1)}, u32[]{:S(2)}, u32[]{:S(2)}) collective-permute-start(bf16[4,320,128]{2,1,0:T(8,128)(2,1)S(1)} %collective-permute-done.9.rest_3_), channel_id=1, source_target_pairs={{0,1},{1,0},{2,3},{3,2},{4,5},{5,4},{6,7},{7,6},{8,9},{9,8},{10,11... | collective-permute-start | bytes 983048 | tf_op jit(solution)/shard_map/ppermute | solution.py:159

commit v3 on v0

--- a/solution.py
+++ b/solution.py
@@ -1,6 +1,10 @@
+import functools
+
 import jax
 import jax.numpy as jnp
 from jax import lax
+from jax.experimental import pallas as pl
+from jax.experimental.pallas import tpu as pltpu
 from jax.sharding import PartitionSpec as P
 
 DH = 128
@@ -15,7 +19,164 @@
     return (centered * lax.rsqrt(spread + 1e-05)).reshape(x.shape)
 
 
-def shards(queries, latents, image_span, image_owner, kv_weight, attn_gate):
+def row_norm(x):
+    centered = x - jnp.mean(x, -1, keepdims=True)
+    spread = jnp.mean(centered * centered, -1, keepdims=True)
+    return centered * lax.rsqrt(spread + 1e-05)
+
+
+def panel_kernel(meta_ref, meta_y_ref, *rest):
+    *stores, panel_ref = rest
+    images = meta_ref.shape[1]
+    lat, half = stores[0].shape[1:]
+    place = lax.axis_index("ctx")
+    for r, meta in enumerate((meta_ref, meta_y_ref)):
+        for i in range(images):
+            turn = meta[2, i] ^ place
+            slot = turn // 2
+            to = slice((r * images + i) * lat, (r * images + i + 1) * lat)
+            for k in range(2):
+                near, far = stores[4 * k + 2 * r : 4 * k + 2 * r + 2]
+                panel_ref[to, k * half : (k + 1) * half] = jnp.where(turn % 2 == 0, near[slot], far[slot])
+
+
+def attend_kernel(sizes, meta_ref, meta_y_ref, gate_ref, got_ref, panel, out_ref, weight):
+    ctx_count, rows, lat, part, heads, images = sizes
+    half = ctx_count // 2 * rows
+    piece = rows // 2
+    group = lax.axis_index("groups")
+    core = lax.axis_index("head")
+    for k in range(2):
+        first = (core ^ k) * (ctx_count // 2)
+        for s in range(ctx_count // 2):
+            for g in range(2):
+                to = slice(k * half + s * rows + g * piece, k * half + s * rows + (g + 1) * piece)
+                for n in range(heads * 2):
+                    weight[to, n * DH : (n + 1) * DH] = got_ref[
+                        g * ctx_count + first + s, n * piece : (n + 1) * piece, :
+                    ]
+    count = ctx_count * 2 * part
+    queries = []
+    for r in range(2):
+        query = got_ref[pl.ds((group ^ r) * ctx_count, ctx_count), rows : rows + 2 * part, :]
+        queries.append(row_norm(query.reshape(count, DH).astype(jnp.float32)).astype(jnp.bfloat16))
+    gate = jnp.tanh(gate_ref[...])
+    row = lax.broadcasted_iota(jnp.int32, (1, count), 1)
+    block = row // part
+    position = (block // 2 * 2 + (block % 2 ^ core)) * part + row % part
+    both = jnp.dot(panel[...], weight[...], preferred_element_type=jnp.float32)
+    keys = row_norm(both[:, :DH]).astype(jnp.bfloat16)
+    values = both[:, DH:].astype(jnp.bfloat16)
+    for r, spans in enumerate((meta_ref, meta_y_ref)):
+        at = r * images * lat
+        scores = lax.dot_general(
+            keys[at : at + images * lat], queries[r], (((1,), (1,)), ((), ())), preferred_element_type=jnp.float32
+        ) * DH ** (-0.5)
+        weighted = []
+        for i in range(images):
+            inside = (position >= spans[0, i]) & (position < spans[1, i])
+            weighted.append(jnp.where(inside, jnp.exp(scores[i * lat : (i + 1) * lat]), 0.0))
+        total = sum(jnp.sum(w, 0, keepdims=True) for w in weighted)
+        scale = 1.0 / jnp.where(total > 0.0, total, 1.0)
+        probs = jnp.concatenate([(w * scale).astype(jnp.bfloat16) for w in weighted], 0)
+        attended = lax.dot_general(values[at : at + images * lat], probs, (((0,), (0,)), ((), ())), preferred_element_type=jnp.float32).T
+        gated = (gate * attended).astype(jnp.bfloat16).reshape(ctx_count, 2, part, DH)
+        for c in range(ctx_count):
+            for d in range(2):
+                to = ((group ^ r) * ctx_count + c) * 2 + (core ^ d)
+                out_ref[to] = gated[c, d]
+
+
+def split_kernel(query_ref, own_ref, core_ref):
+    core = lax.axis_index("head")
+    count = own_ref.shape[0]
+    for k, to in enumerate((own_ref, core_ref)):
+        for c in range(count):
+            to[c] = query_ref[:, pl.ds(pl.multiple_of(((core ^ k) * count + c) * DH, DH), DH)]
+
+
+def join_kernel(weight_ref, *rest):
+    *pieces, out_ref = rest
+    rows = weight_ref.shape[1]
+    part = pieces[0].shape[1]
+    out_ref[:, :rows, :] = weight_ref[...]
+    for k, piece in enumerate(pieces):
+        out_ref[:, rows + k * part : rows + (k + 1) * part, :] = piece[...]
+
+
+def by_heads(queries, latents, image_span, image_owner, kv_weight, attn_gate):
+    ctx_count = lax.axis_size("ctx")
+    group = lax.axis_index("groups")
+    place = lax.axis_index("ctx")
+    core = lax.axis_index("head")
+    part = queries.shape[0]
+    width = kv_weight.shape[2]
+    span = width // 2
+    rows = kv_weight.shape[0]
+    lat, depth = latents.shape[1:]
+    images = image_span.shape[0]
+    swap = [(0, 1), (1, 0)]
+    smem = pl.BlockSpec(memory_space=pltpu.SMEM)
+    vmem = pl.BlockSpec(memory_space=pltpu.VMEM)
+
+    def across(x, turn):
+        return lax.ppermute(x, "ctx", [(i, i ^ turn) for i in range(ctx_count)])
+
+    share = lax.dynamic_slice_in_dim(latents[0], core * (depth // 2), depth // 2, 1)
+    held = [share] + [across(share, 2 * k) for k in range(1, ctx_count // 2)]
+    piece = jax.ShapeDtypeStruct((2 * ctx_count, part, DH), jnp.bfloat16)
+    own, sent = pl.pallas_call(
+        split_kernel,
+        out_shape=[piece] * 2,
+        in_specs=[vmem],
+        out_specs=[vmem] * 2,
+        compiler_params=pltpu.CompilerParams(vmem_limit_bytes=4 * 1024 * 1024),
+    )(queries)
+    came = lax.ppermute(sent, "head", swap)
+    own, meta = lax.optimization_barrier((own, (image_span.T, image_owner[None, :])))
+    meta = jnp.concatenate(meta, 0)
+    meta_y = lax.ppermute(meta, "groups", swap)
+    half = rows // 2
+    weight = lax.dynamic_slice_in_dim(kv_weight, group * half, half, 0)
+    weight = weight.reshape(half, 2, 2 * ctx_count, DH).transpose(2, 1, 0, 3)
+    weight = weight.reshape(2 * ctx_count, 2 * half, DH)
+    outgoing = pl.pallas_call(
+        join_kernel,
+        out_shape=jax.ShapeDtypeStruct((2 * ctx_count, 2 * half + 2 * part, DH), jnp.bfloat16),
+        in_specs=[vmem] * 3,
+        out_specs=vmem,
+        compiler_params=pltpu.CompilerParams(vmem_limit_bytes=6 * 1024 * 1024),
+    )(weight, own, came)
+    outgoing, meta_y, *held = lax.optimization_barrier((outgoing, meta_y, *held))
+    got = lax.all_to_all(outgoing, ("groups", "ctx"), split_axis=0, concat_axis=0, tiled=True)
+    near = jnp.stack(held)
+    near_y, far = lax.optimization_barrier((lax.ppermute(near, "groups", swap), across(near, 1)))
+    stores = [near, far, near_y, across(near_y, 1)]
+    stores += [lax.ppermute(x, "head", swap) for x in stores]
+    gate = lax.dynamic_slice_in_dim(attn_gate.reshape(-1, DH), group * ctx_count + place, 1, 0)
+    panel = pl.pallas_call(
+        panel_kernel,
+        out_shape=jax.ShapeDtypeStruct((2 * images * lat, depth), jnp.bfloat16),
+        in_specs=[smem] * 2 + [vmem] * 8,
+        out_specs=vmem,
+        cost_estimate=pl.CostEstimate(flops=9_200_000_000, bytes_accessed=4 * 1024 * 1024, transcendentals=0),
+        compiler_params=pltpu.CompilerParams(vmem_limit_bytes=8 * 1024 * 1024),
+    )(meta, meta_y, *stores)
+    gated = pl.pallas_call(
+        functools.partial(attend_kernel, (ctx_count, rows, lat, part, 1, images)),
+        out_shape=jax.ShapeDtypeStruct((ctx_count * 4, part, DH), jnp.bfloat16),
+        in_specs=[smem] * 2 + [vmem] * 3,
+        out_specs=vmem,
+        scratch_shapes=[pltpu.VMEM((depth, 2 * DH), jnp.bfloat16)],
+        compiler_params=pltpu.CompilerParams(vmem_limit_bytes=16 * 1024 * 1024),
+    )(meta, meta_y, gate, got, panel)
+    every = ("groups", "ctx", "head")
+    back = lax.all_to_all(gated, every, split_axis=0, concat_axis=0, tiled=True)
+    back = back.reshape(2, ctx_count, 2, part, DH).transpose(3, 2, 0, 1, 4)
+    return back.reshape(part, 2 * width)
+
+
+def by_tokens(queries, latents, image_span, image_owner, kv_weight, attn_gate):
     ctx_count = lax.axis_size("ctx")
     rows = lax.all_to_all(queries, "head", split_axis=1, concat_axis=0, tiled=True)
     tok = rows.shape[0]
@@ -72,6 +233,17 @@
     return lax.all_to_all(gated, "head", split_axis=0, concat_axis=1, tiled=True)
 
 
+def shards(*args):
+    ctx_count = lax.axis_size("ctx")
+    weight = args[4]
+    pairs = lax.axis_size("groups") == 2 and lax.axis_size("head") == 2
+    whole_heads = weight.shape[2] == 2 * ctx_count * DH
+    whole_blocks = args[1].shape[2] % (2 * DH) == 0 and weight.shape[0] % 32 == 0
+    if pairs and whole_heads and whole_blocks and ctx_count & (ctx_count - 1) == 0:
+        return by_heads(*args)
+    return by_tokens(*args)
+
+
 def solution(mesh):
     placed = (
         P(("groups", "ctx", "head"), None),

time: 229 us -> 63.3 us (0.28)
  waiting for transfers between devices: 147 us -> 20.3 us
  local copies, waits for them, and re-layouts: 27.9 us -> 7.36 us
  between operations: 13.7 us -> 0.09 us
  other arithmetic: 13.7 us -> 0.76 us
  blocking collectives: 3.94 us -> 13.9 us
  matrix products: 7.57 us -> 0 us
  Pallas kernels: 0 us -> 5.17 us
    all_gather x1 -> x0, waiting for transfers between devices: 92.1 us -> none  [shards(): gathered = lax.all_gather(kv_weight, 'ctx', axis=0, tiled=True)]
    all_to_all x3 -> x1, waiting for transfers between devices: 54.5 us -> 1.98 us  [by_heads(): lax.all_to_all(outgoing, ('groups', 'ctx'), split_axis=0, concat_axis=0,...]
    ppermute x0 -> x12, waiting for transfers between devices: none -> 18.3 us  [the longest x5 11.7 us: across(): return lax.ppermute(x, 'ctx', [(i, i ^ turn) for i in range(ctx_count)])]
    unnamed x21 -> x9, local copies, waits for them, and re-layouts: 20.4 us -> 4.37 us
    ppermute x0 -> x12, starting transfers between devices: none -> 11 us  [the longest x5 7.25 us: across(): return lax.ppermute(x, 'ctx', [(i, i ^ turn) for i in range(ctx_count)])]
    all_to_all x3 -> x1, starting transfers between devices: 14.4 us -> 4.47 us  [by_heads(): lax.all_to_all(outgoing, ('groups', 'ctx'), split_axis=0, concat_axis=0,...]
    all_to_all x1, blocking collectives: 3.94 us -> 13.9 us  [by_heads(): back = lax.all_to_all(gated, every, split_axis=0, concat_axis=0, tiled=True)]
    dot_general x3 -> x0, matrix products: 7.57 us -> none  [the longest x1 5.65 us: shards(): jnp.dot(panels.reshape(MAXIMG * lat, panels.shape[3]), flat_weight, prefe...]
  transfers between devices with their start and end apart: 4 -> 13, of which waited for: 3 -> 7; matrix products, arithmetic and copies ran while one was open for 8% -> 4% of each run, Pallas kernels for 0% -> 4%
where the time goes in v3:
time: 63.3 us; the launch traced here: 62.9 us
  waiting for transfers between devices  20.3 us (32%)
  starting transfers between devices  15.4 us (24%)
  blocking collectives  13.9 us (22%)
  local copies, waits for them, and re-layouts  7.36 us (12%)
  Pallas kernels  5.17 us (8%)
  other arithmetic  0.76 us (1%)
    all_to_all x1, blocking collectives, by_heads(): back = lax.all_to_all(gated, every, split_axis=0, concat_axis=0, tiled=True)  13.9 us
    ppermute x5, waiting for transfers between devices, across(): return lax.ppermute(x, 'ctx', [(i, i ^ turn) for i in range(ctx_count)])  11.7 us
    ppermute x5, starting transfers between devices, across(): return lax.ppermute(x, 'ctx', [(i, i ^ turn) for i in range(ctx_count)])  7.25 us
    ppermute x1, waiting for transfers between devices, by_heads(): lax.ppermute(near, 'groups', swap)  5.35 us
    all_to_all x1, starting transfers between devices, by_heads(): lax.all_to_all(outgoing, ('groups', 'ctx'), split_axis=0, concat_axis=0,...  4.47 us
    unnamed x9, local copies, waits for them, and re-layouts  4.37 us
    pallas_call x1, Pallas kernels, by_heads(): pl.pallas_call(functools.partial(attend_kernel, (ctx_count, rows, lat, pa...  2.6 us
    all_to_all x1, waiting for transfers between devices, by_heads(): lax.all_to_all(outgoing, ('groups', 'ctx'), split_axis=0, concat_axis=0,...  1.98 us
  transfers between devices with their start and end apart: 13, of which 7 were waited for; matrix products, arithmetic and copies ran while one was open for 4% of the time, Pallas kernels for 4%

profile of v3, /device:TPU:0, one launch (start us, length us, event | category | flops | bytes accessed | tf_op | source)
XLA Modules:
  0.0 62.9 jit_solution(9750077236099176424)
XLA Ops:
  0.0 0.0 copy-start
  0.0 1.0 %dynamic-slice_bitcast_fusion = bf16[64,640]{1,0:T(8,128)(2,1)S(1)} fusion(bf16[1,64,1280]{2,1,0:T(8,128)(2,1)} %param.7, s32[]{:T(128)S(6)} %select_n.10), kind=kLoop, calls=%fused_computation.2 | loop fusion | bytes 163844 | tf_op jit(solution)/shard_map/dynamic_slice | solution.py:125
  1.0 5.0 %collective-permute-start.4 = (bf16[64,640]{1,0:T(8,128)(2,1)S(1)}, bf16[64,640]{1,0:T(8,128)(2,1)S(1)}, u32[]{:S(2)}, u32[]{:S(2)}) collective-permute-start(bf16[64,640]{1,0:T(8,128)(2,1)S(1)} %dynamic-slice_bitcast_fusion), channel_id=1, source_target_pairs={{0,12},{2,14},{4,8},{6,10},{8,4},{10,6},{12,0},{14,2},{1,13},{3,15... | collective-permute-start | bytes 245768 | tf_op jit(solution)/shard_map/ppermute | solution.py:123
  6.1 0.0 collective-permute-start.3
  6.1 0.6 %collective-permute-start.2 = (bf16[64,640]{1,0:T(8,128)(2,1)S(1)}, bf16[64,640]{1,0:T(8,128)(2,1)S(1)}, u32[]{:S(2)}, u32[]{:S(2)}) collective-permute-start(bf16[64,640]{1,0:T(8,128)(2,1)S(1)} %dynamic-slice_bitcast_fusion), channel_id=1, source_target_pairs={{0,4},{2,6},{4,0},{6,2},{8,12},{10,14},{12,8},{14,10},{1,5},{3,7},... | collective-permute-start | bytes 245768 | tf_op jit(solution)/shard_map/ppermute | solution.py:123
  6.7 0.0 copy-start.3
  6.7 0.9 %copy-done.3 = bf16[32,4096]{1,0:T(8,128)(2,1)S(1)} copy-done((bf16[32,4096]{1,0:T(8,128)(2,1)S(1)}, bf16[32,4096]{1,0:T(8,128)(2,1)}, u32[]{:S(2)}) %copy-start.3) | copy-done | bytes 262168
  7.6 0.1 shard_map.64
  7.7 0.7 %pad_add_fusion.meta_ref = s32[3,5]{1,0:T(4,128)S(1)} fusion(s32[1,5]{1,0:T(1,128)} %bitcast.29, s32[2,5]{1,0:T(2,128)} %bitcast.28), kind=kLoop, calls=%fused_computation.3 | loop fusion | flops 15 | bytes 120 | tf_op jit(solution)/shard_map/concatenate | solution.py:137
  8.4 1.7 %collective-permute-start.1 = (s32[3,5]{1,0:T(4,128)S(1)}, s32[3,5]{1,0:T(4,128)S(1)}, u32[]{:S(2)}, u32[]{:S(2)}) collective-permute-start(s32[3,5]{1,0:T(4,128)S(1)} %pad_add_fusion.meta_ref), channel_id=1, source_target_pairs={{0,16},{16,0},{1,17},{17,1},{2,18},{18,2},{3,19},{19,3},{4,20},{20... | collective-permute-start | bytes 188 | tf_op jit(solution)/shard_map/ppermute | solution.py:138
  10.1 0.0 collective-permute-start
  10.1 0.0 copy-done
  10.1 0.5 constant_dynamic-slice_fusion.1
  10.5 0.4 reshape.21
  11.0 0.3 copy.9
  11.2 0.2 collective-permute-done.rest_1_
  11.4 1.0 %shard_map.65 = bf16[16,224,128]{2,1,0:T(8,128)(2,1)} custom-call(bf16[16,160,128]{2,1,0:T(8,128)(2,1)S(1)} %bitcast.20, bf16[16,32,128]{2,1,0:T(8,128)(2,1)S(1)} %get-tuple-element.21.rest_0_, bf16[16,32,128]{2,1,0:T(8,128)(2,1)S(1)} %collective-permute-done.rest_1_), custom_call_target="tpu_custom_call" | custom-call | tf_op jit(solution)/shard_map/pallas_call | solution.py:143
  12.4 0.0 collective-permute-done.1.meta_y_ref
  12.4 0.0 collective-permute-done.4
  12.4 0.5 collective-permute-done.3
  12.9 0.0 collective-permute-done.2
  12.9 0.1 pad_maximum_fusion.rest_0_
  13.0 1.6 %collective-permute-start.6 = (bf16[4,64,640]{2,1,0:T(8,128)(2,1)S(1)}, bf16[4,64,640]{2,1,0:T(8,128)(2,1)S(1)}, u32[]{:S(2)}, u32[]{:S(2)}) collective-permute-start(bf16[4,64,640]{2,1,0:T(8,128)(2,1)S(1)} %pad_maximum_fusion.rest_0_), channel_id=1, source_target_pairs={{0,2},{2,0},{4,6},{6,4},{8,10},{10,8},{12,14},{14,12},{1,3},{3,1},... | collective-permute-start | bytes 983048 | tf_op jit(solution)/shard_map/ppermute | solution.py:123
  14.5 1.5 %collective-permute-start.5 = (bf16[4,64,640]{2,1,0:T(8,128)(2,1)S(1)}, bf16[4,64,640]{2,1,0:T(8,128)(2,1)S(1)}, u32[]{:S(2)}, u32[]{:S(2)}) collective-permute-start(bf16[4,64,640]{2,1,0:T(8,128)(2,1)S(1)} %pad_maximum_fusion.rest_0_), channel_id=1, source_target_pairs={{0,16},{16,0},{1,17},{17,1},{2,18},{18,2},{3,19},{19,3},{4,20},{20... | collective-permute-start | bytes 983048 | tf_op jit(solution)/shard_map/ppermute | solution.py:153
  16.1 4.5 %all-to-all-start = ((bf16[16,224,128]{2,1,0:T(8,128)(2,1)}), bf16[16,224,128]{2,1,0:T(8,128)(2,1)S(1)}, u32[]{:S(2)}, u32[]{:S(2)}) async-start(bf16[16,224,128]{2,1,0:T(8,128)(2,1)} %shard_map.65), calls=%async_computation | async-start | bytes 1835008 | tf_op jit(solution)/shard_map/all_to_all | solution.py:151
  20.5 2.0 %collective-permute-done.6.rest_1_ = bf16[4,64,640]{2,1,0:T(8,128)(2,1)S(1)} collective-permute-done((bf16[4,64,640]{2,1,0:T(8,128)(2,1)S(1)}, bf16[4,64,640]{2,1,0:T(8,128)(2,1)S(1)}, u32[]{:S(2)}, u32[]{:S(2)}) %collective-permute-start.6) | collective-permute-done | bytes 327712 | tf_op jit(solution)/shard_map/ppermute | solution.py:123
  22.5 5.4 %collective-permute-done.5.rest_2_ = bf16[4,64,640]{2,1,0:T(8,128)(2,1)S(1)} collective-permute-done((bf16[4,64,640]{2,1,0:T(8,128)(2,1)S(1)}, bf16[4,64,640]{2,1,0:T(8,128)(2,1)S(1)}, u32[]{:S(2)}, u32[]{:S(2)}) %collective-permute-start.5) | collective-permute-done | bytes 327712 | tf_op jit(solution)/shard_map/ppermute | solution.py:153
  27.9 0.0 collective-permute-start.7
  27.9 0.0 collective-permute-start.8
  27.9 0.5 collective-permute-start.10
  28.4 0.0 collective-permute-start.9
  28.4 9.2 %collective-permute-done.7.rest_3_ = bf16[4,64,640]{2,1,0:T(8,128)(2,1)S(1)} collective-permute-done((bf16[4,64,640]{2,1,0:T(8,128)(2,1)S(1)}, bf16[4,64,640]{2,1,0:T(8,128)(2,1)S(1)}, u32[]{:S(2)}, u32[]{:S(2)}) %collective-permute-start.7) | collective-permute-done | bytes 327712 | tf_op jit(solution)/shard_map/ppermute | solution.py:123
  37.6 0.0 collective-permute-start.11
  37.6 0.7 %constant_dynamic-slice_fusion.gate_ref = f32[1,128]{1,0:T(1,128)S(1)} fusion(f32[16,128]{1,0:T(8,128)} %bitcast.30, s32[]{:T(128)S(6)} %select_n.11), kind=kLoop, calls=%fused_computation.4 | loop fusion | bytes 1028 | tf_op jit(solution)/shard_map/dynamic_slice | solution.py:156
  38.3 0.0 collective-permute-done.8.rest_4_
  38.3 0.0 collective-permute-done.9.rest_5_
  38.3 0.0 collective-permute-done.10.rest_6_
  38.3 1.0 %collective-permute-done.11.rest_7_ = bf16[4,64,640]{2,1,0:T(8,128)(2,1)} collective-permute-done((bf16[4,64,640]{2,1,0:T(8,128)(2,1)S(1)}, bf16[4,64,640]{2,1,0:T(8,128)(2,1)}, u32[]{:S(2)}, u32[]{:S(2)}) %collective-permute-start.11) | collective-permute-done | bytes 327712 | tf_op jit(solution)/shard_map/ppermute | solution.py:155
  39.4 1.5 %shard_map.66.panel = bf16[640,1280]{1,0:T(8,128)(2,1)S(1)} custom-call(s32[3,5]{1,0:T(4,128)S(1)} %pad_add_fusion.meta_ref, s32[3,5]{1,0:T(4,128)S(1)} %collective-permute-done.1.meta_y_ref, bf16[4,64,640]{2,1,0:T(8,128)(2,1)S(1)} %pad_maximum_fusion.rest_0_, bf16[4,64,640]{2,1,0:T(8,128)(2,1)S(1)} %collective-permute-done.6.rest_1_, ...), custom_call_target="tpu_custom_call" | custom-call | flops 9200000000 | bytes 4194304 | tf_op jit(solution)/shard_map/pallas_call | solution.py:157
  40.9 0.0 copy-start.1
  40.9 1.2 %copy-done.1 = bf16[640,1280]{1,0:T(8,128)(2,1)} copy-done((bf16[640,1280]{1,0:T(8,128)(2,1)}, bf16[640,1280]{1,0:T(8,128)(2,1)S(1)}, u32[]{:S(2)}) %copy-start.1) | copy-done | bytes 1638424
  42.1 2.0 %all-to-all-done.got_ref = bf16[16,224,128]{2,1,0:T(8,128)(2,1)S(1)} async-done(((bf16[16,224,128]{2,1,0:T(8,128)(2,1)}), bf16[16,224,128]{2,1,0:T(8,128)(2,1)S(1)}, u32[]{:S(2)}, u32[]{:S(2)}) %all-to-all-start) | async-done | bytes 917536 | tf_op jit(solution)/shard_map/all_to_all | solution.py:151
  44.0 0.0 copy-start.2
  44.0 1.4 %copy-done.2 = bf16[640,1280]{1,0:T(8,128)(2,1)S(1)} copy-done((bf16[640,1280]{1,0:T(8,128)(2,1)S(1)}, bf16[640,1280]{1,0:T(8,128)(2,1)}, u32[]{:S(2)}) %copy-start.2) | copy-done | bytes 1638424
  45.5 2.6 %shard_map.67 = bf16[32,32,128]{2,1,0:T(8,128)(2,1)S(1)} custom-call(s32[3,5]{1,0:T(4,128)S(1)} %pad_add_fusion.meta_ref, s32[3,5]{1,0:T(4,128)S(1)} %collective-permute-done.1.meta_y_ref, f32[1,128]{1,0:T(1,128)S(1)} %constant_dynamic-slice_fusion.gate_ref, bf16[16,224,128]{2,1,0:T(8,128)(2,1)S(1)} %all-to-all-done.got_ref, bf16[640,1280]{1,0:T(8,128)(2,1)S(1)} %copy-done.2), custom_call_target="tpu_custom_call" | custom-call | tf_op jit(solution)/shard_map/pallas_call | solution.py:165
  48.1 13.9 %all_to_all.10 = bf16[32,32,128]{2,1,0:T(8,128)(2,1)S(1)} all-to-all(bf16[32,32,128]{2,1,0:T(8,128)(2,1)S(1)} %shard_map.67), channel_id=1, replica_groups=mesh['groups'=2,'ctx'=8,'head'=2] {'groups','ctx','head'}, dimensions={0} | all-to-all | bytes 524288 | tf_op jit(solution)/shard_map/all_to_all | solution.py:174
  61.9 0.2 copy.10
  62.1 0.8 %copy.15 = bf16[4,8,32,128]{3,1,2,0:T(8,128)(2,1)} copy(bf16[4,8,32,128]{3,2,1,0:T(8,128)(2,1)S(1)} %bitcast.23) | data formatting | bytes 524288
Async XLA Ops:
  0.0 10.1 %copy-start = (bf16[160,2,2048]{2,1,0:T(2,128)(2,1)S(1)}, bf16[160,2,2048]{2,1,0:T(2,128)(2,1)}, u32[]{:S(2)}) copy-start(bf16[160,2,2048]{2,1,0:T(2,128)(2,1)} %param.10) | copy-start | bytes 3932164
  1.0 11.4 %collective-permute-start.4 = (bf16[64,640]{1,0:T(8,128)(2,1)S(1)}, bf16[64,640]{1,0:T(8,128)(2,1)S(1)}, u32[]{:S(2)}, u32[]{:S(2)}) collective-permute-start(bf16[64,640]{1,0:T(8,128)(2,1)S(1)} %dynamic-slice_bitcast_fusion), channel_id=1, source_target_pairs={{0,12},{2,14},{4,8},{6,10},{8,4},{10,6},{12,0},{14,2},{1,13},{3,15... | collective-permute-start | bytes 245768 | tf_op jit(solution)/shard_map/ppermute | solution.py:123
  6.1 6.9 %collective-permute-start.3 = (bf16[64,640]{1,0:T(8,128)(2,1)S(1)}, bf16[64,640]{1,0:T(8,128)(2,1)S(1)}, u32[]{:S(2)}, u32[]{:S(2)}) collective-permute-start(bf16[64,640]{1,0:T(8,128)(2,1)S(1)} %dynamic-slice_bitcast_fusion), channel_id=1, source_target_pairs={{0,8},{2,10},{4,12},{6,14},{8,0},{10,2},{12,4},{14,6},{1,9},{3,11}... | collective-permute-start | bytes 245768 | tf_op jit(solution)/shard_map/ppermute | solution.py:123
  6.1 6.9 %collective-permute-start.2 = (bf16[64,640]{1,0:T(8,128)(2,1)S(1)}, bf16[64,640]{1,0:T(8,128)(2,1)S(1)}, u32[]{:S(2)}, u32[]{:S(2)}) collective-permute-start(bf16[64,640]{1,0:T(8,128)(2,1)S(1)} %dynamic-slice_bitcast_fusion), channel_id=1, source_target_pairs={{0,4},{2,6},{4,0},{6,2},{8,12},{10,14},{12,8},{14,10},{1,5},{3,7},... | collective-permute-start | bytes 245768 | tf_op jit(solution)/shard_map/ppermute | solution.py:123
  6.7 0.9 %copy-start.3 = (bf16[32,4096]{1,0:T(8,128)(2,1)S(1)}, bf16[32,4096]{1,0:T(8,128)(2,1)}, u32[]{:S(2)}) copy-start(bf16[32,4096]{1,0:T(8,128)(2,1)} %query_ref.1) | copy-start | bytes 786436
  8.4 4.0 %collective-permute-start.1 = (s32[3,5]{1,0:T(4,128)S(1)}, s32[3,5]{1,0:T(4,128)S(1)}, u32[]{:S(2)}, u32[]{:S(2)}) collective-permute-start(s32[3,5]{1,0:T(4,128)S(1)} %pad_add_fusion.meta_ref), channel_id=1, source_target_pairs={{0,16},{16,0},{1,17},{17,1},{2,18},{18,2},{3,19},{19,3},{4,20},{20... | collective-permute-start | bytes 188 | tf_op jit(solution)/shard_map/ppermute | solution.py:138
  10.1 1.3 %collective-permute-start = (bf16[16,32,128]{2,1,0:T(8,128)(2,1)S(1)}, bf16[16,32,128]{2,1,0:T(8,128)(2,1)S(1)}, u32[]{:S(2)}, u32[]{:S(2)}) collective-permute-start(bf16[16,32,128]{2,1,0:T(8,128)(2,1)S(1)} %get-tuple-element.22), channel_id=1, source_target_pairs={{0,1},{1,0},{2,3},{3,2},{4,5},{5,4},{6,7},{7,6},{8,9},{9,8},{10,11... | collective-permute-start | bytes 393224 | tf_op jit(solution)/shard_map/ppermute | solution.py:135
  13.0 9.5 %collective-permute-start.6 = (bf16[4,64,640]{2,1,0:T(8,128)(2,1)S(1)}, bf16[4,64,640]{2,1,0:T(8,128)(2,1)S(1)}, u32[]{:S(2)}, u32[]{:S(2)}) collective-permute-start(bf16[4,64,640]{2,1,0:T(8,128)(2,1)S(1)} %pad_maximum_fusion.rest_0_), channel_id=1, source_target_pairs={{0,2},{2,0},{4,6},{6,4},{8,10},{10,8},{12,14},{14,12},{1,3},{3,1},... | collective-permute-start | bytes 983048 | tf_op jit(solution)/shard_map/ppermute | solution.py:123
  14.5 13.3 %collective-permute-start.5 = (bf16[4,64,640]{2,1,0:T(8,128)(2,1)S(1)}, bf16[4,64,640]{2,1,0:T(8,128)(2,1)S(1)}, u32[]{:S(2)}, u32[]{:S(2)}) collective-permute-start(bf16[4,64,640]{2,1,0:T(8,128)(2,1)S(1)} %pad_maximum_fusion.rest_0_), channel_id=1, source_target_pairs={{0,16},{16,0},{1,17},{17,1},{2,18},{18,2},{3,19},{19,3},{4,20},{20... | collective-permute-start | bytes 983048 | tf_op jit(solution)/shard_map/ppermute | solution.py:153
  16.1 28.0 %all-to-all-start = ((bf16[16,224,128]{2,1,0:T(8,128)(2,1)}), bf16[16,224,128]{2,1,0:T(8,128)(2,1)S(1)}, u32[]{:S(2)}, u32[]{:S(2)}) async-start(bf16[16,224,128]{2,1,0:T(8,128)(2,1)} %shard_map.65), calls=%async_computation | async-start | bytes 1835008 | tf_op jit(solution)/shard_map/all_to_all | solution.py:151
  27.9 9.7 %collective-permute-start.7 = (bf16[4,64,640]{2,1,0:T(8,128)(2,1)S(1)}, bf16[4,64,640]{2,1,0:T(8,128)(2,1)S(1)}, u32[]{:S(2)}, u32[]{:S(2)}) collective-permute-start(bf16[4,64,640]{2,1,0:T(8,128)(2,1)S(1)} %collective-permute-done.5.rest_2_), channel_id=1, source_target_pairs={{0,2},{2,0},{4,6},{6,4},{8,10},{10,8},{12,14},{14,12},{1,3},{3,1},... | collective-permute-start | bytes 983048 | tf_op jit(solution)/shard_map/ppermute | solution.py:123
  27.9 10.4 %collective-permute-start.8 = (bf16[4,64,640]{2,1,0:T(8,128)(2,1)S(1)}, bf16[4,64,640]{2,1,0:T(8,128)(2,1)}, u32[]{:S(2)}, u32[]{:S(2)}) collective-permute-start(bf16[4,64,640]{2,1,0:T(8,128)(2,1)S(1)} %pad_maximum_fusion.rest_0_), channel_id=1, source_target_pairs={{0,1},{1,0},{2,3},{3,2},{4,5},{5,4},{6,7},{7,6},{8,9},{9,8},{10,11... | collective-permute-start | bytes 983048 | tf_op jit(solution)/shard_map/ppermute | solution.py:155
  27.9 10.4 %collective-permute-start.10 = (bf16[4,64,640]{2,1,0:T(8,128)(2,1)S(1)}, bf16[4,64,640]{2,1,0:T(8,128)(2,1)}, u32[]{:S(2)}, u32[]{:S(2)}) collective-permute-start(bf16[4,64,640]{2,1,0:T(8,128)(2,1)S(1)} %collective-permute-done.5.rest_2_), channel_id=1, source_target_pairs={{0,1},{1,0},{2,3},{3,2},{4,5},{5,4},{6,7},{7,6},{8,9},{9,8},{10,11... | collective-permute-start | bytes 983048 | tf_op jit(solution)/shard_map/ppermute | solution.py:155
  28.4 9.9 %collective-permute-start.9 = (bf16[4,64,640]{2,1,0:T(8,128)(2,1)S(1)}, bf16[4,64,640]{2,1,0:T(8,128)(2,1)}, u32[]{:S(2)}, u32[]{:S(2)}) collective-permute-start(bf16[4,64,640]{2,1,0:T(8,128)(2,1)S(1)} %collective-permute-done.6.rest_1_), channel_id=1, source_target_pairs={{0,1},{1,0},{2,3},{3,2},{4,5},{5,4},{6,7},{7,6},{8,9},{9,8},{10,11... | collective-permute-start | bytes 983048 | tf_op jit(solution)/shard_map/ppermute | solution.py:155
  37.6 1.8 %collective-permute-start.11 = (bf16[4,64,640]{2,1,0:T(8,128)(2,1)S(1)}, bf16[4,64,640]{2,1,0:T(8,128)(2,1)}, u32[]{:S(2)}, u32[]{:S(2)}) collective-permute-start(bf16[4,64,640]{2,1,0:T(8,128)(2,1)S(1)} %collective-permute-done.7.rest_3_), channel_id=1, source_target_pairs={{0,1},{1,0},{2,3},{3,2},{4,5},{5,4},{6,7},{7,6},{8,9},{9,8},{10,11... | collective-permute-start | bytes 983048 | tf_op jit(solution)/shard_map/ppermute | solution.py:155
  40.9 1.2 %copy-start.1 = (bf16[640,1280]{1,0:T(8,128)(2,1)}, bf16[640,1280]{1,0:T(8,128)(2,1)S(1)}, u32[]{:S(2)}) copy-start(bf16[640,1280]{1,0:T(8,128)(2,1)S(1)} %shard_map.66.panel) | copy-start | bytes 4915204
  44.0 1.4 %copy-start.2 = (bf16[640,1280]{1,0:T(8,128)(2,1)S(1)}, bf16[640,1280]{1,0:T(8,128)(2,1)}, u32[]{:S(2)}) copy-start(bf16[640,1280]{1,0:T(8,128)(2,1)} %copy-done.1) | copy-start | bytes 4915204

commit v4 on v3

--- a/solution.py
+++ b/solution.py
@@ -41,21 +41,23 @@
 
 
 def attend_kernel(sizes, meta_ref, meta_y_ref, gate_ref, got_ref, panel, out_ref, weight):
-    ctx_count, rows, lat, part, heads, images = sizes
+    ctx_count, rows, lat, part, images = sizes
     half = ctx_count // 2 * rows
     piece = rows // 2
+    size = images * lat
+    count = ctx_count * 2 * part
     group = lax.axis_index("groups")
     core = lax.axis_index("head")
+    metas = (meta_ref, meta_y_ref)
     for k in range(2):
         first = (core ^ k) * (ctx_count // 2)
         for s in range(ctx_count // 2):
             for g in range(2):
-                to = slice(k * half + s * rows + g * piece, k * half + s * rows + (g + 1) * piece)
-                for n in range(heads * 2):
-                    weight[to, n * DH : (n + 1) * DH] = got_ref[
+                at = k * half + s * rows + g * piece
+                for n in range(2):
+                    weight[at : at + piece, n * DH : (n + 1) * DH] = got_ref[
                         g * ctx_count + first + s, n * piece : (n + 1) * piece, :
                     ]
-    count = ctx_count * 2 * part
     queries = []
     for r in range(2):
         query = got_ref[pl.ds((group ^ r) * ctx_count, ctx_count), rows : rows + 2 * part, :]
@@ -64,27 +66,38 @@
     row = lax.broadcasted_iota(jnp.int32, (1, count), 1)
     block = row // part
     position = (block // 2 * 2 + (block % 2 ^ core)) * part + row % part
-    both = jnp.dot(panel[...], weight[...], preferred_element_type=jnp.float32)
-    keys = row_norm(both[:, :DH]).astype(jnp.bfloat16)
-    values = both[:, DH:].astype(jnp.bfloat16)
-    for r, spans in enumerate((meta_ref, meta_y_ref)):
-        at = r * images * lat
-        scores = lax.dot_general(
-            keys[at : at + images * lat], queries[r], (((1,), (1,)), ((), ())), preferred_element_type=jnp.float32
+
+    def project(r):
+        both = jnp.dot(
+            panel[r * size : (r + 1) * size, :], weight[...], preferred_element_type=jnp.float32
+        )
+        return row_norm(both[:, :DH]).astype(jnp.bfloat16), both[:, DH:].astype(jnp.bfloat16)
+
+    def score(r, keys):
+        return lax.dot_general(
+            keys, queries[r], (((1,), (1,)), ((), ())), preferred_element_type=jnp.float32
         ) * DH ** (-0.5)
+
+    def finish(r, scores, values):
         weighted = []
         for i in range(images):
-            inside = (position >= spans[0, i]) & (position < spans[1, i])
+            inside = (position >= metas[r][0, i]) & (position < metas[r][1, i])
             weighted.append(jnp.where(inside, jnp.exp(scores[i * lat : (i + 1) * lat]), 0.0))
         total = sum(jnp.sum(w, 0, keepdims=True) for w in weighted)
         scale = 1.0 / jnp.where(total > 0.0, total, 1.0)
         probs = jnp.concatenate([(w * scale).astype(jnp.bfloat16) for w in weighted], 0)
-        attended = lax.dot_general(values[at : at + images * lat], probs, (((0,), (0,)), ((), ())), preferred_element_type=jnp.float32).T
+        attended = lax.dot_general(
+            values, probs, (((0,), (0,)), ((), ())), preferred_element_type=jnp.float32
+        ).T
         gated = (gate * attended).astype(jnp.bfloat16).reshape(ctx_count, 2, part, DH)
         for c in range(ctx_count):
             for d in range(2):
-                to = ((group ^ r) * ctx_count + c) * 2 + (core ^ d)
-                out_ref[to] = gated[c, d]
+                out_ref[((group ^ r) * ctx_count + c) * 2 + (core ^ d)] = gated[c, d]
+
+    projected = [project(r) for r in range(2)]
+    scores = [score(r, projected[r][0]) for r in range(2)]
+    for r in range(2):
+        finish(r, scores[r], projected[r][1])
 
 
 def split_kernel(query_ref, own_ref, core_ref):
@@ -102,6 +115,14 @@
     out_ref[:, :rows, :] = weight_ref[...]
     for k, piece in enumerate(pieces):
         out_ref[:, rows + k * part : rows + (k + 1) * part, :] = piece[...]
+
+
+def merge_kernel(back_ref, out_ref):
+    count = back_ref.shape[0] // 4
+    for n in range(4 * count):
+        g, c, h = n // (2 * count), n // 2 % count, n % 2
+        at = ((h * 2 + g) * count + c) * DH
+        out_ref[:, at : at + DH] = back_ref[n]
 
 
 def by_heads(queries, latents, image_span, image_owner, kv_weight, attn_gate):
@@ -163,7 +184,7 @@
         compiler_params=pltpu.CompilerParams(vmem_limit_bytes=8 * 1024 * 1024),
     )(meta, meta_y, *stores)
     gated = pl.pallas_call(
-        functools.partial(attend_kernel, (ctx_count, rows, lat, part, 1, images)),
+        functools.partial(attend_kernel, (ctx_count, rows, lat, part, images)),
         out_shape=jax.ShapeDtypeStruct((ctx_count * 4, part, DH), jnp.bfloat16),
         in_specs=[smem] * 2 + [vmem] * 3,
         out_specs=vmem,
@@ -172,8 +193,13 @@
     )(meta, meta_y, gate, got, panel)
     every = ("groups", "ctx", "head")
     back = lax.all_to_all(gated, every, split_axis=0, concat_axis=0, tiled=True)
-    back = back.reshape(2, ctx_count, 2, part, DH).transpose(3, 2, 0, 1, 4)
-    return back.reshape(part, 2 * width)
+    return pl.pallas_call(
+        merge_kernel,
+        out_shape=jax.ShapeDtypeStruct((part, 2 * width), jnp.bfloat16),
+        in_specs=[vmem],
+        out_specs=vmem,
+        compiler_params=pltpu.CompilerParams(vmem_limit_bytes=4 * 1024 * 1024),
+    )(back)
 
 
 def by_tokens(queries, latents, image_span, image_owner, kv_weight, attn_gate):

time: 63.3 us -> 62.7 us (level)
  local copies, waits for them, and re-layouts: 7.36 us -> 6.38 us
    unnamed x9 -> x8, local copies, waits for them, and re-layouts: 4.37 us -> 3.56 us
    pallas_call x0 -> x1, Pallas kernels: none -> 0.75 us  [by_heads(): pl.pallas_call(merge_kernel, out_shape=jax.ShapeDtypeStruct((part, 2 * wi...]
where the time goes in v4:
time: 62.7 us; the launch traced here: 62.3 us
  waiting for transfers between devices  20.3 us (32%)
  starting transfers between devices  15.4 us (25%)
  blocking collectives  13.9 us (22%)
  local copies, waits for them, and re-layouts  6.38 us (10%)
  Pallas kernels  5.53 us (9%)
  other arithmetic  0.76 us (1%)
    all_to_all x1, blocking collectives, by_heads(): back = lax.all_to_all(gated, every, split_axis=0, concat_axis=0, tiled=True)  13.9 us
    ppermute x5, waiting for transfers between devices, across(): return lax.ppermute(x, 'ctx', [(i, i ^ turn) for i in range(ctx_count)])  11.7 us
    ppermute x5, starting transfers between devices, across(): return lax.ppermute(x, 'ctx', [(i, i ^ turn) for i in range(ctx_count)])  7.25 us
    ppermute x1, waiting for transfers between devices, by_heads(): lax.ppermute(near, 'groups', swap)  5.35 us
    all_to_all x1, starting transfers between devices, by_heads(): lax.all_to_all(outgoing, ('groups', 'ctx'), split_axis=0, concat_axis=0,...  4.47 us
    unnamed x8, local copies, waits for them, and re-layouts  3.56 us
    pallas_call x1, Pallas kernels, by_heads(): pl.pallas_call(functools.partial(attend_kernel, (ctx_count, rows, lat, pa...  2.21 us
    all_to_all x1, waiting for transfers between devices, by_heads(): lax.all_to_all(outgoing, ('groups', 'ctx'), split_axis=0, concat_axis=0,...  1.98 us
  transfers between devices with their start and end apart: 13, of which 7 were waited for; matrix products, arithmetic and copies ran while one was open for 4% of the time, Pallas kernels for 4%

profile of v4, /device:TPU:0, one launch (start us, length us, event | category | flops | bytes accessed | tf_op | source)
XLA Modules:
  0.0 62.3 jit_solution(3609187516259661629)
XLA Ops:
  0.0 0.0 copy-start
  0.0 1.0 %dynamic-slice_bitcast_fusion = bf16[64,640]{1,0:T(8,128)(2,1)S(1)} fusion(bf16[1,64,1280]{2,1,0:T(8,128)(2,1)} %param.7, s32[]{:T(128)S(6)} %select_n.10), kind=kLoop, calls=%fused_computation.1 | loop fusion | bytes 163844 | tf_op jit(solution)/shard_map/dynamic_slice | solution.py:146
  1.0 5.0 %collective-permute-start.4 = (bf16[64,640]{1,0:T(8,128)(2,1)S(1)}, bf16[64,640]{1,0:T(8,128)(2,1)S(1)}, u32[]{:S(2)}, u32[]{:S(2)}) collective-permute-start(bf16[64,640]{1,0:T(8,128)(2,1)S(1)} %dynamic-slice_bitcast_fusion), channel_id=1, source_target_pairs={{0,12},{2,14},{4,8},{6,10},{8,4},{10,6},{12,0},{14,2},{1,13},{3,15... | collective-permute-start | bytes 245768 | tf_op jit(solution)/shard_map/ppermute | solution.py:144
  6.1 0.0 collective-permute-start.3
  6.1 0.6 %collective-permute-start.2 = (bf16[64,640]{1,0:T(8,128)(2,1)S(1)}, bf16[64,640]{1,0:T(8,128)(2,1)S(1)}, u32[]{:S(2)}, u32[]{:S(2)}) collective-permute-start(bf16[64,640]{1,0:T(8,128)(2,1)S(1)} %dynamic-slice_bitcast_fusion), channel_id=1, source_target_pairs={{0,4},{2,6},{4,0},{6,2},{8,12},{10,14},{12,8},{14,10},{1,5},{3,7},... | collective-permute-start | bytes 245768 | tf_op jit(solution)/shard_map/ppermute | solution.py:144
  6.7 0.0 copy-start.3
  6.7 0.9 %copy-done.3 = bf16[32,4096]{1,0:T(8,128)(2,1)S(1)} copy-done((bf16[32,4096]{1,0:T(8,128)(2,1)S(1)}, bf16[32,4096]{1,0:T(8,128)(2,1)}, u32[]{:S(2)}) %copy-start.3) | copy-done | bytes 262168
  7.6 0.1 shard_map.64
  7.7 0.7 %pad_add_fusion.meta_ref = s32[3,5]{1,0:T(4,128)S(1)} fusion(s32[1,5]{1,0:T(1,128)} %bitcast.19, s32[2,5]{1,0:T(2,128)} %bitcast.18), kind=kLoop, calls=%fused_computation.2 | loop fusion | flops 15 | bytes 120 | tf_op jit(solution)/shard_map/concatenate | solution.py:158
  8.4 1.7 %collective-permute-start.1 = (s32[3,5]{1,0:T(4,128)S(1)}, s32[3,5]{1,0:T(4,128)S(1)}, u32[]{:S(2)}, u32[]{:S(2)}) collective-permute-start(s32[3,5]{1,0:T(4,128)S(1)} %pad_add_fusion.meta_ref), channel_id=1, source_target_pairs={{0,16},{16,0},{1,17},{17,1},{2,18},{18,2},{3,19},{19,3},{4,20},{20... | collective-permute-start | bytes 188 | tf_op jit(solution)/shard_map/ppermute | solution.py:159
  10.1 0.0 collective-permute-start
  10.1 0.0 copy-done
  10.1 0.5 constant_dynamic-slice_fusion.1
  10.5 0.4 reshape.13
  11.0 0.3 copy.8
  11.2 0.2 collective-permute-done.rest_1_
  11.4 1.0 %shard_map.65 = bf16[16,224,128]{2,1,0:T(8,128)(2,1)} custom-call(bf16[16,160,128]{2,1,0:T(8,128)(2,1)S(1)} %bitcast.12, bf16[16,32,128]{2,1,0:T(8,128)(2,1)S(1)} %get-tuple-element.21.rest_0_, bf16[16,32,128]{2,1,0:T(8,128)(2,1)S(1)} %collective-permute-done.rest_1_), custom_call_target="tpu_custom_call" | custom-call | tf_op jit(solution)/shard_map/pallas_call | solution.py:164
  12.4 0.0 collective-permute-done.1.meta_y_ref
  12.4 0.0 collective-permute-done.4
  12.4 0.5 collective-permute-done.3
  12.9 0.0 collective-permute-done.2
  12.9 0.1 pad_maximum_fusion.rest_0_
  13.0 1.6 %collective-permute-start.6 = (bf16[4,64,640]{2,1,0:T(8,128)(2,1)S(1)}, bf16[4,64,640]{2,1,0:T(8,128)(2,1)S(1)}, u32[]{:S(2)}, u32[]{:S(2)}) collective-permute-start(bf16[4,64,640]{2,1,0:T(8,128)(2,1)S(1)} %pad_maximum_fusion.rest_0_), channel_id=1, source_target_pairs={{0,2},{2,0},{4,6},{6,4},{8,10},{10,8},{12,14},{14,12},{1,3},{3,1},... | collective-permute-start | bytes 983048 | tf_op jit(solution)/shard_map/ppermute | solution.py:144
  14.5 1.5 %collective-permute-start.5 = (bf16[4,64,640]{2,1,0:T(8,128)(2,1)S(1)}, bf16[4,64,640]{2,1,0:T(8,128)(2,1)S(1)}, u32[]{:S(2)}, u32[]{:S(2)}) collective-permute-start(bf16[4,64,640]{2,1,0:T(8,128)(2,1)S(1)} %pad_maximum_fusion.rest_0_), channel_id=1, source_target_pairs={{0,16},{16,0},{1,17},{17,1},{2,18},{18,2},{3,19},{19,3},{4,20},{20... | collective-permute-start | bytes 983048 | tf_op jit(solution)/shard_map/ppermute | solution.py:174
  16.1 4.5 %all-to-all-start = ((bf16[16,224,128]{2,1,0:T(8,128)(2,1)}), bf16[16,224,128]{2,1,0:T(8,128)(2,1)S(1)}, u32[]{:S(2)}, u32[]{:S(2)}) async-start(bf16[16,224,128]{2,1,0:T(8,128)(2,1)} %shard_map.65), calls=%async_computation | async-start | bytes 1835008 | tf_op jit(solution)/shard_map/all_to_all | solution.py:172
  20.5 2.0 %collective-permute-done.6.rest_1_ = bf16[4,64,640]{2,1,0:T(8,128)(2,1)S(1)} collective-permute-done((bf16[4,64,640]{2,1,0:T(8,128)(2,1)S(1)}, bf16[4,64,640]{2,1,0:T(8,128)(2,1)S(1)}, u32[]{:S(2)}, u32[]{:S(2)}) %collective-permute-start.6) | collective-permute-done | bytes 327712 | tf_op jit(solution)/shard_map/ppermute | solution.py:144
  22.5 5.4 %collective-permute-done.5.rest_2_ = bf16[4,64,640]{2,1,0:T(8,128)(2,1)S(1)} collective-permute-done((bf16[4,64,640]{2,1,0:T(8,128)(2,1)S(1)}, bf16[4,64,640]{2,1,0:T(8,128)(2,1)S(1)}, u32[]{:S(2)}, u32[]{:S(2)}) %collective-permute-start.5) | collective-permute-done | bytes 327712 | tf_op jit(solution)/shard_map/ppermute | solution.py:174
  27.9 0.0 collective-permute-start.7
  27.9 0.0 collective-permute-start.8
  27.9 0.5 collective-permute-start.10
  28.4 0.0 collective-permute-start.9
  28.4 9.2 %collective-permute-done.7.rest_3_ = bf16[4,64,640]{2,1,0:T(8,128)(2,1)S(1)} collective-permute-done((bf16[4,64,640]{2,1,0:T(8,128)(2,1)S(1)}, bf16[4,64,640]{2,1,0:T(8,128)(2,1)S(1)}, u32[]{:S(2)}, u32[]{:S(2)}) %collective-permute-start.7) | collective-permute-done | bytes 327712 | tf_op jit(solution)/shard_map/ppermute | solution.py:144
  37.6 0.0 collective-permute-start.11
  37.6 0.7 %constant_dynamic-slice_fusion.gate_ref = f32[1,128]{1,0:T(1,128)S(1)} fusion(f32[16,128]{1,0:T(8,128)} %bitcast.20, s32[]{:T(128)S(6)} %select_n.11), kind=kLoop, calls=%fused_computation.3 | loop fusion | bytes 1028 | tf_op jit(solution)/shard_map/dynamic_slice | solution.py:177
  38.3 0.0 collective-permute-done.8.rest_4_
  38.3 0.0 collective-permute-done.9.rest_5_
  38.3 0.0 collective-permute-done.10.rest_6_
  38.3 1.0 %collective-permute-done.11.rest_7_ = bf16[4,64,640]{2,1,0:T(8,128)(2,1)} collective-permute-done((bf16[4,64,640]{2,1,0:T(8,128)(2,1)S(1)}, bf16[4,64,640]{2,1,0:T(8,128)(2,1)}, u32[]{:S(2)}, u32[]{:S(2)}) %collective-permute-start.11) | collective-permute-done | bytes 327712 | tf_op jit(solution)/shard_map/ppermute | solution.py:176
  39.4 1.5 %shard_map.66.panel = bf16[640,1280]{1,0:T(8,128)(2,1)S(1)} custom-call(s32[3,5]{1,0:T(4,128)S(1)} %pad_add_fusion.meta_ref, s32[3,5]{1,0:T(4,128)S(1)} %collective-permute-done.1.meta_y_ref, bf16[4,64,640]{2,1,0:T(8,128)(2,1)S(1)} %pad_maximum_fusion.rest_0_, bf16[4,64,640]{2,1,0:T(8,128)(2,1)S(1)} %collective-permute-done.6.rest_1_, ...), custom_call_target="tpu_custom_call" | custom-call | flops 9200000000 | bytes 4194304 | tf_op jit(solution)/shard_map/pallas_call | solution.py:178
  40.9 0.0 copy-start.1
  40.9 1.2 %copy-done.1 = bf16[640,1280]{1,0:T(8,128)(2,1)} copy-done((bf16[640,1280]{1,0:T(8,128)(2,1)}, bf16[640,1280]{1,0:T(8,128)(2,1)S(1)}, u32[]{:S(2)}) %copy-start.1) | copy-done | bytes 1638424
  42.1 2.0 %all-to-all-done.got_ref = bf16[16,224,128]{2,1,0:T(8,128)(2,1)S(1)} async-done(((bf16[16,224,128]{2,1,0:T(8,128)(2,1)}), bf16[16,224,128]{2,1,0:T(8,128)(2,1)S(1)}, u32[]{:S(2)}, u32[]{:S(2)}) %all-to-all-start) | async-done | bytes 917536 | tf_op jit(solution)/shard_map/all_to_all | solution.py:172
  44.0 0.0 copy-start.2
  44.0 1.4 %copy-done.2 = bf16[640,1280]{1,0:T(8,128)(2,1)S(1)} copy-done((bf16[640,1280]{1,0:T(8,128)(2,1)S(1)}, bf16[640,1280]{1,0:T(8,128)(2,1)}, u32[]{:S(2)}) %copy-start.2) | copy-done | bytes 1638424
  45.5 2.2 %shard_map.67 = bf16[32,32,128]{2,1,0:T(8,128)(2,1)S(1)} custom-call(s32[3,5]{1,0:T(4,128)S(1)} %pad_add_fusion.meta_ref, s32[3,5]{1,0:T(4,128)S(1)} %collective-permute-done.1.meta_y_ref, f32[1,128]{1,0:T(1,128)S(1)} %constant_dynamic-slice_fusion.gate_ref, bf16[16,224,128]{2,1,0:T(8,128)(2,1)S(1)} %all-to-all-done.got_ref, bf16[640,1280]{1,0:T(8,128)(2,1)S(1)} %copy-done.2), custom_call_target="tpu_custom_call" | custom-call | tf_op jit(solution)/shard_map/pallas_call | solution.py:186
  47.7 13.9 %all_to_all.10.back_ref = bf16[32,32,128]{2,1,0:T(8,128)(2,1)S(1)} all-to-all(bf16[32,32,128]{2,1,0:T(8,128)(2,1)S(1)} %shard_map.67), channel_id=1, replica_groups=mesh['groups'=2,'ctx'=8,'head'=2] {'groups','ctx','head'}, dimensions={0} | all-to-all | bytes 524288 | tf_op jit(solution)/shard_map/all_to_all | solution.py:195
  61.5 0.8 %shard_map.68 = bf16[32,4096]{1,0:T(8,128)(2,1)} custom-call(bf16[32,32,128]{2,1,0:T(8,128)(2,1)S(1)} %all_to_all.10.back_ref), custom_call_target="tpu_custom_call" | custom-call | tf_op jit(solution)/shard_map/pallas_call | solution.py:196
Async XLA Ops:
  0.0 10.1 %copy-start = (bf16[160,2,2048]{2,1,0:T(2,128)(2,1)S(1)}, bf16[160,2,2048]{2,1,0:T(2,128)(2,1)}, u32[]{:S(2)}) copy-start(bf16[160,2,2048]{2,1,0:T(2,128)(2,1)} %param.10) | copy-start | bytes 3932164
  1.0 11.4 %collective-permute-start.4 = (bf16[64,640]{1,0:T(8,128)(2,1)S(1)}, bf16[64,640]{1,0:T(8,128)(2,1)S(1)}, u32[]{:S(2)}, u32[]{:S(2)}) collective-permute-start(bf16[64,640]{1,0:T(8,128)(2,1)S(1)} %dynamic-slice_bitcast_fusion), channel_id=1, source_target_pairs={{0,12},{2,14},{4,8},{6,10},{8,4},{10,6},{12,0},{14,2},{1,13},{3,15... | collective-permute-start | bytes 245768 | tf_op jit(solution)/shard_map/ppermute | solution.py:144
  6.1 6.9 %collective-permute-start.3 = (bf16[64,640]{1,0:T(8,128)(2,1)S(1)}, bf16[64,640]{1,0:T(8,128)(2,1)S(1)}, u32[]{:S(2)}, u32[]{:S(2)}) collective-permute-start(bf16[64,640]{1,0:T(8,128)(2,1)S(1)} %dynamic-slice_bitcast_fusion), channel_id=1, source_target_pairs={{0,8},{2,10},{4,12},{6,14},{8,0},{10,2},{12,4},{14,6},{1,9},{3,11}... | collective-permute-start | bytes 245768 | tf_op jit(solution)/shard_map/ppermute | solution.py:144
  6.1 6.9 %collective-permute-start.2 = (bf16[64,640]{1,0:T(8,128)(2,1)S(1)}, bf16[64,640]{1,0:T(8,128)(2,1)S(1)}, u32[]{:S(2)}, u32[]{:S(2)}) collective-permute-start(bf16[64,640]{1,0:T(8,128)(2,1)S(1)} %dynamic-slice_bitcast_fusion), channel_id=1, source_target_pairs={{0,4},{2,6},{4,0},{6,2},{8,12},{10,14},{12,8},{14,10},{1,5},{3,7},... | collective-permute-start | bytes 245768 | tf_op jit(solution)/shard_map/ppermute | solution.py:144
  6.7 0.9 %copy-start.3 = (bf16[32,4096]{1,0:T(8,128)(2,1)S(1)}, bf16[32,4096]{1,0:T(8,128)(2,1)}, u32[]{:S(2)}) copy-start(bf16[32,4096]{1,0:T(8,128)(2,1)} %query_ref.1) | copy-start | bytes 786436
  8.4 4.0 %collective-permute-start.1 = (s32[3,5]{1,0:T(4,128)S(1)}, s32[3,5]{1,0:T(4,128)S(1)}, u32[]{:S(2)}, u32[]{:S(2)}) collective-permute-start(s32[3,5]{1,0:T(4,128)S(1)} %pad_add_fusion.meta_ref), channel_id=1, source_target_pairs={{0,16},{16,0},{1,17},{17,1},{2,18},{18,2},{3,19},{19,3},{4,20},{20... | collective-permute-start | bytes 188 | tf_op jit(solution)/shard_map/ppermute | solution.py:159
  10.1 1.3 %collective-permute-start = (bf16[16,32,128]{2,1,0:T(8,128)(2,1)S(1)}, bf16[16,32,128]{2,1,0:T(8,128)(2,1)S(1)}, u32[]{:S(2)}, u32[]{:S(2)}) collective-permute-start(bf16[16,32,128]{2,1,0:T(8,128)(2,1)S(1)} %get-tuple-element.22), channel_id=1, source_target_pairs={{0,1},{1,0},{2,3},{3,2},{4,5},{5,4},{6,7},{7,6},{8,9},{9,8},{10,11... | collective-permute-start | bytes 393224 | tf_op jit(solution)/shard_map/ppermute | solution.py:156
  13.0 9.5 %collective-permute-start.6 = (bf16[4,64,640]{2,1,0:T(8,128)(2,1)S(1)}, bf16[4,64,640]{2,1,0:T(8,128)(2,1)S(1)}, u32[]{:S(2)}, u32[]{:S(2)}) collective-permute-start(bf16[4,64,640]{2,1,0:T(8,128)(2,1)S(1)} %pad_maximum_fusion.rest_0_), channel_id=1, source_target_pairs={{0,2},{2,0},{4,6},{6,4},{8,10},{10,8},{12,14},{14,12},{1,3},{3,1},... | collective-permute-start | bytes 983048 | tf_op jit(solution)/shard_map/ppermute | solution.py:144
  14.5 13.3 %collective-permute-start.5 = (bf16[4,64,640]{2,1,0:T(8,128)(2,1)S(1)}, bf16[4,64,640]{2,1,0:T(8,128)(2,1)S(1)}, u32[]{:S(2)}, u32[]{:S(2)}) collective-permute-start(bf16[4,64,640]{2,1,0:T(8,128)(2,1)S(1)} %pad_maximum_fusion.rest_0_), channel_id=1, source_target_pairs={{0,16},{16,0},{1,17},{17,1},{2,18},{18,2},{3,19},{19,3},{4,20},{20... | collective-permute-start | bytes 983048 | tf_op jit(solution)/shard_map/ppermute | solution.py:174
  16.1 28.0 %all-to-all-start = ((bf16[16,224,128]{2,1,0:T(8,128)(2,1)}), bf16[16,224,128]{2,1,0:T(8,128)(2,1)S(1)}, u32[]{:S(2)}, u32[]{:S(2)}) async-start(bf16[16,224,128]{2,1,0:T(8,128)(2,1)} %shard_map.65), calls=%async_computation | async-start | bytes 1835008 | tf_op jit(solution)/shard_map/all_to_all | solution.py:172
  27.9 9.7 %collective-permute-start.7 = (bf16[4,64,640]{2,1,0:T(8,128)(2,1)S(1)}, bf16[4,64,640]{2,1,0:T(8,128)(2,1)S(1)}, u32[]{:S(2)}, u32[]{:S(2)}) collective-permute-start(bf16[4,64,640]{2,1,0:T(8,128)(2,1)S(1)} %collective-permute-done.5.rest_2_), channel_id=1, source_target_pairs={{0,2},{2,0},{4,6},{6,4},{8,10},{10,8},{12,14},{14,12},{1,3},{3,1},... | collective-permute-start | bytes 983048 | tf_op jit(solution)/shard_map/ppermute | solution.py:144
  27.9 10.4 %collective-permute-start.8 = (bf16[4,64,640]{2,1,0:T(8,128)(2,1)S(1)}, bf16[4,64,640]{2,1,0:T(8,128)(2,1)}, u32[]{:S(2)}, u32[]{:S(2)}) collective-permute-start(bf16[4,64,640]{2,1,0:T(8,128)(2,1)S(1)} %pad_maximum_fusion.rest_0_), channel_id=1, source_target_pairs={{0,1},{1,0},{2,3},{3,2},{4,5},{5,4},{6,7},{7,6},{8,9},{9,8},{10,11... | collective-permute-start | bytes 983048 | tf_op jit(solution)/shard_map/ppermute | solution.py:176
  27.9 10.4 %collective-permute-start.10 = (bf16[4,64,640]{2,1,0:T(8,128)(2,1)S(1)}, bf16[4,64,640]{2,1,0:T(8,128)(2,1)}, u32[]{:S(2)}, u32[]{:S(2)}) collective-permute-start(bf16[4,64,640]{2,1,0:T(8,128)(2,1)S(1)} %collective-permute-done.5.rest_2_), channel_id=1, source_target_pairs={{0,1},{1,0},{2,3},{3,2},{4,5},{5,4},{6,7},{7,6},{8,9},{9,8},{10,11... | collective-permute-start | bytes 983048 | tf_op jit(solution)/shard_map/ppermute | solution.py:176
  28.4 9.9 %collective-permute-start.9 = (bf16[4,64,640]{2,1,0:T(8,128)(2,1)S(1)}, bf16[4,64,640]{2,1,0:T(8,128)(2,1)}, u32[]{:S(2)}, u32[]{:S(2)}) collective-permute-start(bf16[4,64,640]{2,1,0:T(8,128)(2,1)S(1)} %collective-permute-done.6.rest_1_), channel_id=1, source_target_pairs={{0,1},{1,0},{2,3},{3,2},{4,5},{5,4},{6,7},{7,6},{8,9},{9,8},{10,11... | collective-permute-start | bytes 983048 | tf_op jit(solution)/shard_map/ppermute | solution.py:176
  37.6 1.8 %collective-permute-start.11 = (bf16[4,64,640]{2,1,0:T(8,128)(2,1)S(1)}, bf16[4,64,640]{2,1,0:T(8,128)(2,1)}, u32[]{:S(2)}, u32[]{:S(2)}) collective-permute-start(bf16[4,64,640]{2,1,0:T(8,128)(2,1)S(1)} %collective-permute-done.7.rest_3_), channel_id=1, source_target_pairs={{0,1},{1,0},{2,3},{3,2},{4,5},{5,4},{6,7},{7,6},{8,9},{9,8},{10,11... | collective-permute-start | bytes 983048 | tf_op jit(solution)/shard_map/ppermute | solution.py:176
  40.9 1.2 %copy-start.1 = (bf16[640,1280]{1,0:T(8,128)(2,1)}, bf16[640,1280]{1,0:T(8,128)(2,1)S(1)}, u32[]{:S(2)}) copy-start(bf16[640,1280]{1,0:T(8,128)(2,1)S(1)} %shard_map.66.panel) | copy-start | bytes 4915204
  44.0 1.4 %copy-start.2 = (bf16[640,1280]{1,0:T(8,128)(2,1)S(1)}, bf16[640,1280]{1,0:T(8,128)(2,1)}, u32[]{:S(2)}) copy-start(bf16[640,1280]{1,0:T(8,128)(2,1)} %copy-done.1) | copy-start | bytes 4915204

commit v5 on v4

--- a/solution.py
+++ b/solution.py
@@ -36,8 +36,13 @@
             slot = turn // 2
             to = slice((r * images + i) * lat, (r * images + i + 1) * lat)
             for k in range(2):
-                near, far = stores[4 * k + 2 * r : 4 * k + 2 * r + 2]
-                panel_ref[to, k * half : (k + 1) * half] = jnp.where(turn % 2 == 0, near[slot], far[slot])
+                near, far, near_y, far_y, last_y = stores[5 * k : 5 * k + 5]
+                cut = far_y.shape[0]
+                if r == 0:
+                    one, other = near[slot], far[slot]
+                else:
+                    one, other = near_y[slot], jnp.where(slot < cut, far_y[slot % cut], last_y[slot % cut])
+                panel_ref[to, k * half : (k + 1) * half] = jnp.where(turn % 2 == 0, one, other)
 
 
 def attend_kernel(sizes, meta_ref, meta_y_ref, gate_ref, got_ref, panel, out_ref, weight):
@@ -172,15 +177,16 @@
     got = lax.all_to_all(outgoing, ("groups", "ctx"), split_axis=0, concat_axis=0, tiled=True)
     near = jnp.stack(held)
     near_y, far = lax.optimization_barrier((lax.ppermute(near, "groups", swap), across(near, 1)))
-    stores = [near, far, near_y, across(near_y, 1)]
+    cut = ctx_count // 4
+    stores = [near, far, near_y, lax.ppermute(far[:cut], "groups", swap), across(near_y[cut:], 1)]
     stores += [lax.ppermute(x, "head", swap) for x in stores]
     gate = lax.dynamic_slice_in_dim(attn_gate.reshape(-1, DH), group * ctx_count + place, 1, 0)
     panel = pl.pallas_call(
         panel_kernel,
         out_shape=jax.ShapeDtypeStruct((2 * images * lat, depth), jnp.bfloat16),
-        in_specs=[smem] * 2 + [vmem] * 8,
-        out_specs=vmem,
-        cost_estimate=pl.CostEstimate(flops=9_200_000_000, bytes_accessed=4 * 1024 * 1024, transcendentals=0),
+        in_specs=[smem] * 2 + [vmem] * 10,
+        out_specs=vmem,
+        cost_estimate=pl.CostEstimate(flops=12_650_000_000, bytes_accessed=4 * 1024 * 1024, transcendentals=0),
         compiler_params=pltpu.CompilerParams(vmem_limit_bytes=8 * 1024 * 1024),
     )(meta, meta_y, *stores)
     gated = pl.pallas_call(
@@ -264,7 +270,7 @@
     weight = args[4]
     pairs = lax.axis_size("groups") == 2 and lax.axis_size("head") == 2
     whole_heads = weight.shape[2] == 2 * ctx_count * DH
-    whole_blocks = args[1].shape[2] % (2 * DH) == 0 and weight.shape[0] % 32 == 0
+    whole_blocks = ctx_count % 4 == 0 and args[1].shape[2] % (2 * DH) == 0 and weight.shape[0] % 32 == 0
     if pairs and whole_heads and whole_blocks and ctx_count & (ctx_count - 1) == 0:
         return by_heads(*args)
     return by_tokens(*args)

time: 62.7 us -> 61.4 us (0.979)
  waiting for transfers between devices: 20.3 us -> 16.8 us
  starting transfers between devices: 15.4 us -> 18.7 us
  blocking collectives: 13.9 us -> 12.5 us
    ppermute x5, waiting for transfers between devices: 11.7 us -> 5.78 us  [across(): return lax.ppermute(x, 'ctx', [(i, i ^ turn) for i in range(ctx_count)])]
    ppermute x0 -> x1, starting transfers between devices: none -> 2.69 us  [by_heads(): lax.ppermute(far[:cut], 'groups', swap)]
    all_to_all x1, waiting for transfers between devices: 1.98 us -> 4 us  [by_heads(): lax.all_to_all(outgoing, ('groups', 'ctx'), split_axis=0, concat_axis=0,...]
    all_to_all x1, blocking collectives: 13.9 us -> 12.5 us  [by_heads(): back = lax.all_to_all(gated, every, split_axis=0, concat_axis=0, tiled=True)]
  transfers between devices with their start and end apart: 13 -> 15, of which waited for: 7 -> 9; matrix products, arithmetic and copies ran while one was open for 4% -> 4% of each run, Pallas kernels for 4% -> 5%
where the time goes in v5:
time: 61.4 us; the launch traced here: 61 us
  starting transfers between devices  18.7 us (30%)
  waiting for transfers between devices  16.8 us (27%)
  blocking collectives  12.5 us (20%)
  local copies, waits for them, and re-layouts  6.4 us (10%)
  Pallas kernels  5.76 us (9%)
  other arithmetic  0.76 us (1%)
    all_to_all x1, blocking collectives, by_heads(): back = lax.all_to_all(gated, every, split_axis=0, concat_axis=0, tiled=True)  12.5 us
    ppermute x5, starting transfers between devices, across(): return lax.ppermute(x, 'ctx', [(i, i ^ turn) for i in range(ctx_count)])  7.31 us
    ppermute x1, waiting for transfers between devices, by_heads(): lax.ppermute(near, 'groups', swap)  5.94 us
    ppermute x5, waiting for transfers between devices, across(): return lax.ppermute(x, 'ctx', [(i, i ^ turn) for i in range(ctx_count)])  5.78 us
    all_to_all x1, starting transfers between devices, by_heads(): lax.all_to_all(outgoing, ('groups', 'ctx'), split_axis=0, concat_axis=0,...  4.5 us
    all_to_all x1, waiting for transfers between devices, by_heads(): lax.all_to_all(outgoing, ('groups', 'ctx'), split_axis=0, concat_axis=0,...  4 us
    unnamed x8, local copies, waits for them, and re-layouts  3.55 us
    ppermute x1, starting transfers between devices, by_heads(): lax.ppermute(far[:cut], 'groups', swap)  2.69 us
  transfers between devices with their start and end apart: 15, of which 9 were waited for; matrix products, arithmetic and copies ran while one was open for 4% of the time, Pallas kernels for 5%

profile of v5, /device:TPU:0, one launch (start us, length us, event | category | flops | bytes accessed | tf_op | source)
XLA Modules:
  0.0 61.0 jit_solution(16806743110403782248)
XLA Ops:
  0.0 0.0 copy-start
  0.0 1.0 %dynamic-slice_bitcast_fusion = bf16[64,640]{1,0:T(8,128)(2,1)S(1)} fusion(bf16[1,64,1280]{2,1,0:T(8,128)(2,1)} %param.7, s32[]{:T(128)S(6)} %select_n.10), kind=kLoop, calls=%fused_computation.1 | loop fusion | bytes 163844 | tf_op jit(solution)/shard_map/dynamic_slice | solution.py:151
  1.0 5.0 %collective-permute-start.4 = (bf16[64,640]{1,0:T(8,128)(2,1)S(1)}, bf16[64,640]{1,0:T(8,128)(2,1)S(1)}, u32[]{:S(2)}, u32[]{:S(2)}) collective-permute-start(bf16[64,640]{1,0:T(8,128)(2,1)S(1)} %dynamic-slice_bitcast_fusion), channel_id=1, source_target_pairs={{0,12},{2,14},{4,8},{6,10},{8,4},{10,6},{12,0},{14,2},{1,13},{3,15... | collective-permute-start | bytes 245768 | tf_op jit(solution)/shard_map/ppermute | solution.py:149
  6.1 0.0 collective-permute-start.3
  6.1 0.6 %collective-permute-start.2 = (bf16[64,640]{1,0:T(8,128)(2,1)S(1)}, bf16[64,640]{1,0:T(8,128)(2,1)S(1)}, u32[]{:S(2)}, u32[]{:S(2)}) collective-permute-start(bf16[64,640]{1,0:T(8,128)(2,1)S(1)} %dynamic-slice_bitcast_fusion), channel_id=1, source_target_pairs={{0,4},{2,6},{4,0},{6,2},{8,12},{10,14},{12,8},{14,10},{1,5},{3,7},... | collective-permute-start | bytes 245768 | tf_op jit(solution)/shard_map/ppermute | solution.py:149
  6.7 0.0 copy-start.3
  6.7 0.9 %copy-done.3 = bf16[32,4096]{1,0:T(8,128)(2,1)S(1)} copy-done((bf16[32,4096]{1,0:T(8,128)(2,1)S(1)}, bf16[32,4096]{1,0:T(8,128)(2,1)}, u32[]{:S(2)}) %copy-start.3) | copy-done | bytes 262168
  7.6 0.1 shard_map.64
  7.7 0.7 %pad_add_fusion.meta_ref = s32[3,5]{1,0:T(4,128)S(1)} fusion(s32[1,5]{1,0:T(1,128)} %bitcast.19, s32[2,5]{1,0:T(2,128)} %bitcast.18), kind=kLoop, calls=%fused_computation.2 | loop fusion | flops 15 | bytes 120 | tf_op jit(solution)/shard_map/concatenate | solution.py:163
  8.4 1.7 %collective-permute-start.1 = (s32[3,5]{1,0:T(4,128)S(1)}, s32[3,5]{1,0:T(4,128)S(1)}, u32[]{:S(2)}, u32[]{:S(2)}) collective-permute-start(s32[3,5]{1,0:T(4,128)S(1)} %pad_add_fusion.meta_ref), channel_id=1, source_target_pairs={{0,16},{16,0},{1,17},{17,1},{2,18},{18,2},{3,19},{19,3},{4,20},{20... | collective-permute-start | bytes 188 | tf_op jit(solution)/shard_map/ppermute | solution.py:164
  10.1 0.0 collective-permute-start
  10.1 0.0 copy-done
  10.1 0.5 constant_dynamic-slice_fusion.1
  10.5 0.4 reshape.13
  11.0 0.3 copy.8
  11.2 0.2 collective-permute-done.rest_1_
  11.4 1.0 %shard_map.65 = bf16[16,224,128]{2,1,0:T(8,128)(2,1)} custom-call(bf16[16,160,128]{2,1,0:T(8,128)(2,1)S(1)} %bitcast.12, bf16[16,32,128]{2,1,0:T(8,128)(2,1)S(1)} %get-tuple-element.21.rest_0_, bf16[16,32,128]{2,1,0:T(8,128)(2,1)S(1)} %collective-permute-done.rest_1_), custom_call_target="tpu_custom_call" | custom-call | tf_op jit(solution)/shard_map/pallas_call | solution.py:169
  12.5 0.0 collective-permute-done.1.meta_y_ref
  12.5 0.0 collective-permute-done.4
  12.5 0.4 collective-permute-done.3
  12.9 0.0 collective-permute-done.2
  12.9 0.1 pad_maximum_fusion.rest_0_
  13.0 1.6 %collective-permute-start.6 = (bf16[4,64,640]{2,1,0:T(8,128)(2,1)S(1)}, bf16[4,64,640]{2,1,0:T(8,128)(2,1)S(1)}, u32[]{:S(2)}, u32[]{:S(2)}) collective-permute-start(bf16[4,64,640]{2,1,0:T(8,128)(2,1)S(1)} %pad_maximum_fusion.rest_0_), channel_id=1, source_target_pairs={{0,2},{2,0},{4,6},{6,4},{8,10},{10,8},{12,14},{14,12},{1,3},{3,1},... | collective-permute-start | bytes 983048 | tf_op jit(solution)/shard_map/ppermute | solution.py:149
  14.5 1.5 %collective-permute-start.5 = (bf16[4,64,640]{2,1,0:T(8,128)(2,1)S(1)}, bf16[4,64,640]{2,1,0:T(8,128)(2,1)S(1)}, u32[]{:S(2)}, u32[]{:S(2)}) collective-permute-start(bf16[4,64,640]{2,1,0:T(8,128)(2,1)S(1)} %pad_maximum_fusion.rest_0_), channel_id=1, source_target_pairs={{0,16},{16,0},{1,17},{17,1},{2,18},{18,2},{3,19},{19,3},{4,20},{20... | collective-permute-start | bytes 983048 | tf_op jit(solution)/shard_map/ppermute | solution.py:179
  16.1 4.5 %all-to-all-start = ((bf16[16,224,128]{2,1,0:T(8,128)(2,1)}), bf16[16,224,128]{2,1,0:T(8,128)(2,1)S(1)}, u32[]{:S(2)}, u32[]{:S(2)}) async-start(bf16[16,224,128]{2,1,0:T(8,128)(2,1)} %shard_map.65), calls=%async_computation | async-start | bytes 1835008 | tf_op jit(solution)/shard_map/all_to_all | solution.py:177
  20.6 0.1 collective-permute-start.9
  20.6 1.9 %collective-permute-done.6.rest_1_ = bf16[4,64,640]{2,1,0:T(8,128)(2,1)S(1)} collective-permute-done((bf16[4,64,640]{2,1,0:T(8,128)(2,1)S(1)}, bf16[4,64,640]{2,1,0:T(8,128)(2,1)S(1)}, u32[]{:S(2)}, u32[]{:S(2)}) %collective-permute-start.6) | collective-permute-done | bytes 327712 | tf_op jit(solution)/shard_map/ppermute | solution.py:149
  22.5 5.9 %collective-permute-done.5.rest_2_ = bf16[4,64,640]{2,1,0:T(8,128)(2,1)S(1)} collective-permute-done((bf16[4,64,640]{2,1,0:T(8,128)(2,1)S(1)}, bf16[4,64,640]{2,1,0:T(8,128)(2,1)S(1)}, u32[]{:S(2)}, u32[]{:S(2)}) %collective-permute-start.5) | collective-permute-done | bytes 327712 | tf_op jit(solution)/shard_map/ppermute | solution.py:179
  28.5 0.1 collective-permute-start.8
  28.6 2.7 %collective-permute-start.7 = (bf16[2,64,640]{2,1,0:T(8,128)(2,1)S(1)}, bf16[2,64,640]{2,1,0:T(8,128)(2,1)}, u32[]{:S(2)}, u32[]{:S(2)}) collective-permute-start(bf16[2,64,640]{2,1,0:T(8,128)(2,1)S(1)} %slice.6), channel_id=1, source_target_pairs={{0,16},{16,0},{1,17},{17,1},{2,18},{18,2},{3,19},{19,3},{4,20},{20... | collective-permute-start | bytes 491528 | tf_op jit(solution)/shard_map/ppermute | solution.py:181
  31.3 0.0 collective-permute-start.10
  31.3 0.5 collective-permute-start.11
  31.8 3.4 %collective-permute-done.8.rest_4_ = bf16[2,64,640]{2,1,0:T(8,128)(2,1)} collective-permute-done((bf16[2,64,640]{2,1,0:T(8,128)(2,1)S(1)}, bf16[2,64,640]{2,1,0:T(8,128)(2,1)}, u32[]{:S(2)}, u32[]{:S(2)}) %collective-permute-start.8) | collective-permute-done | bytes 163872 | tf_op jit(solution)/shard_map/ppermute | solution.py:149
  35.2 0.0 collective-permute-start.13
  35.2 0.1 collective-permute-done.7.rest_3_
  35.3 0.4 collective-permute-start.12
  35.7 0.7 %constant_dynamic-slice_fusion.gate_ref = f32[1,128]{1,0:T(1,128)S(1)} fusion(f32[16,128]{1,0:T(8,128)} %bitcast.20, s32[]{:T(128)S(6)} %select_n.11), kind=kLoop, calls=%fused_computation.3 | loop fusion | bytes 1028 | tf_op jit(solution)/shard_map/dynamic_slice | solution.py:183
  36.4 0.0 collective-permute-done.9.rest_5_
  36.4 0.5 collective-permute-done.13.rest_9_
  37.0 0.2 collective-permute-done.12.rest_8_
  37.2 0.0 collective-permute-done.10.rest_6_
  37.2 0.0 collective-permute-done.11.rest_7_
  37.2 1.7 %shard_map.66.panel = bf16[640,1280]{1,0:T(8,128)(2,1)S(1)} custom-call(s32[3,5]{1,0:T(4,128)S(1)} %pad_add_fusion.meta_ref, s32[3,5]{1,0:T(4,128)S(1)} %collective-permute-done.1.meta_y_ref, bf16[4,64,640]{2,1,0:T(8,128)(2,1)S(1)} %pad_maximum_fusion.rest_0_, bf16[4,64,640]{2,1,0:T(8,128)(2,1)S(1)} %collective-permute-done.6.rest_1_, ...), custom_call_target="tpu_custom_call" | custom-call | flops 12650000384 | bytes 4194304 | tf_op jit(solution)/shard_map/pallas_call | solution.py:184
  38.9 0.0 copy-start.1
  38.9 1.2 %copy-done.1 = bf16[640,1280]{1,0:T(8,128)(2,1)} copy-done((bf16[640,1280]{1,0:T(8,128)(2,1)}, bf16[640,1280]{1,0:T(8,128)(2,1)S(1)}, u32[]{:S(2)}) %copy-start.1) | copy-done | bytes 1638424
  40.1 4.0 %all-to-all-done.got_ref = bf16[16,224,128]{2,1,0:T(8,128)(2,1)S(1)} async-done(((bf16[16,224,128]{2,1,0:T(8,128)(2,1)}), bf16[16,224,128]{2,1,0:T(8,128)(2,1)S(1)}, u32[]{:S(2)}, u32[]{:S(2)}) %all-to-all-start) | async-done | bytes 917536 | tf_op jit(solution)/shard_map/all_to_all | solution.py:177
  44.1 0.0 copy-start.2
  44.1 1.4 %copy-done.2 = bf16[640,1280]{1,0:T(8,128)(2,1)S(1)} copy-done((bf16[640,1280]{1,0:T(8,128)(2,1)S(1)}, bf16[640,1280]{1,0:T(8,128)(2,1)}, u32[]{:S(2)}) %copy-start.2) | copy-done | bytes 1638424
  45.5 2.2 %shard_map.67 = bf16[32,32,128]{2,1,0:T(8,128)(2,1)S(1)} custom-call(s32[3,5]{1,0:T(4,128)S(1)} %pad_add_fusion.meta_ref, s32[3,5]{1,0:T(4,128)S(1)} %collective-permute-done.1.meta_y_ref, f32[1,128]{1,0:T(1,128)S(1)} %constant_dynamic-slice_fusion.gate_ref, bf16[16,224,128]{2,1,0:T(8,128)(2,1)S(1)} %all-to-all-done.got_ref, bf16[640,1280]{1,0:T(8,128)(2,1)S(1)} %copy-done.2), custom_call_target="tpu_custom_call" | custom-call | tf_op jit(solution)/shard_map/pallas_call | solution.py:192
  47.7 12.5 %all_to_all.10.back_ref = bf16[32,32,128]{2,1,0:T(8,128)(2,1)S(1)} all-to-all(bf16[32,32,128]{2,1,0:T(8,128)(2,1)S(1)} %shard_map.67), channel_id=1, replica_groups=mesh['groups'=2,'ctx'=8,'head'=2] {'groups','ctx','head'}, dimensions={0} | all-to-all | bytes 524288 | tf_op jit(solution)/shard_map/all_to_all | solution.py:201
  60.2 0.8 %shard_map.68 = bf16[32,4096]{1,0:T(8,128)(2,1)} custom-call(bf16[32,32,128]{2,1,0:T(8,128)(2,1)S(1)} %all_to_all.10.back_ref), custom_call_target="tpu_custom_call" | custom-call | tf_op jit(solution)/shard_map/pallas_call | solution.py:202
  (2 shorter events, 0.0 us)
Async XLA Ops:
  0.0 10.1 %copy-start = (bf16[160,2,2048]{2,1,0:T(2,128)(2,1)S(1)}, bf16[160,2,2048]{2,1,0:T(2,128)(2,1)}, u32[]{:S(2)}) copy-start(bf16[160,2,2048]{2,1,0:T(2,128)(2,1)} %param.10) | copy-start | bytes 3932164
  1.0 11.5 %collective-permute-start.4 = (bf16[64,640]{1,0:T(8,128)(2,1)S(1)}, bf16[64,640]{1,0:T(8,128)(2,1)S(1)}, u32[]{:S(2)}, u32[]{:S(2)}) collective-permute-start(bf16[64,640]{1,0:T(8,128)(2,1)S(1)} %dynamic-slice_bitcast_fusion), channel_id=1, source_target_pairs={{0,12},{2,14},{4,8},{6,10},{8,4},{10,6},{12,0},{14,2},{1,13},{3,15... | collective-permute-start | bytes 245768 | tf_op jit(solution)/shard_map/ppermute | solution.py:149
  6.1 6.9 %collective-permute-start.3 = (bf16[64,640]{1,0:T(8,128)(2,1)S(1)}, bf16[64,640]{1,0:T(8,128)(2,1)S(1)}, u32[]{:S(2)}, u32[]{:S(2)}) collective-permute-start(bf16[64,640]{1,0:T(8,128)(2,1)S(1)} %dynamic-slice_bitcast_fusion), channel_id=1, source_target_pairs={{0,8},{2,10},{4,12},{6,14},{8,0},{10,2},{12,4},{14,6},{1,9},{3,11}... | collective-permute-start | bytes 245768 | tf_op jit(solution)/shard_map/ppermute | solution.py:149
  6.1 6.9 %collective-permute-start.2 = (bf16[64,640]{1,0:T(8,128)(2,1)S(1)}, bf16[64,640]{1,0:T(8,128)(2,1)S(1)}, u32[]{:S(2)}, u32[]{:S(2)}) collective-permute-start(bf16[64,640]{1,0:T(8,128)(2,1)S(1)} %dynamic-slice_bitcast_fusion), channel_id=1, source_target_pairs={{0,4},{2,6},{4,0},{6,2},{8,12},{10,14},{12,8},{14,10},{1,5},{3,7},... | collective-permute-start | bytes 245768 | tf_op jit(solution)/shard_map/ppermute | solution.py:149
  6.7 0.9 %copy-start.3 = (bf16[32,4096]{1,0:T(8,128)(2,1)S(1)}, bf16[32,4096]{1,0:T(8,128)(2,1)}, u32[]{:S(2)}) copy-start(bf16[32,4096]{1,0:T(8,128)(2,1)} %query_ref.1) | copy-start | bytes 786436
  8.4 4.0 %collective-permute-start.1 = (s32[3,5]{1,0:T(4,128)S(1)}, s32[3,5]{1,0:T(4,128)S(1)}, u32[]{:S(2)}, u32[]{:S(2)}) collective-permute-start(s32[3,5]{1,0:T(4,128)S(1)} %pad_add_fusion.meta_ref), channel_id=1, source_target_pairs={{0,16},{16,0},{1,17},{17,1},{2,18},{18,2},{3,19},{19,3},{4,20},{20... | collective-permute-start | bytes 188 | tf_op jit(solution)/shard_map/ppermute | solution.py:164
  10.1 1.3 %collective-permute-start = (bf16[16,32,128]{2,1,0:T(8,128)(2,1)S(1)}, bf16[16,32,128]{2,1,0:T(8,128)(2,1)S(1)}, u32[]{:S(2)}, u32[]{:S(2)}) collective-permute-start(bf16[16,32,128]{2,1,0:T(8,128)(2,1)S(1)} %get-tuple-element.22), channel_id=1, source_target_pairs={{0,1},{1,0},{2,3},{3,2},{4,5},{5,4},{6,7},{7,6},{8,9},{9,8},{10,11... | collective-permute-start | bytes 393224 | tf_op jit(solution)/shard_map/ppermute | solution.py:161
  13.0 9.6 %collective-permute-start.6 = (bf16[4,64,640]{2,1,0:T(8,128)(2,1)S(1)}, bf16[4,64,640]{2,1,0:T(8,128)(2,1)S(1)}, u32[]{:S(2)}, u32[]{:S(2)}) collective-permute-start(bf16[4,64,640]{2,1,0:T(8,128)(2,1)S(1)} %pad_maximum_fusion.rest_0_), channel_id=1, source_target_pairs={{0,2},{2,0},{4,6},{6,4},{8,10},{10,8},{12,14},{14,12},{1,3},{3,1},... | collective-permute-start | bytes 983048 | tf_op jit(solution)/shard_map/ppermute | solution.py:149
  14.5 14.0 %collective-permute-start.5 = (bf16[4,64,640]{2,1,0:T(8,128)(2,1)S(1)}, bf16[4,64,640]{2,1,0:T(8,128)(2,1)S(1)}, u32[]{:S(2)}, u32[]{:S(2)}) collective-permute-start(bf16[4,64,640]{2,1,0:T(8,128)(2,1)S(1)} %pad_maximum_fusion.rest_0_), channel_id=1, source_target_pairs={{0,16},{16,0},{1,17},{17,1},{2,18},{18,2},{3,19},{19,3},{4,20},{20... | collective-permute-start | bytes 983048 | tf_op jit(solution)/shard_map/ppermute | solution.py:179
  16.1 28.0 %all-to-all-start = ((bf16[16,224,128]{2,1,0:T(8,128)(2,1)}), bf16[16,224,128]{2,1,0:T(8,128)(2,1)S(1)}, u32[]{:S(2)}, u32[]{:S(2)}) async-start(bf16[16,224,128]{2,1,0:T(8,128)(2,1)} %shard_map.65), calls=%async_computation | async-start | bytes 1835008 | tf_op jit(solution)/shard_map/all_to_all | solution.py:177
  20.6 15.9 %collective-permute-start.9 = (bf16[4,64,640]{2,1,0:T(8,128)(2,1)S(1)}, bf16[4,64,640]{2,1,0:T(8,128)(2,1)S(1)}, u32[]{:S(2)}, u32[]{:S(2)}) collective-permute-start(bf16[4,64,640]{2,1,0:T(8,128)(2,1)S(1)} %pad_maximum_fusion.rest_0_), channel_id=1, source_target_pairs={{0,1},{1,0},{2,3},{3,2},{4,5},{5,4},{6,7},{7,6},{8,9},{9,8},{10,11... | collective-permute-start | bytes 983048 | tf_op jit(solution)/shard_map/ppermute | solution.py:182
  28.5 6.7 %collective-permute-start.8 = (bf16[2,64,640]{2,1,0:T(8,128)(2,1)S(1)}, bf16[2,64,640]{2,1,0:T(8,128)(2,1)}, u32[]{:S(2)}, u32[]{:S(2)}) collective-permute-start(bf16[2,64,640]{2,1,0:T(8,128)(2,1)S(1)} %slice.7), channel_id=1, source_target_pairs={{0,2},{2,0},{4,6},{6,4},{8,10},{10,8},{12,14},{14,12},{1,3},{3,1},... | collective-permute-start | bytes 491528 | tf_op jit(solution)/shard_map/ppermute | solution.py:149
  28.6 6.7 %collective-permute-start.7 = (bf16[2,64,640]{2,1,0:T(8,128)(2,1)S(1)}, bf16[2,64,640]{2,1,0:T(8,128)(2,1)}, u32[]{:S(2)}, u32[]{:S(2)}) collective-permute-start(bf16[2,64,640]{2,1,0:T(8,128)(2,1)S(1)} %slice.6), channel_id=1, source_target_pairs={{0,16},{16,0},{1,17},{17,1},{2,18},{18,2},{3,19},{19,3},{4,20},{20... | collective-permute-start | bytes 491528 | tf_op jit(solution)/shard_map/ppermute | solution.py:181
  31.3 5.9 %collective-permute-start.10 = (bf16[4,64,640]{2,1,0:T(8,128)(2,1)S(1)}, bf16[4,64,640]{2,1,0:T(8,128)(2,1)}, u32[]{:S(2)}, u32[]{:S(2)}) collective-permute-start(bf16[4,64,640]{2,1,0:T(8,128)(2,1)S(1)} %collective-permute-done.6.rest_1_), channel_id=1, source_target_pairs={{0,1},{1,0},{2,3},{3,2},{4,5},{5,4},{6,7},{7,6},{8,9},{9,8},{10,11... | collective-permute-start | bytes 983048 | tf_op jit(solution)/shard_map/ppermute | solution.py:182
  31.3 5.9 %collective-permute-start.11 = (bf16[4,64,640]{2,1,0:T(8,128)(2,1)S(1)}, bf16[4,64,640]{2,1,0:T(8,128)(2,1)}, u32[]{:S(2)}, u32[]{:S(2)}) collective-permute-start(bf16[4,64,640]{2,1,0:T(8,128)(2,1)S(1)} %collective-permute-done.5.rest_2_), channel_id=1, source_target_pairs={{0,1},{1,0},{2,3},{3,2},{4,5},{5,4},{6,7},{7,6},{8,9},{9,8},{10,11... | collective-permute-start | bytes 983048 | tf_op jit(solution)/shard_map/ppermute | solution.py:182
  35.2 1.7 %collective-permute-start.13 = (bf16[2,64,640]{2,1,0:T(8,128)(2,1)}, bf16[2,64,640]{2,1,0:T(8,128)(2,1)}, u32[]{:S(2)}, u32[]{:S(2)}) collective-permute-start(bf16[2,64,640]{2,1,0:T(8,128)(2,1)} %collective-permute-done.8.rest_4_), channel_id=1, source_target_pairs={{0,1},{1,0},{2,3},{3,2},{4,5},{5,4},{6,7},{7,6},{8,9},{9,8},{10,11... | collective-permute-start | bytes 491528 | tf_op jit(solution)/shard_map/ppermute | solution.py:182
  35.3 1.9 %collective-permute-start.12 = (bf16[2,64,640]{2,1,0:T(8,128)(2,1)}, bf16[2,64,640]{2,1,0:T(8,128)(2,1)}, u32[]{:S(2)}, u32[]{:S(2)}) collective-permute-start(bf16[2,64,640]{2,1,0:T(8,128)(2,1)} %collective-permute-done.7.rest_3_), channel_id=1, source_target_pairs={{0,1},{1,0},{2,3},{3,2},{4,5},{5,4},{6,7},{7,6},{8,9},{9,8},{10,11... | collective-permute-start | bytes 491528 | tf_op jit(solution)/shard_map/ppermute | solution.py:182
  38.9 1.2 %copy-start.1 = (bf16[640,1280]{1,0:T(8,128)(2,1)}, bf16[640,1280]{1,0:T(8,128)(2,1)S(1)}, u32[]{:S(2)}) copy-start(bf16[640,1280]{1,0:T(8,128)(2,1)S(1)} %shard_map.66.panel) | copy-start | bytes 4915204
  44.1 1.4 %copy-start.2 = (bf16[640,1280]{1,0:T(8,128)(2,1)S(1)}, bf16[640,1280]{1,0:T(8,128)(2,1)}, u32[]{:S(2)}) copy-start(bf16[640,1280]{1,0:T(8,128)(2,1)} %copy-done.1) | copy-start | bytes 4915204

commit v6 on v4

--- a/solution.py
+++ b/solution.py
@@ -1,5 +1,3 @@
-import functools
-
 import jax
 import jax.numpy as jnp
 from jax import lax
@@ -25,52 +23,70 @@
     return centered * lax.rsqrt(spread + 1e-05)
 
 
-def panel_kernel(meta_ref, meta_y_ref, *rest):
-    *stores, panel_ref = rest
+def panel_kernel(meta_ref, meta_y_ref, near, last, far, last_x, near_y, last_y, far_y, third, fourth, panel_ref):
     images = meta_ref.shape[1]
-    lat, half = stores[0].shape[1:]
+    lat = near.shape[1]
     place = lax.axis_index("ctx")
+
+    def pick(few, one, slot):
+        return jnp.where(slot < 3, few[jnp.minimum(slot, 2)], one[0])
+
     for r, meta in enumerate((meta_ref, meta_y_ref)):
         for i in range(images):
             turn = meta[2, i] ^ place
             slot = turn // 2
+            if r == 0:
+                one, other = pick(near, last, slot), pick(far, last_x, slot)
+            else:
+                one = pick(near_y, last_y, slot)
+                other = jnp.where(slot == 2, third[0], fourth[0])
+                other = jnp.where(slot < 2, far_y[jnp.minimum(slot, 1)], other)
             to = slice((r * images + i) * lat, (r * images + i + 1) * lat)
-            for k in range(2):
-                near, far = stores[4 * k + 2 * r : 4 * k + 2 * r + 2]
-                panel_ref[to, k * half : (k + 1) * half] = jnp.where(turn % 2 == 0, near[slot], far[slot])
-
-
-def attend_kernel(sizes, meta_ref, meta_y_ref, gate_ref, got_ref, panel, out_ref, weight):
-    ctx_count, rows, lat, part, images = sizes
-    half = ctx_count // 2 * rows
+            panel_ref[to, :] = jnp.where(turn % 2 == 0, one, other)
+
+
+def project_kernel(got_ref, other_ref, query_ref, weight_ref, partial_ref, weight):
+    ctx_count, _, part, _ = query_ref.shape[1:]
+    half = weight_ref.shape[0]
+    rows = half // (ctx_count // 2)
     piece = rows // 2
-    size = images * lat
+    group = lax.axis_index("groups")
+    core = lax.axis_index("head")
+    for k, to_ref in enumerate((weight_ref, weight)):
+        first = (core ^ k) * (ctx_count // 2)
+        for s in range(ctx_count // 2):
+            for g in range(2):
+                at = s * rows + g * piece
+                for n in range(2):
+                    to_ref[at : at + piece, n * DH : (n + 1) * DH] = got_ref[
+                        g * ctx_count + first + s, n * piece : (n + 1) * piece, :
+                    ]
+    partial_ref[...] = jnp.dot(other_ref[...], weight[...], preferred_element_type=jnp.float32)
+    for r in range(2):
+        query = got_ref[pl.ds((group ^ r) * ctx_count, ctx_count), rows : rows + 2 * part, :]
+        query = query.reshape(ctx_count * 2 * part, DH).astype(jnp.float32)
+        query_ref[r] = row_norm(query).astype(jnp.bfloat16).reshape(query_ref.shape[1:])
+
+
+def attend_kernel(meta_ref, meta_y_ref, gate_ref, query_ref, weight_ref, partial_ref, own_ref, out_ref):
+    ctx_count, _, part, _ = query_ref.shape[1:]
+    images = meta_ref.shape[1]
+    size = own_ref.shape[0] // 2
+    lat = size // images
     count = ctx_count * 2 * part
     group = lax.axis_index("groups")
     core = lax.axis_index("head")
     metas = (meta_ref, meta_y_ref)
-    for k in range(2):
-        first = (core ^ k) * (ctx_count // 2)
-        for s in range(ctx_count // 2):
-            for g in range(2):
-                at = k * half + s * rows + g * piece
-                for n in range(2):
-                    weight[at : at + piece, n * DH : (n + 1) * DH] = got_ref[
-                        g * ctx_count + first + s, n * piece : (n + 1) * piece, :
-                    ]
-    queries = []
-    for r in range(2):
-        query = got_ref[pl.ds((group ^ r) * ctx_count, ctx_count), rows : rows + 2 * part, :]
-        queries.append(row_norm(query.reshape(count, DH).astype(jnp.float32)).astype(jnp.bfloat16))
+    queries = [query_ref[r].reshape(count, DH) for r in range(2)]
     gate = jnp.tanh(gate_ref[...])
     row = lax.broadcasted_iota(jnp.int32, (1, count), 1)
     block = row // part
     position = (block // 2 * 2 + (block % 2 ^ core)) * part + row % part
 
     def project(r):
-        both = jnp.dot(
-            panel[r * size : (r + 1) * size, :], weight[...], preferred_element_type=jnp.float32
-        )
+        at = slice(r * size, (r + 1) * size)
+        both = jnp.dot(own_ref[at, :], weight_ref[...], preferred_element_type=jnp.float32)
+        both += partial_ref[at, :]
         return row_norm(both[:, :DH]).astype(jnp.bfloat16), both[:, DH:].astype(jnp.bfloat16)
 
     def score(r, keys):
@@ -144,7 +160,9 @@
         return lax.ppermute(x, "ctx", [(i, i ^ turn) for i in range(ctx_count)])
 
     share = lax.dynamic_slice_in_dim(latents[0], core * (depth // 2), depth // 2, 1)
-    held = [share] + [across(share, 2 * k) for k in range(1, ctx_count // 2)]
+    share, meta = lax.optimization_barrier((share, (image_span.T, image_owner[None, :])))
+    meta = jnp.concatenate(meta, 0)
+    held = [share, across(share, 2), across(share, 4)]
     piece = jax.ShapeDtypeStruct((2 * ctx_count, part, DH), jnp.bfloat16)
     own, sent = pl.pallas_call(
         split_kernel,
@@ -154,8 +172,6 @@
         compiler_params=pltpu.CompilerParams(vmem_limit_bytes=4 * 1024 * 1024),
     )(queries)
     came = lax.ppermute(sent, "head", swap)
-    own, meta = lax.optimization_barrier((own, (image_span.T, image_owner[None, :])))
-    meta = jnp.concatenate(meta, 0)
     meta_y = lax.ppermute(meta, "groups", swap)
     half = rows // 2
     weight = lax.dynamic_slice_in_dim(kv_weight, group * half, half, 0)
@@ -171,26 +187,48 @@
     outgoing, meta_y, *held = lax.optimization_barrier((outgoing, meta_y, *held))
     got = lax.all_to_all(outgoing, ("groups", "ctx"), split_axis=0, concat_axis=0, tiled=True)
     near = jnp.stack(held)
-    near_y, far = lax.optimization_barrier((lax.ppermute(near, "groups", swap), across(near, 1)))
-    stores = [near, far, near_y, across(near_y, 1)]
+    near_y, far, last = lax.optimization_barrier(
+        (lax.ppermute(near, "groups", swap), across(near, 1), across(held[2], 2))
+    )
+    last = last[None]
+    last_y = lax.ppermute(last, "groups", swap)
+    last_x = across(last, 1)
+    far_y = [lax.ppermute(far[:2], "groups", swap), across(near_y[2:], 1), across(last_y, 1)]
+    stores = [near, last, far, last_x, near_y, last_y] + far_y
     stores += [lax.ppermute(x, "head", swap) for x in stores]
     gate = lax.dynamic_slice_in_dim(attn_gate.reshape(-1, DH), group * ctx_count + place, 1, 0)
-    panel = pl.pallas_call(
-        panel_kernel,
-        out_shape=jax.ShapeDtypeStruct((2 * images * lat, depth), jnp.bfloat16),
-        in_specs=[smem] * 2 + [vmem] * 8,
+    panels = [
+        pl.pallas_call(
+            panel_kernel,
+            out_shape=jax.ShapeDtypeStruct((2 * images * lat, depth // 2), jnp.bfloat16),
+            in_specs=[smem] * 2 + [vmem] * 9,
+            out_specs=vmem,
+            cost_estimate=pl.CostEstimate(flops=8050000000, bytes_accessed=2 * 1024 * 1024, transcendentals=0),
+            compiler_params=pltpu.CompilerParams(vmem_limit_bytes=6 * 1024 * 1024),
+        )(meta, meta_y, *stores[9 * k : 9 * k + 9])
+        for k in range(2)
+    ]
+    query, weight, partial = pl.pallas_call(
+        project_kernel,
+        out_shape=[
+            jax.ShapeDtypeStruct((2, ctx_count, 2, part, DH), jnp.bfloat16),
+            jax.ShapeDtypeStruct((depth // 2, 2 * DH), jnp.bfloat16),
+            jax.ShapeDtypeStruct((2 * images * lat, 2 * DH), jnp.float32),
+        ],
+        in_specs=[vmem] * 2,
+        out_specs=[vmem] * 3,
+        scratch_shapes=[pltpu.VMEM((depth // 2, 2 * DH), jnp.bfloat16)],
+        cost_estimate=pl.CostEstimate(flops=2 * 10**8, bytes_accessed=16000000, transcendentals=0),
+        compiler_params=pltpu.CompilerParams(vmem_limit_bytes=8 * 1024 * 1024),
+    )(got, panels[1])
+    gated = pl.pallas_call(
+        attend_kernel,
+        out_shape=jax.ShapeDtypeStruct((ctx_count * 4, part, DH), jnp.bfloat16),
+        in_specs=[smem] * 2 + [vmem] * 5,
         out_specs=vmem,
-        cost_estimate=pl.CostEstimate(flops=9_200_000_000, bytes_accessed=4 * 1024 * 1024, transcendentals=0),
-        compiler_params=pltpu.CompilerParams(vmem_limit_bytes=8 * 1024 * 1024),
-    )(meta, meta_y, *stores)
-    gated = pl.pallas_call(
-        functools.partial(attend_kernel, (ctx_count, rows, lat, part, images)),
-        out_shape=jax.ShapeDtypeStruct((ctx_count * 4, part, DH), jnp.bfloat16),
-        in_specs=[smem] * 2 + [vmem] * 3,
-        out_specs=vmem,
-        scratch_shapes=[pltpu.VMEM((depth, 2 * DH), jnp.bfloat16)],
+        cost_estimate=pl.CostEstimate(flops=20000000000, bytes_accessed=4 * 1024 * 1024, transcendentals=0),
         compiler_params=pltpu.CompilerParams(vmem_limit_bytes=16 * 1024 * 1024),
-    )(meta, meta_y, gate, got, panel)
+    )(meta, meta_y, gate, query, weight, partial, panels[0])
     every = ("groups", "ctx", "head")
     back = lax.all_to_all(gated, every, split_axis=0, concat_axis=0, tiled=True)
     return pl.pallas_call(
@@ -264,7 +302,7 @@
     weight = args[4]
     pairs = lax.axis_size("groups") == 2 and lax.axis_size("head") == 2
     whole_heads = weight.shape[2] == 2 * ctx_count * DH
-    whole_blocks = args[1].shape[2] % (2 * DH) == 0 and weight.shape[0] % 32 == 0
+    whole_blocks = ctx_count == 8 and args[1].shape[2] % (2 * DH) == 0 and weight.shape[0] % 32 == 0
     if pairs and whole_heads and whole_blocks and ctx_count & (ctx_count - 1) == 0:
         return by_heads(*args)
     return by_tokens(*args)

time: 62.7 us -> 60 us (0.957)
  waiting for transfers between devices: 20.3 us -> 10.7 us
  starting transfers between devices: 15.4 us -> 22 us
  Pallas kernels: 5.53 us -> 6.39 us
  blocking collectives: 13.9 us -> 13.1 us
    ppermute x5 -> x7, waiting for transfers between devices: 11.7 us -> 2.28 us  [across(): return lax.ppermute(x, 'ctx', [(i, i ^ turn) for i in range(ctx_count)])]
    ppermute x5 -> x7, starting transfers between devices: 7.25 us -> 12.3 us  [across(): return lax.ppermute(x, 'ctx', [(i, i ^ turn) for i in range(ctx_count)])]
    ppermute x1, waiting for transfers between devices: 5.35 us -> 1.32 us  [by_heads(): lax.ppermute(near, 'groups', swap)]
    ppermute x0 -> x2, waiting for transfers between devices: none -> 3.41 us  [the longest x1 3.41 us: by_heads(): last_y = lax.ppermute(last, 'groups', swap)]
    ppermute x0 -> x2, starting transfers between devices: none -> 2.03 us  [the longest x1 1.52 us: by_heads(): last_y = lax.ppermute(last, 'groups', swap)]
    all_to_all x1, waiting for transfers between devices: 1.98 us -> 3.45 us  [by_heads(): lax.all_to_all(outgoing, ('groups', 'ctx'), split_axis=0, concat_axis=0,...]
    slice x0 -> x2, local copies, waits for them, and re-layouts: none -> 1.32 us  [the longest x1 0.68 us: by_heads(): far[:2]]
    ppermute x4 -> x9, starting transfers between devices: 0.52 us -> 1.61 us  [by_heads(): stores += [lax.ppermute(x, 'head', swap) for x in stores]]
  transfers between devices with their start and end apart: 13 -> 22, of which waited for: 7 -> 7; matrix products, arithmetic and copies ran while one was open for 4% -> 6% of each run, Pallas kernels for 4% -> 5%
where the time goes in v6:
time: 60 us; the launch traced here: 59.6 us
  starting transfers between devices  22 us (37%)
  blocking collectives  13.1 us (22%)
  waiting for transfers between devices  10.7 us (18%)
  local copies, waits for them, and re-layouts  6.62 us (11%)
  Pallas kernels  6.39 us (11%)
  other arithmetic  0.74 us (1%)
    all_to_all x1, blocking collectives, by_heads(): back = lax.all_to_all(gated, every, split_axis=0, concat_axis=0, tiled=True)  13.1 us
    ppermute x7, starting transfers between devices, across(): return lax.ppermute(x, 'ctx', [(i, i ^ turn) for i in range(ctx_count)])  12.3 us
    all_to_all x1, starting transfers between devices, by_heads(): lax.all_to_all(outgoing, ('groups', 'ctx'), split_axis=0, concat_axis=0,...  3.91 us
    all_to_all x1, waiting for transfers between devices, by_heads(): lax.all_to_all(outgoing, ('groups', 'ctx'), split_axis=0, concat_axis=0,...  3.45 us
    ppermute x1, waiting for transfers between devices, by_heads(): last_y = lax.ppermute(last, 'groups', swap)  3.41 us
    unnamed x8, local copies, waits for them, and re-layouts  2.48 us
    ppermute x7, waiting for transfers between devices, across(): return lax.ppermute(x, 'ctx', [(i, i ^ turn) for i in range(ctx_count)])  2.28 us
    pallas_call x2, Pallas kernels, by_heads(): pl.pallas_call(panel_kernel, out_shape=jax.ShapeDtypeStruct((2 * images *...  2.01 us
  transfers between devices with their start and end apart: 22, of which 7 were waited for; matrix products, arithmetic and copies ran while one was open for 6% of the time, Pallas kernels for 5%

profile of v6, /device:TPU:0, one launch (start us, length us, event | category | flops | bytes accessed | tf_op | source)
XLA Modules:
  0.0 59.6 jit_solution(1089245480892021548)
XLA Ops:
  0.0 1.0 %dynamic-slice_bitcast_fusion = bf16[64,640]{1,0:T(8,128)(2,1)S(1)} fusion(bf16[1,64,1280]{2,1,0:T(8,128)(2,1)} %param.7, s32[]{:T(128)S(6)} %select_n.9), kind=kLoop, calls=%fused_computation.1 | loop fusion | bytes 163844 | tf_op jit(solution)/shard_map/dynamic_slice | solution.py:162
  1.0 3.0 %collective-permute-start.2 = (bf16[64,640]{1,0:T(8,128)(2,1)S(1)}, bf16[64,640]{1,0:T(8,128)(2,1)S(1)}, u32[]{:S(2)}, u32[]{:S(2)}) collective-permute-start(bf16[64,640]{1,0:T(8,128)(2,1)S(1)} %dynamic-slice_bitcast_fusion), channel_id=1, source_target_pairs={{0,4},{2,6},{4,0},{6,2},{8,12},{10,14},{12,8},{14,10},{1,5},{3,7},... | collective-permute-start | bytes 245768 | tf_op jit(solution)/shard_map/ppermute | solution.py:160
  4.0 2.6 %collective-permute-start.3 = (bf16[64,640]{1,0:T(8,128)(2,1)S(1)}, bf16[64,640]{1,0:T(8,128)(2,1)S(1)}, u32[]{:S(2)}, u32[]{:S(2)}) collective-permute-start(bf16[64,640]{1,0:T(8,128)(2,1)S(1)} %dynamic-slice_bitcast_fusion), channel_id=1, source_target_pairs={{0,8},{2,10},{4,12},{6,14},{8,0},{10,2},{12,4},{14,6},{1,9},{3,11}... | collective-permute-start | bytes 245768 | tf_op jit(solution)/shard_map/ppermute | solution.py:160
  6.6 0.7 %pad_add_fusion.meta_ref = s32[3,5]{1,0:T(4,128)S(1)} fusion(s32[1,5]{1,0:T(1,128)} %bitcast.22, s32[2,5]{1,0:T(2,128)} %bitcast.21), kind=kLoop, calls=%fused_computation.2 | loop fusion | flops 15 | bytes 120 | tf_op jit(solution)/shard_map/concatenate | solution.py:164
  7.3 1.5 %collective-permute-start.1 = (s32[3,5]{1,0:T(4,128)S(1)}, s32[3,5]{1,0:T(4,128)S(1)}, u32[]{:S(2)}, u32[]{:S(2)}) collective-permute-start(s32[3,5]{1,0:T(4,128)S(1)} %pad_add_fusion.meta_ref), channel_id=1, source_target_pairs={{0,16},{16,0},{1,17},{17,1},{2,18},{18,2},{3,19},{19,3},{4,20},{20... | collective-permute-start | bytes 188 | tf_op jit(solution)/shard_map/ppermute | solution.py:175
  8.8 0.9 %copy-done.1 = bf16[32,4096]{1,0:T(8,128)(2,1)S(1)} copy-done((bf16[32,4096]{1,0:T(8,128)(2,1)S(1)}, bf16[32,4096]{1,0:T(8,128)(2,1)}, u32[]{:S(2)}) %copy-start.1) | copy-done | bytes 262168
  9.8 0.1 shard_map.64
  9.9 0.1 collective-permute-start
  9.9 0.0 copy-done
  10.0 0.5 constant_dynamic-slice_fusion.1
  10.4 0.4 reshape.13
  10.8 0.3 copy.8
  11.1 0.2 collective-permute-done.rest_1_
  11.3 1.0 %shard_map.65 = bf16[16,224,128]{2,1,0:T(8,128)(2,1)} custom-call(bf16[16,160,128]{2,1,0:T(8,128)(2,1)S(1)} %bitcast.12, bf16[16,32,128]{2,1,0:T(8,128)(2,1)S(1)} %get-tuple-element.23.rest_0_, bf16[16,32,128]{2,1,0:T(8,128)(2,1)S(1)} %collective-permute-done.rest_1_), custom_call_target="tpu_custom_call" | custom-call | tf_op jit(solution)/shard_map/pallas_call | solution.py:180
  12.3 0.0 collective-permute-done.1.meta_y_ref
  12.3 0.0 collective-permute-done.2
  12.3 0.0 collective-permute-done.3
  12.3 0.6 collective-permute-start.5
  12.9 1.5 %collective-permute-start.6 = (bf16[3,64,640]{2,1,0:T(8,128)(2,1)S(1)}, bf16[3,64,640]{2,1,0:T(8,128)(2,1)S(1)}, u32[]{:S(2)}, u32[]{:S(2)}) collective-permute-start(bf16[3,64,640]{2,1,0:T(8,128)(2,1)S(1)} %pad_maximum_fusion.near), channel_id=1, source_target_pairs={{0,2},{2,0},{4,6},{6,4},{8,10},{10,8},{12,14},{14,12},{1,3},{3,1},... | collective-permute-start | bytes 737288 | tf_op jit(solution)/shard_map/ppermute | solution.py:160
  14.4 0.0 collective-permute-start.4
  14.4 0.4 collective-permute-start.7
  14.9 3.9 %all-to-all-start = ((bf16[16,224,128]{2,1,0:T(8,128)(2,1)}), bf16[16,224,128]{2,1,0:T(8,128)(2,1)S(1)}, u32[]{:S(2)}, u32[]{:S(2)}) async-start(bf16[16,224,128]{2,1,0:T(8,128)(2,1)} %shard_map.65), calls=%async_computation | async-start | bytes 1835008 | tf_op jit(solution)/shard_map/all_to_all | solution.py:188
  18.8 0.5 collective-permute-done.7
  19.3 1.3 %collective-permute-done.5.near_y = bf16[3,64,640]{2,1,0:T(8,128)(2,1)S(1)} collective-permute-done((bf16[3,64,640]{2,1,0:T(8,128)(2,1)S(1)}, bf16[3,64,640]{2,1,0:T(8,128)(2,1)S(1)}, u32[]{:S(2)}, u32[]{:S(2)}) %collective-permute-start.5) | collective-permute-done | bytes 245792 | tf_op jit(solution)/shard_map/ppermute | solution.py:191
  20.6 0.2 collective-permute-done.6.far
  20.8 1.5 %collective-permute-start.13 = (bf16[1,64,640]{2,1,0:T(8,128)(2,1)S(1)}, bf16[1,64,640]{2,1,0:T(8,128)(2,1)S(1)}, u32[]{:S(2)}, u32[]{:S(2)}) collective-permute-start(bf16[1,64,640]{2,1,0:T(8,128)(2,1)S(1)} %bitcast.13), channel_id=1, source_target_pairs={{0,16},{16,0},{1,17},{17,1},{2,18},{18,2},{3,19},{19,3},{4,20},{20... | collective-permute-start | bytes 245768 | tf_op jit(solution)/shard_map/ppermute | solution.py:194
  22.3 0.6 %slice.7 = bf16[1,64,640]{2,1,0:T(8,128)(2,1)} slice(bf16[3,64,640]{2,1,0:T(8,128)(2,1)S(1)} %collective-permute-done.5.near_y), slice={[2:3], [0:64], [0:640]} | slice | bytes 163840 | tf_op jit(solution)/shard_map/slice | solution.py:196
  23.0 1.8 %collective-permute-start.17 = (bf16[1,64,640]{2,1,0:T(8,128)(2,1)}, bf16[1,64,640]{2,1,0:T(8,128)(2,1)}, u32[]{:S(2)}, u32[]{:S(2)}) collective-permute-start(bf16[1,64,640]{2,1,0:T(8,128)(2,1)} %slice.7), channel_id=1, source_target_pairs={{0,2},{2,0},{4,6},{6,4},{8,10},{10,8},{12,14},{14,12},{1,3},{3,1},... | collective-permute-start | bytes 245768 | tf_op jit(solution)/shard_map/ppermute | solution.py:160
  24.8 0.2 collective-permute-start.10
  25.0 0.7 %slice.6 = bf16[2,64,640]{2,1,0:T(8,128)(2,1)} slice(bf16[3,64,640]{2,1,0:T(8,128)(2,1)S(1)} %collective-permute-done.6.far), slice={[0:2], [0:64], [0:640]} | slice | bytes 327680 | tf_op jit(solution)/shard_map/slice | solution.py:196
  25.7 0.5 collective-permute-start.15
  26.2 0.0 collective-permute-done.4.near
  26.2 0.0 collective-permute-start.8
  26.2 3.4 %collective-permute-done.13.last_y = bf16[1,64,640]{2,1,0:T(8,128)(2,1)S(1)} collective-permute-done((bf16[1,64,640]{2,1,0:T(8,128)(2,1)S(1)}, bf16[1,64,640]{2,1,0:T(8,128)(2,1)S(1)}, u32[]{:S(2)}, u32[]{:S(2)}) %collective-permute-start.13) | collective-permute-done | bytes 81952 | tf_op jit(solution)/shard_map/ppermute | solution.py:194
  29.6 2.7 %collective-permute-start.19 = (bf16[1,64,640]{2,1,0:T(8,128)(2,1)S(1)}, bf16[1,64,640]{2,1,0:T(8,128)(2,1)S(1)}, u32[]{:S(2)}, u32[]{:S(2)}) collective-permute-start(bf16[1,64,640]{2,1,0:T(8,128)(2,1)S(1)} %collective-permute-done.13.last_y), channel_id=1, source_target_pairs={{0,2},{2,0},{4,6},{6,4},{8,10},{10,8},{12,14},{14,12},{1,3},{3,1},... | collective-permute-start | bytes 245768 | tf_op jit(solution)/shard_map/ppermute | solution.py:160
  32.3 0.0 collective-permute-done.17.third
  32.3 0.0 collective-permute-start.18
  32.3 0.0 collective-permute-done.10.last_x
  32.3 0.5 collective-permute-start.11
  32.8 0.7 %constant_dynamic-slice_fusion.gate_ref = f32[1,128]{1,0:T(1,128)S(1)} fusion(f32[16,128]{1,0:T(8,128)} %bitcast.23, s32[]{:T(128)S(6)} %select_n.11), kind=kLoop, calls=%fused_computation.3 | loop fusion | bytes 1028 | tf_op jit(solution)/shard_map/dynamic_slice | solution.py:199
  33.5 0.0 collective-permute-done.8.last
  33.5 0.1 collective-permute-start.12
  33.6 1.6 %collective-permute-done.19.fourth = bf16[1,64,640]{2,1,0:T(8,128)(2,1)S(1)} collective-permute-done((bf16[1,64,640]{2,1,0:T(8,128)(2,1)S(1)}, bf16[1,64,640]{2,1,0:T(8,128)(2,1)S(1)}, u32[]{:S(2)}, u32[]{:S(2)}) %collective-permute-start.19) | collective-permute-done | bytes 81952 | tf_op jit(solution)/shard_map/ppermute | solution.py:160
  35.1 0.0 collective-permute-start.9
  35.1 0.0 collective-permute-done.18.third
  35.1 0.5 collective-permute-start.14
  35.6 0.0 collective-permute-done.11.last_x
  35.6 0.1 collective-permute-start.20
  35.7 0.0 collective-permute-done.15.far_y
  35.7 0.4 collective-permute-start.16
  36.2 1.2 %shard_map.68.own_ref = bf16[640,640]{1,0:T(8,128)(2,1)S(1)} custom-call(s32[3,5]{1,0:T(4,128)S(1)} %pad_add_fusion.meta_ref, s32[3,5]{1,0:T(4,128)S(1)} %collective-permute-done.1.meta_y_ref, bf16[3,64,640]{2,1,0:T(8,128)(2,1)S(1)} %pad_maximum_fusion.near, bf16[1,64,640]{2,1,0:T(8,128)(2,1)S(1)} %bitcast.16, ...), custom_call_target="tpu_custom_call" | custom-call | flops 8049999872 | bytes 2097152 | tf_op jit(solution)/shard_map/pallas_call | solution.py:201
  37.3 0.9 %copy-done.2 = bf16[640,640]{1,0:T(8,128)(2,1)} copy-done((bf16[640,640]{1,0:T(8,128)(2,1)}, bf16[640,640]{1,0:T(8,128)(2,1)S(1)}, u32[]{:S(2)}) %copy-start.2) | copy-done | bytes 819224
  38.3 0.0 collective-permute-done.14.last_y
  38.3 0.0 collective-permute-done.20.fourth
  38.3 0.0 collective-permute-done.12.near_y
  38.3 0.0 collective-permute-done.9.far
  38.3 0.0 collective-permute-done.16.far_y
  38.3 0.8 %shard_map.66.other_ref = bf16[640,640]{1,0:T(8,128)(2,1)S(1)} custom-call(s32[3,5]{1,0:T(4,128)S(1)} %pad_add_fusion.meta_ref, s32[3,5]{1,0:T(4,128)S(1)} %collective-permute-done.1.meta_y_ref, bf16[3,64,640]{2,1,0:T(8,128)(2,1)S(1)} %collective-permute-done.4.near, bf16[1,64,640]{2,1,0:T(8,128)(2,1)S(1)} %collective-permute-done.8.last, ...), custom_call_target="tpu_custom_call" | custom-call | flops 8049999872 | bytes 2097152 | tf_op jit(solution)/shard_map/pallas_call | solution.py:201
  39.1 3.5 %all-to-all-done.got_ref = bf16[16,224,128]{2,1,0:T(8,128)(2,1)S(1)} async-done(((bf16[16,224,128]{2,1,0:T(8,128)(2,1)}), bf16[16,224,128]{2,1,0:T(8,128)(2,1)S(1)}, u32[]{:S(2)}, u32[]{:S(2)}) %all-to-all-start) | async-done | bytes 917536 | tf_op jit(solution)/shard_map/all_to_all | solution.py:188
  42.6 0.5 shard_map.67
  43.1 0.6 %copy-done.3 = bf16[640,640]{1,0:T(8,128)(2,1)S(1)} copy-done((bf16[640,640]{1,0:T(8,128)(2,1)S(1)}, bf16[640,640]{1,0:T(8,128)(2,1)}, u32[]{:S(2)}) %copy-start.3) | copy-done | bytes 819224
  43.7 2.0 %shard_map.69 = bf16[32,32,128]{2,1,0:T(8,128)(2,1)S(1)} custom-call(s32[3,5]{1,0:T(4,128)S(1)} %pad_add_fusion.meta_ref, s32[3,5]{1,0:T(4,128)S(1)} %collective-permute-done.1.meta_y_ref, f32[1,128]{1,0:T(1,128)S(1)} %constant_dynamic-slice_fusion.gate_ref, bf16[2,8,2,32,128]{4,3,2,1,0:T(8,128)(2,1)S(1)} %get-tuple-element.34.query_ref, ...), custom_call_target="tpu_custom_call" | custom-call | flops 20000000000 | bytes 4194304 | tf_op jit(solution)/shard_map/pallas_call | solution.py:224
  45.8 13.1 %all_to_all.10.back_ref = bf16[32,32,128]{2,1,0:T(8,128)(2,1)S(1)} all-to-all(bf16[32,32,128]{2,1,0:T(8,128)(2,1)S(1)} %shard_map.69), channel_id=1, replica_groups=mesh['groups'=2,'ctx'=8,'head'=2] {'groups','ctx','head'}, dimensions={0} | all-to-all | bytes 524288 | tf_op jit(solution)/shard_map/all_to_all | solution.py:233
  58.9 0.8 %shard_map.70 = bf16[32,4096]{1,0:T(8,128)(2,1)} custom-call(bf16[32,32,128]{2,1,0:T(8,128)(2,1)S(1)} %all_to_all.10.back_ref), custom_call_target="tpu_custom_call" | custom-call | tf_op jit(solution)/shard_map/pallas_call | solution.py:234
  (5 shorter events, 0.0 us)
Async XLA Ops:
  0.0 9.9 %copy-start = (bf16[160,2,2048]{2,1,0:T(2,128)(2,1)S(1)}, bf16[160,2,2048]{2,1,0:T(2,128)(2,1)}, u32[]{:S(2)}) copy-start(bf16[160,2,2048]{2,1,0:T(2,128)(2,1)} %param.10) | copy-start | bytes 3932164
  1.0 11.3 %collective-permute-start.2 = (bf16[64,640]{1,0:T(8,128)(2,1)S(1)}, bf16[64,640]{1,0:T(8,128)(2,1)S(1)}, u32[]{:S(2)}, u32[]{:S(2)}) collective-permute-start(bf16[64,640]{1,0:T(8,128)(2,1)S(1)} %dynamic-slice_bitcast_fusion), channel_id=1, source_target_pairs={{0,4},{2,6},{4,0},{6,2},{8,12},{10,14},{12,8},{14,10},{1,5},{3,7},... | collective-permute-start | bytes 245768 | tf_op jit(solution)/shard_map/ppermute | solution.py:160
  4.0 8.3 %collective-permute-start.3 = (bf16[64,640]{1,0:T(8,128)(2,1)S(1)}, bf16[64,640]{1,0:T(8,128)(2,1)S(1)}, u32[]{:S(2)}, u32[]{:S(2)}) collective-permute-start(bf16[64,640]{1,0:T(8,128)(2,1)S(1)} %dynamic-slice_bitcast_fusion), channel_id=1, source_target_pairs={{0,8},{2,10},{4,12},{6,14},{8,0},{10,2},{12,4},{14,6},{1,9},{3,11}... | collective-permute-start | bytes 245768 | tf_op jit(solution)/shard_map/ppermute | solution.py:160
  7.3 5.0 %collective-permute-start.1 = (s32[3,5]{1,0:T(4,128)S(1)}, s32[3,5]{1,0:T(4,128)S(1)}, u32[]{:S(2)}, u32[]{:S(2)}) collective-permute-start(s32[3,5]{1,0:T(4,128)S(1)} %pad_add_fusion.meta_ref), channel_id=1, source_target_pairs={{0,16},{16,0},{1,17},{17,1},{2,18},{18,2},{3,19},{19,3},{4,20},{20... | collective-permute-start | bytes 188 | tf_op jit(solution)/shard_map/ppermute | solution.py:175
  8.8 0.9 %copy-start.1 = (bf16[32,4096]{1,0:T(8,128)(2,1)S(1)}, bf16[32,4096]{1,0:T(8,128)(2,1)}, u32[]{:S(2)}) copy-start(bf16[32,4096]{1,0:T(8,128)(2,1)} %query_ref.1) | copy-start | bytes 786436
  9.9 1.4 %collective-permute-start = (bf16[16,32,128]{2,1,0:T(8,128)(2,1)S(1)}, bf16[16,32,128]{2,1,0:T(8,128)(2,1)S(1)}, u32[]{:S(2)}, u32[]{:S(2)}) collective-permute-start(bf16[16,32,128]{2,1,0:T(8,128)(2,1)S(1)} %get-tuple-element.24), channel_id=1, source_target_pairs={{0,1},{1,0},{2,3},{3,2},{4,5},{5,4},{6,7},{7,6},{8,9},{9,8},{10,11... | collective-permute-start | bytes 393224 | tf_op jit(solution)/shard_map/ppermute | solution.py:174
  12.3 8.2 %collective-permute-start.5 = (bf16[3,64,640]{2,1,0:T(8,128)(2,1)S(1)}, bf16[3,64,640]{2,1,0:T(8,128)(2,1)S(1)}, u32[]{:S(2)}, u32[]{:S(2)}) collective-permute-start(bf16[3,64,640]{2,1,0:T(8,128)(2,1)S(1)} %pad_maximum_fusion.near), channel_id=1, source_target_pairs={{0,16},{16,0},{1,17},{17,1},{2,18},{18,2},{3,19},{19,3},{4,20},{20... | collective-permute-start | bytes 737288 | tf_op jit(solution)/shard_map/ppermute | solution.py:191
  12.9 7.9 %collective-permute-start.6 = (bf16[3,64,640]{2,1,0:T(8,128)(2,1)S(1)}, bf16[3,64,640]{2,1,0:T(8,128)(2,1)S(1)}, u32[]{:S(2)}, u32[]{:S(2)}) collective-permute-start(bf16[3,64,640]{2,1,0:T(8,128)(2,1)S(1)} %pad_maximum_fusion.near), channel_id=1, source_target_pairs={{0,2},{2,0},{4,6},{6,4},{8,10},{10,8},{12,14},{14,12},{1,3},{3,1},... | collective-permute-start | bytes 737288 | tf_op jit(solution)/shard_map/ppermute | solution.py:160
  14.4 11.8 %collective-permute-start.4 = (bf16[3,64,640]{2,1,0:T(8,128)(2,1)S(1)}, bf16[3,64,640]{2,1,0:T(8,128)(2,1)S(1)}, u32[]{:S(2)}, u32[]{:S(2)}) collective-permute-start(bf16[3,64,640]{2,1,0:T(8,128)(2,1)S(1)} %pad_maximum_fusion.near), channel_id=1, source_target_pairs={{0,1},{1,0},{2,3},{3,2},{4,5},{5,4},{6,7},{7,6},{8,9},{9,8},{10,11... | collective-permute-start | bytes 737288 | tf_op jit(solution)/shard_map/ppermute | solution.py:198
  14.4 4.9 %collective-permute-start.7 = (bf16[64,640]{1,0:T(8,128)(2,1)S(1)}, bf16[64,640]{1,0:T(8,128)(2,1)S(1)}, u32[]{:S(2)}, u32[]{:S(2)}) collective-permute-start(bf16[64,640]{1,0:T(8,128)(2,1)S(1)} %collective-permute-done.3), channel_id=1, source_target_pairs={{0,4},{2,6},{4,0},{6,2},{8,12},{10,14},{12,8},{14,10},{1,5},{3,7},... | collective-permute-start | bytes 245768 | tf_op jit(solution)/shard_map/ppermute | solution.py:160
  14.9 27.7 %all-to-all-start = ((bf16[16,224,128]{2,1,0:T(8,128)(2,1)}), bf16[16,224,128]{2,1,0:T(8,128)(2,1)S(1)}, u32[]{:S(2)}, u32[]{:S(2)}) async-start(bf16[16,224,128]{2,1,0:T(8,128)(2,1)} %shard_map.65), calls=%async_computation | async-start | bytes 1835008 | tf_op jit(solution)/shard_map/all_to_all | solution.py:188
  20.8 8.8 %collective-permute-start.13 = (bf16[1,64,640]{2,1,0:T(8,128)(2,1)S(1)}, bf16[1,64,640]{2,1,0:T(8,128)(2,1)S(1)}, u32[]{:S(2)}, u32[]{:S(2)}) collective-permute-start(bf16[1,64,640]{2,1,0:T(8,128)(2,1)S(1)} %bitcast.13), channel_id=1, source_target_pairs={{0,16},{16,0},{1,17},{17,1},{2,18},{18,2},{3,19},{19,3},{4,20},{20... | collective-permute-start | bytes 245768 | tf_op jit(solution)/shard_map/ppermute | solution.py:194
  23.0 9.3 %collective-permute-start.17 = (bf16[1,64,640]{2,1,0:T(8,128)(2,1)}, bf16[1,64,640]{2,1,0:T(8,128)(2,1)}, u32[]{:S(2)}, u32[]{:S(2)}) collective-permute-start(bf16[1,64,640]{2,1,0:T(8,128)(2,1)} %slice.7), channel_id=1, source_target_pairs={{0,2},{2,0},{4,6},{6,4},{8,10},{10,8},{12,14},{14,12},{1,3},{3,1},... | collective-permute-start | bytes 245768 | tf_op jit(solution)/shard_map/ppermute | solution.py:160
  24.8 7.5 %collective-permute-start.10 = (bf16[1,64,640]{2,1,0:T(8,128)(2,1)S(1)}, bf16[1,64,640]{2,1,0:T(8,128)(2,1)}, u32[]{:S(2)}, u32[]{:S(2)}) collective-permute-start(bf16[1,64,640]{2,1,0:T(8,128)(2,1)S(1)} %bitcast.14), channel_id=1, source_target_pairs={{0,2},{2,0},{4,6},{6,4},{8,10},{10,8},{12,14},{14,12},{1,3},{3,1},... | collective-permute-start | bytes 245768 | tf_op jit(solution)/shard_map/ppermute | solution.py:160
  25.7 10.0 %collective-permute-start.15 = (bf16[2,64,640]{2,1,0:T(8,128)(2,1)}, bf16[2,64,640]{2,1,0:T(8,128)(2,1)S(1)}, u32[]{:S(2)}, u32[]{:S(2)}) collective-permute-start(bf16[2,64,640]{2,1,0:T(8,128)(2,1)} %slice.6), channel_id=1, source_target_pairs={{0,16},{16,0},{1,17},{17,1},{2,18},{18,2},{3,19},{19,3},{4,20},{20... | collective-permute-start | bytes 491528 | tf_op jit(solution)/shard_map/ppermute | solution.py:196
  26.2 7.3 %collective-permute-start.8 = (bf16[1,64,640]{2,1,0:T(8,128)(2,1)S(1)}, bf16[1,64,640]{2,1,0:T(8,128)(2,1)S(1)}, u32[]{:S(2)}, u32[]{:S(2)}) collective-permute-start(bf16[1,64,640]{2,1,0:T(8,128)(2,1)S(1)} %bitcast.15), channel_id=1, source_target_pairs={{0,1},{1,0},{2,3},{3,2},{4,5},{5,4},{6,7},{7,6},{8,9},{9,8},{10,11... | collective-permute-start | bytes 245768 | tf_op jit(solution)/shard_map/ppermute | solution.py:198
  29.6 5.5 %collective-permute-start.19 = (bf16[1,64,640]{2,1,0:T(8,128)(2,1)S(1)}, bf16[1,64,640]{2,1,0:T(8,128)(2,1)S(1)}, u32[]{:S(2)}, u32[]{:S(2)}) collective-permute-start(bf16[1,64,640]{2,1,0:T(8,128)(2,1)S(1)} %collective-permute-done.13.last_y), channel_id=1, source_target_pairs={{0,2},{2,0},{4,6},{6,4},{8,10},{10,8},{12,14},{14,12},{1,3},{3,1},... | collective-permute-start | bytes 245768 | tf_op jit(solution)/shard_map/ppermute | solution.py:160
  32.3 2.8 %collective-permute-start.18 = (bf16[1,64,640]{2,1,0:T(8,128)(2,1)}, bf16[1,64,640]{2,1,0:T(8,128)(2,1)S(1)}, u32[]{:S(2)}, u32[]{:S(2)}) collective-permute-start(bf16[1,64,640]{2,1,0:T(8,128)(2,1)} %collective-permute-done.17.third), channel_id=1, source_target_pairs={{0,1},{1,0},{2,3},{3,2},{4,5},{5,4},{6,7},{7,6},{8,9},{9,8},{10,11... | collective-permute-start | bytes 245768 | tf_op jit(solution)/shard_map/ppermute | solution.py:198
  32.3 3.3 %collective-permute-start.11 = (bf16[1,64,640]{2,1,0:T(8,128)(2,1)}, bf16[1,64,640]{2,1,0:T(8,128)(2,1)S(1)}, u32[]{:S(2)}, u32[]{:S(2)}) collective-permute-start(bf16[1,64,640]{2,1,0:T(8,128)(2,1)} %collective-permute-done.10.last_x), channel_id=1, source_target_pairs={{0,1},{1,0},{2,3},{3,2},{4,5},{5,4},{6,7},{7,6},{8,9},{9,8},{10,11... | collective-permute-start | bytes 245768 | tf_op jit(solution)/shard_map/ppermute | solution.py:198
  33.5 4.8 %collective-permute-start.12 = (bf16[3,64,640]{2,1,0:T(8,128)(2,1)S(1)}, bf16[3,64,640]{2,1,0:T(8,128)(2,1)S(1)}, u32[]{:S(2)}, u32[]{:S(2)}) collective-permute-start(bf16[3,64,640]{2,1,0:T(8,128)(2,1)S(1)} %collective-permute-done.5.near_y), channel_id=1, source_target_pairs={{0,1},{1,0},{2,3},{3,2},{4,5},{5,4},{6,7},{7,6},{8,9},{9,8},{10,11... | collective-permute-start | bytes 737288 | tf_op jit(solution)/shard_map/ppermute | solution.py:198
  35.1 3.1 %collective-permute-start.9 = (bf16[3,64,640]{2,1,0:T(8,128)(2,1)S(1)}, bf16[3,64,640]{2,1,0:T(8,128)(2,1)S(1)}, u32[]{:S(2)}, u32[]{:S(2)}) collective-permute-start(bf16[3,64,640]{2,1,0:T(8,128)(2,1)S(1)} %collective-permute-done.6.far), channel_id=1, source_target_pairs={{0,1},{1,0},{2,3},{3,2},{4,5},{5,4},{6,7},{7,6},{8,9},{9,8},{10,11... | collective-permute-start | bytes 737288 | tf_op jit(solution)/shard_map/ppermute | solution.py:198
  35.1 3.1 %collective-permute-start.14 = (bf16[1,64,640]{2,1,0:T(8,128)(2,1)S(1)}, bf16[1,64,640]{2,1,0:T(8,128)(2,1)S(1)}, u32[]{:S(2)}, u32[]{:S(2)}) collective-permute-start(bf16[1,64,640]{2,1,0:T(8,128)(2,1)S(1)} %collective-permute-done.13.last_y), channel_id=1, source_target_pairs={{0,1},{1,0},{2,3},{3,2},{4,5},{5,4},{6,7},{7,6},{8,9},{9,8},{10,11... | collective-permute-start | bytes 245768 | tf_op jit(solution)/shard_map/ppermute | solution.py:198
  35.6 2.6 %collective-permute-start.20 = (bf16[1,64,640]{2,1,0:T(8,128)(2,1)S(1)}, bf16[1,64,640]{2,1,0:T(8,128)(2,1)S(1)}, u32[]{:S(2)}, u32[]{:S(2)}) collective-permute-start(bf16[1,64,640]{2,1,0:T(8,128)(2,1)S(1)} %collective-permute-done.19.fourth), channel_id=1, source_target_pairs={{0,1},{1,0},{2,3},{3,2},{4,5},{5,4},{6,7},{7,6},{8,9},{9,8},{10,11... | collective-permute-start | bytes 245768 | tf_op jit(solution)/shard_map/ppermute | solution.py:198
  35.7 2.6 %collective-permute-start.16 = (bf16[2,64,640]{2,1,0:T(8,128)(2,1)S(1)}, bf16[2,64,640]{2,1,0:T(8,128)(2,1)S(1)}, u32[]{:S(2)}, u32[]{:S(2)}) collective-permute-start(bf16[2,64,640]{2,1,0:T(8,128)(2,1)S(1)} %collective-permute-done.15.far_y), channel_id=1, source_target_pairs={{0,1},{1,0},{2,3},{3,2},{4,5},{5,4},{6,7},{7,6},{8,9},{9,8},{10,11... | collective-permute-start | bytes 491528 | tf_op jit(solution)/shard_map/ppermute | solution.py:198
  37.3 0.9 %copy-start.2 = (bf16[640,640]{1,0:T(8,128)(2,1)}, bf16[640,640]{1,0:T(8,128)(2,1)S(1)}, u32[]{:S(2)}) copy-start(bf16[640,640]{1,0:T(8,128)(2,1)S(1)} %shard_map.68.own_ref) | copy-start | bytes 2457604
  42.6 1.1 %copy-start.3 = (bf16[640,640]{1,0:T(8,128)(2,1)S(1)}, bf16[640,640]{1,0:T(8,128)(2,1)}, u32[]{:S(2)}) copy-start(bf16[640,640]{1,0:T(8,128)(2,1)} %copy-done.2) | copy-start | bytes 2457604

commit v7 on v6

--- a/solution.py
+++ b/solution.py
@@ -193,7 +193,7 @@
     last = last[None]
     last_y = lax.ppermute(last, "groups", swap)
     last_x = across(last, 1)
-    far_y = [lax.ppermute(far[:2], "groups", swap), across(near_y[2:], 1), across(last_y, 1)]
+    far_y = [across(near_y[:2], 1), lax.ppermute(far[2:], "groups", swap), lax.ppermute(last_x, "groups", swap)]
     stores = [near, last, far, last_x, near_y, last_y] + far_y
     stores += [lax.ppermute(x, "head", swap) for x in stores]
     gate = lax.dynamic_slice_in_dim(attn_gate.reshape(-1, DH), group * ctx_count + place, 1, 0)
@@ -203,7 +203,7 @@
             out_shape=jax.ShapeDtypeStruct((2 * images * lat, depth // 2), jnp.bfloat16),
             in_specs=[smem] * 2 + [vmem] * 9,
             out_specs=vmem,
-            cost_estimate=pl.CostEstimate(flops=8050000000, bytes_accessed=2 * 1024 * 1024, transcendentals=0),
+            cost_estimate=pl.CostEstimate(flops=8_050_000_000, bytes_accessed=2 * 1024 * 1024, transcendentals=0),
             compiler_params=pltpu.CompilerParams(vmem_limit_bytes=6 * 1024 * 1024),
         )(meta, meta_y, *stores[9 * k : 9 * k + 9])
         for k in range(2)
@@ -218,7 +218,7 @@
         in_specs=[vmem] * 2,
         out_specs=[vmem] * 3,
         scratch_shapes=[pltpu.VMEM((depth // 2, 2 * DH), jnp.bfloat16)],
-        cost_estimate=pl.CostEstimate(flops=2 * 10**8, bytes_accessed=16000000, transcendentals=0),
+        cost_estimate=pl.CostEstimate(flops=2 * 10**8, bytes_accessed=16_000_000, transcendentals=0),
         compiler_params=pltpu.CompilerParams(vmem_limit_bytes=8 * 1024 * 1024),
     )(got, panels[1])
     gated = pl.pallas_call(
@@ -226,7 +226,7 @@
         out_shape=jax.ShapeDtypeStruct((ctx_count * 4, part, DH), jnp.bfloat16),
         in_specs=[smem] * 2 + [vmem] * 5,
         out_specs=vmem,
-        cost_estimate=pl.CostEstimate(flops=20000000000, bytes_accessed=4 * 1024 * 1024, transcendentals=0),
+        cost_estimate=pl.CostEstimate(flops=20_000_000_000, bytes_accessed=4 * 1024 * 1024, transcendentals=0),
         compiler_params=pltpu.CompilerParams(vmem_limit_bytes=16 * 1024 * 1024),
     )(meta, meta_y, gate, query, weight, partial, panels[0])
     every = ("groups", "ctx", "head")

time: 60 us -> 59.2 us (0.987)
  starting transfers between devices: 22 us -> 20.7 us
  waiting for transfers between devices: 10.7 us -> 11.7 us
    ppermute x7 -> x6, starting transfers between devices: 12.3 us -> 9.58 us  [across(): return lax.ppermute(x, 'ctx', [(i, i ^ turn) for i in range(ctx_count)])]
    ppermute x1 -> x2, starting transfers between devices: 0.51 us -> 2.83 us  [the longest x1 1.49 us: by_heads(): lax.ppermute(last_x, 'groups', swap)]
    ppermute x1 -> x2, waiting for transfers between devices: 0.01 us -> 2.1 us  [the longest x1 1.86 us: by_heads(): lax.ppermute(far[2:], 'groups', swap)]
    ppermute x7 -> x6, waiting for transfers between devices: 2.28 us -> 0.82 us  [across(): return lax.ppermute(x, 'ctx', [(i, i ^ turn) for i in range(ctx_count)])]
    ppermute x1, starting transfers between devices: 1.52 us -> 0.69 us  [by_heads(): last_y = lax.ppermute(last, 'groups', swap)]
  transfers between devices with their start and end apart: 22 -> 22, of which waited for: 7 -> 9; matrix products, arithmetic and copies ran while one was open for 6% -> 7% of each run, Pallas kernels for 5% -> 5%
where the time goes in v7:
time: 59.2 us; the launch traced here: 58.8 us
  starting transfers between devices  20.7 us (35%)
  blocking collectives  12.6 us (21%)
  waiting for transfers between devices  11.7 us (20%)
  local copies, waits for them, and re-layouts  6.62 us (11%)
  Pallas kernels  6.4 us (11%)
  other arithmetic  0.74 us (1%)
    all_to_all x1, blocking collectives, by_heads(): back = lax.all_to_all(gated, every, split_axis=0, concat_axis=0, tiled=True)  12.6 us
    ppermute x6, starting transfers between devices, across(): return lax.ppermute(x, 'ctx', [(i, i ^ turn) for i in range(ctx_count)])  9.58 us
    all_to_all x1, waiting for transfers between devices, by_heads(): lax.all_to_all(outgoing, ('groups', 'ctx'), split_axis=0, concat_axis=0,...  3.96 us
    all_to_all x1, starting transfers between devices, by_heads(): lax.all_to_all(outgoing, ('groups', 'ctx'), split_axis=0, concat_axis=0,...  3.91 us
    ppermute x1, waiting for transfers between devices, by_heads(): last_y = lax.ppermute(last, 'groups', swap)  3.25 us
    unnamed x8, local copies, waits for them, and re-layouts  2.48 us
    pallas_call x2, Pallas kernels, by_heads(): pl.pallas_call(panel_kernel, out_shape=jax.ShapeDtypeStruct((2 * images *...  2.03 us
    pallas_call x1, Pallas kernels, by_heads(): pl.pallas_call(attend_kernel, out_shape=jax.ShapeDtypeStruct((ctx_count *...  2 us
  transfers between devices with their start and end apart: 22, of which 9 were waited for; matrix products, arithmetic and copies ran while one was open for 7% of the time, Pallas kernels for 5%

profile of v7, /device:TPU:0, one launch (start us, length us, event | category | flops | bytes accessed | tf_op | source)
XLA Modules:
  0.0 58.8 jit_solution(2423050798161890837)
XLA Ops:
  0.0 1.0 %dynamic-slice_bitcast_fusion = bf16[64,640]{1,0:T(8,128)(2,1)S(1)} fusion(bf16[1,64,1280]{2,1,0:T(8,128)(2,1)} %param.7, s32[]{:T(128)S(6)} %select_n.9), kind=kLoop, calls=%fused_computation.1 | loop fusion | bytes 163844 | tf_op jit(solution)/shard_map/dynamic_slice | solution.py:162
  1.0 3.0 %collective-permute-start.2 = (bf16[64,640]{1,0:T(8,128)(2,1)S(1)}, bf16[64,640]{1,0:T(8,128)(2,1)S(1)}, u32[]{:S(2)}, u32[]{:S(2)}) collective-permute-start(bf16[64,640]{1,0:T(8,128)(2,1)S(1)} %dynamic-slice_bitcast_fusion), channel_id=1, source_target_pairs={{0,4},{2,6},{4,0},{6,2},{8,12},{10,14},{12,8},{14,10},{1,5},{3,7},... | collective-permute-start | bytes 245768 | tf_op jit(solution)/shard_map/ppermute | solution.py:160
  4.0 2.6 %collective-permute-start.3 = (bf16[64,640]{1,0:T(8,128)(2,1)S(1)}, bf16[64,640]{1,0:T(8,128)(2,1)S(1)}, u32[]{:S(2)}, u32[]{:S(2)}) collective-permute-start(bf16[64,640]{1,0:T(8,128)(2,1)S(1)} %dynamic-slice_bitcast_fusion), channel_id=1, source_target_pairs={{0,8},{2,10},{4,12},{6,14},{8,0},{10,2},{12,4},{14,6},{1,9},{3,11}... | collective-permute-start | bytes 245768 | tf_op jit(solution)/shard_map/ppermute | solution.py:160
  6.6 0.7 %pad_add_fusion.meta_ref = s32[3,5]{1,0:T(4,128)S(1)} fusion(s32[1,5]{1,0:T(1,128)} %bitcast.22, s32[2,5]{1,0:T(2,128)} %bitcast.21), kind=kLoop, calls=%fused_computation.2 | loop fusion | flops 15 | bytes 120 | tf_op jit(solution)/shard_map/concatenate | solution.py:164
  7.3 1.5 %collective-permute-start.1 = (s32[3,5]{1,0:T(4,128)S(1)}, s32[3,5]{1,0:T(4,128)S(1)}, u32[]{:S(2)}, u32[]{:S(2)}) collective-permute-start(s32[3,5]{1,0:T(4,128)S(1)} %pad_add_fusion.meta_ref), channel_id=1, source_target_pairs={{0,16},{16,0},{1,17},{17,1},{2,18},{18,2},{3,19},{19,3},{4,20},{20... | collective-permute-start | bytes 188 | tf_op jit(solution)/shard_map/ppermute | solution.py:175
  8.8 0.9 %copy-done.1 = bf16[32,4096]{1,0:T(8,128)(2,1)S(1)} copy-done((bf16[32,4096]{1,0:T(8,128)(2,1)S(1)}, bf16[32,4096]{1,0:T(8,128)(2,1)}, u32[]{:S(2)}) %copy-start.1) | copy-done | bytes 262168
  9.8 0.1 shard_map.64
  9.9 0.1 collective-permute-start
  9.9 0.0 copy-done
  10.0 0.5 constant_dynamic-slice_fusion.1
  10.4 0.4 reshape.13
  10.8 0.3 copy.8
  11.1 0.2 collective-permute-done.rest_1_
  11.3 1.0 %shard_map.65 = bf16[16,224,128]{2,1,0:T(8,128)(2,1)} custom-call(bf16[16,160,128]{2,1,0:T(8,128)(2,1)S(1)} %bitcast.12, bf16[16,32,128]{2,1,0:T(8,128)(2,1)S(1)} %get-tuple-element.23.rest_0_, bf16[16,32,128]{2,1,0:T(8,128)(2,1)S(1)} %collective-permute-done.rest_1_), custom_call_target="tpu_custom_call" | custom-call | tf_op jit(solution)/shard_map/pallas_call | solution.py:180
  12.3 0.0 collective-permute-done.1.meta_y_ref
  12.3 0.0 collective-permute-done.2
  12.3 0.0 collective-permute-done.3
  12.3 0.6 collective-permute-start.5
  12.9 1.5 %collective-permute-start.6 = (bf16[3,64,640]{2,1,0:T(8,128)(2,1)S(1)}, bf16[3,64,640]{2,1,0:T(8,128)(2,1)S(1)}, u32[]{:S(2)}, u32[]{:S(2)}) collective-permute-start(bf16[3,64,640]{2,1,0:T(8,128)(2,1)S(1)} %pad_maximum_fusion.near), channel_id=1, source_target_pairs={{0,2},{2,0},{4,6},{6,4},{8,10},{10,8},{12,14},{14,12},{1,3},{3,1},... | collective-permute-start | bytes 737288 | tf_op jit(solution)/shard_map/ppermute | solution.py:160
  14.4 0.0 collective-permute-start.4
  14.4 0.4 collective-permute-start.7
  14.9 3.9 %all-to-all-start = ((bf16[16,224,128]{2,1,0:T(8,128)(2,1)}), bf16[16,224,128]{2,1,0:T(8,128)(2,1)S(1)}, u32[]{:S(2)}, u32[]{:S(2)}) async-start(bf16[16,224,128]{2,1,0:T(8,128)(2,1)} %shard_map.65), calls=%async_computation | async-start | bytes 1835008 | tf_op jit(solution)/shard_map/all_to_all | solution.py:188
  18.8 0.5 collective-permute-done.7
  19.3 1.3 %collective-permute-done.5.near_y = bf16[3,64,640]{2,1,0:T(8,128)(2,1)S(1)} collective-permute-done((bf16[3,64,640]{2,1,0:T(8,128)(2,1)S(1)}, bf16[3,64,640]{2,1,0:T(8,128)(2,1)S(1)}, u32[]{:S(2)}, u32[]{:S(2)}) %collective-permute-start.5) | collective-permute-done | bytes 245792 | tf_op jit(solution)/shard_map/ppermute | solution.py:191
  20.6 0.2 collective-permute-done.6.far
  20.8 2.0 %collective-permute-start.10 = (bf16[1,64,640]{2,1,0:T(8,128)(2,1)S(1)}, bf16[1,64,640]{2,1,0:T(8,128)(2,1)S(1)}, u32[]{:S(2)}, u32[]{:S(2)}) collective-permute-start(bf16[1,64,640]{2,1,0:T(8,128)(2,1)S(1)} %bitcast.13), channel_id=1, source_target_pairs={{0,2},{2,0},{4,6},{6,4},{8,10},{10,8},{12,14},{14,12},{1,3},{3,1},... | collective-permute-start | bytes 245768 | tf_op jit(solution)/shard_map/ppermute | solution.py:160
  22.8 0.6 %slice.7 = bf16[1,64,640]{2,1,0:T(8,128)(2,1)} slice(bf16[3,64,640]{2,1,0:T(8,128)(2,1)S(1)} %collective-permute-done.6.far), slice={[2:3], [0:64], [0:640]} | slice | bytes 163840 | tf_op jit(solution)/shard_map/slice | solution.py:196
  23.4 1.3 %collective-permute-start.17 = (bf16[1,64,640]{2,1,0:T(8,128)(2,1)}, bf16[1,64,640]{2,1,0:T(8,128)(2,1)}, u32[]{:S(2)}, u32[]{:S(2)}) collective-permute-start(bf16[1,64,640]{2,1,0:T(8,128)(2,1)} %slice.7), channel_id=1, source_target_pairs={{0,16},{16,0},{1,17},{17,1},{2,18},{18,2},{3,19},{19,3},{4,20},{20... | collective-permute-start | bytes 245768 | tf_op jit(solution)/shard_map/ppermute | solution.py:196
  24.8 0.7 %collective-permute-start.13 = (bf16[1,64,640]{2,1,0:T(8,128)(2,1)S(1)}, bf16[1,64,640]{2,1,0:T(8,128)(2,1)}, u32[]{:S(2)}, u32[]{:S(2)}) collective-permute-start(bf16[1,64,640]{2,1,0:T(8,128)(2,1)S(1)} %bitcast.14), channel_id=1, source_target_pairs={{0,16},{16,0},{1,17},{17,1},{2,18},{18,2},{3,19},{19,3},{4,20},{20... | collective-permute-start | bytes 245768 | tf_op jit(solution)/shard_map/ppermute | solution.py:194
  25.5 0.7 %slice.6 = bf16[2,64,640]{2,1,0:T(8,128)(2,1)} slice(bf16[3,64,640]{2,1,0:T(8,128)(2,1)S(1)} %collective-permute-done.5.near_y), slice={[0:2], [0:64], [0:640]} | slice | bytes 327680 | tf_op jit(solution)/shard_map/slice | solution.py:196
  26.1 0.0 collective-permute-start.15
  26.2 0.0 collective-permute-done.4.near
  26.2 0.0 collective-permute-start.8
  26.2 0.1 collective-permute-done.10.last_x
  26.3 1.5 %collective-permute-start.19 = (bf16[1,64,640]{2,1,0:T(8,128)(2,1)S(1)}, bf16[1,64,640]{2,1,0:T(8,128)(2,1)S(1)}, u32[]{:S(2)}, u32[]{:S(2)}) collective-permute-start(bf16[1,64,640]{2,1,0:T(8,128)(2,1)S(1)} %collective-permute-done.10.last_x), channel_id=1, source_target_pairs={{0,16},{16,0},{1,17},{17,1},{2,18},{18,2},{3,19},{19,3},{4,20},{20... | collective-permute-start | bytes 245768 | tf_op jit(solution)/shard_map/ppermute | solution.py:196
  27.8 1.9 %collective-permute-done.17.third = bf16[1,64,640]{2,1,0:T(8,128)(2,1)} collective-permute-done((bf16[1,64,640]{2,1,0:T(8,128)(2,1)}, bf16[1,64,640]{2,1,0:T(8,128)(2,1)}, u32[]{:S(2)}, u32[]{:S(2)}) %collective-permute-start.17) | collective-permute-done | bytes 81952 | tf_op jit(solution)/shard_map/ppermute | solution.py:196
  29.6 0.0 collective-permute-start.11
  29.7 3.3 %collective-permute-done.13.last_y = bf16[1,64,640]{2,1,0:T(8,128)(2,1)} collective-permute-done((bf16[1,64,640]{2,1,0:T(8,128)(2,1)S(1)}, bf16[1,64,640]{2,1,0:T(8,128)(2,1)}, u32[]{:S(2)}, u32[]{:S(2)}) %collective-permute-start.13) | collective-permute-done | bytes 81952 | tf_op jit(solution)/shard_map/ppermute | solution.py:194
  32.9 0.0 collective-permute-start.18
  32.9 0.7 %constant_dynamic-slice_fusion.gate_ref = f32[1,128]{1,0:T(1,128)S(1)} fusion(f32[16,128]{1,0:T(8,128)} %bitcast.23, s32[]{:T(128)S(6)} %select_n.11), kind=kLoop, calls=%fused_computation.3 | loop fusion | bytes 1028 | tf_op jit(solution)/shard_map/dynamic_slice | solution.py:199
  33.6 0.0 collective-permute-done.8.last
  33.6 0.5 collective-permute-start.12
  34.1 0.2 collective-permute-done.19.fourth
  34.4 0.0 collective-permute-start.9
  34.4 0.0 collective-permute-done.18.third
  34.4 0.5 collective-permute-start.14
  34.9 0.0 collective-permute-done.11.last_x
  34.9 0.1 collective-permute-start.20
  34.9 0.0 collective-permute-done.15.far_y
  35.0 0.4 collective-permute-start.16
  35.4 1.2 %shard_map.68.own_ref = bf16[640,640]{1,0:T(8,128)(2,1)S(1)} custom-call(s32[3,5]{1,0:T(4,128)S(1)} %pad_add_fusion.meta_ref, s32[3,5]{1,0:T(4,128)S(1)} %collective-permute-done.1.meta_y_ref, bf16[3,64,640]{2,1,0:T(8,128)(2,1)S(1)} %pad_maximum_fusion.near, bf16[1,64,640]{2,1,0:T(8,128)(2,1)S(1)} %bitcast.16, ...), custom_call_target="tpu_custom_call" | custom-call | flops 8049999872 | bytes 2097152 | tf_op jit(solution)/shard_map/pallas_call | solution.py:201
  36.6 0.9 %copy-done.2 = bf16[640,640]{1,0:T(8,128)(2,1)} copy-done((bf16[640,640]{1,0:T(8,128)(2,1)}, bf16[640,640]{1,0:T(8,128)(2,1)S(1)}, u32[]{:S(2)}) %copy-start.2) | copy-done | bytes 819224
  37.5 0.0 collective-permute-done.14.last_y
  37.5 0.0 collective-permute-done.20.fourth
  37.5 0.0 collective-permute-done.12.near_y
  37.5 0.0 collective-permute-done.9.far
  37.5 0.0 collective-permute-done.16.far_y
  37.5 0.8 %shard_map.66.other_ref = bf16[640,640]{1,0:T(8,128)(2,1)S(1)} custom-call(s32[3,5]{1,0:T(4,128)S(1)} %pad_add_fusion.meta_ref, s32[3,5]{1,0:T(4,128)S(1)} %collective-permute-done.1.meta_y_ref, bf16[3,64,640]{2,1,0:T(8,128)(2,1)S(1)} %collective-permute-done.4.near, bf16[1,64,640]{2,1,0:T(8,128)(2,1)S(1)} %collective-permute-done.8.last, ...), custom_call_target="tpu_custom_call" | custom-call | flops 8049999872 | bytes 2097152 | tf_op jit(solution)/shard_map/pallas_call | solution.py:201
  38.4 4.0 %all-to-all-done.got_ref = bf16[16,224,128]{2,1,0:T(8,128)(2,1)S(1)} async-done(((bf16[16,224,128]{2,1,0:T(8,128)(2,1)}), bf16[16,224,128]{2,1,0:T(8,128)(2,1)S(1)}, u32[]{:S(2)}, u32[]{:S(2)}) %all-to-all-start) | async-done | bytes 917536 | tf_op jit(solution)/shard_map/all_to_all | solution.py:188
  42.3 0.5 shard_map.67
  42.9 0.6 %copy-done.3 = bf16[640,640]{1,0:T(8,128)(2,1)S(1)} copy-done((bf16[640,640]{1,0:T(8,128)(2,1)S(1)}, bf16[640,640]{1,0:T(8,128)(2,1)}, u32[]{:S(2)}) %copy-start.3) | copy-done | bytes 819224
  43.5 2.0 %shard_map.69 = bf16[32,32,128]{2,1,0:T(8,128)(2,1)S(1)} custom-call(s32[3,5]{1,0:T(4,128)S(1)} %pad_add_fusion.meta_ref, s32[3,5]{1,0:T(4,128)S(1)} %collective-permute-done.1.meta_y_ref, f32[1,128]{1,0:T(1,128)S(1)} %constant_dynamic-slice_fusion.gate_ref, bf16[2,8,2,32,128]{4,3,2,1,0:T(8,128)(2,1)S(1)} %get-tuple-element.34.query_ref, ...), custom_call_target="tpu_custom_call" | custom-call | flops 20000000000 | bytes 4194304 | tf_op jit(solution)/shard_map/pallas_call | solution.py:224
  45.5 12.6 %all_to_all.10.back_ref = bf16[32,32,128]{2,1,0:T(8,128)(2,1)S(1)} all-to-all(bf16[32,32,128]{2,1,0:T(8,128)(2,1)S(1)} %shard_map.69), channel_id=1, replica_groups=mesh['groups'=2,'ctx'=8,'head'=2] {'groups','ctx','head'}, dimensions={0} | all-to-all | bytes 524288 | tf_op jit(solution)/shard_map/all_to_all | solution.py:233
  58.1 0.8 %shard_map.70 = bf16[32,4096]{1,0:T(8,128)(2,1)} custom-call(bf16[32,32,128]{2,1,0:T(8,128)(2,1)S(1)} %all_to_all.10.back_ref), custom_call_target="tpu_custom_call" | custom-call | tf_op jit(solution)/shard_map/pallas_call | solution.py:234
  (5 shorter events, 0.0 us)
Async XLA Ops:
  0.0 9.9 %copy-start = (bf16[160,2,2048]{2,1,0:T(2,128)(2,1)S(1)}, bf16[160,2,2048]{2,1,0:T(2,128)(2,1)}, u32[]{:S(2)}) copy-start(bf16[160,2,2048]{2,1,0:T(2,128)(2,1)} %param.10) | copy-start | bytes 3932164
  1.0 11.3 %collective-permute-start.2 = (bf16[64,640]{1,0:T(8,128)(2,1)S(1)}, bf16[64,640]{1,0:T(8,128)(2,1)S(1)}, u32[]{:S(2)}, u32[]{:S(2)}) collective-permute-start(bf16[64,640]{1,0:T(8,128)(2,1)S(1)} %dynamic-slice_bitcast_fusion), channel_id=1, source_target_pairs={{0,4},{2,6},{4,0},{6,2},{8,12},{10,14},{12,8},{14,10},{1,5},{3,7},... | collective-permute-start | bytes 245768 | tf_op jit(solution)/shard_map/ppermute | solution.py:160
  4.0 8.3 %collective-permute-start.3 = (bf16[64,640]{1,0:T(8,128)(2,1)S(1)}, bf16[64,640]{1,0:T(8,128)(2,1)S(1)}, u32[]{:S(2)}, u32[]{:S(2)}) collective-permute-start(bf16[64,640]{1,0:T(8,128)(2,1)S(1)} %dynamic-slice_bitcast_fusion), channel_id=1, source_target_pairs={{0,8},{2,10},{4,12},{6,14},{8,0},{10,2},{12,4},{14,6},{1,9},{3,11}... | collective-permute-start | bytes 245768 | tf_op jit(solution)/shard_map/ppermute | solution.py:160
  7.3 5.0 %collective-permute-start.1 = (s32[3,5]{1,0:T(4,128)S(1)}, s32[3,5]{1,0:T(4,128)S(1)}, u32[]{:S(2)}, u32[]{:S(2)}) collective-permute-start(s32[3,5]{1,0:T(4,128)S(1)} %pad_add_fusion.meta_ref), channel_id=1, source_target_pairs={{0,16},{16,0},{1,17},{17,1},{2,18},{18,2},{3,19},{19,3},{4,20},{20... | collective-permute-start | bytes 188 | tf_op jit(solution)/shard_map/ppermute | solution.py:175
  8.8 0.9 %copy-start.1 = (bf16[32,4096]{1,0:T(8,128)(2,1)S(1)}, bf16[32,4096]{1,0:T(8,128)(2,1)}, u32[]{:S(2)}) copy-start(bf16[32,4096]{1,0:T(8,128)(2,1)} %query_ref.1) | copy-start | bytes 786436
  9.9 1.4 %collective-permute-start = (bf16[16,32,128]{2,1,0:T(8,128)(2,1)S(1)}, bf16[16,32,128]{2,1,0:T(8,128)(2,1)S(1)}, u32[]{:S(2)}, u32[]{:S(2)}) collective-permute-start(bf16[16,32,128]{2,1,0:T(8,128)(2,1)S(1)} %get-tuple-element.24), channel_id=1, source_target_pairs={{0,1},{1,0},{2,3},{3,2},{4,5},{5,4},{6,7},{7,6},{8,9},{9,8},{10,11... | collective-permute-start | bytes 393224 | tf_op jit(solution)/shard_map/ppermute | solution.py:174
  12.3 8.2 %collective-permute-start.5 = (bf16[3,64,640]{2,1,0:T(8,128)(2,1)S(1)}, bf16[3,64,640]{2,1,0:T(8,128)(2,1)S(1)}, u32[]{:S(2)}, u32[]{:S(2)}) collective-permute-start(bf16[3,64,640]{2,1,0:T(8,128)(2,1)S(1)} %pad_maximum_fusion.near), channel_id=1, source_target_pairs={{0,16},{16,0},{1,17},{17,1},{2,18},{18,2},{3,19},{19,3},{4,20},{20... | collective-permute-start | bytes 737288 | tf_op jit(solution)/shard_map/ppermute | solution.py:191
  12.9 7.9 %collective-permute-start.6 = (bf16[3,64,640]{2,1,0:T(8,128)(2,1)S(1)}, bf16[3,64,640]{2,1,0:T(8,128)(2,1)S(1)}, u32[]{:S(2)}, u32[]{:S(2)}) collective-permute-start(bf16[3,64,640]{2,1,0:T(8,128)(2,1)S(1)} %pad_maximum_fusion.near), channel_id=1, source_target_pairs={{0,2},{2,0},{4,6},{6,4},{8,10},{10,8},{12,14},{14,12},{1,3},{3,1},... | collective-permute-start | bytes 737288 | tf_op jit(solution)/shard_map/ppermute | solution.py:160
  14.4 11.8 %collective-permute-start.4 = (bf16[3,64,640]{2,1,0:T(8,128)(2,1)S(1)}, bf16[3,64,640]{2,1,0:T(8,128)(2,1)S(1)}, u32[]{:S(2)}, u32[]{:S(2)}) collective-permute-start(bf16[3,64,640]{2,1,0:T(8,128)(2,1)S(1)} %pad_maximum_fusion.near), channel_id=1, source_target_pairs={{0,1},{1,0},{2,3},{3,2},{4,5},{5,4},{6,7},{7,6},{8,9},{9,8},{10,11... | collective-permute-start | bytes 737288 | tf_op jit(solution)/shard_map/ppermute | solution.py:198
  14.4 4.9 %collective-permute-start.7 = (bf16[64,640]{1,0:T(8,128)(2,1)S(1)}, bf16[64,640]{1,0:T(8,128)(2,1)S(1)}, u32[]{:S(2)}, u32[]{:S(2)}) collective-permute-start(bf16[64,640]{1,0:T(8,128)(2,1)S(1)} %collective-permute-done.3), channel_id=1, source_target_pairs={{0,4},{2,6},{4,0},{6,2},{8,12},{10,14},{12,8},{14,10},{1,5},{3,7},... | collective-permute-start | bytes 245768 | tf_op jit(solution)/shard_map/ppermute | solution.py:160
  14.9 27.5 %all-to-all-start = ((bf16[16,224,128]{2,1,0:T(8,128)(2,1)}), bf16[16,224,128]{2,1,0:T(8,128)(2,1)S(1)}, u32[]{:S(2)}, u32[]{:S(2)}) async-start(bf16[16,224,128]{2,1,0:T(8,128)(2,1)} %shard_map.65), calls=%async_computation | async-start | bytes 1835008 | tf_op jit(solution)/shard_map/all_to_all | solution.py:188
  20.8 5.5 %collective-permute-start.10 = (bf16[1,64,640]{2,1,0:T(8,128)(2,1)S(1)}, bf16[1,64,640]{2,1,0:T(8,128)(2,1)S(1)}, u32[]{:S(2)}, u32[]{:S(2)}) collective-permute-start(bf16[1,64,640]{2,1,0:T(8,128)(2,1)S(1)} %bitcast.13), channel_id=1, source_target_pairs={{0,2},{2,0},{4,6},{6,4},{8,10},{10,8},{12,14},{14,12},{1,3},{3,1},... | collective-permute-start | bytes 245768 | tf_op jit(solution)/shard_map/ppermute | solution.py:160
  23.4 6.2 %collective-permute-start.17 = (bf16[1,64,640]{2,1,0:T(8,128)(2,1)}, bf16[1,64,640]{2,1,0:T(8,128)(2,1)}, u32[]{:S(2)}, u32[]{:S(2)}) collective-permute-start(bf16[1,64,640]{2,1,0:T(8,128)(2,1)} %slice.7), channel_id=1, source_target_pairs={{0,16},{16,0},{1,17},{17,1},{2,18},{18,2},{3,19},{19,3},{4,20},{20... | collective-permute-start | bytes 245768 | tf_op jit(solution)/shard_map/ppermute | solution.py:196
  24.8 8.1 %collective-permute-start.13 = (bf16[1,64,640]{2,1,0:T(8,128)(2,1)S(1)}, bf16[1,64,640]{2,1,0:T(8,128)(2,1)}, u32[]{:S(2)}, u32[]{:S(2)}) collective-permute-start(bf16[1,64,640]{2,1,0:T(8,128)(2,1)S(1)} %bitcast.14), channel_id=1, source_target_pairs={{0,16},{16,0},{1,17},{17,1},{2,18},{18,2},{3,19},{19,3},{4,20},{20... | collective-permute-start | bytes 245768 | tf_op jit(solution)/shard_map/ppermute | solution.py:194
  26.1 8.8 %collective-permute-start.15 = (bf16[2,64,640]{2,1,0:T(8,128)(2,1)}, bf16[2,64,640]{2,1,0:T(8,128)(2,1)S(1)}, u32[]{:S(2)}, u32[]{:S(2)}) collective-permute-start(bf16[2,64,640]{2,1,0:T(8,128)(2,1)} %slice.6), channel_id=1, source_target_pairs={{0,2},{2,0},{4,6},{6,4},{8,10},{10,8},{12,14},{14,12},{1,3},{3,1},... | collective-permute-start | bytes 491528 | tf_op jit(solution)/shard_map/ppermute | solution.py:160
  26.2 7.4 %collective-permute-start.8 = (bf16[1,64,640]{2,1,0:T(8,128)(2,1)S(1)}, bf16[1,64,640]{2,1,0:T(8,128)(2,1)S(1)}, u32[]{:S(2)}, u32[]{:S(2)}) collective-permute-start(bf16[1,64,640]{2,1,0:T(8,128)(2,1)S(1)} %bitcast.15), channel_id=1, source_target_pairs={{0,1},{1,0},{2,3},{3,2},{4,5},{5,4},{6,7},{7,6},{8,9},{9,8},{10,11... | collective-permute-start | bytes 245768 | tf_op jit(solution)/shard_map/ppermute | solution.py:198
  26.3 8.1 %collective-permute-start.19 = (bf16[1,64,640]{2,1,0:T(8,128)(2,1)S(1)}, bf16[1,64,640]{2,1,0:T(8,128)(2,1)S(1)}, u32[]{:S(2)}, u32[]{:S(2)}) collective-permute-start(bf16[1,64,640]{2,1,0:T(8,128)(2,1)S(1)} %collective-permute-done.10.last_x), channel_id=1, source_target_pairs={{0,16},{16,0},{1,17},{17,1},{2,18},{18,2},{3,19},{19,3},{4,20},{20... | collective-permute-start | bytes 245768 | tf_op jit(solution)/shard_map/ppermute | solution.py:196
  29.6 5.2 %collective-permute-start.11 = (bf16[1,64,640]{2,1,0:T(8,128)(2,1)S(1)}, bf16[1,64,640]{2,1,0:T(8,128)(2,1)S(1)}, u32[]{:S(2)}, u32[]{:S(2)}) collective-permute-start(bf16[1,64,640]{2,1,0:T(8,128)(2,1)S(1)} %collective-permute-done.10.last_x), channel_id=1, source_target_pairs={{0,1},{1,0},{2,3},{3,2},{4,5},{5,4},{6,7},{7,6},{8,9},{9,8},{10,11... | collective-permute-start | bytes 245768 | tf_op jit(solution)/shard_map/ppermute | solution.py:198
  32.9 1.5 %collective-permute-start.18 = (bf16[1,64,640]{2,1,0:T(8,128)(2,1)}, bf16[1,64,640]{2,1,0:T(8,128)(2,1)S(1)}, u32[]{:S(2)}, u32[]{:S(2)}) collective-permute-start(bf16[1,64,640]{2,1,0:T(8,128)(2,1)} %collective-permute-done.17.third), channel_id=1, source_target_pairs={{0,1},{1,0},{2,3},{3,2},{4,5},{5,4},{6,7},{7,6},{8,9},{9,8},{10,11... | collective-permute-start | bytes 245768 | tf_op jit(solution)/shard_map/ppermute | solution.py:198
  33.6 3.9 %collective-permute-start.12 = (bf16[3,64,640]{2,1,0:T(8,128)(2,1)S(1)}, bf16[3,64,640]{2,1,0:T(8,128)(2,1)S(1)}, u32[]{:S(2)}, u32[]{:S(2)}) collective-permute-start(bf16[3,64,640]{2,1,0:T(8,128)(2,1)S(1)} %collective-permute-done.5.near_y), channel_id=1, source_target_pairs={{0,1},{1,0},{2,3},{3,2},{4,5},{5,4},{6,7},{7,6},{8,9},{9,8},{10,11... | collective-permute-start | bytes 737288 | tf_op jit(solution)/shard_map/ppermute | solution.py:198
  34.4 3.2 %collective-permute-start.9 = (bf16[3,64,640]{2,1,0:T(8,128)(2,1)S(1)}, bf16[3,64,640]{2,1,0:T(8,128)(2,1)S(1)}, u32[]{:S(2)}, u32[]{:S(2)}) collective-permute-start(bf16[3,64,640]{2,1,0:T(8,128)(2,1)S(1)} %collective-permute-done.6.far), channel_id=1, source_target_pairs={{0,1},{1,0},{2,3},{3,2},{4,5},{5,4},{6,7},{7,6},{8,9},{9,8},{10,11... | collective-permute-start | bytes 737288 | tf_op jit(solution)/shard_map/ppermute | solution.py:198
  34.4 3.1 %collective-permute-start.14 = (bf16[1,64,640]{2,1,0:T(8,128)(2,1)}, bf16[1,64,640]{2,1,0:T(8,128)(2,1)S(1)}, u32[]{:S(2)}, u32[]{:S(2)}) collective-permute-start(bf16[1,64,640]{2,1,0:T(8,128)(2,1)} %collective-permute-done.13.last_y), channel_id=1, source_target_pairs={{0,1},{1,0},{2,3},{3,2},{4,5},{5,4},{6,7},{7,6},{8,9},{9,8},{10,11... | collective-permute-start | bytes 245768 | tf_op jit(solution)/shard_map/ppermute | solution.py:198
  34.9 2.6 %collective-permute-start.20 = (bf16[1,64,640]{2,1,0:T(8,128)(2,1)S(1)}, bf16[1,64,640]{2,1,0:T(8,128)(2,1)S(1)}, u32[]{:S(2)}, u32[]{:S(2)}) collective-permute-start(bf16[1,64,640]{2,1,0:T(8,128)(2,1)S(1)} %collective-permute-done.19.fourth), channel_id=1, source_target_pairs={{0,1},{1,0},{2,3},{3,2},{4,5},{5,4},{6,7},{7,6},{8,9},{9,8},{10,11... | collective-permute-start | bytes 245768 | tf_op jit(solution)/shard_map/ppermute | solution.py:198
  35.0 2.6 %collective-permute-start.16 = (bf16[2,64,640]{2,1,0:T(8,128)(2,1)S(1)}, bf16[2,64,640]{2,1,0:T(8,128)(2,1)S(1)}, u32[]{:S(2)}, u32[]{:S(2)}) collective-permute-start(bf16[2,64,640]{2,1,0:T(8,128)(2,1)S(1)} %collective-permute-done.15.far_y), channel_id=1, source_target_pairs={{0,1},{1,0},{2,3},{3,2},{4,5},{5,4},{6,7},{7,6},{8,9},{9,8},{10,11... | collective-permute-start | bytes 491528 | tf_op jit(solution)/shard_map/ppermute | solution.py:198
  36.6 0.9 %copy-start.2 = (bf16[640,640]{1,0:T(8,128)(2,1)}, bf16[640,640]{1,0:T(8,128)(2,1)S(1)}, u32[]{:S(2)}) copy-start(bf16[640,640]{1,0:T(8,128)(2,1)S(1)} %shard_map.68.own_ref) | copy-start | bytes 2457604
  42.3 1.1 %copy-start.3 = (bf16[640,640]{1,0:T(8,128)(2,1)S(1)}, bf16[640,640]{1,0:T(8,128)(2,1)}, u32[]{:S(2)}) copy-start(bf16[640,640]{1,0:T(8,128)(2,1)} %copy-done.2) | copy-start | bytes 2457604

commit v8 on v7

--- a/solution.py
+++ b/solution.py
@@ -23,7 +23,7 @@
     return centered * lax.rsqrt(spread + 1e-05)
 
 
-def panel_kernel(meta_ref, meta_y_ref, near, last, far, last_x, near_y, last_y, far_y, third, fourth, panel_ref):
+def place_images(meta_ref, meta_y_ref, near, last, far, last_x, near_y, last_y, far_y, third, fourth, put):
     images = meta_ref.shape[1]
     lat = near.shape[1]
     place = lax.axis_index("ctx")
@@ -42,36 +42,60 @@
                 other = jnp.where(slot == 2, third[0], fourth[0])
                 other = jnp.where(slot < 2, far_y[jnp.minimum(slot, 1)], other)
             to = slice((r * images + i) * lat, (r * images + i + 1) * lat)
-            panel_ref[to, :] = jnp.where(turn % 2 == 0, one, other)
-
-
-def project_kernel(got_ref, other_ref, query_ref, weight_ref, partial_ref, weight):
+            put(to, jnp.where(turn % 2 == 0, one, other))
+
+
+def own_kernel(meta_ref, meta_y_ref, *rest):
+    *stores, first_ref, late_ref = rest
+    cut = first_ref.shape[1]
+
+    def put(to, image):
+        first_ref[to, :] = image[:, :cut]
+        late_ref[to, :] = image[:, cut:]
+
+    place_images(meta_ref, meta_y_ref, *stores, put)
+
+
+def kept_kernel(meta_ref, meta_y_ref, *rest):
+    *stores, first_ref, kept_ref = rest
+    half = stores[0].shape[2]
+
+    def put(to, image):
+        kept_ref[to, :half] = image
+
+    place_images(meta_ref, meta_y_ref, *stores, put)
+    kept_ref[:, half:] = first_ref[...]
+
+
+def project_kernel(got_ref, kept_ref, query_ref, weight_ref, partial_ref, weight):
     ctx_count, _, part, _ = query_ref.shape[1:]
-    half = weight_ref.shape[0]
+    half = weight.shape[0] // 2
     rows = half // (ctx_count // 2)
     piece = rows // 2
     group = lax.axis_index("groups")
     core = lax.axis_index("head")
-    for k, to_ref in enumerate((weight_ref, weight)):
-        first = (core ^ k) * (ctx_count // 2)
+    for k in range(2):
+        first = (core ^ 1 ^ k) * (ctx_count // 2)
         for s in range(ctx_count // 2):
             for g in range(2):
-                at = s * rows + g * piece
+                at = k * half + s * rows + g * piece
                 for n in range(2):
-                    to_ref[at : at + piece, n * DH : (n + 1) * DH] = got_ref[
+                    weight[at : at + piece, n * DH : (n + 1) * DH] = got_ref[
                         g * ctx_count + first + s, n * piece : (n + 1) * piece, :
                     ]
-    partial_ref[...] = jnp.dot(other_ref[...], weight[...], preferred_element_type=jnp.float32)
+    cut = kept_ref.shape[1]
+    partial_ref[...] = jnp.dot(kept_ref[...], weight[:cut, :], preferred_element_type=jnp.float32)
+    weight_ref[...] = weight[cut:, :]
     for r in range(2):
         query = got_ref[pl.ds((group ^ r) * ctx_count, ctx_count), rows : rows + 2 * part, :]
         query = query.reshape(ctx_count * 2 * part, DH).astype(jnp.float32)
         query_ref[r] = row_norm(query).astype(jnp.bfloat16).reshape(query_ref.shape[1:])
 
 
-def attend_kernel(meta_ref, meta_y_ref, gate_ref, query_ref, weight_ref, partial_ref, own_ref, out_ref):
+def attend_kernel(meta_ref, meta_y_ref, gate_ref, query_ref, weight_ref, partial_ref, late_ref, out_ref):
     ctx_count, _, part, _ = query_ref.shape[1:]
     images = meta_ref.shape[1]
-    size = own_ref.shape[0] // 2
+    size = late_ref.shape[0] // 2
     lat = size // images
     count = ctx_count * 2 * part
     group = lax.axis_index("groups")
@@ -85,7 +109,7 @@
 
     def project(r):
         at = slice(r * size, (r + 1) * size)
-        both = jnp.dot(own_ref[at, :], weight_ref[...], preferred_element_type=jnp.float32)
+        both = jnp.dot(late_ref[at, :], weight_ref[...], preferred_element_type=jnp.float32)
         both += partial_ref[at, :]
         return row_norm(both[:, :DH]).astype(jnp.bfloat16), both[:, DH:].astype(jnp.bfloat16)
 
@@ -197,30 +221,40 @@
     stores = [near, last, far, last_x, near_y, last_y] + far_y
     stores += [lax.ppermute(x, "head", swap) for x in stores]
     gate = lax.dynamic_slice_in_dim(attn_gate.reshape(-1, DH), group * ctx_count + place, 1, 0)
-    panels = [
-        pl.pallas_call(
-            panel_kernel,
-            out_shape=jax.ShapeDtypeStruct((2 * images * lat, depth // 2), jnp.bfloat16),
-            in_specs=[smem] * 2 + [vmem] * 9,
-            out_specs=vmem,
-            cost_estimate=pl.CostEstimate(flops=8_050_000_000, bytes_accessed=2 * 1024 * 1024, transcendentals=0),
-            compiler_params=pltpu.CompilerParams(vmem_limit_bytes=6 * 1024 * 1024),
-        )(meta, meta_y, *stores[9 * k : 9 * k + 9])
-        for k in range(2)
-    ]
+    late = 3 * DH
+    size = 2 * images * lat
+    first, last_columns = pl.pallas_call(
+        own_kernel,
+        out_shape=[
+            jax.ShapeDtypeStruct((size, depth // 2 - late), jnp.bfloat16),
+            jax.ShapeDtypeStruct((size, late), jnp.bfloat16),
+        ],
+        in_specs=[smem] * 2 + [vmem] * 9,
+        out_specs=[vmem] * 2,
+        cost_estimate=pl.CostEstimate(flops=8_050_000_000, bytes_accessed=2 * 1024 * 1024, transcendentals=0),
+        compiler_params=pltpu.CompilerParams(vmem_limit_bytes=6 * 1024 * 1024),
+    )(meta, meta_y, *stores[:9])
+    kept = pl.pallas_call(
+        kept_kernel,
+        out_shape=jax.ShapeDtypeStruct((size, depth - late), jnp.bfloat16),
+        in_specs=[smem] * 2 + [vmem] * 10,
+        out_specs=vmem,
+        cost_estimate=pl.CostEstimate(flops=8_050_000_000, bytes_accessed=2 * 1024 * 1024, transcendentals=0),
+        compiler_params=pltpu.CompilerParams(vmem_limit_bytes=6 * 1024 * 1024),
+    )(meta, meta_y, *stores[9:], first)
     query, weight, partial = pl.pallas_call(
         project_kernel,
         out_shape=[
             jax.ShapeDtypeStruct((2, ctx_count, 2, part, DH), jnp.bfloat16),
-            jax.ShapeDtypeStruct((depth // 2, 2 * DH), jnp.bfloat16),
+            jax.ShapeDtypeStruct((late, 2 * DH), jnp.bfloat16),
             jax.ShapeDtypeStruct((2 * images * lat, 2 * DH), jnp.float32),
         ],
         in_specs=[vmem] * 2,
         out_specs=[vmem] * 3,
-        scratch_shapes=[pltpu.VMEM((depth // 2, 2 * DH), jnp.bfloat16)],
+        scratch_shapes=[pltpu.VMEM((depth, 2 * DH), jnp.bfloat16)],
         cost_estimate=pl.CostEstimate(flops=2 * 10**8, bytes_accessed=16_000_000, transcendentals=0),
         compiler_params=pltpu.CompilerParams(vmem_limit_bytes=8 * 1024 * 1024),
-    )(got, panels[1])
+    )(got, kept)
     gated = pl.pallas_call(
         attend_kernel,
         out_shape=jax.ShapeDtypeStruct((ctx_count * 4, part, DH), jnp.bfloat16),
@@ -228,7 +262,7 @@
         out_specs=vmem,
         cost_estimate=pl.CostEstimate(flops=20_000_000_000, bytes_accessed=4 * 1024 * 1024, transcendentals=0),
         compiler_params=pltpu.CompilerParams(vmem_limit_bytes=16 * 1024 * 1024),
-    )(meta, meta_y, gate, query, weight, partial, panels[0])
+    )(meta, meta_y, gate, query, weight, partial, last_columns)
     every = ("groups", "ctx", "head")
     back = lax.all_to_all(gated, every, split_axis=0, concat_axis=0, tiled=True)
     return pl.pallas_call(
@@ -302,7 +336,7 @@
     weight = args[4]
     pairs = lax.axis_size("groups") == 2 and lax.axis_size("head") == 2
     whole_heads = weight.shape[2] == 2 * ctx_count * DH
-    whole_blocks = ctx_count == 8 and args[1].shape[2] % (2 * DH) == 0 and weight.shape[0] % 32 == 0
+    whole_blocks = ctx_count == 8 and args[1].shape[2] % (2 * DH) == 0 and args[1].shape[2] > 6 * DH and weight.shape[0] % 32 == 0
     if pairs and whole_heads and whole_blocks and ctx_count & (ctx_count - 1) == 0:
         return by_heads(*args)
     return by_tokens(*args)

time: 59.2 us -> 59 us (level)
  waiting for transfers between devices: 11.7 us -> 10.8 us
  local copies, waits for them, and re-layouts: 6.62 us -> 7.24 us
    all_to_all x1, waiting for transfers between devices: 3.96 us -> 3.16 us  [by_heads(): lax.all_to_all(outgoing, ('groups', 'ctx'), split_axis=0, concat_axis=0,...]
    unnamed x8 -> x12, local copies, waits for them, and re-layouts: 2.48 us -> 3.1 us
where the time goes in v8:
time: 59 us; the launch traced here: 58.6 us
  starting transfers between devices  20.7 us (35%)
  blocking collectives  12.6 us (21%)
  waiting for transfers between devices  10.8 us (18%)
  local copies, waits for them, and re-layouts  7.24 us (12%)
  Pallas kernels  6.34 us (11%)
  other arithmetic  0.74 us (1%)
    all_to_all x1, blocking collectives, by_heads(): back = lax.all_to_all(gated, every, split_axis=0, concat_axis=0, tiled=True)  12.6 us
    ppermute x6, starting transfers between devices, across(): return lax.ppermute(x, 'ctx', [(i, i ^ turn) for i in range(ctx_count)])  9.58 us
    all_to_all x1, starting transfers between devices, by_heads(): lax.all_to_all(outgoing, ('groups', 'ctx'), split_axis=0, concat_axis=0,...  3.91 us
    ppermute x1, waiting for transfers between devices, by_heads(): last_y = lax.ppermute(last, 'groups', swap)  3.25 us
    all_to_all x1, waiting for transfers between devices, by_heads(): lax.all_to_all(outgoing, ('groups', 'ctx'), split_axis=0, concat_axis=0,...  3.16 us
    unnamed x12, local copies, waits for them, and re-layouts  3.1 us
    pallas_call x1, Pallas kernels, by_heads(): pl.pallas_call(attend_kernel, out_shape=jax.ShapeDtypeStruct((ctx_count *...  1.93 us
    ppermute x1, waiting for transfers between devices, by_heads(): lax.ppermute(far[2:], 'groups', swap)  1.85 us
  transfers between devices with their start and end apart: 22, of which 9 were waited for; matrix products, arithmetic and copies ran while one was open for 7% of the time, Pallas kernels for 5%

profile of v8, /device:TPU:0, one launch (start us, length us, event | category | flops | bytes accessed | tf_op | source)
XLA Modules:
  0.0 58.6 jit_solution(6791861741161773520)
XLA Ops:
  0.0 1.0 %dynamic-slice_bitcast_fusion = bf16[64,640]{1,0:T(8,128)(2,1)S(1)} fusion(bf16[1,64,1280]{2,1,0:T(8,128)(2,1)} %param.7, s32[]{:T(128)S(6)} %select_n.9), kind=kLoop, calls=%fused_computation.1 | loop fusion | bytes 163844 | tf_op jit(solution)/shard_map/dynamic_slice | solution.py:186
  1.0 3.0 %collective-permute-start.2 = (bf16[64,640]{1,0:T(8,128)(2,1)S(1)}, bf16[64,640]{1,0:T(8,128)(2,1)S(1)}, u32[]{:S(2)}, u32[]{:S(2)}) collective-permute-start(bf16[64,640]{1,0:T(8,128)(2,1)S(1)} %dynamic-slice_bitcast_fusion), channel_id=1, source_target_pairs={{0,4},{2,6},{4,0},{6,2},{8,12},{10,14},{12,8},{14,10},{1,5},{3,7},... | collective-permute-start | bytes 245768 | tf_op jit(solution)/shard_map/ppermute | solution.py:184
  4.0 2.6 %collective-permute-start.3 = (bf16[64,640]{1,0:T(8,128)(2,1)S(1)}, bf16[64,640]{1,0:T(8,128)(2,1)S(1)}, u32[]{:S(2)}, u32[]{:S(2)}) collective-permute-start(bf16[64,640]{1,0:T(8,128)(2,1)S(1)} %dynamic-slice_bitcast_fusion), channel_id=1, source_target_pairs={{0,8},{2,10},{4,12},{6,14},{8,0},{10,2},{12,4},{14,6},{1,9},{3,11}... | collective-permute-start | bytes 245768 | tf_op jit(solution)/shard_map/ppermute | solution.py:184
  6.6 0.7 %pad_add_fusion.meta_ref = s32[3,5]{1,0:T(4,128)S(1)} fusion(s32[1,5]{1,0:T(1,128)} %bitcast.22, s32[2,5]{1,0:T(2,128)} %bitcast.21), kind=kLoop, calls=%fused_computation.2 | loop fusion | flops 15 | bytes 120 | tf_op jit(solution)/shard_map/concatenate | solution.py:188
  7.3 1.5 %collective-permute-start.1 = (s32[3,5]{1,0:T(4,128)S(1)}, s32[3,5]{1,0:T(4,128)S(1)}, u32[]{:S(2)}, u32[]{:S(2)}) collective-permute-start(s32[3,5]{1,0:T(4,128)S(1)} %pad_add_fusion.meta_ref), channel_id=1, source_target_pairs={{0,16},{16,0},{1,17},{17,1},{2,18},{18,2},{3,19},{19,3},{4,20},{20... | collective-permute-start | bytes 188 | tf_op jit(solution)/shard_map/ppermute | solution.py:199
  8.8 0.9 %copy-done.1 = bf16[32,4096]{1,0:T(8,128)(2,1)S(1)} copy-done((bf16[32,4096]{1,0:T(8,128)(2,1)S(1)}, bf16[32,4096]{1,0:T(8,128)(2,1)}, u32[]{:S(2)}) %copy-start.1) | copy-done | bytes 262168
  9.8 0.1 shard_map.64
  9.9 0.1 collective-permute-start
  10.0 0.5 constant_dynamic-slice_fusion.1
  10.4 0.4 reshape.13
  10.8 0.3 copy.8
  11.1 0.2 collective-permute-done.rest_1_
  11.3 1.0 %shard_map.65 = bf16[16,224,128]{2,1,0:T(8,128)(2,1)} custom-call(bf16[16,160,128]{2,1,0:T(8,128)(2,1)S(1)} %bitcast.12, bf16[16,32,128]{2,1,0:T(8,128)(2,1)S(1)} %get-tuple-element.25.rest_0_, bf16[16,32,128]{2,1,0:T(8,128)(2,1)S(1)} %collective-permute-done.rest_1_), custom_call_target="tpu_custom_call" | custom-call | tf_op jit(solution)/shard_map/pallas_call | solution.py:204
  12.3 0.0 collective-permute-done.1.meta_y_ref
  12.3 0.0 collective-permute-done.2
  12.3 0.0 collective-permute-done.3
  12.3 0.6 collective-permute-start.5
  12.9 1.5 %collective-permute-start.6 = (bf16[3,64,640]{2,1,0:T(8,128)(2,1)S(1)}, bf16[3,64,640]{2,1,0:T(8,128)(2,1)S(1)}, u32[]{:S(2)}, u32[]{:S(2)}) collective-permute-start(bf16[3,64,640]{2,1,0:T(8,128)(2,1)S(1)} %pad_maximum_fusion.rest_0_), channel_id=1, source_target_pairs={{0,2},{2,0},{4,6},{6,4},{8,10},{10,8},{12,14},{14,12},{1,3},{3,1},... | collective-permute-start | bytes 737288 | tf_op jit(solution)/shard_map/ppermute | solution.py:184
  14.4 0.0 collective-permute-start.4
  14.4 0.4 collective-permute-start.7
  14.8 3.9 %all-to-all-start = ((bf16[16,224,128]{2,1,0:T(8,128)(2,1)}), bf16[16,224,128]{2,1,0:T(8,128)(2,1)S(1)}, u32[]{:S(2)}, u32[]{:S(2)}) async-start(bf16[16,224,128]{2,1,0:T(8,128)(2,1)} %shard_map.65), calls=%async_computation | async-start | bytes 1835008 | tf_op jit(solution)/shard_map/all_to_all | solution.py:212
  18.8 0.5 collective-permute-done.7
  19.3 1.3 %collective-permute-done.5.rest_4_ = bf16[3,64,640]{2,1,0:T(8,128)(2,1)S(1)} collective-permute-done((bf16[3,64,640]{2,1,0:T(8,128)(2,1)S(1)}, bf16[3,64,640]{2,1,0:T(8,128)(2,1)S(1)}, u32[]{:S(2)}, u32[]{:S(2)}) %collective-permute-start.5) | collective-permute-done | bytes 245792 | tf_op jit(solution)/shard_map/ppermute | solution.py:215
  20.6 0.2 collective-permute-done.6.rest_2_
  20.8 2.0 %collective-permute-start.10 = (bf16[1,64,640]{2,1,0:T(8,128)(2,1)S(1)}, bf16[1,64,640]{2,1,0:T(8,128)(2,1)S(1)}, u32[]{:S(2)}, u32[]{:S(2)}) collective-permute-start(bf16[1,64,640]{2,1,0:T(8,128)(2,1)S(1)} %bitcast.13), channel_id=1, source_target_pairs={{0,2},{2,0},{4,6},{6,4},{8,10},{10,8},{12,14},{14,12},{1,3},{3,1},... | collective-permute-start | bytes 245768 | tf_op jit(solution)/shard_map/ppermute | solution.py:184
  22.8 0.6 %slice.7 = bf16[1,64,640]{2,1,0:T(8,128)(2,1)} slice(bf16[3,64,640]{2,1,0:T(8,128)(2,1)S(1)} %collective-permute-done.6.rest_2_), slice={[2:3], [0:64], [0:640]} | slice | bytes 163840 | tf_op jit(solution)/shard_map/slice | solution.py:220
  23.4 1.3 %collective-permute-start.17 = (bf16[1,64,640]{2,1,0:T(8,128)(2,1)}, bf16[1,64,640]{2,1,0:T(8,128)(2,1)}, u32[]{:S(2)}, u32[]{:S(2)}) collective-permute-start(bf16[1,64,640]{2,1,0:T(8,128)(2,1)} %slice.7), channel_id=1, source_target_pairs={{0,16},{16,0},{1,17},{17,1},{2,18},{18,2},{3,19},{19,3},{4,20},{20... | collective-permute-start | bytes 245768 | tf_op jit(solution)/shard_map/ppermute | solution.py:220
  24.8 0.7 %collective-permute-start.13 = (bf16[1,64,640]{2,1,0:T(8,128)(2,1)S(1)}, bf16[1,64,640]{2,1,0:T(8,128)(2,1)}, u32[]{:S(2)}, u32[]{:S(2)}) collective-permute-start(bf16[1,64,640]{2,1,0:T(8,128)(2,1)S(1)} %bitcast.14), channel_id=1, source_target_pairs={{0,16},{16,0},{1,17},{17,1},{2,18},{18,2},{3,19},{19,3},{4,20},{20... | collective-permute-start | bytes 245768 | tf_op jit(solution)/shard_map/ppermute | solution.py:218
  25.4 0.7 %slice.6 = bf16[2,64,640]{2,1,0:T(8,128)(2,1)} slice(bf16[3,64,640]{2,1,0:T(8,128)(2,1)S(1)} %collective-permute-done.5.rest_4_), slice={[0:2], [0:64], [0:640]} | slice | bytes 327680 | tf_op jit(solution)/shard_map/slice | solution.py:220
  26.1 0.0 collective-permute-start.15
  26.2 0.0 collective-permute-done.4.rest_0_
  26.2 0.0 collective-permute-start.8
  26.2 0.1 collective-permute-done.10.rest_3_
  26.3 1.5 %collective-permute-start.19 = (bf16[1,64,640]{2,1,0:T(8,128)(2,1)S(1)}, bf16[1,64,640]{2,1,0:T(8,128)(2,1)S(1)}, u32[]{:S(2)}, u32[]{:S(2)}) collective-permute-start(bf16[1,64,640]{2,1,0:T(8,128)(2,1)S(1)} %collective-permute-done.10.rest_3_), channel_id=1, source_target_pairs={{0,16},{16,0},{1,17},{17,1},{2,18},{18,2},{3,19},{19,3},{4,20},{20... | collective-permute-start | bytes 245768 | tf_op jit(solution)/shard_map/ppermute | solution.py:220
  27.8 1.9 %collective-permute-done.17.rest_7_ = bf16[1,64,640]{2,1,0:T(8,128)(2,1)} collective-permute-done((bf16[1,64,640]{2,1,0:T(8,128)(2,1)}, bf16[1,64,640]{2,1,0:T(8,128)(2,1)}, u32[]{:S(2)}, u32[]{:S(2)}) %collective-permute-start.17) | collective-permute-done | bytes 81952 | tf_op jit(solution)/shard_map/ppermute | solution.py:220
  29.6 0.0 collective-permute-start.11
  29.6 3.3 %collective-permute-done.13.rest_5_ = bf16[1,64,640]{2,1,0:T(8,128)(2,1)} collective-permute-done((bf16[1,64,640]{2,1,0:T(8,128)(2,1)S(1)}, bf16[1,64,640]{2,1,0:T(8,128)(2,1)}, u32[]{:S(2)}, u32[]{:S(2)}) %collective-permute-start.13) | collective-permute-done | bytes 81952 | tf_op jit(solution)/shard_map/ppermute | solution.py:218
  32.9 0.0 collective-permute-start.18
  32.9 0.7 %constant_dynamic-slice_fusion.gate_ref = f32[1,128]{1,0:T(1,128)S(1)} fusion(f32[16,128]{1,0:T(8,128)} %bitcast.23, s32[]{:T(128)S(6)} %select_n.11), kind=kLoop, calls=%fused_computation.3 | loop fusion | bytes 1028 | tf_op jit(solution)/shard_map/dynamic_slice | solution.py:223
  33.6 0.0 collective-permute-done.8.rest_1_
  33.6 0.5 collective-permute-start.12
  34.1 0.2 collective-permute-done.19.rest_8_
  34.3 0.0 collective-permute-start.9
  34.3 0.0 collective-permute-done.18.rest_7_
  34.4 0.5 collective-permute-start.14
  34.9 0.0 collective-permute-done.11.rest_3_
  34.9 0.1 collective-permute-start.20
  34.9 0.0 collective-permute-done.15.rest_6_
  34.9 0.4 collective-permute-start.16
  35.4 1.2 %shard_map.66 = (bf16[640,256]{1,0:T(8,128)(2,1)S(1)}, bf16[640,384]{1,0:T(8,128)(2,1)S(1)}) custom-call(s32[3,5]{1,0:T(4,128)S(1)} %pad_add_fusion.meta_ref, s32[3,5]{1,0:T(4,128)S(1)} %collective-permute-done.1.meta_y_ref, bf16[3,64,640]{2,1,0:T(8,128)(2,1)S(1)} %pad_maximum_fusion.rest_0_, bf16[1,64,640]{2,1,0:T(8,128)(2,1)S(1)} %bitcast.16, ...), custom_call_target="tpu_custom_call" | custom-call | flops 8049999872 | bytes 2097152 | tf_op jit(solution)/shard_map/pallas_call | solution.py:226
  36.6 0.8 %copy-done.4 = bf16[640,384]{1,0:T(8,128)(2,1)} copy-done((bf16[640,384]{1,0:T(8,128)(2,1)}, bf16[640,384]{1,0:T(8,128)(2,1)S(1)}, u32[]{:S(2)}) %copy-start.4) | copy-done | bytes 491544
  37.3 0.0 collective-permute-done.14.rest_5_
  37.3 0.0 collective-permute-done.20.rest_8_
  37.3 0.0 collective-permute-done.12.rest_4_
  37.3 0.0 collective-permute-done.9.rest_2_
  37.4 0.0 copy-start.3
  37.4 0.9 %copy-done.3 = bf16[3,64,640]{2,1,0:T(8,128)(2,1)S(1)} copy-done((bf16[3,64,640]{2,1,0:T(8,128)(2,1)S(1)}, bf16[3,64,640]{2,1,0:T(8,128)(2,1)}, u32[]{:S(2)}) %copy-start.3) | copy-done | bytes 245784
  38.3 0.8 %shard_map.67.kept_ref = bf16[640,896]{1,0:T(8,128)(2,1)S(1)} custom-call(s32[3,5]{1,0:T(4,128)S(1)} %pad_add_fusion.meta_ref, s32[3,5]{1,0:T(4,128)S(1)} %collective-permute-done.1.meta_y_ref, bf16[3,64,640]{2,1,0:T(8,128)(2,1)S(1)} %copy-done.3, bf16[1,64,640]{2,1,0:T(8,128)(2,1)S(1)} %collective-permute-done.8.rest_1_, ...), custom_call_target="tpu_custom_call" | custom-call | flops 8049999872 | bytes 2097152 | tf_op jit(solution)/shard_map/pallas_call | solution.py:237
  39.2 3.2 %all-to-all-done.got_ref = bf16[16,224,128]{2,1,0:T(8,128)(2,1)S(1)} async-done(((bf16[16,224,128]{2,1,0:T(8,128)(2,1)}), bf16[16,224,128]{2,1,0:T(8,128)(2,1)S(1)}, u32[]{:S(2)}, u32[]{:S(2)}) %all-to-all-start) | async-done | bytes 917536 | tf_op jit(solution)/shard_map/all_to_all | solution.py:212
  42.3 0.6 %shard_map.68 = (bf16[2,8,2,32,128]{4,3,2,1,0:T(8,128)(2,1)S(1)}, bf16[384,256]{1,0:T(8,128)(2,1)S(1)}, f32[640,256]{1,0:T(8,128)S(1)}) custom-call(bf16[16,224,128]{2,1,0:T(8,128)(2,1)S(1)} %all-to-all-done.got_ref, bf16[640,896]{1,0:T(8,128)(2,1)S(1)} %shard_map.67.kept_ref), custom_call_target="tpu_custom_call" | custom-call | flops 200000000 | bytes 16000000 | tf_op jit(solution)/shard_map/pallas_call | solution.py:245
  42.9 0.4 copy-done.5
  43.4 1.9 %shard_map.69 = bf16[32,32,128]{2,1,0:T(8,128)(2,1)S(1)} custom-call(s32[3,5]{1,0:T(4,128)S(1)} %pad_add_fusion.meta_ref, s32[3,5]{1,0:T(4,128)S(1)} %collective-permute-done.1.meta_y_ref, f32[1,128]{1,0:T(1,128)S(1)} %constant_dynamic-slice_fusion.gate_ref, bf16[2,8,2,32,128]{4,3,2,1,0:T(8,128)(2,1)S(1)} %get-tuple-element.37.query_ref, ...), custom_call_target="tpu_custom_call" | custom-call | flops 20000000000 | bytes 4194304 | tf_op jit(solution)/shard_map/pallas_call | solution.py:258
  45.3 12.6 %all_to_all.10.back_ref = bf16[32,32,128]{2,1,0:T(8,128)(2,1)S(1)} all-to-all(bf16[32,32,128]{2,1,0:T(8,128)(2,1)S(1)} %shard_map.69), channel_id=1, replica_groups=mesh['groups'=2,'ctx'=8,'head'=2] {'groups','ctx','head'}, dimensions={0} | all-to-all | bytes 524288 | tf_op jit(solution)/shard_map/all_to_all | solution.py:267
  57.9 0.8 %shard_map.70 = bf16[32,4096]{1,0:T(8,128)(2,1)} custom-call(bf16[32,32,128]{2,1,0:T(8,128)(2,1)S(1)} %all_to_all.10.back_ref), custom_call_target="tpu_custom_call" | custom-call | tf_op jit(solution)/shard_map/pallas_call | solution.py:268
  (9 shorter events, 0.1 us)
Async XLA Ops:
  0.0 9.9 %copy-start = (bf16[160,2,2048]{2,1,0:T(2,128)(2,1)S(1)}, bf16[160,2,2048]{2,1,0:T(2,128)(2,1)}, u32[]{:S(2)}) copy-start(bf16[160,2,2048]{2,1,0:T(2,128)(2,1)} %param.10) | copy-start | bytes 3932164
  1.0 11.3 %collective-permute-start.2 = (bf16[64,640]{1,0:T(8,128)(2,1)S(1)}, bf16[64,640]{1,0:T(8,128)(2,1)S(1)}, u32[]{:S(2)}, u32[]{:S(2)}) collective-permute-start(bf16[64,640]{1,0:T(8,128)(2,1)S(1)} %dynamic-slice_bitcast_fusion), channel_id=1, source_target_pairs={{0,4},{2,6},{4,0},{6,2},{8,12},{10,14},{12,8},{14,10},{1,5},{3,7},... | collective-permute-start | bytes 245768 | tf_op jit(solution)/shard_map/ppermute | solution.py:184
  4.0 8.3 %collective-permute-start.3 = (bf16[64,640]{1,0:T(8,128)(2,1)S(1)}, bf16[64,640]{1,0:T(8,128)(2,1)S(1)}, u32[]{:S(2)}, u32[]{:S(2)}) collective-permute-start(bf16[64,640]{1,0:T(8,128)(2,1)S(1)} %dynamic-slice_bitcast_fusion), channel_id=1, source_target_pairs={{0,8},{2,10},{4,12},{6,14},{8,0},{10,2},{12,4},{14,6},{1,9},{3,11}... | collective-permute-start | bytes 245768 | tf_op jit(solution)/shard_map/ppermute | solution.py:184
  7.3 5.0 %collective-permute-start.1 = (s32[3,5]{1,0:T(4,128)S(1)}, s32[3,5]{1,0:T(4,128)S(1)}, u32[]{:S(2)}, u32[]{:S(2)}) collective-permute-start(s32[3,5]{1,0:T(4,128)S(1)} %pad_add_fusion.meta_ref), channel_id=1, source_target_pairs={{0,16},{16,0},{1,17},{17,1},{2,18},{18,2},{3,19},{19,3},{4,20},{20... | collective-permute-start | bytes 188 | tf_op jit(solution)/shard_map/ppermute | solution.py:199
  8.8 0.9 %copy-start.1 = (bf16[32,4096]{1,0:T(8,128)(2,1)S(1)}, bf16[32,4096]{1,0:T(8,128)(2,1)}, u32[]{:S(2)}) copy-start(bf16[32,4096]{1,0:T(8,128)(2,1)} %query_ref.1) | copy-start | bytes 786436
  9.9 1.4 %collective-permute-start = (bf16[16,32,128]{2,1,0:T(8,128)(2,1)S(1)}, bf16[16,32,128]{2,1,0:T(8,128)(2,1)S(1)}, u32[]{:S(2)}, u32[]{:S(2)}) collective-permute-start(bf16[16,32,128]{2,1,0:T(8,128)(2,1)S(1)} %get-tuple-element.26), channel_id=1, source_target_pairs={{0,1},{1,0},{2,3},{3,2},{4,5},{5,4},{6,7},{7,6},{8,9},{9,8},{10,11... | collective-permute-start | bytes 393224 | tf_op jit(solution)/shard_map/ppermute | solution.py:198
  12.3 8.2 %collective-permute-start.5 = (bf16[3,64,640]{2,1,0:T(8,128)(2,1)S(1)}, bf16[3,64,640]{2,1,0:T(8,128)(2,1)S(1)}, u32[]{:S(2)}, u32[]{:S(2)}) collective-permute-start(bf16[3,64,640]{2,1,0:T(8,128)(2,1)S(1)} %pad_maximum_fusion.rest_0_), channel_id=1, source_target_pairs={{0,16},{16,0},{1,17},{17,1},{2,18},{18,2},{3,19},{19,3},{4,20},{20... | collective-permute-start | bytes 737288 | tf_op jit(solution)/shard_map/ppermute | solution.py:215
  12.9 7.9 %collective-permute-start.6 = (bf16[3,64,640]{2,1,0:T(8,128)(2,1)S(1)}, bf16[3,64,640]{2,1,0:T(8,128)(2,1)S(1)}, u32[]{:S(2)}, u32[]{:S(2)}) collective-permute-start(bf16[3,64,640]{2,1,0:T(8,128)(2,1)S(1)} %pad_maximum_fusion.rest_0_), channel_id=1, source_target_pairs={{0,2},{2,0},{4,6},{6,4},{8,10},{10,8},{12,14},{14,12},{1,3},{3,1},... | collective-permute-start | bytes 737288 | tf_op jit(solution)/shard_map/ppermute | solution.py:184
  14.4 11.8 %collective-permute-start.4 = (bf16[3,64,640]{2,1,0:T(8,128)(2,1)S(1)}, bf16[3,64,640]{2,1,0:T(8,128)(2,1)S(1)}, u32[]{:S(2)}, u32[]{:S(2)}) collective-permute-start(bf16[3,64,640]{2,1,0:T(8,128)(2,1)S(1)} %pad_maximum_fusion.rest_0_), channel_id=1, source_target_pairs={{0,1},{1,0},{2,3},{3,2},{4,5},{5,4},{6,7},{7,6},{8,9},{9,8},{10,11... | collective-permute-start | bytes 737288 | tf_op jit(solution)/shard_map/ppermute | solution.py:222
  14.4 4.9 %collective-permute-start.7 = (bf16[64,640]{1,0:T(8,128)(2,1)S(1)}, bf16[64,640]{1,0:T(8,128)(2,1)S(1)}, u32[]{:S(2)}, u32[]{:S(2)}) collective-permute-start(bf16[64,640]{1,0:T(8,128)(2,1)S(1)} %collective-permute-done.3), channel_id=1, source_target_pairs={{0,4},{2,6},{4,0},{6,2},{8,12},{10,14},{12,8},{14,10},{1,5},{3,7},... | collective-permute-start | bytes 245768 | tf_op jit(solution)/shard_map/ppermute | solution.py:184
  14.8 27.5 %all-to-all-start = ((bf16[16,224,128]{2,1,0:T(8,128)(2,1)}), bf16[16,224,128]{2,1,0:T(8,128)(2,1)S(1)}, u32[]{:S(2)}, u32[]{:S(2)}) async-start(bf16[16,224,128]{2,1,0:T(8,128)(2,1)} %shard_map.65), calls=%async_computation | async-start | bytes 1835008 | tf_op jit(solution)/shard_map/all_to_all | solution.py:212
  20.8 5.5 %collective-permute-start.10 = (bf16[1,64,640]{2,1,0:T(8,128)(2,1)S(1)}, bf16[1,64,640]{2,1,0:T(8,128)(2,1)S(1)}, u32[]{:S(2)}, u32[]{:S(2)}) collective-permute-start(bf16[1,64,640]{2,1,0:T(8,128)(2,1)S(1)} %bitcast.13), channel_id=1, source_target_pairs={{0,2},{2,0},{4,6},{6,4},{8,10},{10,8},{12,14},{14,12},{1,3},{3,1},... | collective-permute-start | bytes 245768 | tf_op jit(solution)/shard_map/ppermute | solution.py:184
  23.4 6.2 %collective-permute-start.17 = (bf16[1,64,640]{2,1,0:T(8,128)(2,1)}, bf16[1,64,640]{2,1,0:T(8,128)(2,1)}, u32[]{:S(2)}, u32[]{:S(2)}) collective-permute-start(bf16[1,64,640]{2,1,0:T(8,128)(2,1)} %slice.7), channel_id=1, source_target_pairs={{0,16},{16,0},{1,17},{17,1},{2,18},{18,2},{3,19},{19,3},{4,20},{20... | collective-permute-start | bytes 245768 | tf_op jit(solution)/shard_map/ppermute | solution.py:220
  24.8 8.1 %collective-permute-start.13 = (bf16[1,64,640]{2,1,0:T(8,128)(2,1)S(1)}, bf16[1,64,640]{2,1,0:T(8,128)(2,1)}, u32[]{:S(2)}, u32[]{:S(2)}) collective-permute-start(bf16[1,64,640]{2,1,0:T(8,128)(2,1)S(1)} %bitcast.14), channel_id=1, source_target_pairs={{0,16},{16,0},{1,17},{17,1},{2,18},{18,2},{3,19},{19,3},{4,20},{20... | collective-permute-start | bytes 245768 | tf_op jit(solution)/shard_map/ppermute | solution.py:218
  26.1 8.8 %collective-permute-start.15 = (bf16[2,64,640]{2,1,0:T(8,128)(2,1)}, bf16[2,64,640]{2,1,0:T(8,128)(2,1)S(1)}, u32[]{:S(2)}, u32[]{:S(2)}) collective-permute-start(bf16[2,64,640]{2,1,0:T(8,128)(2,1)} %slice.6), channel_id=1, source_target_pairs={{0,2},{2,0},{4,6},{6,4},{8,10},{10,8},{12,14},{14,12},{1,3},{3,1},... | collective-permute-start | bytes 491528 | tf_op jit(solution)/shard_map/ppermute | solution.py:184
  26.2 10.4 %copy-start.2 = (bf16[3,64,640]{2,1,0:T(8,128)(2,1)}, bf16[3,64,640]{2,1,0:T(8,128)(2,1)S(1)}, u32[]{:S(2)}) copy-start(bf16[3,64,640]{2,1,0:T(8,128)(2,1)S(1)} %collective-permute-done.4.rest_0_) | copy-start | bytes 737284
  26.2 7.4 %collective-permute-start.8 = (bf16[1,64,640]{2,1,0:T(8,128)(2,1)S(1)}, bf16[1,64,640]{2,1,0:T(8,128)(2,1)S(1)}, u32[]{:S(2)}, u32[]{:S(2)}) collective-permute-start(bf16[1,64,640]{2,1,0:T(8,128)(2,1)S(1)} %bitcast.15), channel_id=1, source_target_pairs={{0,1},{1,0},{2,3},{3,2},{4,5},{5,4},{6,7},{7,6},{8,9},{9,8},{10,11... | collective-permute-start | bytes 245768 | tf_op jit(solution)/shard_map/ppermute | solution.py:222
  26.3 8.1 %collective-permute-start.19 = (bf16[1,64,640]{2,1,0:T(8,128)(2,1)S(1)}, bf16[1,64,640]{2,1,0:T(8,128)(2,1)S(1)}, u32[]{:S(2)}, u32[]{:S(2)}) collective-permute-start(bf16[1,64,640]{2,1,0:T(8,128)(2,1)S(1)} %collective-permute-done.10.rest_3_), channel_id=1, source_target_pairs={{0,16},{16,0},{1,17},{17,1},{2,18},{18,2},{3,19},{19,3},{4,20},{20... | collective-permute-start | bytes 245768 | tf_op jit(solution)/shard_map/ppermute | solution.py:220
  29.6 5.2 %collective-permute-start.11 = (bf16[1,64,640]{2,1,0:T(8,128)(2,1)S(1)}, bf16[1,64,640]{2,1,0:T(8,128)(2,1)S(1)}, u32[]{:S(2)}, u32[]{:S(2)}) collective-permute-start(bf16[1,64,640]{2,1,0:T(8,128)(2,1)S(1)} %collective-permute-done.10.rest_3_), channel_id=1, source_target_pairs={{0,1},{1,0},{2,3},{3,2},{4,5},{5,4},{6,7},{7,6},{8,9},{9,8},{10,11... | collective-permute-start | bytes 245768 | tf_op jit(solution)/shard_map/ppermute | solution.py:222
  32.9 1.5 %collective-permute-start.18 = (bf16[1,64,640]{2,1,0:T(8,128)(2,1)}, bf16[1,64,640]{2,1,0:T(8,128)(2,1)S(1)}, u32[]{:S(2)}, u32[]{:S(2)}) collective-permute-start(bf16[1,64,640]{2,1,0:T(8,128)(2,1)} %collective-permute-done.17.rest_7_), channel_id=1, source_target_pairs={{0,1},{1,0},{2,3},{3,2},{4,5},{5,4},{6,7},{7,6},{8,9},{9,8},{10,11... | collective-permute-start | bytes 245768 | tf_op jit(solution)/shard_map/ppermute | solution.py:222
  33.6 3.7 %collective-permute-start.12 = (bf16[3,64,640]{2,1,0:T(8,128)(2,1)S(1)}, bf16[3,64,640]{2,1,0:T(8,128)(2,1)S(1)}, u32[]{:S(2)}, u32[]{:S(2)}) collective-permute-start(bf16[3,64,640]{2,1,0:T(8,128)(2,1)S(1)} %collective-permute-done.5.rest_4_), channel_id=1, source_target_pairs={{0,1},{1,0},{2,3},{3,2},{4,5},{5,4},{6,7},{7,6},{8,9},{9,8},{10,11... | collective-permute-start | bytes 737288 | tf_op jit(solution)/shard_map/ppermute | solution.py:222
  34.3 3.0 %collective-permute-start.9 = (bf16[3,64,640]{2,1,0:T(8,128)(2,1)S(1)}, bf16[3,64,640]{2,1,0:T(8,128)(2,1)S(1)}, u32[]{:S(2)}, u32[]{:S(2)}) collective-permute-start(bf16[3,64,640]{2,1,0:T(8,128)(2,1)S(1)} %collective-permute-done.6.rest_2_), channel_id=1, source_target_pairs={{0,1},{1,0},{2,3},{3,2},{4,5},{5,4},{6,7},{7,6},{8,9},{9,8},{10,11... | collective-permute-start | bytes 737288 | tf_op jit(solution)/shard_map/ppermute | solution.py:222
  34.4 3.0 %collective-permute-start.14 = (bf16[1,64,640]{2,1,0:T(8,128)(2,1)}, bf16[1,64,640]{2,1,0:T(8,128)(2,1)S(1)}, u32[]{:S(2)}, u32[]{:S(2)}) collective-permute-start(bf16[1,64,640]{2,1,0:T(8,128)(2,1)} %collective-permute-done.13.rest_5_), channel_id=1, source_target_pairs={{0,1},{1,0},{2,3},{3,2},{4,5},{5,4},{6,7},{7,6},{8,9},{9,8},{10,11... | collective-permute-start | bytes 245768 | tf_op jit(solution)/shard_map/ppermute | solution.py:222
  34.9 2.5 %collective-permute-start.20 = (bf16[1,64,640]{2,1,0:T(8,128)(2,1)S(1)}, bf16[1,64,640]{2,1,0:T(8,128)(2,1)S(1)}, u32[]{:S(2)}, u32[]{:S(2)}) collective-permute-start(bf16[1,64,640]{2,1,0:T(8,128)(2,1)S(1)} %collective-permute-done.19.rest_8_), channel_id=1, source_target_pairs={{0,1},{1,0},{2,3},{3,2},{4,5},{5,4},{6,7},{7,6},{8,9},{9,8},{10,11... | collective-permute-start | bytes 245768 | tf_op jit(solution)/shard_map/ppermute | solution.py:222
  34.9 2.4 %collective-permute-start.16 = (bf16[2,64,640]{2,1,0:T(8,128)(2,1)S(1)}, bf16[2,64,640]{2,1,0:T(8,128)(2,1)S(1)}, u32[]{:S(2)}, u32[]{:S(2)}) collective-permute-start(bf16[2,64,640]{2,1,0:T(8,128)(2,1)S(1)} %collective-permute-done.15.rest_6_), channel_id=1, source_target_pairs={{0,1},{1,0},{2,3},{3,2},{4,5},{5,4},{6,7},{7,6},{8,9},{9,8},{10,11... | collective-permute-start | bytes 491528 | tf_op jit(solution)/shard_map/ppermute | solution.py:222
  36.5 0.8 %copy-start.4 = (bf16[640,384]{1,0:T(8,128)(2,1)}, bf16[640,384]{1,0:T(8,128)(2,1)S(1)}, u32[]{:S(2)}) copy-start(bf16[640,384]{1,0:T(8,128)(2,1)S(1)} %get-tuple-element.40.late_ref) | copy-start | bytes 1474564
  37.4 0.9 %copy-start.3 = (bf16[3,64,640]{2,1,0:T(8,128)(2,1)S(1)}, bf16[3,64,640]{2,1,0:T(8,128)(2,1)}, u32[]{:S(2)}) copy-start(bf16[3,64,640]{2,1,0:T(8,128)(2,1)} %copy-done.2) | copy-start | bytes 737284
  42.3 1.0 %copy-start.5 = (bf16[640,384]{1,0:T(8,128)(2,1)S(1)}, bf16[640,384]{1,0:T(8,128)(2,1)}, u32[]{:S(2)}) copy-start(bf16[640,384]{1,0:T(8,128)(2,1)} %copy-done.4) | copy-start | bytes 1474564

commit v9 on v8

--- a/solution.py
+++ b/solution.py
@@ -102,7 +102,7 @@
     core = lax.axis_index("head")
     metas = (meta_ref, meta_y_ref)
     queries = [query_ref[r].reshape(count, DH) for r in range(2)]
-    gate = jnp.tanh(gate_ref[...])
+    gate = jnp.tanh(gate_ref[pl.ds(group * ctx_count + lax.axis_index("ctx"), 1), :])
     row = lax.broadcasted_iota(jnp.int32, (1, count), 1)
     block = row // part
     position = (block // 2 * 2 + (block % 2 ^ core)) * part + row % part
@@ -220,7 +220,7 @@
     far_y = [across(near_y[:2], 1), lax.ppermute(far[2:], "groups", swap), lax.ppermute(last_x, "groups", swap)]
     stores = [near, last, far, last_x, near_y, last_y] + far_y
     stores += [lax.ppermute(x, "head", swap) for x in stores]
-    gate = lax.dynamic_slice_in_dim(attn_gate.reshape(-1, DH), group * ctx_count + place, 1, 0)
+    gate = attn_gate.reshape(-1, DH)
     late = 3 * DH
     size = 2 * images * lat
     first, last_columns = pl.pallas_call(

time: 59 us -> 59 us (level)
  waiting for transfers between devices: 10.8 us -> 13.1 us
  local copies, waits for them, and re-layouts: 7.24 us -> 5.24 us
    ppermute x6, waiting for transfers between devices: 0.78 us -> 2.49 us  [across(): return lax.ppermute(x, 'ctx', [(i, i ^ turn) for i in range(ctx_count)])]
    ppermute x1, waiting for transfers between devices: 0.25 us -> 1.08 us  [by_heads(): lax.ppermute(last_x, 'groups', swap)]
    dynamic_slice x1 -> x0, local copies, waits for them, and re-layouts: 0.69 us -> none  [by_heads(): lax.dynamic_slice_in_dim(attn_gate.reshape(-1, DH), group * ctx_count + p...]
    slice x1, local copies, waits for them, and re-layouts: 0.68 us -> 0.01 us  [by_heads(): near_y[:2]]
    ppermute x1, waiting for transfers between devices: 1.85 us -> 1.21 us  [by_heads(): lax.ppermute(far[2:], 'groups', swap)]
    slice x1, local copies, waits for them, and re-layouts: 0.63 us -> 0.01 us  [by_heads(): far[2:]]
    unnamed x12 -> x14, local copies, waits for them, and re-layouts: 3.1 us -> 3.09 us
  transfers between devices with their start and end apart: 22 -> 22, of which waited for: 9 -> 9; matrix products, arithmetic and copies ran while one was open for 7% -> 3% of each run, Pallas kernels for 5% -> 5%
where the time goes in v9:
time: 59 us; the launch traced here: 58.6 us
  starting transfers between devices  20.8 us (35%)
  waiting for transfers between devices  13.1 us (22%)
  blocking collectives  12.6 us (21%)
  Pallas kernels  5.98 us (10%)
  local copies, waits for them, and re-layouts  5.24 us (9%)
  other arithmetic  0.74 us (1%)
    all_to_all x1, blocking collectives, by_heads(): back = lax.all_to_all(gated, every, split_axis=0, concat_axis=0, tiled=True)  12.6 us
    ppermute x6, starting transfers between devices, across(): return lax.ppermute(x, 'ctx', [(i, i ^ turn) for i in range(ctx_count)])  9.64 us
    all_to_all x1, starting transfers between devices, by_heads(): lax.all_to_all(outgoing, ('groups', 'ctx'), split_axis=0, concat_axis=0,...  3.91 us
    all_to_all x1, waiting for transfers between devices, by_heads(): lax.all_to_all(outgoing, ('groups', 'ctx'), split_axis=0, concat_axis=0,...  3.49 us
    ppermute x1, waiting for transfers between devices, by_heads(): last_y = lax.ppermute(last, 'groups', swap)  3.27 us
    unnamed x14, local copies, waits for them, and re-layouts  3.09 us
    ppermute x6, waiting for transfers between devices, across(): return lax.ppermute(x, 'ctx', [(i, i ^ turn) for i in range(ctx_count)])  2.49 us
    pallas_call x1, Pallas kernels, by_heads(): pl.pallas_call(attend_kernel, out_shape=jax.ShapeDtypeStruct((ctx_count *...  1.93 us
  transfers between devices with their start and end apart: 22, of which 9 were waited for; matrix products, arithmetic and copies ran while one was open for 3% of the time, Pallas kernels for 5%

profile of v9, /device:TPU:0, one launch (start us, length us, event | category | flops | bytes accessed | tf_op | source)
XLA Modules:
  0.0 58.6 jit_solution(17090298933786966912)
XLA Ops:
  0.0 1.0 %dynamic-slice_bitcast_fusion = bf16[64,640]{1,0:T(8,128)(2,1)S(1)} fusion(bf16[1,64,1280]{2,1,0:T(8,128)(2,1)} %param.7, s32[]{:T(128)S(6)} %select_n.6), kind=kLoop, calls=%fused_computation.1 | loop fusion | bytes 163844 | tf_op jit(solution)/shard_map/dynamic_slice | solution.py:186
  1.0 3.0 %collective-permute-start.2 = (bf16[64,640]{1,0:T(8,128)(2,1)S(1)}, bf16[64,640]{1,0:T(8,128)(2,1)S(1)}, u32[]{:S(2)}, u32[]{:S(2)}) collective-permute-start(bf16[64,640]{1,0:T(8,128)(2,1)S(1)} %dynamic-slice_bitcast_fusion), channel_id=1, source_target_pairs={{0,4},{2,6},{4,0},{6,2},{8,12},{10,14},{12,8},{14,10},{1,5},{3,7},... | collective-permute-start | bytes 245768 | tf_op jit(solution)/shard_map/ppermute | solution.py:184
  4.0 2.6 %collective-permute-start.3 = (bf16[64,640]{1,0:T(8,128)(2,1)S(1)}, bf16[64,640]{1,0:T(8,128)(2,1)S(1)}, u32[]{:S(2)}, u32[]{:S(2)}) collective-permute-start(bf16[64,640]{1,0:T(8,128)(2,1)S(1)} %dynamic-slice_bitcast_fusion), channel_id=1, source_target_pairs={{0,8},{2,10},{4,12},{6,14},{8,0},{10,2},{12,4},{14,6},{1,9},{3,11}... | collective-permute-start | bytes 245768 | tf_op jit(solution)/shard_map/ppermute | solution.py:184
  6.6 0.7 %pad_add_fusion.meta_ref = s32[3,5]{1,0:T(4,128)S(1)} fusion(s32[1,5]{1,0:T(1,128)} %bitcast.23, s32[2,5]{1,0:T(2,128)} %bitcast.22), kind=kLoop, calls=%fused_computation.2 | loop fusion | flops 15 | bytes 120 | tf_op jit(solution)/shard_map/concatenate | solution.py:188
  7.3 1.5 %collective-permute-start.1 = (s32[3,5]{1,0:T(4,128)S(1)}, s32[3,5]{1,0:T(4,128)S(1)}, u32[]{:S(2)}, u32[]{:S(2)}) collective-permute-start(s32[3,5]{1,0:T(4,128)S(1)} %pad_add_fusion.meta_ref), channel_id=1, source_target_pairs={{0,16},{16,0},{1,17},{17,1},{2,18},{18,2},{3,19},{19,3},{4,20},{20... | collective-permute-start | bytes 188 | tf_op jit(solution)/shard_map/ppermute | solution.py:199
  8.8 0.9 %copy-done.1 = bf16[32,4096]{1,0:T(8,128)(2,1)S(1)} copy-done((bf16[32,4096]{1,0:T(8,128)(2,1)S(1)}, bf16[32,4096]{1,0:T(8,128)(2,1)}, u32[]{:S(2)}) %copy-start.1) | copy-done | bytes 262168
  9.8 0.1 shard_map.64
  9.9 0.1 collective-permute-start
  10.0 0.5 constant_dynamic-slice_fusion
  10.4 0.4 reshape.13
  10.8 0.3 copy.8
  11.1 0.2 collective-permute-done.rest_1_
  11.3 1.0 %shard_map.65 = bf16[16,224,128]{2,1,0:T(8,128)(2,1)} custom-call(bf16[16,160,128]{2,1,0:T(8,128)(2,1)S(1)} %bitcast.12, bf16[16,32,128]{2,1,0:T(8,128)(2,1)S(1)} %get-tuple-element.25.rest_0_, bf16[16,32,128]{2,1,0:T(8,128)(2,1)S(1)} %collective-permute-done.rest_1_), custom_call_target="tpu_custom_call" | custom-call | tf_op jit(solution)/shard_map/pallas_call | solution.py:204
  12.3 0.0 collective-permute-done.1.meta_y_ref
  12.3 0.0 collective-permute-done.2
  12.3 0.0 collective-permute-done.3
  12.3 0.6 collective-permute-start.5
  12.9 1.5 %collective-permute-start.6 = (bf16[3,64,640]{2,1,0:T(8,128)(2,1)S(1)}, bf16[3,64,640]{2,1,0:T(8,128)(2,1)S(1)}, u32[]{:S(2)}, u32[]{:S(2)}) collective-permute-start(bf16[3,64,640]{2,1,0:T(8,128)(2,1)S(1)} %pad_maximum_fusion.rest_0_), channel_id=1, source_target_pairs={{0,2},{2,0},{4,6},{6,4},{8,10},{10,8},{12,14},{14,12},{1,3},{3,1},... | collective-permute-start | bytes 737288 | tf_op jit(solution)/shard_map/ppermute | solution.py:184
  14.4 0.0 collective-permute-start.4
  14.4 0.4 collective-permute-start.7
  14.8 3.9 %all-to-all-start = ((bf16[16,224,128]{2,1,0:T(8,128)(2,1)}), bf16[16,224,128]{2,1,0:T(8,128)(2,1)S(1)}, u32[]{:S(2)}, u32[]{:S(2)}) async-start(bf16[16,224,128]{2,1,0:T(8,128)(2,1)} %shard_map.65), calls=%async_computation | async-start | bytes 1835008 | tf_op jit(solution)/shard_map/all_to_all | solution.py:212
  18.8 0.5 collective-permute-done.7
  19.3 1.3 %collective-permute-done.5.rest_4_ = bf16[3,64,640]{2,1,0:T(8,128)(2,1)S(1)} collective-permute-done((bf16[3,64,640]{2,1,0:T(8,128)(2,1)S(1)}, bf16[3,64,640]{2,1,0:T(8,128)(2,1)S(1)}, u32[]{:S(2)}, u32[]{:S(2)}) %collective-permute-start.5) | collective-permute-done | bytes 245792 | tf_op jit(solution)/shard_map/ppermute | solution.py:215
  20.6 0.2 collective-permute-done.6.rest_2_
  20.8 2.0 %collective-permute-start.10 = (bf16[1,64,640]{2,1,0:T(8,128)(2,1)S(1)}, bf16[1,64,640]{2,1,0:T(8,128)(2,1)S(1)}, u32[]{:S(2)}, u32[]{:S(2)}) collective-permute-start(bf16[1,64,640]{2,1,0:T(8,128)(2,1)S(1)} %bitcast.13), channel_id=1, source_target_pairs={{0,2},{2,0},{4,6},{6,4},{8,10},{10,8},{12,14},{14,12},{1,3},{3,1},... | collective-permute-start | bytes 245768 | tf_op jit(solution)/shard_map/ppermute | solution.py:184
  22.8 1.4 %collective-permute-start.17 = (bf16[1,64,640]{2,1,0:T(8,128)(2,1)S(1)}, bf16[1,64,640]{2,1,0:T(8,128)(2,1)S(1)}, u32[]{:S(2)}, u32[]{:S(2)}) collective-permute-start(bf16[1,64,640]{2,1,0:T(8,128)(2,1)S(1)} %slice.7), channel_id=1, source_target_pairs={{0,16},{16,0},{1,17},{17,1},{2,18},{18,2},{3,19},{19,3},{4,20},{20... | collective-permute-start | bytes 245768 | tf_op jit(solution)/shard_map/ppermute | solution.py:220
  24.2 0.7 %collective-permute-start.13 = (bf16[1,64,640]{2,1,0:T(8,128)(2,1)S(1)}, bf16[1,64,640]{2,1,0:T(8,128)(2,1)S(1)}, u32[]{:S(2)}, u32[]{:S(2)}) collective-permute-start(bf16[1,64,640]{2,1,0:T(8,128)(2,1)S(1)} %bitcast.14), channel_id=1, source_target_pairs={{0,16},{16,0},{1,17},{17,1},{2,18},{18,2},{3,19},{19,3},{4,20},{20... | collective-permute-start | bytes 245768 | tf_op jit(solution)/shard_map/ppermute | solution.py:218
  24.9 0.1 collective-permute-start.15
  25.0 0.0 collective-permute-done.4.rest_0_
  25.0 0.1 collective-permute-start.8
  25.1 1.8 %collective-permute-done.10.rest_3_ = bf16[1,64,640]{2,1,0:T(8,128)(2,1)S(1)} collective-permute-done((bf16[1,64,640]{2,1,0:T(8,128)(2,1)S(1)}, bf16[1,64,640]{2,1,0:T(8,128)(2,1)S(1)}, u32[]{:S(2)}, u32[]{:S(2)}) %collective-permute-start.10) | collective-permute-done | bytes 81952 | tf_op jit(solution)/shard_map/ppermute | solution.py:184
  26.9 1.4 %collective-permute-start.19 = (bf16[1,64,640]{2,1,0:T(8,128)(2,1)S(1)}, bf16[1,64,640]{2,1,0:T(8,128)(2,1)S(1)}, u32[]{:S(2)}, u32[]{:S(2)}) collective-permute-start(bf16[1,64,640]{2,1,0:T(8,128)(2,1)S(1)} %collective-permute-done.10.rest_3_), channel_id=1, source_target_pairs={{0,16},{16,0},{1,17},{17,1},{2,18},{18,2},{3,19},{19,3},{4,20},{20... | collective-permute-start | bytes 245768 | tf_op jit(solution)/shard_map/ppermute | solution.py:220
  28.3 1.2 %collective-permute-done.17.rest_7_ = bf16[1,64,640]{2,1,0:T(8,128)(2,1)S(1)} collective-permute-done((bf16[1,64,640]{2,1,0:T(8,128)(2,1)S(1)}, bf16[1,64,640]{2,1,0:T(8,128)(2,1)S(1)}, u32[]{:S(2)}, u32[]{:S(2)}) %collective-permute-start.17) | collective-permute-done | bytes 81952 | tf_op jit(solution)/shard_map/ppermute | solution.py:220
  29.5 0.0 collective-permute-start.18
  29.5 3.3 %collective-permute-done.13.rest_5_ = bf16[1,64,640]{2,1,0:T(8,128)(2,1)S(1)} collective-permute-done((bf16[1,64,640]{2,1,0:T(8,128)(2,1)S(1)}, bf16[1,64,640]{2,1,0:T(8,128)(2,1)S(1)}, u32[]{:S(2)}, u32[]{:S(2)}) %collective-permute-start.13) | collective-permute-done | bytes 81952 | tf_op jit(solution)/shard_map/ppermute | solution.py:218
  32.8 0.0 collective-permute-start.11
  32.8 0.0 collective-permute-done.8.rest_1_
  32.8 0.5 collective-permute-start.12
  33.3 1.1 %collective-permute-done.19.rest_8_ = bf16[1,64,640]{2,1,0:T(8,128)(2,1)S(1)} collective-permute-done((bf16[1,64,640]{2,1,0:T(8,128)(2,1)S(1)}, bf16[1,64,640]{2,1,0:T(8,128)(2,1)S(1)}, u32[]{:S(2)}, u32[]{:S(2)}) %collective-permute-start.19) | collective-permute-done | bytes 81952 | tf_op jit(solution)/shard_map/ppermute | solution.py:220
  34.4 0.0 collective-permute-start.9
  34.4 0.0 collective-permute-done.18.rest_7_
  34.4 0.5 collective-permute-start.14
  34.9 0.0 collective-permute-done.11.rest_3_
  34.9 0.1 collective-permute-start.20
  35.0 0.0 collective-permute-done.15.rest_6_
  35.0 0.4 collective-permute-start.16
  35.4 0.8 %shard_map.66 = (bf16[640,256]{1,0:T(8,128)(2,1)S(1)}, bf16[640,384]{1,0:T(8,128)(2,1)S(1)}) custom-call(s32[3,5]{1,0:T(4,128)S(1)} %pad_add_fusion.meta_ref, s32[3,5]{1,0:T(4,128)S(1)} %collective-permute-done.1.meta_y_ref, bf16[3,64,640]{2,1,0:T(8,128)(2,1)S(1)} %pad_maximum_fusion.rest_0_, bf16[1,64,640]{2,1,0:T(8,128)(2,1)S(1)} %bitcast.16, ...), custom_call_target="tpu_custom_call" | custom-call | flops 8049999872 | bytes 2097152 | tf_op jit(solution)/shard_map/pallas_call | solution.py:226
  36.2 0.0 copy-start.5
  36.3 0.8 %copy-done.5 = bf16[640,384]{1,0:T(8,128)(2,1)} copy-done((bf16[640,384]{1,0:T(8,128)(2,1)}, bf16[640,384]{1,0:T(8,128)(2,1)S(1)}, u32[]{:S(2)}) %copy-start.5) | copy-done | bytes 491544
  37.0 0.0 collective-permute-done.14.rest_5_
  37.0 0.0 collective-permute-done.20.rest_8_
  37.0 0.0 collective-permute-done.12.rest_4_
  37.0 0.0 collective-permute-done.9.rest_2_
  37.1 0.0 collective-permute-done.16.rest_6_
  37.1 0.0 copy-start.3
  37.1 0.9 %copy-done.3 = bf16[3,64,640]{2,1,0:T(8,128)(2,1)S(1)} copy-done((bf16[3,64,640]{2,1,0:T(8,128)(2,1)S(1)}, bf16[3,64,640]{2,1,0:T(8,128)(2,1)}, u32[]{:S(2)}) %copy-start.3) | copy-done | bytes 245784
  38.0 0.8 %shard_map.67.kept_ref = bf16[640,896]{1,0:T(8,128)(2,1)S(1)} custom-call(s32[3,5]{1,0:T(4,128)S(1)} %pad_add_fusion.meta_ref, s32[3,5]{1,0:T(4,128)S(1)} %collective-permute-done.1.meta_y_ref, bf16[3,64,640]{2,1,0:T(8,128)(2,1)S(1)} %copy-done.3, bf16[1,64,640]{2,1,0:T(8,128)(2,1)S(1)} %collective-permute-done.8.rest_1_, ...), custom_call_target="tpu_custom_call" | custom-call | flops 8049999872 | bytes 2097152 | tf_op jit(solution)/shard_map/pallas_call | solution.py:237
  38.8 0.0 copy-start.4
  38.8 3.5 %all-to-all-done.got_ref = bf16[16,224,128]{2,1,0:T(8,128)(2,1)S(1)} async-done(((bf16[16,224,128]{2,1,0:T(8,128)(2,1)}), bf16[16,224,128]{2,1,0:T(8,128)(2,1)S(1)}, u32[]{:S(2)}, u32[]{:S(2)}) %all-to-all-start) | async-done | bytes 917536 | tf_op jit(solution)/shard_map/all_to_all | solution.py:212
  42.3 0.6 %shard_map.68 = (bf16[2,8,2,32,128]{4,3,2,1,0:T(8,128)(2,1)S(1)}, bf16[384,256]{1,0:T(8,128)(2,1)S(1)}, f32[640,256]{1,0:T(8,128)S(1)}) custom-call(bf16[16,224,128]{2,1,0:T(8,128)(2,1)S(1)} %all-to-all-done.got_ref, bf16[640,896]{1,0:T(8,128)(2,1)S(1)} %shard_map.67.kept_ref), custom_call_target="tpu_custom_call" | custom-call | flops 200000000 | bytes 16000000 | tf_op jit(solution)/shard_map/pallas_call | solution.py:245
  42.9 0.4 copy-done.6
  43.4 1.9 %shard_map.69 = bf16[32,32,128]{2,1,0:T(8,128)(2,1)S(1)} custom-call(s32[3,5]{1,0:T(4,128)S(1)} %pad_add_fusion.meta_ref, s32[3,5]{1,0:T(4,128)S(1)} %collective-permute-done.1.meta_y_ref, f32[16,128]{1,0:T(8,128)S(1)} %bitcast.17, bf16[2,8,2,32,128]{4,3,2,1,0:T(8,128)(2,1)S(1)} %get-tuple-element.37.query_ref, ...), custom_call_target="tpu_custom_call" | custom-call | flops 20000000000 | bytes 4194304 | tf_op jit(solution)/shard_map/pallas_call | solution.py:258
  45.3 12.6 %all_to_all.10.back_ref = bf16[32,32,128]{2,1,0:T(8,128)(2,1)S(1)} all-to-all(bf16[32,32,128]{2,1,0:T(8,128)(2,1)S(1)} %shard_map.69), channel_id=1, replica_groups=mesh['groups'=2,'ctx'=8,'head'=2] {'groups','ctx','head'}, dimensions={0} | all-to-all | bytes 524288 | tf_op jit(solution)/shard_map/all_to_all | solution.py:267
  57.9 0.8 %shard_map.70 = bf16[32,4096]{1,0:T(8,128)(2,1)} custom-call(bf16[32,32,128]{2,1,0:T(8,128)(2,1)S(1)} %all_to_all.10.back_ref), custom_call_target="tpu_custom_call" | custom-call | tf_op jit(solution)/shard_map/pallas_call | solution.py:268
  (10 shorter events, 0.1 us)
Async XLA Ops:
  0.0 9.9 %copy-start = (bf16[160,2,2048]{2,1,0:T(2,128)(2,1)S(1)}, bf16[160,2,2048]{2,1,0:T(2,128)(2,1)}, u32[]{:S(2)}) copy-start(bf16[160,2,2048]{2,1,0:T(2,128)(2,1)} %param.10) | copy-start | bytes 3932164
  1.0 11.3 %collective-permute-start.2 = (bf16[64,640]{1,0:T(8,128)(2,1)S(1)}, bf16[64,640]{1,0:T(8,128)(2,1)S(1)}, u32[]{:S(2)}, u32[]{:S(2)}) collective-permute-start(bf16[64,640]{1,0:T(8,128)(2,1)S(1)} %dynamic-slice_bitcast_fusion), channel_id=1, source_target_pairs={{0,4},{2,6},{4,0},{6,2},{8,12},{10,14},{12,8},{14,10},{1,5},{3,7},... | collective-permute-start | bytes 245768 | tf_op jit(solution)/shard_map/ppermute | solution.py:184
  4.0 8.3 %collective-permute-start.3 = (bf16[64,640]{1,0:T(8,128)(2,1)S(1)}, bf16[64,640]{1,0:T(8,128)(2,1)S(1)}, u32[]{:S(2)}, u32[]{:S(2)}) collective-permute-start(bf16[64,640]{1,0:T(8,128)(2,1)S(1)} %dynamic-slice_bitcast_fusion), channel_id=1, source_target_pairs={{0,8},{2,10},{4,12},{6,14},{8,0},{10,2},{12,4},{14,6},{1,9},{3,11}... | collective-permute-start | bytes 245768 | tf_op jit(solution)/shard_map/ppermute | solution.py:184
  7.3 5.0 %collective-permute-start.1 = (s32[3,5]{1,0:T(4,128)S(1)}, s32[3,5]{1,0:T(4,128)S(1)}, u32[]{:S(2)}, u32[]{:S(2)}) collective-permute-start(s32[3,5]{1,0:T(4,128)S(1)} %pad_add_fusion.meta_ref), channel_id=1, source_target_pairs={{0,16},{16,0},{1,17},{17,1},{2,18},{18,2},{3,19},{19,3},{4,20},{20... | collective-permute-start | bytes 188 | tf_op jit(solution)/shard_map/ppermute | solution.py:199
  8.8 0.9 %copy-start.1 = (bf16[32,4096]{1,0:T(8,128)(2,1)S(1)}, bf16[32,4096]{1,0:T(8,128)(2,1)}, u32[]{:S(2)}) copy-start(bf16[32,4096]{1,0:T(8,128)(2,1)} %query_ref.1) | copy-start | bytes 786436
  9.9 1.4 %collective-permute-start = (bf16[16,32,128]{2,1,0:T(8,128)(2,1)S(1)}, bf16[16,32,128]{2,1,0:T(8,128)(2,1)S(1)}, u32[]{:S(2)}, u32[]{:S(2)}) collective-permute-start(bf16[16,32,128]{2,1,0:T(8,128)(2,1)S(1)} %get-tuple-element.26), channel_id=1, source_target_pairs={{0,1},{1,0},{2,3},{3,2},{4,5},{5,4},{6,7},{7,6},{8,9},{9,8},{10,11... | collective-permute-start | bytes 393224 | tf_op jit(solution)/shard_map/ppermute | solution.py:198
  12.3 8.2 %collective-permute-start.5 = (bf16[3,64,640]{2,1,0:T(8,128)(2,1)S(1)}, bf16[3,64,640]{2,1,0:T(8,128)(2,1)S(1)}, u32[]{:S(2)}, u32[]{:S(2)}) collective-permute-start(bf16[3,64,640]{2,1,0:T(8,128)(2,1)S(1)} %pad_maximum_fusion.rest_0_), channel_id=1, source_target_pairs={{0,16},{16,0},{1,17},{17,1},{2,18},{18,2},{3,19},{19,3},{4,20},{20... | collective-permute-start | bytes 737288 | tf_op jit(solution)/shard_map/ppermute | solution.py:215
  12.9 7.9 %collective-permute-start.6 = (bf16[3,64,640]{2,1,0:T(8,128)(2,1)S(1)}, bf16[3,64,640]{2,1,0:T(8,128)(2,1)S(1)}, u32[]{:S(2)}, u32[]{:S(2)}) collective-permute-start(bf16[3,64,640]{2,1,0:T(8,128)(2,1)S(1)} %pad_maximum_fusion.rest_0_), channel_id=1, source_target_pairs={{0,2},{2,0},{4,6},{6,4},{8,10},{10,8},{12,14},{14,12},{1,3},{3,1},... | collective-permute-start | bytes 737288 | tf_op jit(solution)/shard_map/ppermute | solution.py:184
  14.4 10.6 %collective-permute-start.4 = (bf16[3,64,640]{2,1,0:T(8,128)(2,1)S(1)}, bf16[3,64,640]{2,1,0:T(8,128)(2,1)S(1)}, u32[]{:S(2)}, u32[]{:S(2)}) collective-permute-start(bf16[3,64,640]{2,1,0:T(8,128)(2,1)S(1)} %pad_maximum_fusion.rest_0_), channel_id=1, source_target_pairs={{0,1},{1,0},{2,3},{3,2},{4,5},{5,4},{6,7},{7,6},{8,9},{9,8},{10,11... | collective-permute-start | bytes 737288 | tf_op jit(solution)/shard_map/ppermute | solution.py:222
  14.4 4.9 %collective-permute-start.7 = (bf16[64,640]{1,0:T(8,128)(2,1)S(1)}, bf16[64,640]{1,0:T(8,128)(2,1)S(1)}, u32[]{:S(2)}, u32[]{:S(2)}) collective-permute-start(bf16[64,640]{1,0:T(8,128)(2,1)S(1)} %collective-permute-done.3), channel_id=1, source_target_pairs={{0,4},{2,6},{4,0},{6,2},{8,12},{10,14},{12,8},{14,10},{1,5},{3,7},... | collective-permute-start | bytes 245768 | tf_op jit(solution)/shard_map/ppermute | solution.py:184
  14.8 27.5 %all-to-all-start = ((bf16[16,224,128]{2,1,0:T(8,128)(2,1)}), bf16[16,224,128]{2,1,0:T(8,128)(2,1)S(1)}, u32[]{:S(2)}, u32[]{:S(2)}) async-start(bf16[16,224,128]{2,1,0:T(8,128)(2,1)} %shard_map.65), calls=%async_computation | async-start | bytes 1835008 | tf_op jit(solution)/shard_map/all_to_all | solution.py:212
  20.8 6.1 %collective-permute-start.10 = (bf16[1,64,640]{2,1,0:T(8,128)(2,1)S(1)}, bf16[1,64,640]{2,1,0:T(8,128)(2,1)S(1)}, u32[]{:S(2)}, u32[]{:S(2)}) collective-permute-start(bf16[1,64,640]{2,1,0:T(8,128)(2,1)S(1)} %bitcast.13), channel_id=1, source_target_pairs={{0,2},{2,0},{4,6},{6,4},{8,10},{10,8},{12,14},{14,12},{1,3},{3,1},... | collective-permute-start | bytes 245768 | tf_op jit(solution)/shard_map/ppermute | solution.py:184
  22.8 6.7 %collective-permute-start.17 = (bf16[1,64,640]{2,1,0:T(8,128)(2,1)S(1)}, bf16[1,64,640]{2,1,0:T(8,128)(2,1)S(1)}, u32[]{:S(2)}, u32[]{:S(2)}) collective-permute-start(bf16[1,64,640]{2,1,0:T(8,128)(2,1)S(1)} %slice.7), channel_id=1, source_target_pairs={{0,16},{16,0},{1,17},{17,1},{2,18},{18,2},{3,19},{19,3},{4,20},{20... | collective-permute-start | bytes 245768 | tf_op jit(solution)/shard_map/ppermute | solution.py:220
  24.2 8.6 %collective-permute-start.13 = (bf16[1,64,640]{2,1,0:T(8,128)(2,1)S(1)}, bf16[1,64,640]{2,1,0:T(8,128)(2,1)S(1)}, u32[]{:S(2)}, u32[]{:S(2)}) collective-permute-start(bf16[1,64,640]{2,1,0:T(8,128)(2,1)S(1)} %bitcast.14), channel_id=1, source_target_pairs={{0,16},{16,0},{1,17},{17,1},{2,18},{18,2},{3,19},{19,3},{4,20},{20... | collective-permute-start | bytes 245768 | tf_op jit(solution)/shard_map/ppermute | solution.py:218
  24.9 10.1 %collective-permute-start.15 = (bf16[2,64,640]{2,1,0:T(8,128)(2,1)S(1)}, bf16[2,64,640]{2,1,0:T(8,128)(2,1)S(1)}, u32[]{:S(2)}, u32[]{:S(2)}) collective-permute-start(bf16[2,64,640]{2,1,0:T(8,128)(2,1)S(1)} %slice.6), channel_id=1, source_target_pairs={{0,2},{2,0},{4,6},{6,4},{8,10},{10,8},{12,14},{14,12},{1,3},{3,1},... | collective-permute-start | bytes 491528 | tf_op jit(solution)/shard_map/ppermute | solution.py:184
  25.0 11.2 %copy-start.2 = (bf16[3,64,640]{2,1,0:T(8,128)(2,1)}, bf16[3,64,640]{2,1,0:T(8,128)(2,1)S(1)}, u32[]{:S(2)}) copy-start(bf16[3,64,640]{2,1,0:T(8,128)(2,1)S(1)} %collective-permute-done.4.rest_0_) | copy-start | bytes 737284
  25.0 7.8 %collective-permute-start.8 = (bf16[1,64,640]{2,1,0:T(8,128)(2,1)S(1)}, bf16[1,64,640]{2,1,0:T(8,128)(2,1)S(1)}, u32[]{:S(2)}, u32[]{:S(2)}) collective-permute-start(bf16[1,64,640]{2,1,0:T(8,128)(2,1)S(1)} %bitcast.15), channel_id=1, source_target_pairs={{0,1},{1,0},{2,3},{3,2},{4,5},{5,4},{6,7},{7,6},{8,9},{9,8},{10,11... | collective-permute-start | bytes 245768 | tf_op jit(solution)/shard_map/ppermute | solution.py:222
  26.9 7.5 %collective-permute-start.19 = (bf16[1,64,640]{2,1,0:T(8,128)(2,1)S(1)}, bf16[1,64,640]{2,1,0:T(8,128)(2,1)S(1)}, u32[]{:S(2)}, u32[]{:S(2)}) collective-permute-start(bf16[1,64,640]{2,1,0:T(8,128)(2,1)S(1)} %collective-permute-done.10.rest_3_), channel_id=1, source_target_pairs={{0,16},{16,0},{1,17},{17,1},{2,18},{18,2},{3,19},{19,3},{4,20},{20... | collective-permute-start | bytes 245768 | tf_op jit(solution)/shard_map/ppermute | solution.py:220
  29.5 4.9 %collective-permute-start.18 = (bf16[1,64,640]{2,1,0:T(8,128)(2,1)S(1)}, bf16[1,64,640]{2,1,0:T(8,128)(2,1)S(1)}, u32[]{:S(2)}, u32[]{:S(2)}) collective-permute-start(bf16[1,64,640]{2,1,0:T(8,128)(2,1)S(1)} %collective-permute-done.17.rest_7_), channel_id=1, source_target_pairs={{0,1},{1,0},{2,3},{3,2},{4,5},{5,4},{6,7},{7,6},{8,9},{9,8},{10,11... | collective-permute-start | bytes 245768 | tf_op jit(solution)/shard_map/ppermute | solution.py:222
  32.8 2.1 %collective-permute-start.11 = (bf16[1,64,640]{2,1,0:T(8,128)(2,1)S(1)}, bf16[1,64,640]{2,1,0:T(8,128)(2,1)S(1)}, u32[]{:S(2)}, u32[]{:S(2)}) collective-permute-start(bf16[1,64,640]{2,1,0:T(8,128)(2,1)S(1)} %collective-permute-done.10.rest_3_), channel_id=1, source_target_pairs={{0,1},{1,0},{2,3},{3,2},{4,5},{5,4},{6,7},{7,6},{8,9},{9,8},{10,11... | collective-permute-start | bytes 245768 | tf_op jit(solution)/shard_map/ppermute | solution.py:222
  32.8 4.3 %collective-permute-start.12 = (bf16[3,64,640]{2,1,0:T(8,128)(2,1)S(1)}, bf16[3,64,640]{2,1,0:T(8,128)(2,1)S(1)}, u32[]{:S(2)}, u32[]{:S(2)}) collective-permute-start(bf16[3,64,640]{2,1,0:T(8,128)(2,1)S(1)} %collective-permute-done.5.rest_4_), channel_id=1, source_target_pairs={{0,1},{1,0},{2,3},{3,2},{4,5},{5,4},{6,7},{7,6},{8,9},{9,8},{10,11... | collective-permute-start | bytes 737288 | tf_op jit(solution)/shard_map/ppermute | solution.py:222
  34.4 2.7 %collective-permute-start.9 = (bf16[3,64,640]{2,1,0:T(8,128)(2,1)S(1)}, bf16[3,64,640]{2,1,0:T(8,128)(2,1)S(1)}, u32[]{:S(2)}, u32[]{:S(2)}) collective-permute-start(bf16[3,64,640]{2,1,0:T(8,128)(2,1)S(1)} %collective-permute-done.6.rest_2_), channel_id=1, source_target_pairs={{0,1},{1,0},{2,3},{3,2},{4,5},{5,4},{6,7},{7,6},{8,9},{9,8},{10,11... | collective-permute-start | bytes 737288 | tf_op jit(solution)/shard_map/ppermute | solution.py:222
  34.4 2.7 %collective-permute-start.14 = (bf16[1,64,640]{2,1,0:T(8,128)(2,1)S(1)}, bf16[1,64,640]{2,1,0:T(8,128)(2,1)S(1)}, u32[]{:S(2)}, u32[]{:S(2)}) collective-permute-start(bf16[1,64,640]{2,1,0:T(8,128)(2,1)S(1)} %collective-permute-done.13.rest_5_), channel_id=1, source_target_pairs={{0,1},{1,0},{2,3},{3,2},{4,5},{5,4},{6,7},{7,6},{8,9},{9,8},{10,11... | collective-permute-start | bytes 245768 | tf_op jit(solution)/shard_map/ppermute | solution.py:222
  34.9 2.1 %collective-permute-start.20 = (bf16[1,64,640]{2,1,0:T(8,128)(2,1)S(1)}, bf16[1,64,640]{2,1,0:T(8,128)(2,1)S(1)}, u32[]{:S(2)}, u32[]{:S(2)}) collective-permute-start(bf16[1,64,640]{2,1,0:T(8,128)(2,1)S(1)} %collective-permute-done.19.rest_8_), channel_id=1, source_target_pairs={{0,1},{1,0},{2,3},{3,2},{4,5},{5,4},{6,7},{7,6},{8,9},{9,8},{10,11... | collective-permute-start | bytes 245768 | tf_op jit(solution)/shard_map/ppermute | solution.py:222
  35.0 2.1 %collective-permute-start.16 = (bf16[2,64,640]{2,1,0:T(8,128)(2,1)S(1)}, bf16[2,64,640]{2,1,0:T(8,128)(2,1)S(1)}, u32[]{:S(2)}, u32[]{:S(2)}) collective-permute-start(bf16[2,64,640]{2,1,0:T(8,128)(2,1)S(1)} %collective-permute-done.15.rest_6_), channel_id=1, source_target_pairs={{0,1},{1,0},{2,3},{3,2},{4,5},{5,4},{6,7},{7,6},{8,9},{9,8},{10,11... | collective-permute-start | bytes 491528 | tf_op jit(solution)/shard_map/ppermute | solution.py:222
  36.2 0.8 %copy-start.5 = (bf16[640,384]{1,0:T(8,128)(2,1)}, bf16[640,384]{1,0:T(8,128)(2,1)S(1)}, u32[]{:S(2)}) copy-start(bf16[640,384]{1,0:T(8,128)(2,1)S(1)} %get-tuple-element.40.late_ref) | copy-start | bytes 1474564
  37.1 0.9 %copy-start.3 = (bf16[3,64,640]{2,1,0:T(8,128)(2,1)S(1)}, bf16[3,64,640]{2,1,0:T(8,128)(2,1)}, u32[]{:S(2)}) copy-start(bf16[3,64,640]{2,1,0:T(8,128)(2,1)} %copy-done.2) | copy-start | bytes 737284
  38.8 4.1 %copy-start.4 = (f32[2048]{0:T(1024)S(1)}, f32[2048]{0:T(1024)}, u32[]{:S(2)}) copy-start(f32[2048]{0:T(1024)} %param.11) | copy-start | bytes 24580
  42.3 1.0 %copy-start.6 = (bf16[640,384]{1,0:T(8,128)(2,1)S(1)}, bf16[640,384]{1,0:T(8,128)(2,1)}, u32[]{:S(2)}) copy-start(bf16[640,384]{1,0:T(8,128)(2,1)} %copy-done.5) | copy-start | bytes 1474564

commit v10 on v9

--- a/solution.py
+++ b/solution.py
@@ -125,10 +125,11 @@
             weighted.append(jnp.where(inside, jnp.exp(scores[i * lat : (i + 1) * lat]), 0.0))
         total = sum(jnp.sum(w, 0, keepdims=True) for w in weighted)
         scale = 1.0 / jnp.where(total > 0.0, total, 1.0)
-        probs = jnp.concatenate([(w * scale).astype(jnp.bfloat16) for w in weighted], 0)
+        probs = jnp.concatenate([w.astype(jnp.bfloat16) for w in weighted], 0)
         attended = lax.dot_general(
             values, probs, (((0,), (0,)), ((), ())), preferred_element_type=jnp.float32
-        ).T
+        )
+        attended = (attended * scale).T
         gated = (gate * attended).astype(jnp.bfloat16).reshape(ctx_count, 2, part, DH)
         for c in range(ctx_count):
             for d in range(2):

time: 59 us -> 58.9 us (level)
  no operation moved by 1% of the time
where the time goes in v10:
time: 58.9 us; the launch traced here: 58.6 us
  starting transfers between devices  20.8 us (35%)
  waiting for transfers between devices  13.1 us (22%)
  blocking collectives  12.6 us (21%)
  Pallas kernels  5.91 us (10%)
  local copies, waits for them, and re-layouts  5.24 us (9%)
  other arithmetic  0.74 us (1%)
    all_to_all x1, blocking collectives, by_heads(): back = lax.all_to_all(gated, every, split_axis=0, concat_axis=0, tiled=True)  12.6 us
    ppermute x6, starting transfers between devices, across(): return lax.ppermute(x, 'ctx', [(i, i ^ turn) for i in range(ctx_count)])  9.64 us
    all_to_all x1, starting transfers between devices, by_heads(): lax.all_to_all(outgoing, ('groups', 'ctx'), split_axis=0, concat_axis=0,...  3.91 us
    all_to_all x1, waiting for transfers between devices, by_heads(): lax.all_to_all(outgoing, ('groups', 'ctx'), split_axis=0, concat_axis=0,...  3.49 us
    ppermute x1, waiting for transfers between devices, by_heads(): last_y = lax.ppermute(last, 'groups', swap)  3.27 us
    unnamed x14, local copies, waits for them, and re-layouts  3.09 us
    ppermute x6, waiting for transfers between devices, across(): return lax.ppermute(x, 'ctx', [(i, i ^ turn) for i in range(ctx_count)])  2.49 us
    pallas_call x1, Pallas kernels, by_heads(): pl.pallas_call(attend_kernel, out_shape=jax.ShapeDtypeStruct((ctx_count *...  1.86 us
  transfers between devices with their start and end apart: 22, of which 9 were waited for; matrix products, arithmetic and copies ran while one was open for 3% of the time, Pallas kernels for 5%

profile of v10, /device:TPU:0, one launch (start us, length us, event | category | flops | bytes accessed | tf_op | source)
XLA Modules:
  0.0 58.6 jit_solution(4913692081821875007)
XLA Ops:
  0.0 1.0 %dynamic-slice_bitcast_fusion = bf16[64,640]{1,0:T(8,128)(2,1)S(1)} fusion(bf16[1,64,1280]{2,1,0:T(8,128)(2,1)} %param.7, s32[]{:T(128)S(6)} %select_n.6), kind=kLoop, calls=%fused_computation.1 | loop fusion | bytes 163844 | tf_op jit(solution)/shard_map/dynamic_slice | solution.py:187
  1.0 3.0 %collective-permute-start.2 = (bf16[64,640]{1,0:T(8,128)(2,1)S(1)}, bf16[64,640]{1,0:T(8,128)(2,1)S(1)}, u32[]{:S(2)}, u32[]{:S(2)}) collective-permute-start(bf16[64,640]{1,0:T(8,128)(2,1)S(1)} %dynamic-slice_bitcast_fusion), channel_id=1, source_target_pairs={{0,4},{2,6},{4,0},{6,2},{8,12},{10,14},{12,8},{14,10},{1,5},{3,7},... | collective-permute-start | bytes 245768 | tf_op jit(solution)/shard_map/ppermute | solution.py:185
  4.0 2.6 %collective-permute-start.3 = (bf16[64,640]{1,0:T(8,128)(2,1)S(1)}, bf16[64,640]{1,0:T(8,128)(2,1)S(1)}, u32[]{:S(2)}, u32[]{:S(2)}) collective-permute-start(bf16[64,640]{1,0:T(8,128)(2,1)S(1)} %dynamic-slice_bitcast_fusion), channel_id=1, source_target_pairs={{0,8},{2,10},{4,12},{6,14},{8,0},{10,2},{12,4},{14,6},{1,9},{3,11}... | collective-permute-start | bytes 245768 | tf_op jit(solution)/shard_map/ppermute | solution.py:185
  6.6 0.7 %pad_add_fusion.meta_ref = s32[3,5]{1,0:T(4,128)S(1)} fusion(s32[1,5]{1,0:T(1,128)} %bitcast.23, s32[2,5]{1,0:T(2,128)} %bitcast.22), kind=kLoop, calls=%fused_computation.2 | loop fusion | flops 15 | bytes 120 | tf_op jit(solution)/shard_map/concatenate | solution.py:189
  7.3 1.5 %collective-permute-start.1 = (s32[3,5]{1,0:T(4,128)S(1)}, s32[3,5]{1,0:T(4,128)S(1)}, u32[]{:S(2)}, u32[]{:S(2)}) collective-permute-start(s32[3,5]{1,0:T(4,128)S(1)} %pad_add_fusion.meta_ref), channel_id=1, source_target_pairs={{0,16},{16,0},{1,17},{17,1},{2,18},{18,2},{3,19},{19,3},{4,20},{20... | collective-permute-start | bytes 188 | tf_op jit(solution)/shard_map/ppermute | solution.py:200
  8.8 0.9 %copy-done.1 = bf16[32,4096]{1,0:T(8,128)(2,1)S(1)} copy-done((bf16[32,4096]{1,0:T(8,128)(2,1)S(1)}, bf16[32,4096]{1,0:T(8,128)(2,1)}, u32[]{:S(2)}) %copy-start.1) | copy-done | bytes 262168
  9.8 0.1 shard_map.64
  9.9 0.1 collective-permute-start
  10.0 0.5 constant_dynamic-slice_fusion
  10.4 0.4 reshape.13
  10.8 0.3 copy.8
  11.1 0.2 collective-permute-done.rest_1_
  11.3 1.0 %shard_map.65 = bf16[16,224,128]{2,1,0:T(8,128)(2,1)} custom-call(bf16[16,160,128]{2,1,0:T(8,128)(2,1)S(1)} %bitcast.12, bf16[16,32,128]{2,1,0:T(8,128)(2,1)S(1)} %get-tuple-element.25.rest_0_, bf16[16,32,128]{2,1,0:T(8,128)(2,1)S(1)} %collective-permute-done.rest_1_), custom_call_target="tpu_custom_call" | custom-call | tf_op jit(solution)/shard_map/pallas_call | solution.py:205
  12.3 0.0 collective-permute-done.1.meta_y_ref
  12.3 0.0 collective-permute-done.2
  12.3 0.0 collective-permute-done.3
  12.3 0.6 collective-permute-start.5
  12.9 1.5 %collective-permute-start.6 = (bf16[3,64,640]{2,1,0:T(8,128)(2,1)S(1)}, bf16[3,64,640]{2,1,0:T(8,128)(2,1)S(1)}, u32[]{:S(2)}, u32[]{:S(2)}) collective-permute-start(bf16[3,64,640]{2,1,0:T(8,128)(2,1)S(1)} %pad_maximum_fusion.rest_0_), channel_id=1, source_target_pairs={{0,2},{2,0},{4,6},{6,4},{8,10},{10,8},{12,14},{14,12},{1,3},{3,1},... | collective-permute-start | bytes 737288 | tf_op jit(solution)/shard_map/ppermute | solution.py:185
  14.4 0.0 collective-permute-start.4
  14.4 0.4 collective-permute-start.7
  14.8 3.9 %all-to-all-start = ((bf16[16,224,128]{2,1,0:T(8,128)(2,1)}), bf16[16,224,128]{2,1,0:T(8,128)(2,1)S(1)}, u32[]{:S(2)}, u32[]{:S(2)}) async-start(bf16[16,224,128]{2,1,0:T(8,128)(2,1)} %shard_map.65), calls=%async_computation | async-start | bytes 1835008 | tf_op jit(solution)/shard_map/all_to_all | solution.py:213
  18.8 0.5 collective-permute-done.7
  19.3 1.3 %collective-permute-done.5.rest_4_ = bf16[3,64,640]{2,1,0:T(8,128)(2,1)S(1)} collective-permute-done((bf16[3,64,640]{2,1,0:T(8,128)(2,1)S(1)}, bf16[3,64,640]{2,1,0:T(8,128)(2,1)S(1)}, u32[]{:S(2)}, u32[]{:S(2)}) %collective-permute-start.5) | collective-permute-done | bytes 245792 | tf_op jit(solution)/shard_map/ppermute | solution.py:216
  20.6 0.2 collective-permute-done.6.rest_2_
  20.8 2.0 %collective-permute-start.10 = (bf16[1,64,640]{2,1,0:T(8,128)(2,1)S(1)}, bf16[1,64,640]{2,1,0:T(8,128)(2,1)S(1)}, u32[]{:S(2)}, u32[]{:S(2)}) collective-permute-start(bf16[1,64,640]{2,1,0:T(8,128)(2,1)S(1)} %bitcast.13), channel_id=1, source_target_pairs={{0,2},{2,0},{4,6},{6,4},{8,10},{10,8},{12,14},{14,12},{1,3},{3,1},... | collective-permute-start | bytes 245768 | tf_op jit(solution)/shard_map/ppermute | solution.py:185
  22.8 1.4 %collective-permute-start.17 = (bf16[1,64,640]{2,1,0:T(8,128)(2,1)S(1)}, bf16[1,64,640]{2,1,0:T(8,128)(2,1)S(1)}, u32[]{:S(2)}, u32[]{:S(2)}) collective-permute-start(bf16[1,64,640]{2,1,0:T(8,128)(2,1)S(1)} %slice.7), channel_id=1, source_target_pairs={{0,16},{16,0},{1,17},{17,1},{2,18},{18,2},{3,19},{19,3},{4,20},{20... | collective-permute-start | bytes 245768 | tf_op jit(solution)/shard_map/ppermute | solution.py:221
  24.2 0.7 %collective-permute-start.13 = (bf16[1,64,640]{2,1,0:T(8,128)(2,1)S(1)}, bf16[1,64,640]{2,1,0:T(8,128)(2,1)S(1)}, u32[]{:S(2)}, u32[]{:S(2)}) collective-permute-start(bf16[1,64,640]{2,1,0:T(8,128)(2,1)S(1)} %bitcast.14), channel_id=1, source_target_pairs={{0,16},{16,0},{1,17},{17,1},{2,18},{18,2},{3,19},{19,3},{4,20},{20... | collective-permute-start | bytes 245768 | tf_op jit(solution)/shard_map/ppermute | solution.py:219
  24.9 0.1 collective-permute-start.15
  25.0 0.0 collective-permute-done.4.rest_0_
  25.0 0.1 collective-permute-start.8
  25.1 1.8 %collective-permute-done.10.rest_3_ = bf16[1,64,640]{2,1,0:T(8,128)(2,1)S(1)} collective-permute-done((bf16[1,64,640]{2,1,0:T(8,128)(2,1)S(1)}, bf16[1,64,640]{2,1,0:T(8,128)(2,1)S(1)}, u32[]{:S(2)}, u32[]{:S(2)}) %collective-permute-start.10) | collective-permute-done | bytes 81952 | tf_op jit(solution)/shard_map/ppermute | solution.py:185
  26.9 1.4 %collective-permute-start.19 = (bf16[1,64,640]{2,1,0:T(8,128)(2,1)S(1)}, bf16[1,64,640]{2,1,0:T(8,128)(2,1)S(1)}, u32[]{:S(2)}, u32[]{:S(2)}) collective-permute-start(bf16[1,64,640]{2,1,0:T(8,128)(2,1)S(1)} %collective-permute-done.10.rest_3_), channel_id=1, source_target_pairs={{0,16},{16,0},{1,17},{17,1},{2,18},{18,2},{3,19},{19,3},{4,20},{20... | collective-permute-start | bytes 245768 | tf_op jit(solution)/shard_map/ppermute | solution.py:221
  28.3 1.2 %collective-permute-done.17.rest_7_ = bf16[1,64,640]{2,1,0:T(8,128)(2,1)S(1)} collective-permute-done((bf16[1,64,640]{2,1,0:T(8,128)(2,1)S(1)}, bf16[1,64,640]{2,1,0:T(8,128)(2,1)S(1)}, u32[]{:S(2)}, u32[]{:S(2)}) %collective-permute-start.17) | collective-permute-done | bytes 81952 | tf_op jit(solution)/shard_map/ppermute | solution.py:221
  29.5 0.0 collective-permute-start.18
  29.5 3.3 %collective-permute-done.13.rest_5_ = bf16[1,64,640]{2,1,0:T(8,128)(2,1)S(1)} collective-permute-done((bf16[1,64,640]{2,1,0:T(8,128)(2,1)S(1)}, bf16[1,64,640]{2,1,0:T(8,128)(2,1)S(1)}, u32[]{:S(2)}, u32[]{:S(2)}) %collective-permute-start.13) | collective-permute-done | bytes 81952 | tf_op jit(solution)/shard_map/ppermute | solution.py:219
  32.8 0.0 collective-permute-start.11
  32.8 0.0 collective-permute-done.8.rest_1_
  32.8 0.5 collective-permute-start.12
  33.3 1.1 %collective-permute-done.19.rest_8_ = bf16[1,64,640]{2,1,0:T(8,128)(2,1)S(1)} collective-permute-done((bf16[1,64,640]{2,1,0:T(8,128)(2,1)S(1)}, bf16[1,64,640]{2,1,0:T(8,128)(2,1)S(1)}, u32[]{:S(2)}, u32[]{:S(2)}) %collective-permute-start.19) | collective-permute-done | bytes 81952 | tf_op jit(solution)/shard_map/ppermute | solution.py:221
  34.4 0.0 collective-permute-start.9
  34.4 0.0 collective-permute-done.18.rest_7_
  34.4 0.5 collective-permute-start.14
  34.9 0.0 collective-permute-done.11.rest_3_
  34.9 0.1 collective-permute-start.20
  35.0 0.0 collective-permute-done.15.rest_6_
  35.0 0.4 collective-permute-start.16
  35.4 0.8 %shard_map.66 = (bf16[640,256]{1,0:T(8,128)(2,1)S(1)}, bf16[640,384]{1,0:T(8,128)(2,1)S(1)}) custom-call(s32[3,5]{1,0:T(4,128)S(1)} %pad_add_fusion.meta_ref, s32[3,5]{1,0:T(4,128)S(1)} %collective-permute-done.1.meta_y_ref, bf16[3,64,640]{2,1,0:T(8,128)(2,1)S(1)} %pad_maximum_fusion.rest_0_, bf16[1,64,640]{2,1,0:T(8,128)(2,1)S(1)} %bitcast.16, ...), custom_call_target="tpu_custom_call" | custom-call | flops 8049999872 | bytes 2097152 | tf_op jit(solution)/shard_map/pallas_call | solution.py:227
  36.2 0.0 copy-start.5
  36.3 0.8 %copy-done.5 = bf16[640,384]{1,0:T(8,128)(2,1)} copy-done((bf16[640,384]{1,0:T(8,128)(2,1)}, bf16[640,384]{1,0:T(8,128)(2,1)S(1)}, u32[]{:S(2)}) %copy-start.5) | copy-done | bytes 491544
  37.0 0.0 collective-permute-done.14.rest_5_
  37.0 0.0 collective-permute-done.20.rest_8_
  37.0 0.0 collective-permute-done.12.rest_4_
  37.0 0.0 collective-permute-done.9.rest_2_
  37.1 0.0 collective-permute-done.16.rest_6_
  37.1 0.0 copy-start.3
  37.1 0.9 %copy-done.3 = bf16[3,64,640]{2,1,0:T(8,128)(2,1)S(1)} copy-done((bf16[3,64,640]{2,1,0:T(8,128)(2,1)S(1)}, bf16[3,64,640]{2,1,0:T(8,128)(2,1)}, u32[]{:S(2)}) %copy-start.3) | copy-done | bytes 245784
  38.0 0.8 %shard_map.67.kept_ref = bf16[640,896]{1,0:T(8,128)(2,1)S(1)} custom-call(s32[3,5]{1,0:T(4,128)S(1)} %pad_add_fusion.meta_ref, s32[3,5]{1,0:T(4,128)S(1)} %collective-permute-done.1.meta_y_ref, bf16[3,64,640]{2,1,0:T(8,128)(2,1)S(1)} %copy-done.3, bf16[1,64,640]{2,1,0:T(8,128)(2,1)S(1)} %collective-permute-done.8.rest_1_, ...), custom_call_target="tpu_custom_call" | custom-call | flops 8049999872 | bytes 2097152 | tf_op jit(solution)/shard_map/pallas_call | solution.py:238
  38.8 0.0 copy-start.4
  38.8 3.5 %all-to-all-done.got_ref = bf16[16,224,128]{2,1,0:T(8,128)(2,1)S(1)} async-done(((bf16[16,224,128]{2,1,0:T(8,128)(2,1)}), bf16[16,224,128]{2,1,0:T(8,128)(2,1)S(1)}, u32[]{:S(2)}, u32[]{:S(2)}) %all-to-all-start) | async-done | bytes 917536 | tf_op jit(solution)/shard_map/all_to_all | solution.py:213
  42.3 0.6 %shard_map.68 = (bf16[2,8,2,32,128]{4,3,2,1,0:T(8,128)(2,1)S(1)}, bf16[384,256]{1,0:T(8,128)(2,1)S(1)}, f32[640,256]{1,0:T(8,128)S(1)}) custom-call(bf16[16,224,128]{2,1,0:T(8,128)(2,1)S(1)} %all-to-all-done.got_ref, bf16[640,896]{1,0:T(8,128)(2,1)S(1)} %shard_map.67.kept_ref), custom_call_target="tpu_custom_call" | custom-call | flops 200000000 | bytes 16000000 | tf_op jit(solution)/shard_map/pallas_call | solution.py:246
  42.9 0.4 copy-done.6
  43.4 1.9 %shard_map.69 = bf16[32,32,128]{2,1,0:T(8,128)(2,1)S(1)} custom-call(s32[3,5]{1,0:T(4,128)S(1)} %pad_add_fusion.meta_ref, s32[3,5]{1,0:T(4,128)S(1)} %collective-permute-done.1.meta_y_ref, f32[16,128]{1,0:T(8,128)S(1)} %bitcast.17, bf16[2,8,2,32,128]{4,3,2,1,0:T(8,128)(2,1)S(1)} %get-tuple-element.37.query_ref, ...), custom_call_target="tpu_custom_call" | custom-call | flops 20000000000 | bytes 4194304 | tf_op jit(solution)/shard_map/pallas_call | solution.py:259
  45.2 12.6 %all_to_all.10.back_ref = bf16[32,32,128]{2,1,0:T(8,128)(2,1)S(1)} all-to-all(bf16[32,32,128]{2,1,0:T(8,128)(2,1)S(1)} %shard_map.69), channel_id=1, replica_groups=mesh['groups'=2,'ctx'=8,'head'=2] {'groups','ctx','head'}, dimensions={0} | all-to-all | bytes 524288 | tf_op jit(solution)/shard_map/all_to_all | solution.py:268
  57.8 0.8 %shard_map.70 = bf16[32,4096]{1,0:T(8,128)(2,1)} custom-call(bf16[32,32,128]{2,1,0:T(8,128)(2,1)S(1)} %all_to_all.10.back_ref), custom_call_target="tpu_custom_call" | custom-call | tf_op jit(solution)/shard_map/pallas_call | solution.py:269
  (10 shorter events, 0.1 us)
Async XLA Ops:
  0.0 9.9 %copy-start = (bf16[160,2,2048]{2,1,0:T(2,128)(2,1)S(1)}, bf16[160,2,2048]{2,1,0:T(2,128)(2,1)}, u32[]{:S(2)}) copy-start(bf16[160,2,2048]{2,1,0:T(2,128)(2,1)} %param.10) | copy-start | bytes 3932164
  1.0 11.3 %collective-permute-start.2 = (bf16[64,640]{1,0:T(8,128)(2,1)S(1)}, bf16[64,640]{1,0:T(8,128)(2,1)S(1)}, u32[]{:S(2)}, u32[]{:S(2)}) collective-permute-start(bf16[64,640]{1,0:T(8,128)(2,1)S(1)} %dynamic-slice_bitcast_fusion), channel_id=1, source_target_pairs={{0,4},{2,6},{4,0},{6,2},{8,12},{10,14},{12,8},{14,10},{1,5},{3,7},... | collective-permute-start | bytes 245768 | tf_op jit(solution)/shard_map/ppermute | solution.py:185
  4.0 8.3 %collective-permute-start.3 = (bf16[64,640]{1,0:T(8,128)(2,1)S(1)}, bf16[64,640]{1,0:T(8,128)(2,1)S(1)}, u32[]{:S(2)}, u32[]{:S(2)}) collective-permute-start(bf16[64,640]{1,0:T(8,128)(2,1)S(1)} %dynamic-slice_bitcast_fusion), channel_id=1, source_target_pairs={{0,8},{2,10},{4,12},{6,14},{8,0},{10,2},{12,4},{14,6},{1,9},{3,11}... | collective-permute-start | bytes 245768 | tf_op jit(solution)/shard_map/ppermute | solution.py:185
  7.3 5.0 %collective-permute-start.1 = (s32[3,5]{1,0:T(4,128)S(1)}, s32[3,5]{1,0:T(4,128)S(1)}, u32[]{:S(2)}, u32[]{:S(2)}) collective-permute-start(s32[3,5]{1,0:T(4,128)S(1)} %pad_add_fusion.meta_ref), channel_id=1, source_target_pairs={{0,16},{16,0},{1,17},{17,1},{2,18},{18,2},{3,19},{19,3},{4,20},{20... | collective-permute-start | bytes 188 | tf_op jit(solution)/shard_map/ppermute | solution.py:200
  8.8 0.9 %copy-start.1 = (bf16[32,4096]{1,0:T(8,128)(2,1)S(1)}, bf16[32,4096]{1,0:T(8,128)(2,1)}, u32[]{:S(2)}) copy-start(bf16[32,4096]{1,0:T(8,128)(2,1)} %query_ref.1) | copy-start | bytes 786436
  9.9 1.4 %collective-permute-start = (bf16[16,32,128]{2,1,0:T(8,128)(2,1)S(1)}, bf16[16,32,128]{2,1,0:T(8,128)(2,1)S(1)}, u32[]{:S(2)}, u32[]{:S(2)}) collective-permute-start(bf16[16,32,128]{2,1,0:T(8,128)(2,1)S(1)} %get-tuple-element.26), channel_id=1, source_target_pairs={{0,1},{1,0},{2,3},{3,2},{4,5},{5,4},{6,7},{7,6},{8,9},{9,8},{10,11... | collective-permute-start | bytes 393224 | tf_op jit(solution)/shard_map/ppermute | solution.py:199
  12.3 8.2 %collective-permute-start.5 = (bf16[3,64,640]{2,1,0:T(8,128)(2,1)S(1)}, bf16[3,64,640]{2,1,0:T(8,128)(2,1)S(1)}, u32[]{:S(2)}, u32[]{:S(2)}) collective-permute-start(bf16[3,64,640]{2,1,0:T(8,128)(2,1)S(1)} %pad_maximum_fusion.rest_0_), channel_id=1, source_target_pairs={{0,16},{16,0},{1,17},{17,1},{2,18},{18,2},{3,19},{19,3},{4,20},{20... | collective-permute-start | bytes 737288 | tf_op jit(solution)/shard_map/ppermute | solution.py:216
  12.9 7.9 %collective-permute-start.6 = (bf16[3,64,640]{2,1,0:T(8,128)(2,1)S(1)}, bf16[3,64,640]{2,1,0:T(8,128)(2,1)S(1)}, u32[]{:S(2)}, u32[]{:S(2)}) collective-permute-start(bf16[3,64,640]{2,1,0:T(8,128)(2,1)S(1)} %pad_maximum_fusion.rest_0_), channel_id=1, source_target_pairs={{0,2},{2,0},{4,6},{6,4},{8,10},{10,8},{12,14},{14,12},{1,3},{3,1},... | collective-permute-start | bytes 737288 | tf_op jit(solution)/shard_map/ppermute | solution.py:185
  14.4 10.6 %collective-permute-start.4 = (bf16[3,64,640]{2,1,0:T(8,128)(2,1)S(1)}, bf16[3,64,640]{2,1,0:T(8,128)(2,1)S(1)}, u32[]{:S(2)}, u32[]{:S(2)}) collective-permute-start(bf16[3,64,640]{2,1,0:T(8,128)(2,1)S(1)} %pad_maximum_fusion.rest_0_), channel_id=1, source_target_pairs={{0,1},{1,0},{2,3},{3,2},{4,5},{5,4},{6,7},{7,6},{8,9},{9,8},{10,11... | collective-permute-start | bytes 737288 | tf_op jit(solution)/shard_map/ppermute | solution.py:223
  14.4 4.9 %collective-permute-start.7 = (bf16[64,640]{1,0:T(8,128)(2,1)S(1)}, bf16[64,640]{1,0:T(8,128)(2,1)S(1)}, u32[]{:S(2)}, u32[]{:S(2)}) collective-permute-start(bf16[64,640]{1,0:T(8,128)(2,1)S(1)} %collective-permute-done.3), channel_id=1, source_target_pairs={{0,4},{2,6},{4,0},{6,2},{8,12},{10,14},{12,8},{14,10},{1,5},{3,7},... | collective-permute-start | bytes 245768 | tf_op jit(solution)/shard_map/ppermute | solution.py:185
  14.8 27.5 %all-to-all-start = ((bf16[16,224,128]{2,1,0:T(8,128)(2,1)}), bf16[16,224,128]{2,1,0:T(8,128)(2,1)S(1)}, u32[]{:S(2)}, u32[]{:S(2)}) async-start(bf16[16,224,128]{2,1,0:T(8,128)(2,1)} %shard_map.65), calls=%async_computation | async-start | bytes 1835008 | tf_op jit(solution)/shard_map/all_to_all | solution.py:213
  20.8 6.1 %collective-permute-start.10 = (bf16[1,64,640]{2,1,0:T(8,128)(2,1)S(1)}, bf16[1,64,640]{2,1,0:T(8,128)(2,1)S(1)}, u32[]{:S(2)}, u32[]{:S(2)}) collective-permute-start(bf16[1,64,640]{2,1,0:T(8,128)(2,1)S(1)} %bitcast.13), channel_id=1, source_target_pairs={{0,2},{2,0},{4,6},{6,4},{8,10},{10,8},{12,14},{14,12},{1,3},{3,1},... | collective-permute-start | bytes 245768 | tf_op jit(solution)/shard_map/ppermute | solution.py:185
  22.8 6.7 %collective-permute-start.17 = (bf16[1,64,640]{2,1,0:T(8,128)(2,1)S(1)}, bf16[1,64,640]{2,1,0:T(8,128)(2,1)S(1)}, u32[]{:S(2)}, u32[]{:S(2)}) collective-permute-start(bf16[1,64,640]{2,1,0:T(8,128)(2,1)S(1)} %slice.7), channel_id=1, source_target_pairs={{0,16},{16,0},{1,17},{17,1},{2,18},{18,2},{3,19},{19,3},{4,20},{20... | collective-permute-start | bytes 245768 | tf_op jit(solution)/shard_map/ppermute | solution.py:221
  24.2 8.6 %collective-permute-start.13 = (bf16[1,64,640]{2,1,0:T(8,128)(2,1)S(1)}, bf16[1,64,640]{2,1,0:T(8,128)(2,1)S(1)}, u32[]{:S(2)}, u32[]{:S(2)}) collective-permute-start(bf16[1,64,640]{2,1,0:T(8,128)(2,1)S(1)} %bitcast.14), channel_id=1, source_target_pairs={{0,16},{16,0},{1,17},{17,1},{2,18},{18,2},{3,19},{19,3},{4,20},{20... | collective-permute-start | bytes 245768 | tf_op jit(solution)/shard_map/ppermute | solution.py:219
  24.9 10.1 %collective-permute-start.15 = (bf16[2,64,640]{2,1,0:T(8,128)(2,1)S(1)}, bf16[2,64,640]{2,1,0:T(8,128)(2,1)S(1)}, u32[]{:S(2)}, u32[]{:S(2)}) collective-permute-start(bf16[2,64,640]{2,1,0:T(8,128)(2,1)S(1)} %slice.6), channel_id=1, source_target_pairs={{0,2},{2,0},{4,6},{6,4},{8,10},{10,8},{12,14},{14,12},{1,3},{3,1},... | collective-permute-start | bytes 491528 | tf_op jit(solution)/shard_map/ppermute | solution.py:185
  25.0 11.2 %copy-start.2 = (bf16[3,64,640]{2,1,0:T(8,128)(2,1)}, bf16[3,64,640]{2,1,0:T(8,128)(2,1)S(1)}, u32[]{:S(2)}) copy-start(bf16[3,64,640]{2,1,0:T(8,128)(2,1)S(1)} %collective-permute-done.4.rest_0_) | copy-start | bytes 737284
  25.0 7.8 %collective-permute-start.8 = (bf16[1,64,640]{2,1,0:T(8,128)(2,1)S(1)}, bf16[1,64,640]{2,1,0:T(8,128)(2,1)S(1)}, u32[]{:S(2)}, u32[]{:S(2)}) collective-permute-start(bf16[1,64,640]{2,1,0:T(8,128)(2,1)S(1)} %bitcast.15), channel_id=1, source_target_pairs={{0,1},{1,0},{2,3},{3,2},{4,5},{5,4},{6,7},{7,6},{8,9},{9,8},{10,11... | collective-permute-start | bytes 245768 | tf_op jit(solution)/shard_map/ppermute | solution.py:223
  26.9 7.5 %collective-permute-start.19 = (bf16[1,64,640]{2,1,0:T(8,128)(2,1)S(1)}, bf16[1,64,640]{2,1,0:T(8,128)(2,1)S(1)}, u32[]{:S(2)}, u32[]{:S(2)}) collective-permute-start(bf16[1,64,640]{2,1,0:T(8,128)(2,1)S(1)} %collective-permute-done.10.rest_3_), channel_id=1, source_target_pairs={{0,16},{16,0},{1,17},{17,1},{2,18},{18,2},{3,19},{19,3},{4,20},{20... | collective-permute-start | bytes 245768 | tf_op jit(solution)/shard_map/ppermute | solution.py:221
  29.5 4.9 %collective-permute-start.18 = (bf16[1,64,640]{2,1,0:T(8,128)(2,1)S(1)}, bf16[1,64,640]{2,1,0:T(8,128)(2,1)S(1)}, u32[]{:S(2)}, u32[]{:S(2)}) collective-permute-start(bf16[1,64,640]{2,1,0:T(8,128)(2,1)S(1)} %collective-permute-done.17.rest_7_), channel_id=1, source_target_pairs={{0,1},{1,0},{2,3},{3,2},{4,5},{5,4},{6,7},{7,6},{8,9},{9,8},{10,11... | collective-permute-start | bytes 245768 | tf_op jit(solution)/shard_map/ppermute | solution.py:223
  32.8 2.1 %collective-permute-start.11 = (bf16[1,64,640]{2,1,0:T(8,128)(2,1)S(1)}, bf16[1,64,640]{2,1,0:T(8,128)(2,1)S(1)}, u32[]{:S(2)}, u32[]{:S(2)}) collective-permute-start(bf16[1,64,640]{2,1,0:T(8,128)(2,1)S(1)} %collective-permute-done.10.rest_3_), channel_id=1, source_target_pairs={{0,1},{1,0},{2,3},{3,2},{4,5},{5,4},{6,7},{7,6},{8,9},{9,8},{10,11... | collective-permute-start | bytes 245768 | tf_op jit(solution)/shard_map/ppermute | solution.py:223
  32.8 4.3 %collective-permute-start.12 = (bf16[3,64,640]{2,1,0:T(8,128)(2,1)S(1)}, bf16[3,64,640]{2,1,0:T(8,128)(2,1)S(1)}, u32[]{:S(2)}, u32[]{:S(2)}) collective-permute-start(bf16[3,64,640]{2,1,0:T(8,128)(2,1)S(1)} %collective-permute-done.5.rest_4_), channel_id=1, source_target_pairs={{0,1},{1,0},{2,3},{3,2},{4,5},{5,4},{6,7},{7,6},{8,9},{9,8},{10,11... | collective-permute-start | bytes 737288 | tf_op jit(solution)/shard_map/ppermute | solution.py:223
  34.4 2.7 %collective-permute-start.9 = (bf16[3,64,640]{2,1,0:T(8,128)(2,1)S(1)}, bf16[3,64,640]{2,1,0:T(8,128)(2,1)S(1)}, u32[]{:S(2)}, u32[]{:S(2)}) collective-permute-start(bf16[3,64,640]{2,1,0:T(8,128)(2,1)S(1)} %collective-permute-done.6.rest_2_), channel_id=1, source_target_pairs={{0,1},{1,0},{2,3},{3,2},{4,5},{5,4},{6,7},{7,6},{8,9},{9,8},{10,11... | collective-permute-start | bytes 737288 | tf_op jit(solution)/shard_map/ppermute | solution.py:223
  34.4 2.7 %collective-permute-start.14 = (bf16[1,64,640]{2,1,0:T(8,128)(2,1)S(1)}, bf16[1,64,640]{2,1,0:T(8,128)(2,1)S(1)}, u32[]{:S(2)}, u32[]{:S(2)}) collective-permute-start(bf16[1,64,640]{2,1,0:T(8,128)(2,1)S(1)} %collective-permute-done.13.rest_5_), channel_id=1, source_target_pairs={{0,1},{1,0},{2,3},{3,2},{4,5},{5,4},{6,7},{7,6},{8,9},{9,8},{10,11... | collective-permute-start | bytes 245768 | tf_op jit(solution)/shard_map/ppermute | solution.py:223
  34.9 2.1 %collective-permute-start.20 = (bf16[1,64,640]{2,1,0:T(8,128)(2,1)S(1)}, bf16[1,64,640]{2,1,0:T(8,128)(2,1)S(1)}, u32[]{:S(2)}, u32[]{:S(2)}) collective-permute-start(bf16[1,64,640]{2,1,0:T(8,128)(2,1)S(1)} %collective-permute-done.19.rest_8_), channel_id=1, source_target_pairs={{0,1},{1,0},{2,3},{3,2},{4,5},{5,4},{6,7},{7,6},{8,9},{9,8},{10,11... | collective-permute-start | bytes 245768 | tf_op jit(solution)/shard_map/ppermute | solution.py:223
  35.0 2.1 %collective-permute-start.16 = (bf16[2,64,640]{2,1,0:T(8,128)(2,1)S(1)}, bf16[2,64,640]{2,1,0:T(8,128)(2,1)S(1)}, u32[]{:S(2)}, u32[]{:S(2)}) collective-permute-start(bf16[2,64,640]{2,1,0:T(8,128)(2,1)S(1)} %collective-permute-done.15.rest_6_), channel_id=1, source_target_pairs={{0,1},{1,0},{2,3},{3,2},{4,5},{5,4},{6,7},{7,6},{8,9},{9,8},{10,11... | collective-permute-start | bytes 491528 | tf_op jit(solution)/shard_map/ppermute | solution.py:223
  36.2 0.8 %copy-start.5 = (bf16[640,384]{1,0:T(8,128)(2,1)}, bf16[640,384]{1,0:T(8,128)(2,1)S(1)}, u32[]{:S(2)}) copy-start(bf16[640,384]{1,0:T(8,128)(2,1)S(1)} %get-tuple-element.40.late_ref) | copy-start | bytes 1474564
  37.1 0.9 %copy-start.3 = (bf16[3,64,640]{2,1,0:T(8,128)(2,1)S(1)}, bf16[3,64,640]{2,1,0:T(8,128)(2,1)}, u32[]{:S(2)}) copy-start(bf16[3,64,640]{2,1,0:T(8,128)(2,1)} %copy-done.2) | copy-start | bytes 737284
  38.8 4.1 %copy-start.4 = (f32[2048]{0:T(1024)S(1)}, f32[2048]{0:T(1024)}, u32[]{:S(2)}) copy-start(f32[2048]{0:T(1024)} %param.11) | copy-start | bytes 24580
  42.3 1.0 %copy-start.6 = (bf16[640,384]{1,0:T(8,128)(2,1)S(1)}, bf16[640,384]{1,0:T(8,128)(2,1)}, u32[]{:S(2)}) copy-start(bf16[640,384]{1,0:T(8,128)(2,1)} %copy-done.5) | copy-start | bytes 1474564

commit v11 on v9

--- a/solution.py
+++ b/solution.py
@@ -221,7 +221,7 @@
     stores = [near, last, far, last_x, near_y, last_y] + far_y
     stores += [lax.ppermute(x, "head", swap) for x in stores]
     gate = attn_gate.reshape(-1, DH)
-    late = 3 * DH
+    late = 4 * DH
     size = 2 * images * lat
     first, last_columns = pl.pallas_call(
         own_kernel,

time: 59 us -> 59 us (level)
  waiting for transfers between devices: 13.1 us -> 13.9 us
  local copies, waits for them, and re-layouts: 5.24 us -> 4.53 us
    all_to_all x1, waiting for transfers between devices: 3.49 us -> 4.28 us  [by_heads(): lax.all_to_all(outgoing, ('groups', 'ctx'), split_axis=0, concat_axis=0,...]
    unnamed x14 -> x10, local copies, waits for them, and re-layouts: 3.09 us -> 2.38 us
where the time goes in v11:
time: 59 us; the launch traced here: 58.7 us
  starting transfers between devices  20.8 us (35%)
  waiting for transfers between devices  13.9 us (24%)
  blocking collectives  12.6 us (21%)
  Pallas kernels  5.98 us (10%)
  local copies, waits for them, and re-layouts  4.53 us (8%)
  other arithmetic  0.74 us (1%)
    all_to_all x1, blocking collectives, by_heads(): back = lax.all_to_all(gated, every, split_axis=0, concat_axis=0, tiled=True)  12.6 us
    ppermute x6, starting transfers between devices, across(): return lax.ppermute(x, 'ctx', [(i, i ^ turn) for i in range(ctx_count)])  9.64 us
    all_to_all x1, waiting for transfers between devices, by_heads(): lax.all_to_all(outgoing, ('groups', 'ctx'), split_axis=0, concat_axis=0,...  4.28 us
    all_to_all x1, starting transfers between devices, by_heads(): lax.all_to_all(outgoing, ('groups', 'ctx'), split_axis=0, concat_axis=0,...  3.91 us
    ppermute x1, waiting for transfers between devices, by_heads(): last_y = lax.ppermute(last, 'groups', swap)  3.27 us
    ppermute x6, waiting for transfers between devices, across(): return lax.ppermute(x, 'ctx', [(i, i ^ turn) for i in range(ctx_count)])  2.5 us
    unnamed x10, local copies, waits for them, and re-layouts  2.38 us
    pallas_call x1, Pallas kernels, by_heads(): pl.pallas_call(attend_kernel, out_shape=jax.ShapeDtypeStruct((ctx_count *...  1.92 us
  transfers between devices with their start and end apart: 22, of which 9 were waited for; matrix products, arithmetic and copies ran while one was open for 3% of the time, Pallas kernels for 5%

profile of v11, /device:TPU:0, one launch (start us, length us, event | category | flops | bytes accessed | tf_op | source)
XLA Modules:
  0.0 58.7 jit_solution(6138080582334841083)
XLA Ops:
  0.0 0.0 copy-start
  0.0 1.0 %dynamic-slice_bitcast_fusion = bf16[64,640]{1,0:T(8,128)(2,1)S(1)} fusion(bf16[1,64,1280]{2,1,0:T(8,128)(2,1)} %param.7, s32[]{:T(128)S(6)} %select_n.6), kind=kLoop, calls=%fused_computation.1 | loop fusion | bytes 163844 | tf_op jit(solution)/shard_map/dynamic_slice | solution.py:186
  1.0 3.0 %collective-permute-start.2 = (bf16[64,640]{1,0:T(8,128)(2,1)S(1)}, bf16[64,640]{1,0:T(8,128)(2,1)S(1)}, u32[]{:S(2)}, u32[]{:S(2)}) collective-permute-start(bf16[64,640]{1,0:T(8,128)(2,1)S(1)} %dynamic-slice_bitcast_fusion), channel_id=1, source_target_pairs={{0,4},{2,6},{4,0},{6,2},{8,12},{10,14},{12,8},{14,10},{1,5},{3,7},... | collective-permute-start | bytes 245768 | tf_op jit(solution)/shard_map/ppermute | solution.py:184
  4.0 2.6 %collective-permute-start.3 = (bf16[64,640]{1,0:T(8,128)(2,1)S(1)}, bf16[64,640]{1,0:T(8,128)(2,1)S(1)}, u32[]{:S(2)}, u32[]{:S(2)}) collective-permute-start(bf16[64,640]{1,0:T(8,128)(2,1)S(1)} %dynamic-slice_bitcast_fusion), channel_id=1, source_target_pairs={{0,8},{2,10},{4,12},{6,14},{8,0},{10,2},{12,4},{14,6},{1,9},{3,11}... | collective-permute-start | bytes 245768 | tf_op jit(solution)/shard_map/ppermute | solution.py:184
  6.6 0.7 %pad_add_fusion.meta_ref = s32[3,5]{1,0:T(4,128)S(1)} fusion(s32[1,5]{1,0:T(1,128)} %bitcast.23, s32[2,5]{1,0:T(2,128)} %bitcast.22), kind=kLoop, calls=%fused_computation.2 | loop fusion | flops 15 | bytes 120 | tf_op jit(solution)/shard_map/concatenate | solution.py:188
  7.3 1.5 %collective-permute-start.1 = (s32[3,5]{1,0:T(4,128)S(1)}, s32[3,5]{1,0:T(4,128)S(1)}, u32[]{:S(2)}, u32[]{:S(2)}) collective-permute-start(s32[3,5]{1,0:T(4,128)S(1)} %pad_add_fusion.meta_ref), channel_id=1, source_target_pairs={{0,16},{16,0},{1,17},{17,1},{2,18},{18,2},{3,19},{19,3},{4,20},{20... | collective-permute-start | bytes 188 | tf_op jit(solution)/shard_map/ppermute | solution.py:199
  8.8 0.9 %copy-done.1 = bf16[32,4096]{1,0:T(8,128)(2,1)S(1)} copy-done((bf16[32,4096]{1,0:T(8,128)(2,1)S(1)}, bf16[32,4096]{1,0:T(8,128)(2,1)}, u32[]{:S(2)}) %copy-start.1) | copy-done | bytes 262168
  9.8 0.1 shard_map.64
  9.9 0.1 collective-permute-start
  9.9 0.0 copy-done
  10.0 0.5 constant_dynamic-slice_fusion
  10.4 0.4 reshape.13
  10.8 0.3 copy.8
  11.1 0.2 collective-permute-done.rest_1_
  11.3 1.0 %shard_map.65 = bf16[16,224,128]{2,1,0:T(8,128)(2,1)} custom-call(bf16[16,160,128]{2,1,0:T(8,128)(2,1)S(1)} %bitcast.12, bf16[16,32,128]{2,1,0:T(8,128)(2,1)S(1)} %get-tuple-element.25.rest_0_, bf16[16,32,128]{2,1,0:T(8,128)(2,1)S(1)} %collective-permute-done.rest_1_), custom_call_target="tpu_custom_call" | custom-call | tf_op jit(solution)/shard_map/pallas_call | solution.py:204
  12.3 0.0 collective-permute-done.1.meta_y_ref
  12.3 0.0 collective-permute-done.2
  12.3 0.0 collective-permute-done.3
  12.3 0.6 collective-permute-start.5
  12.9 1.5 %collective-permute-start.6 = (bf16[3,64,640]{2,1,0:T(8,128)(2,1)S(1)}, bf16[3,64,640]{2,1,0:T(8,128)(2,1)S(1)}, u32[]{:S(2)}, u32[]{:S(2)}) collective-permute-start(bf16[3,64,640]{2,1,0:T(8,128)(2,1)S(1)} %pad_maximum_fusion.rest_0_), channel_id=1, source_target_pairs={{0,2},{2,0},{4,6},{6,4},{8,10},{10,8},{12,14},{14,12},{1,3},{3,1},... | collective-permute-start | bytes 737288 | tf_op jit(solution)/shard_map/ppermute | solution.py:184
  14.4 0.0 collective-permute-start.4
  14.4 0.4 collective-permute-start.7
  14.9 3.9 %all-to-all-start = ((bf16[16,224,128]{2,1,0:T(8,128)(2,1)}), bf16[16,224,128]{2,1,0:T(8,128)(2,1)S(1)}, u32[]{:S(2)}, u32[]{:S(2)}) async-start(bf16[16,224,128]{2,1,0:T(8,128)(2,1)} %shard_map.65), calls=%async_computation | async-start | bytes 1835008 | tf_op jit(solution)/shard_map/all_to_all | solution.py:212
  18.8 0.5 collective-permute-done.7
  19.3 1.3 %collective-permute-done.5.rest_4_ = bf16[3,64,640]{2,1,0:T(8,128)(2,1)S(1)} collective-permute-done((bf16[3,64,640]{2,1,0:T(8,128)(2,1)S(1)}, bf16[3,64,640]{2,1,0:T(8,128)(2,1)S(1)}, u32[]{:S(2)}, u32[]{:S(2)}) %collective-permute-start.5) | collective-permute-done | bytes 245792 | tf_op jit(solution)/shard_map/ppermute | solution.py:215
  20.6 0.2 collective-permute-done.6.rest_2_
  20.8 2.0 %collective-permute-start.10 = (bf16[1,64,640]{2,1,0:T(8,128)(2,1)S(1)}, bf16[1,64,640]{2,1,0:T(8,128)(2,1)S(1)}, u32[]{:S(2)}, u32[]{:S(2)}) collective-permute-start(bf16[1,64,640]{2,1,0:T(8,128)(2,1)S(1)} %bitcast.13), channel_id=1, source_target_pairs={{0,2},{2,0},{4,6},{6,4},{8,10},{10,8},{12,14},{14,12},{1,3},{3,1},... | collective-permute-start | bytes 245768 | tf_op jit(solution)/shard_map/ppermute | solution.py:184
  22.8 1.4 %collective-permute-start.17 = (bf16[1,64,640]{2,1,0:T(8,128)(2,1)S(1)}, bf16[1,64,640]{2,1,0:T(8,128)(2,1)S(1)}, u32[]{:S(2)}, u32[]{:S(2)}) collective-permute-start(bf16[1,64,640]{2,1,0:T(8,128)(2,1)S(1)} %slice.7), channel_id=1, source_target_pairs={{0,16},{16,0},{1,17},{17,1},{2,18},{18,2},{3,19},{19,3},{4,20},{20... | collective-permute-start | bytes 245768 | tf_op jit(solution)/shard_map/ppermute | solution.py:220
  24.2 0.7 %collective-permute-start.13 = (bf16[1,64,640]{2,1,0:T(8,128)(2,1)S(1)}, bf16[1,64,640]{2,1,0:T(8,128)(2,1)S(1)}, u32[]{:S(2)}, u32[]{:S(2)}) collective-permute-start(bf16[1,64,640]{2,1,0:T(8,128)(2,1)S(1)} %bitcast.14), channel_id=1, source_target_pairs={{0,16},{16,0},{1,17},{17,1},{2,18},{18,2},{3,19},{19,3},{4,20},{20... | collective-permute-start | bytes 245768 | tf_op jit(solution)/shard_map/ppermute | solution.py:218
  24.9 0.1 collective-permute-start.15
  25.0 0.0 collective-permute-done.4.rest_0_
  25.0 0.0 collective-permute-start.8
  25.1 1.8 %collective-permute-done.10.rest_3_ = bf16[1,64,640]{2,1,0:T(8,128)(2,1)S(1)} collective-permute-done((bf16[1,64,640]{2,1,0:T(8,128)(2,1)S(1)}, bf16[1,64,640]{2,1,0:T(8,128)(2,1)S(1)}, u32[]{:S(2)}, u32[]{:S(2)}) %collective-permute-start.10) | collective-permute-done | bytes 81952 | tf_op jit(solution)/shard_map/ppermute | solution.py:184
  26.9 1.4 %collective-permute-start.19 = (bf16[1,64,640]{2,1,0:T(8,128)(2,1)S(1)}, bf16[1,64,640]{2,1,0:T(8,128)(2,1)S(1)}, u32[]{:S(2)}, u32[]{:S(2)}) collective-permute-start(bf16[1,64,640]{2,1,0:T(8,128)(2,1)S(1)} %collective-permute-done.10.rest_3_), channel_id=1, source_target_pairs={{0,16},{16,0},{1,17},{17,1},{2,18},{18,2},{3,19},{19,3},{4,20},{20... | collective-permute-start | bytes 245768 | tf_op jit(solution)/shard_map/ppermute | solution.py:220
  28.3 1.2 %collective-permute-done.17.rest_7_ = bf16[1,64,640]{2,1,0:T(8,128)(2,1)S(1)} collective-permute-done((bf16[1,64,640]{2,1,0:T(8,128)(2,1)S(1)}, bf16[1,64,640]{2,1,0:T(8,128)(2,1)S(1)}, u32[]{:S(2)}, u32[]{:S(2)}) %collective-permute-start.17) | collective-permute-done | bytes 81952 | tf_op jit(solution)/shard_map/ppermute | solution.py:220
  29.5 0.0 collective-permute-start.18
  29.5 3.3 %collective-permute-done.13.rest_5_ = bf16[1,64,640]{2,1,0:T(8,128)(2,1)S(1)} collective-permute-done((bf16[1,64,640]{2,1,0:T(8,128)(2,1)S(1)}, bf16[1,64,640]{2,1,0:T(8,128)(2,1)S(1)}, u32[]{:S(2)}, u32[]{:S(2)}) %collective-permute-start.13) | collective-permute-done | bytes 81952 | tf_op jit(solution)/shard_map/ppermute | solution.py:218
  32.8 0.0 collective-permute-start.11
  32.8 0.0 collective-permute-done.8.rest_1_
  32.8 0.5 collective-permute-start.12
  33.3 1.1 %collective-permute-done.19.rest_8_ = bf16[1,64,640]{2,1,0:T(8,128)(2,1)S(1)} collective-permute-done((bf16[1,64,640]{2,1,0:T(8,128)(2,1)S(1)}, bf16[1,64,640]{2,1,0:T(8,128)(2,1)S(1)}, u32[]{:S(2)}, u32[]{:S(2)}) %collective-permute-start.19) | collective-permute-done | bytes 81952 | tf_op jit(solution)/shard_map/ppermute | solution.py:220
  34.4 0.0 collective-permute-start.9
  34.4 0.0 collective-permute-done.18.rest_7_
  34.4 0.5 collective-permute-start.14
  34.9 0.0 collective-permute-done.11.rest_3_
  34.9 0.1 collective-permute-start.20
  35.0 0.0 collective-permute-done.15.rest_6_
  35.0 0.4 collective-permute-start.16
  35.4 0.9 %shard_map.66 = (bf16[640,128]{1,0:T(8,128)(2,1)S(1)}, bf16[640,512]{1,0:T(8,128)(2,1)S(1)}) custom-call(s32[3,5]{1,0:T(4,128)S(1)} %pad_add_fusion.meta_ref, s32[3,5]{1,0:T(4,128)S(1)} %collective-permute-done.1.meta_y_ref, bf16[3,64,640]{2,1,0:T(8,128)(2,1)S(1)} %pad_maximum_fusion.rest_0_, bf16[1,64,640]{2,1,0:T(8,128)(2,1)S(1)} %bitcast.16, ...), custom_call_target="tpu_custom_call" | custom-call | flops 8049999872 | bytes 2097152 | tf_op jit(solution)/shard_map/pallas_call | solution.py:226
  36.3 0.0 copy-start.3
  36.3 0.9 %copy-done.3 = bf16[640,512]{1,0:T(8,128)(2,1)} copy-done((bf16[640,512]{1,0:T(8,128)(2,1)}, bf16[640,512]{1,0:T(8,128)(2,1)S(1)}, u32[]{:S(2)}) %copy-start.3) | copy-done | bytes 655384
  37.2 0.0 collective-permute-done.14.rest_5_
  37.2 0.0 collective-permute-done.20.rest_8_
  37.2 0.0 collective-permute-done.12.rest_4_
  37.2 0.0 collective-permute-done.9.rest_2_
  37.2 0.0 collective-permute-done.16.rest_6_
  37.2 0.9 %shard_map.67.kept_ref = bf16[640,768]{1,0:T(8,128)(2,1)S(1)} custom-call(s32[3,5]{1,0:T(4,128)S(1)} %pad_add_fusion.meta_ref, s32[3,5]{1,0:T(4,128)S(1)} %collective-permute-done.1.meta_y_ref, bf16[3,64,640]{2,1,0:T(8,128)(2,1)S(1)} %collective-permute-done.4.rest_0_, bf16[1,64,640]{2,1,0:T(8,128)(2,1)S(1)} %collective-permute-done.8.rest_1_, ...), custom_call_target="tpu_custom_call" | custom-call | flops 8049999872 | bytes 2097152 | tf_op jit(solution)/shard_map/pallas_call | solution.py:237
  38.0 0.0 copy-start.2
  38.1 4.3 %all-to-all-done.got_ref = bf16[16,224,128]{2,1,0:T(8,128)(2,1)S(1)} async-done(((bf16[16,224,128]{2,1,0:T(8,128)(2,1)}), bf16[16,224,128]{2,1,0:T(8,128)(2,1)S(1)}, u32[]{:S(2)}, u32[]{:S(2)}) %all-to-all-start) | async-done | bytes 917536 | tf_op jit(solution)/shard_map/all_to_all | solution.py:212
  42.3 0.5 shard_map.68
  42.9 0.6 copy-done.4
  43.4 1.9 %shard_map.69 = bf16[32,32,128]{2,1,0:T(8,128)(2,1)S(1)} custom-call(s32[3,5]{1,0:T(4,128)S(1)} %pad_add_fusion.meta_ref, s32[3,5]{1,0:T(4,128)S(1)} %collective-permute-done.1.meta_y_ref, f32[16,128]{1,0:T(8,128)S(1)} %bitcast.17, bf16[2,8,2,32,128]{4,3,2,1,0:T(8,128)(2,1)S(1)} %get-tuple-element.37.query_ref, ...), custom_call_target="tpu_custom_call" | custom-call | flops 20000000000 | bytes 4194304 | tf_op jit(solution)/shard_map/pallas_call | solution.py:258
  45.4 12.6 %all_to_all.10.back_ref = bf16[32,32,128]{2,1,0:T(8,128)(2,1)S(1)} all-to-all(bf16[32,32,128]{2,1,0:T(8,128)(2,1)S(1)} %shard_map.69), channel_id=1, replica_groups=mesh['groups'=2,'ctx'=8,'head'=2] {'groups','ctx','head'}, dimensions={0} | all-to-all | bytes 524288 | tf_op jit(solution)/shard_map/all_to_all | solution.py:267
  57.9 0.8 %shard_map.70 = bf16[32,4096]{1,0:T(8,128)(2,1)} custom-call(bf16[32,32,128]{2,1,0:T(8,128)(2,1)S(1)} %all_to_all.10.back_ref), custom_call_target="tpu_custom_call" | custom-call | tf_op jit(solution)/shard_map/pallas_call | solution.py:268
  (6 shorter events, 0.1 us)
Async XLA Ops:
  0.0 9.9 %copy-start = (bf16[160,2,2048]{2,1,0:T(2,128)(2,1)S(1)}, bf16[160,2,2048]{2,1,0:T(2,128)(2,1)}, u32[]{:S(2)}) copy-start(bf16[160,2,2048]{2,1,0:T(2,128)(2,1)} %param.10) | copy-start | bytes 3932164
  1.0 11.3 %collective-permute-start.2 = (bf16[64,640]{1,0:T(8,128)(2,1)S(1)}, bf16[64,640]{1,0:T(8,128)(2,1)S(1)}, u32[]{:S(2)}, u32[]{:S(2)}) collective-permute-start(bf16[64,640]{1,0:T(8,128)(2,1)S(1)} %dynamic-slice_bitcast_fusion), channel_id=1, source_target_pairs={{0,4},{2,6},{4,0},{6,2},{8,12},{10,14},{12,8},{14,10},{1,5},{3,7},... | collective-permute-start | bytes 245768 | tf_op jit(solution)/shard_map/ppermute | solution.py:184
  4.0 8.3 %collective-permute-start.3 = (bf16[64,640]{1,0:T(8,128)(2,1)S(1)}, bf16[64,640]{1,0:T(8,128)(2,1)S(1)}, u32[]{:S(2)}, u32[]{:S(2)}) collective-permute-start(bf16[64,640]{1,0:T(8,128)(2,1)S(1)} %dynamic-slice_bitcast_fusion), channel_id=1, source_target_pairs={{0,8},{2,10},{4,12},{6,14},{8,0},{10,2},{12,4},{14,6},{1,9},{3,11}... | collective-permute-start | bytes 245768 | tf_op jit(solution)/shard_map/ppermute | solution.py:184
  7.3 5.0 %collective-permute-start.1 = (s32[3,5]{1,0:T(4,128)S(1)}, s32[3,5]{1,0:T(4,128)S(1)}, u32[]{:S(2)}, u32[]{:S(2)}) collective-permute-start(s32[3,5]{1,0:T(4,128)S(1)} %pad_add_fusion.meta_ref), channel_id=1, source_target_pairs={{0,16},{16,0},{1,17},{17,1},{2,18},{18,2},{3,19},{19,3},{4,20},{20... | collective-permute-start | bytes 188 | tf_op jit(solution)/shard_map/ppermute | solution.py:199
  8.8 0.9 %copy-start.1 = (bf16[32,4096]{1,0:T(8,128)(2,1)S(1)}, bf16[32,4096]{1,0:T(8,128)(2,1)}, u32[]{:S(2)}) copy-start(bf16[32,4096]{1,0:T(8,128)(2,1)} %query_ref.1) | copy-start | bytes 786436
  9.9 1.4 %collective-permute-start = (bf16[16,32,128]{2,1,0:T(8,128)(2,1)S(1)}, bf16[16,32,128]{2,1,0:T(8,128)(2,1)S(1)}, u32[]{:S(2)}, u32[]{:S(2)}) collective-permute-start(bf16[16,32,128]{2,1,0:T(8,128)(2,1)S(1)} %get-tuple-element.26), channel_id=1, source_target_pairs={{0,1},{1,0},{2,3},{3,2},{4,5},{5,4},{6,7},{7,6},{8,9},{9,8},{10,11... | collective-permute-start | bytes 393224 | tf_op jit(solution)/shard_map/ppermute | solution.py:198
  12.3 8.2 %collective-permute-start.5 = (bf16[3,64,640]{2,1,0:T(8,128)(2,1)S(1)}, bf16[3,64,640]{2,1,0:T(8,128)(2,1)S(1)}, u32[]{:S(2)}, u32[]{:S(2)}) collective-permute-start(bf16[3,64,640]{2,1,0:T(8,128)(2,1)S(1)} %pad_maximum_fusion.rest_0_), channel_id=1, source_target_pairs={{0,16},{16,0},{1,17},{17,1},{2,18},{18,2},{3,19},{19,3},{4,20},{20... | collective-permute-start | bytes 737288 | tf_op jit(solution)/shard_map/ppermute | solution.py:215
  12.9 7.9 %collective-permute-start.6 = (bf16[3,64,640]{2,1,0:T(8,128)(2,1)S(1)}, bf16[3,64,640]{2,1,0:T(8,128)(2,1)S(1)}, u32[]{:S(2)}, u32[]{:S(2)}) collective-permute-start(bf16[3,64,640]{2,1,0:T(8,128)(2,1)S(1)} %pad_maximum_fusion.rest_0_), channel_id=1, source_target_pairs={{0,2},{2,0},{4,6},{6,4},{8,10},{10,8},{12,14},{14,12},{1,3},{3,1},... | collective-permute-start | bytes 737288 | tf_op jit(solution)/shard_map/ppermute | solution.py:184
  14.4 10.6 %collective-permute-start.4 = (bf16[3,64,640]{2,1,0:T(8,128)(2,1)S(1)}, bf16[3,64,640]{2,1,0:T(8,128)(2,1)S(1)}, u32[]{:S(2)}, u32[]{:S(2)}) collective-permute-start(bf16[3,64,640]{2,1,0:T(8,128)(2,1)S(1)} %pad_maximum_fusion.rest_0_), channel_id=1, source_target_pairs={{0,1},{1,0},{2,3},{3,2},{4,5},{5,4},{6,7},{7,6},{8,9},{9,8},{10,11... | collective-permute-start | bytes 737288 | tf_op jit(solution)/shard_map/ppermute | solution.py:222
  14.4 4.9 %collective-permute-start.7 = (bf16[64,640]{1,0:T(8,128)(2,1)S(1)}, bf16[64,640]{1,0:T(8,128)(2,1)S(1)}, u32[]{:S(2)}, u32[]{:S(2)}) collective-permute-start(bf16[64,640]{1,0:T(8,128)(2,1)S(1)} %collective-permute-done.3), channel_id=1, source_target_pairs={{0,4},{2,6},{4,0},{6,2},{8,12},{10,14},{12,8},{14,10},{1,5},{3,7},... | collective-permute-start | bytes 245768 | tf_op jit(solution)/shard_map/ppermute | solution.py:184
  14.9 27.5 %all-to-all-start = ((bf16[16,224,128]{2,1,0:T(8,128)(2,1)}), bf16[16,224,128]{2,1,0:T(8,128)(2,1)S(1)}, u32[]{:S(2)}, u32[]{:S(2)}) async-start(bf16[16,224,128]{2,1,0:T(8,128)(2,1)} %shard_map.65), calls=%async_computation | async-start | bytes 1835008 | tf_op jit(solution)/shard_map/all_to_all | solution.py:212
  20.8 6.1 %collective-permute-start.10 = (bf16[1,64,640]{2,1,0:T(8,128)(2,1)S(1)}, bf16[1,64,640]{2,1,0:T(8,128)(2,1)S(1)}, u32[]{:S(2)}, u32[]{:S(2)}) collective-permute-start(bf16[1,64,640]{2,1,0:T(8,128)(2,1)S(1)} %bitcast.13), channel_id=1, source_target_pairs={{0,2},{2,0},{4,6},{6,4},{8,10},{10,8},{12,14},{14,12},{1,3},{3,1},... | collective-permute-start | bytes 245768 | tf_op jit(solution)/shard_map/ppermute | solution.py:184
  22.8 6.7 %collective-permute-start.17 = (bf16[1,64,640]{2,1,0:T(8,128)(2,1)S(1)}, bf16[1,64,640]{2,1,0:T(8,128)(2,1)S(1)}, u32[]{:S(2)}, u32[]{:S(2)}) collective-permute-start(bf16[1,64,640]{2,1,0:T(8,128)(2,1)S(1)} %slice.7), channel_id=1, source_target_pairs={{0,16},{16,0},{1,17},{17,1},{2,18},{18,2},{3,19},{19,3},{4,20},{20... | collective-permute-start | bytes 245768 | tf_op jit(solution)/shard_map/ppermute | solution.py:220
  24.2 8.6 %collective-permute-start.13 = (bf16[1,64,640]{2,1,0:T(8,128)(2,1)S(1)}, bf16[1,64,640]{2,1,0:T(8,128)(2,1)S(1)}, u32[]{:S(2)}, u32[]{:S(2)}) collective-permute-start(bf16[1,64,640]{2,1,0:T(8,128)(2,1)S(1)} %bitcast.14), channel_id=1, source_target_pairs={{0,16},{16,0},{1,17},{17,1},{2,18},{18,2},{3,19},{19,3},{4,20},{20... | collective-permute-start | bytes 245768 | tf_op jit(solution)/shard_map/ppermute | solution.py:218
  24.9 10.1 %collective-permute-start.15 = (bf16[2,64,640]{2,1,0:T(8,128)(2,1)S(1)}, bf16[2,64,640]{2,1,0:T(8,128)(2,1)S(1)}, u32[]{:S(2)}, u32[]{:S(2)}) collective-permute-start(bf16[2,64,640]{2,1,0:T(8,128)(2,1)S(1)} %slice.6), channel_id=1, source_target_pairs={{0,2},{2,0},{4,6},{6,4},{8,10},{10,8},{12,14},{14,12},{1,3},{3,1},... | collective-permute-start | bytes 491528 | tf_op jit(solution)/shard_map/ppermute | solution.py:184
  25.0 7.8 %collective-permute-start.8 = (bf16[1,64,640]{2,1,0:T(8,128)(2,1)S(1)}, bf16[1,64,640]{2,1,0:T(8,128)(2,1)S(1)}, u32[]{:S(2)}, u32[]{:S(2)}) collective-permute-start(bf16[1,64,640]{2,1,0:T(8,128)(2,1)S(1)} %bitcast.15), channel_id=1, source_target_pairs={{0,1},{1,0},{2,3},{3,2},{4,5},{5,4},{6,7},{7,6},{8,9},{9,8},{10,11... | collective-permute-start | bytes 245768 | tf_op jit(solution)/shard_map/ppermute | solution.py:222
  26.9 7.5 %collective-permute-start.19 = (bf16[1,64,640]{2,1,0:T(8,128)(2,1)S(1)}, bf16[1,64,640]{2,1,0:T(8,128)(2,1)S(1)}, u32[]{:S(2)}, u32[]{:S(2)}) collective-permute-start(bf16[1,64,640]{2,1,0:T(8,128)(2,1)S(1)} %collective-permute-done.10.rest_3_), channel_id=1, source_target_pairs={{0,16},{16,0},{1,17},{17,1},{2,18},{18,2},{3,19},{19,3},{4,20},{20... | collective-permute-start | bytes 245768 | tf_op jit(solution)/shard_map/ppermute | solution.py:220
  29.5 4.9 %collective-permute-start.18 = (bf16[1,64,640]{2,1,0:T(8,128)(2,1)S(1)}, bf16[1,64,640]{2,1,0:T(8,128)(2,1)S(1)}, u32[]{:S(2)}, u32[]{:S(2)}) collective-permute-start(bf16[1,64,640]{2,1,0:T(8,128)(2,1)S(1)} %collective-permute-done.17.rest_7_), channel_id=1, source_target_pairs={{0,1},{1,0},{2,3},{3,2},{4,5},{5,4},{6,7},{7,6},{8,9},{9,8},{10,11... | collective-permute-start | bytes 245768 | tf_op jit(solution)/shard_map/ppermute | solution.py:222
  32.8 2.1 %collective-permute-start.11 = (bf16[1,64,640]{2,1,0:T(8,128)(2,1)S(1)}, bf16[1,64,640]{2,1,0:T(8,128)(2,1)S(1)}, u32[]{:S(2)}, u32[]{:S(2)}) collective-permute-start(bf16[1,64,640]{2,1,0:T(8,128)(2,1)S(1)} %collective-permute-done.10.rest_3_), channel_id=1, source_target_pairs={{0,1},{1,0},{2,3},{3,2},{4,5},{5,4},{6,7},{7,6},{8,9},{9,8},{10,11... | collective-permute-start | bytes 245768 | tf_op jit(solution)/shard_map/ppermute | solution.py:222
  32.8 4.4 %collective-permute-start.12 = (bf16[3,64,640]{2,1,0:T(8,128)(2,1)S(1)}, bf16[3,64,640]{2,1,0:T(8,128)(2,1)S(1)}, u32[]{:S(2)}, u32[]{:S(2)}) collective-permute-start(bf16[3,64,640]{2,1,0:T(8,128)(2,1)S(1)} %collective-permute-done.5.rest_4_), channel_id=1, source_target_pairs={{0,1},{1,0},{2,3},{3,2},{4,5},{5,4},{6,7},{7,6},{8,9},{9,8},{10,11... | collective-permute-start | bytes 737288 | tf_op jit(solution)/shard_map/ppermute | solution.py:222
  34.4 2.8 %collective-permute-start.9 = (bf16[3,64,640]{2,1,0:T(8,128)(2,1)S(1)}, bf16[3,64,640]{2,1,0:T(8,128)(2,1)S(1)}, u32[]{:S(2)}, u32[]{:S(2)}) collective-permute-start(bf16[3,64,640]{2,1,0:T(8,128)(2,1)S(1)} %collective-permute-done.6.rest_2_), channel_id=1, source_target_pairs={{0,1},{1,0},{2,3},{3,2},{4,5},{5,4},{6,7},{7,6},{8,9},{9,8},{10,11... | collective-permute-start | bytes 737288 | tf_op jit(solution)/shard_map/ppermute | solution.py:222
  34.4 2.8 %collective-permute-start.14 = (bf16[1,64,640]{2,1,0:T(8,128)(2,1)S(1)}, bf16[1,64,640]{2,1,0:T(8,128)(2,1)S(1)}, u32[]{:S(2)}, u32[]{:S(2)}) collective-permute-start(bf16[1,64,640]{2,1,0:T(8,128)(2,1)S(1)} %collective-permute-done.13.rest_5_), channel_id=1, source_target_pairs={{0,1},{1,0},{2,3},{3,2},{4,5},{5,4},{6,7},{7,6},{8,9},{9,8},{10,11... | collective-permute-start | bytes 245768 | tf_op jit(solution)/shard_map/ppermute | solution.py:222
  34.9 2.3 %collective-permute-start.20 = (bf16[1,64,640]{2,1,0:T(8,128)(2,1)S(1)}, bf16[1,64,640]{2,1,0:T(8,128)(2,1)S(1)}, u32[]{:S(2)}, u32[]{:S(2)}) collective-permute-start(bf16[1,64,640]{2,1,0:T(8,128)(2,1)S(1)} %collective-permute-done.19.rest_8_), channel_id=1, source_target_pairs={{0,1},{1,0},{2,3},{3,2},{4,5},{5,4},{6,7},{7,6},{8,9},{9,8},{10,11... | collective-permute-start | bytes 245768 | tf_op jit(solution)/shard_map/ppermute | solution.py:222
  35.0 2.2 %collective-permute-start.16 = (bf16[2,64,640]{2,1,0:T(8,128)(2,1)S(1)}, bf16[2,64,640]{2,1,0:T(8,128)(2,1)S(1)}, u32[]{:S(2)}, u32[]{:S(2)}) collective-permute-start(bf16[2,64,640]{2,1,0:T(8,128)(2,1)S(1)} %collective-permute-done.15.rest_6_), channel_id=1, source_target_pairs={{0,1},{1,0},{2,3},{3,2},{4,5},{5,4},{6,7},{7,6},{8,9},{9,8},{10,11... | collective-permute-start | bytes 491528 | tf_op jit(solution)/shard_map/ppermute | solution.py:222
  36.3 0.9 %copy-start.3 = (bf16[640,512]{1,0:T(8,128)(2,1)}, bf16[640,512]{1,0:T(8,128)(2,1)S(1)}, u32[]{:S(2)}) copy-start(bf16[640,512]{1,0:T(8,128)(2,1)S(1)} %get-tuple-element.40.late_ref) | copy-start | bytes 1966084
  38.0 4.8 %copy-start.2 = (f32[2048]{0:T(1024)S(1)}, f32[2048]{0:T(1024)}, u32[]{:S(2)}) copy-start(f32[2048]{0:T(1024)} %param.11) | copy-start | bytes 24580
  42.3 1.1 %copy-start.4 = (bf16[640,512]{1,0:T(8,128)(2,1)S(1)}, bf16[640,512]{1,0:T(8,128)(2,1)}, u32[]{:S(2)}) copy-start(bf16[640,512]{1,0:T(8,128)(2,1)} %copy-done.3) | copy-start | bytes 1966084
